TPU v7x, 32 devices: a whole 2x2x4 slice. The times are simulated.
32 devices in a mesh: leaf: 8 (over z, y), rhs: 4 (over x, core).
Axes of the slice: x: 2, y: 2, z: 4, core: 2. Of those that a mesh axis runs over, the one named last changes fastest.
Arguments:
- densities: bfloat16 [64, 32768], P('rhs', 'leaf'), may hold values from -6 to 6
- bases: float32 [32, 32768], P(None, 'leaf'), may hold values from -0.5 to 0.5
- near_blocks: bfloat16 [256, 8, 128, 128], P('leaf', 'rhs'), may hold values from -0.1875 to 0.1875
- near_src: int32 [256, 8], P('leaf', 'rhs'), may hold values from 0 to 55, as said below
- send_leaf: int32 [8, 6, 4], replicated, may hold values from -1 to 31, as said below
- far_src: int32 [256, 8], P('leaf'), may hold values from 0 to 31
- leaf_coupling: float32 [256, 8, 32, 32], P('leaf'), may hold values from -0.375 to 0.375
- local_transfer: float32 [8, 64, 32, 32], P('leaf'), may hold values from -0.75 to 0.75
- upper_transfer: float32 [16, 32, 32], replicated, may hold values from -0.75 to 0.75
- up_coupling: float32 [16, 3, 32, 32], replicated, may hold values from -8 to 8
Outputs:
- product: float32 [64, 32768], P('rhs', 'leaf')
Inputs may be any that keep to these rules, and one draw needn't show every extreme that they name: `send_leaf`: entry [e, j, c] is a leaf of device e (local index) whose panel e sends to its face neighbour e + o_j, or -1. Only existing face neighbours receive; the leaves of [e, j] are distinct and come before the -1 entries; every device sends exactly 4 leaves to at least one neighbour, among them its leaf 32 - 1, and exactly 4 to its neighbour at offset -s*s where that exists. `near_src`: A slot of the owner's panel buffer: below 32 a leaf of the same device, else slot 32 + j * 4 + c. It never names an empty slot, and every filled slot is named by some block of the device.
All inputs are finite; a program needn't handle non-finite values.
Results may differ from a plain program's by a relative error of at most 0.0003.
Values may be sent and summed in bfloat16 or wider, within the bound.
No kernel may reach another device: no remote copies, remote signals or barrier semaphores. Data moves between devices by JAX's collectives and lax.ppermute only.
A program may use at most 128 MiB of HBM per device.

v0:
```python
import functools

import jax
import jax.numpy as jnp
from jax import lax
from jax.experimental import pallas as pl
from jax.experimental.pallas import tpu as pltpu
from jax.sharding import Mesh
from jax.sharding import PartitionSpec as P

FACE_SIGNS = ((1, 0), (-1, 0), (1, 1), (-1, 1), (1, 2), (-1, 2))
F32 = jnp.float32
BF16 = jnp.bfloat16
LANES = 128
VMEM = pl.BlockSpec(memory_space=pltpu.VMEM)
HBM = pl.BlockSpec(memory_space=pltpu.HBM)
SMEM = pl.BlockSpec(memory_space=pltpu.SMEM)


def cube_side(device_count):
    return max((edge_len for edge_len in range(1, 65) if edge_len**3 <= device_count))


def face_offsets(device_count):
    side_len = cube_side(device_count)
    return [face_sign * side_len**axis_pos for face_sign, axis_pos in FACE_SIGNS]


def shifted(value, axis, steps):
    count = lax.axis_size(axis)
    first, last = (max(0, -steps), min(count, count - steps))
    return lax.ppermute(value, axis, [(source, source + steps) for source in range(first, last)])


def halves(value):
    high = value.astype(BF16)
    return high, (value - high.astype(F32)).astype(BF16)


def dot_nn(left, right):
    return lax.dot_general(left, right, (((1,), (0,)), ((), ())), preferred_element_type=F32)


def dot_nt(left, right):
    return lax.dot_general(left, right, (((1,), (1,)), ((), ())), preferred_element_type=F32)


def split_dot(dot, rows, right_high, right_low):
    count = rows.shape[0]
    high, low = halves(rows)
    both = jnp.concatenate([high, low], axis=0)
    out = dot(both, right_high) + dot(both, right_low)
    return out[:count] + out[count:]


def spread_bases(block, group):
    rank, lanes = block.shape
    width = lanes // group
    zero = jnp.zeros((rank, width), block.dtype)
    rows = []
    for slot in range(group):
        pieces = [zero] * group
        pieces[slot] = block[:, slot * width : (slot + 1) * width]
        rows.append(jnp.concatenate(pieces, axis=1))
    return jnp.concatenate(rows, axis=0)


def level_tiles(leaf_count, group):
    tiles = {}
    level = 1
    while level < leaf_count:
        children = 2 * level
        span = max(group, min(children, 2 * group))
        tiles[level] = [(children + first, span) for first in range(0, children, span)]
        level = children
    return tiles


def tile_mask(first, span, level, rank, group):
    row = lax.broadcasted_iota(jnp.int32, (span * rank, group * rank), 0)
    lane = lax.broadcasted_iota(jnp.int32, (span * rank, group * rank), 1)
    child = row // rank
    return (child // 2 == lane // rank) & (child + first < 4 * level)


def fetch(pairs, sems):
    copies = []
    for index, (source, target) in enumerate(pairs):
        copy = pltpu.make_async_copy(source, target, sems.at[index])
        copy.start()
        copies.append(copy)
    return copies


def up_kernel(
    dens_hbm, bases_hbm, maps_hbm, coef_ref, high_ref, low_ref, root_ref,
    dens_ref, bases_ref, maps_ref, spread_ref, sems,
):
    copies = fetch([(dens_hbm, dens_ref), (bases_hbm, bases_ref), (maps_hbm, maps_ref)], sems)
    columns, points = dens_ref.shape
    rank = bases_ref.shape[0]
    group = LANES // rank
    node_count = maps_ref.shape[2]
    leaf_count = node_count // 2
    width = points // leaf_count
    copies[0].wait()
    copies[1].wait()
    step = group * width
    coefs = []
    for first in range(0, points, step):
        high, low = halves(bases_ref[:, first : first + step])
        dens = dens_ref[:, first : first + step]
        coefs.append(
            dot_nt(dens, spread_bases(high, group)) + dot_nt(dens, spread_bases(low, group))
        )
    coef = jnp.concatenate(coefs, axis=1)
    coef_ref[...] = coef
    copies[2].wait()
    for row in range(rank):
        slab = jnp.concatenate([maps_ref[row]] * group, axis=0)
        spread_ref[pl.ds(row, node_count, stride=rank), :] = slab.T
    level = leaf_count // 2
    tiles = level_tiles(leaf_count, group)
    while level >= 1:
        parents = []
        for index, (first, span) in enumerate(tiles[level]):
            rows = slice(first * rank, (first + span) * rank)
            masked = jnp.where(tile_mask(first, span, level, rank, group), spread_ref[rows, :], 0.0)
            high, low = halves(masked)
            place = first - 2 * level
            if level > 1:
                high_ref[rows, :] = high
                low_ref[rows, :] = low
            else:
                high_ref[0 : span * rank, :] = high
                low_ref[0 : span * rank, :] = low
            lanes = slice(place * rank, (place + span) * rank)
            parents.append(split_dot(dot_nn, coef[:, lanes], high, low))
        coef = jnp.concatenate(parents, axis=1) if len(parents) > 1 else parents[0]
        level //= 2
    high = coef.astype(BF16).astype(F32)
    rest = coef - high
    middle = rest.astype(BF16).astype(F32)
    last = (rest - middle).astype(BF16).astype(F32)
    packed = high + pltpu.roll(middle, rank, 1) + pltpu.roll(last, 2 * rank, 1)
    root_ref[...] = packed.astype(BF16)


def select_kernel(
    faces, far_groups, extra, where_ref, send_hbm, dens_hbm, root_ref, *refs,
):
    other_refs = refs[: far_groups - 1]
    out_refs = refs[far_groups - 1 + extra : -3]
    send_ref, dens_ref, sems = refs[-3:]
    copies = fetch([(send_hbm, send_ref), (dens_hbm, dens_ref)], sems)
    device = where_ref[0]
    columns = dens_ref.shape[0]
    cap = send_ref.shape[1]
    for copy in copies:
        copy.wait()
    for (directions, stride), out_ref in zip(faces, out_refs):
        direction = directions[0]
        if len(directions) > 1:
            direction = direction + device // stride % 2
        for place in range(cap):
            leaf = jnp.maximum(send_ref[direction, place, device], 0)
            for part, panel_ref in enumerate((dens_ref, *other_refs)):
                row = (place * far_groups + part) * columns
                out_ref[row : row + columns, :] = panel_ref[
                    :, pl.ds(pl.multiple_of(leaf * LANES, LANES), LANES)
                ]
        out_ref[cap * far_groups * columns :, :] = root_ref[...]


def near_kernel(
    faces, far_groups, share, *refs,
):
    source_hbms, refs = refs[:share], refs[share:]
    dens_hbm, refs = refs[0], refs[1:]
    other_refs, refs = refs[: far_groups - 1], refs[far_groups - 1 :]
    got_refs, refs = refs[: len(faces)], refs[len(faces) :]
    block_hbm, refs = refs[0], refs[1:]
    mate_refs, refs = refs[: share - 1], refs[share - 1 :]
    out_refs, refs = refs[:far_groups], refs[far_groups:]
    source_refs, refs = refs[:share], refs[share:]
    dens_ref, block_ref, buffer_ref, small_sems, sems = refs
    columns, points = dens_ref.shape
    leaf_count, near_count, width, _ = block_ref.shape
    chunk_count = sems.shape[0]
    chunk = leaf_count // chunk_count
    copies = fetch(
        [(dens_hbm, dens_ref)] + list(zip(source_hbms, source_refs)), small_sems
    )
    block_copies = fetch(
        [
            (block_hbm.at[pl.ds(index * chunk, chunk)], block_ref.at[pl.ds(index * chunk, chunk)])
            for index in range(chunk_count)
        ],
        sems,
    )
    cap = (got_refs[0].shape[0] // columns - 1) // far_groups
    for (directions, _), got_ref in zip(faces, got_refs):
        for direction in directions:
            for place in range(cap):
                row = place * far_groups * columns
                buffer_ref[leaf_count + direction * cap + place] = got_ref[
                    row : row + far_groups * columns, :
                ]
    copies[0].wait()
    for part, panel_ref in enumerate((dens_ref, *other_refs)):
        rows = slice(part * columns, (part + 1) * columns)
        for leaf in range(leaf_count):
            buffer_ref[leaf, rows, :] = panel_ref[:, leaf * width : (leaf + 1) * width]
    for copy in copies[1:]:
        copy.wait()
    tables = list(zip(source_refs[1:], mate_refs)) + [(source_refs[0], block_ref)]
    for turn, (source_ref, blocks_ref) in enumerate(tables):
        for leaf in range(leaf_count):
            if blocks_ref is block_ref and leaf % chunk == 0:
                block_copies[leaf // chunk].wait()
            panels = [buffer_ref[source_ref[block, leaf]] for block in range(near_count)]
            blocks = [blocks_ref[leaf, block] for block in range(near_count)]
            total = dot_nt(jnp.concatenate(panels, axis=1), jnp.concatenate(blocks, axis=1))
            lanes = slice(leaf * width, (leaf + 1) * width)
            for part, out_ref in enumerate(out_refs):
                term = total[part * columns : (part + 1) * columns]
                out_ref[:, lanes] = term if turn == 0 else out_ref[:, lanes] + term


def couple_kernel(
    far_hbm, coef_ref, coupling_ref, out_ref, far_ref, turned_ref, sems,
):
    copies = fetch([(far_hbm, far_ref)], sems)
    columns, lanes = coef_ref.shape
    leaf_count, far_count, rank = coupling_ref.shape[:3]
    high, low = halves(coef_ref[...])
    both = jnp.concatenate([high.astype(F32), low.astype(F32)], axis=0)
    for first in range(0, lanes, LANES):
        turned_ref[first : first + LANES, :] = both[:, first : first + LANES].T.astype(BF16)
    copies[0].wait()
    group = LANES // rank
    parts = []
    for leaf in range(leaf_count):
        maps = jnp.concatenate([coupling_ref[leaf, j] for j in range(far_count)], axis=1)
        maps = jnp.concatenate(halves(maps), axis=0)
        picked = jnp.concatenate(
            [
                turned_ref[pl.ds(pl.multiple_of(far_ref[j, leaf] * rank, rank), rank), :]
                for j in range(far_count)
            ],
            axis=0,
        )
        out = dot_nn(maps, picked)
        parts.append(out[:rank] + out[rank:])
        if len(parts) == group:
            turned = jnp.concatenate(parts, axis=0).T
            spot = (leaf + 1 - group) * rank
            out_ref[:, spot : spot + LANES] = turned[:columns] + turned[columns:]
            parts = []


def far_kernel(
    roots, where_ref, near_ref, local_ref, bases_ref, high_ref, low_ref, upper_hbm, cross_hbm,
    *refs,
):
    root_refs = refs[: len(roots)]
    out_ref, upper_ref, cross_ref, tree_ref, sems = refs[len(roots) :]
    copies = fetch([(upper_hbm, upper_ref), (cross_hbm, cross_ref)], sems)
    device = where_ref[0]
    columns, points = near_ref.shape
    rank = bases_ref.shape[0]
    group = LANES // rank
    leaf_count = high_ref.shape[0] // (2 * rank)
    device_count = upper_ref.shape[0] // 2
    lane = lax.broadcasted_iota(jnp.int32, (LANES, rank), 0)
    column = lax.broadcasted_iota(jnp.int32, (LANES, rank), 1)
    gather = jnp.where((lane % rank == column) & (lane < 3 * rank), 1.0, 0.0).astype(BF16)
    for tiles, root_ref in zip(roots, root_refs):
        if tiles is None:
            for index in range(device_count):
                tree_ref[device_count + index] = dot_nn(root_ref[index], gather)
        else:
            for turn, row in tiles:
                piece = root_ref[row : row + columns, :]
                tree_ref[device_count + (device ^ turn)] = dot_nn(piece, gather)
    for copy in copies:
        copy.wait()
    level = device_count // 2
    while level >= 4:
        for node in range(level, 2 * level):
            total = None
            for child in (2 * node, 2 * node + 1):
                term = split_dot(dot_nn, tree_ref[child], *halves(upper_ref[child]))
                total = term if total is None else total + term
            tree_ref[node] = total
        level //= 2
    field = None
    level = 4
    while level <= device_count:
        place = device // (device_count // level)
        node = level + place
        third = jnp.where(place % 2 == 0, place + 3, place - 3)
        total = None
        for slot, other in enumerate((place - 2, place + 2, third)):
            inside = (other >= 0) & (other < level)
            value = tree_ref[level + jnp.clip(other, 0, level - 1)]
            value = jnp.where(inside, value, 0.0)
            term = split_dot(dot_nt, value, *halves(cross_ref[node, slot]))
            total = term if total is None else total + term
        if field is not None:
            total = total + split_dot(dot_nt, field, *halves(upper_ref[node]))
        field = total
        level *= 2
    field = jnp.concatenate([field, jnp.zeros((columns, LANES - rank), F32)], axis=1)
    tiles = level_tiles(leaf_count, group)
    level = 1
    while level < leaf_count:
        children = []
        for index, (first, span) in enumerate(tiles[level]):
            start = first * rank if level > 1 else 0
            rows = slice(start, start + span * rank)
            lanes = slice(index * LANES, (index + 1) * LANES)
            children.append(split_dot(dot_nt, field[:, lanes], high_ref[rows, :], low_ref[rows, :]))
        field = jnp.concatenate(children, axis=1) if len(children) > 1 else children[0]
        level *= 2
    width = points // leaf_count
    step = group * width
    for index in range(leaf_count // group):
        lanes = slice(index * LANES, (index + 1) * LANES)
        rows = field[:, lanes] + local_ref[:, lanes]
        spots = slice(index * step, (index + 1) * step)
        high, low = halves(bases_ref[:, spots])
        out_ref[:, spots] = near_ref[:, spots] + split_dot(
            dot_nn, rows, spread_bases(high, group), spread_bases(low, group)
        )


def hbm(value):
    return pltpu.with_memory_space_constraint(value, pltpu.HBM)


def hint(micros):
    return pl.CostEstimate(flops=0, bytes_accessed=int(micros * 3.69e6), transcendentals=0)


def local(
    densities,
    bases,
    near_blocks,
    near_src,
    send_leaf,
    far_src,
    leaf_coupling,
    local_transfer,
    upper_transfer,
    up_coupling,
):
    leaf_devices = lax.axis_size("leaf")
    far_groups = lax.axis_size("far")
    share = lax.axis_size("mate")
    side = cube_side(leaf_devices)
    offsets = face_offsets(leaf_devices)
    columns, points = densities.shape
    leaf_count, near_count, width, _ = near_blocks.shape
    rank = bases.shape[0]
    cap = send_leaf.shape[2]
    node_count = local_transfer.shape[1]
    where = lax.axis_index("leaf").astype(jnp.int32).reshape(1)
    params = pltpu.CompilerParams(vmem_limit_bytes=16 * 2**20)
    dma = pltpu.SemaphoreType.DMA

    def rotated(value, axis, shift):
        count = lax.axis_size(axis)
        return lax.ppermute(value, axis, [(i, (i - shift) % count) for i in range(count)])

    def crossed(value, turn):
        return lax.ppermute(value, "leaf", [(i, i ^ turn) for i in range(leaf_devices)])

    sources = near_src.T
    others = [rotated(densities, "far", part) for part in range(1, far_groups)]
    all_sources = [sources] + [rotated(sources, "mate", part) for part in range(1, share)]
    coef, high, low, root = pl.pallas_call(
        up_kernel,
        out_shape=[
            jax.ShapeDtypeStruct((columns, leaf_count * rank), F32),
            jax.ShapeDtypeStruct((node_count * rank, LANES), BF16),
            jax.ShapeDtypeStruct((node_count * rank, LANES), BF16),
            jax.ShapeDtypeStruct((columns, LANES), BF16),
        ],
        in_specs=[HBM] * 3,
        out_specs=[VMEM] * 4,
        scratch_shapes=[
            pltpu.VMEM(densities.shape, BF16),
            pltpu.VMEM(bases.shape, F32),
            pltpu.VMEM((rank, rank, node_count), F32),
            pltpu.VMEM((node_count * rank, LANES), F32),
            dma((3,)),
        ],
        compiler_params=params,
        cost_estimate=hint(4),
        name="up",
    )(hbm(densities), hbm(bases), hbm(local_transfer[0].transpose(1, 2, 0)))

    later_blocks, others, all_sources, root = lax.optimization_barrier(
        (near_blocks, others, all_sources, root)
    )
    mate_blocks = [rotated(later_blocks, "mate", part) for part in range(1, share)]

    if side == 2:
        faces = [((2 * axis, 2 * axis + 1), 2**axis) for axis in range(3)]
    else:
        faces = [((direction,), offset) for direction, offset in enumerate(offsets)]
    send = send_leaf.transpose(1, 2, 0)
    chunk = (cap * far_groups + 1) * columns
    outgoing = pl.pallas_call(
        functools.partial(select_kernel, faces, far_groups, share - 1),
        out_shape=[jax.ShapeDtypeStruct((chunk, LANES), BF16)] * len(faces),
        in_specs=[SMEM, HBM, HBM] + [VMEM] * far_groups + [HBM] * (share - 1),
        out_specs=[VMEM] * len(faces),
        scratch_shapes=[
            pltpu.SMEM(send.shape, jnp.int32),
            pltpu.VMEM(densities.shape, BF16),
            dma((2,)),
        ],
        compiler_params=params,
        cost_estimate=hint(1),
        name="select",
    )(where, hbm(send), hbm(densities), root, *others, *all_sources[1:])
    tail = cap * far_groups * columns
    if side == 2:
        arrived = [crossed(value, stride) for (_, stride), value in zip(faces, outgoing)]
        held = jnp.concatenate([root] + [value[tail:] for value in arrived], axis=0)
        whole = leaf_devices - 1
        opposite = crossed(held, whole)
        turns = [0] + [stride for _, stride in faces]
        roots = [
            ([(0, 0)], root),
            ([(turn ^ whole, row * columns) for row, turn in enumerate(turns)], opposite),
        ]
        roots += [([(stride, tail)], value) for (_, stride), value in zip(faces, arrived)]
    else:
        arrived = [shifted(value, "leaf", stride) for (_, stride), value in zip(faces, outgoing)]
        roots = [(None, lax.all_gather(root, "leaf", axis=0))]

    slots = leaf_count + len(offsets) * cap
    partials = pl.pallas_call(
        functools.partial(near_kernel, faces, far_groups, share),
        out_shape=[jax.ShapeDtypeStruct((columns, points), F32)] * far_groups,
        in_specs=[HBM] * (share + 1)
        + [VMEM] * (far_groups - 1 + len(faces))
        + [HBM]
        + [VMEM] * (share - 1),
        out_specs=[VMEM] * far_groups,
        scratch_shapes=[pltpu.SMEM(sources.shape, jnp.int32)] * share
        + [
            pltpu.VMEM(densities.shape, BF16),
            pltpu.VMEM(near_blocks.shape, BF16),
            pltpu.VMEM((slots, far_groups * columns, width), BF16),
            dma((1 + share,)),
            dma((4,)),
        ],
        compiler_params=params,
        cost_estimate=hint(3),
        name="near",
    )(
        *map(hbm, all_sources), hbm(densities), *others, *arrived, hbm(near_blocks), *mate_blocks,
    )
    received = [rotated(partials[part], "far", -part) for part in range(1, far_groups)]
    far_table = far_src.T
    leaf_local = pl.pallas_call(
        couple_kernel,
        out_shape=jax.ShapeDtypeStruct(coef.shape, F32),
        in_specs=[HBM, VMEM, VMEM],
        out_specs=VMEM,
        scratch_shapes=[
            pltpu.SMEM(far_table.shape, jnp.int32),
            pltpu.VMEM((leaf_count * rank, 2 * columns), BF16),
            dma((1,)),
        ],
        compiler_params=params,
        cost_estimate=hint(2),
        name="couple",
    )(hbm(far_table), coef, leaf_coupling)
    total = pl.pallas_call(
        functools.partial(far_kernel, [tiles for tiles, _ in roots]),
        out_shape=jax.ShapeDtypeStruct((columns, points), F32),
        in_specs=[SMEM] + [VMEM] * 5 + [HBM] * 2 + [VMEM] * len(roots),
        out_specs=VMEM,
        scratch_shapes=[
            pltpu.VMEM(upper_transfer.shape, F32),
            pltpu.VMEM(up_coupling.shape, F32),
            pltpu.VMEM((2 * leaf_devices, columns, rank), F32),
            dma((2,)),
        ],
        compiler_params=params,
        cost_estimate=hint(2),
        name="far",
    )(
        where, partials[0], leaf_local, bases, high, low, hbm(upper_transfer), hbm(up_coupling),
        *[value for _, value in roots],
    )
    for value in received:
        total = total + value
    return total


def solution(mesh):
    leaf_devices, rhs_devices = mesh.shape["leaf"], mesh.shape["rhs"]
    share = 2 if rhs_devices % 2 == 0 else 1
    split = Mesh(
        mesh.devices.reshape(leaf_devices, rhs_devices // share, share), ("leaf", "far", "mate")
    )
    rhs = ("far", "mate")
    in_specs = (
        P(rhs, "leaf"),
        P(None, "leaf"),
        P("leaf", rhs, None, None),
        P("leaf", rhs),
        P(),
        P("leaf", None),
        P("leaf", None, None, None),
        P("leaf", None, None, None),
        P(),
        P(),
    )
    return jax.shard_map(
        local, mesh=split, in_specs=in_specs, out_specs=P(rhs, "leaf"), check_vma=False
    )
```

profile of v0, /device:TPU:0, one launch (start us, length us, event | category | flops | bytes accessed | tf_op | source)
XLA Modules:
  0.0 31.0 jit_solution(8238168247888532643)
XLA Ops:
  0.0 2.9 %collective-permute-start = (bf16[16,4096]{1,0:T(8,128)(2,1)}, bf16[16,4096]{1,0:T(8,128)(2,1)S(1)}, u32[]{:S(2)}, u32[]{:S(2)}) collective-permute-start(bf16[16,4096]{1,0:T(8,128)(2,1)} %refs_2_.1), channel_id=1, source_target_pairs={{0,2},{2,0},{1,3},{3,1},{4,6},{6,4},{5,7},{7,5},{8,10},{10,8},{9,1... | collective-permute-start | bytes 393224 | tf_op jit(solution)/shard_map/ppermute | solution.py:374
  2.9 0.0 collective-permute-start.1
  2.9 3.4 %up.1 = (f32[16,1024]{1,0:T(8,128)S(1)}, bf16[2048,128]{1,0:T(8,128)(2,1)S(1)}, bf16[2048,128]{1,0:T(8,128)(2,1)S(1)}, bf16[16,128]{1,0:T(8,128)(2,1)S(1)}) custom-call(bf16[16,4096]{1,0:T(8,128)(2,1)} %refs_2_.1, f32[32,4096]{1,0:T(8,128)} %bases_ref.1, f32[32,32,64]{2,1,0:T(8,128)} %bitcast.7), custom_call_target="tpu_custom_call" | custom-call | bytes 14760000 | tf_op jit(solution)/shard_map/up/pallas_call | solution.py:382
  6.4 0.0 collective-permute-done.1.refs_1_
  6.4 0.0 copy-start.2
  6.4 0.2 collective-permute-done.refs_0_.refs_3_
  6.6 0.4 %collective-permute-start.5 = (bf16[32,2,128,128]{3,2,1,0:T(8,128)(2,1)}, bf16[32,2,128,128]{3,2,1,0:T(8,128)(2,1)S(1)}, u32[]{:S(2)}, u32[]{:S(2)}) collective-permute-start(bf16[32,2,128,128]{3,2,1,0:T(8,128)(2,1)} %refs_7_.1), channel_id=1, source_target_pairs={{0,1},{1,0},{2,3},{3,2},{4,5},{5,4},{6,7},{7,6},{8,9},{9,8},{10,11... | collective-permute-start | bytes 6291464 | tf_op jit(solution)/shard_map/ppermute | solution.py:374
  7.0 1.0 %select.1 = (bf16[144,128]{1,0:T(8,128)(2,1)S(1)}, bf16[144,128]{1,0:T(8,128)(2,1)S(1)}, bf16[144,128]{1,0:T(8,128)(2,1)S(1)}) custom-call(s32[1]{0:T(128)} %bitcast.where_ref, s32[6,4,8]{2,1,0:T(4,128)} %bitcast.8, bf16[16,4096]{1,0:T(8,128)(2,1)} %refs_2_.1, bf16[16,128]{1,0:T(8,128)(2,1)S(1)} %get-tuple-element.23.root_ref.refs_0_, ...), custom_call_target="tpu_custom_call" | custom-call | bytes 3690000 | tf_op jit(solution)/shard_map/select/pallas_call | solution.py:415
  8.0 1.6 %collective-permute-start.2 = (bf16[144,128]{1,0:T(8,128)(2,1)S(1)}, bf16[144,128]{1,0:T(8,128)(2,1)S(1)}, u32[]{:S(2)}, u32[]{:S(2)}) collective-permute-start(bf16[144,128]{1,0:T(8,128)(2,1)S(1)} %get-tuple-element.24), channel_id=1, source_target_pairs={{0,4},{4,0},{8,12},{12,8},{16,20},{20,16},{24,28},{28,24},{1,5},{5... | collective-permute-start | bytes 110600 | tf_op jit(solution)/shard_map/ppermute | solution.py:377
  9.6 1.6 %collective-permute-start.3 = (bf16[144,128]{1,0:T(8,128)(2,1)S(1)}, bf16[144,128]{1,0:T(8,128)(2,1)S(1)}, u32[]{:S(2)}, u32[]{:S(2)}) collective-permute-start(bf16[144,128]{1,0:T(8,128)(2,1)S(1)} %get-tuple-element.25), channel_id=1, source_target_pairs={{0,8},{4,12},{8,0},{12,4},{16,24},{20,28},{24,16},{28,20},{1,9},{5... | collective-permute-start | bytes 110600 | tf_op jit(solution)/shard_map/ppermute | solution.py:377
  11.1 0.0 copy-start
  11.1 2.6 %collective-permute-start.4 = (bf16[144,128]{1,0:T(8,128)(2,1)S(1)}, bf16[144,128]{1,0:T(8,128)(2,1)S(1)}, u32[]{:S(2)}, u32[]{:S(2)}) collective-permute-start(bf16[144,128]{1,0:T(8,128)(2,1)S(1)} %get-tuple-element.26), channel_id=1, source_target_pairs={{0,16},{4,20},{8,24},{12,28},{16,0},{20,4},{24,8},{28,12},{1,17},{... | collective-permute-start | bytes 110600 | tf_op jit(solution)/shard_map/ppermute | solution.py:377
  13.7 0.0 collective-permute-done.2.refs_4_.refs_2_
  13.7 0.0 collective-permute-done.3.refs_5_.refs_3_
  13.7 2.6 %collective-permute-done.4.refs_6_.refs_4_ = bf16[144,128]{1,0:T(8,128)(2,1)S(1)} collective-permute-done((bf16[144,128]{1,0:T(8,128)(2,1)S(1)}, bf16[144,128]{1,0:T(8,128)(2,1)S(1)}, u32[]{:S(2)}, u32[]{:S(2)}) %collective-permute-start.4) | collective-permute-done | bytes 36896 | tf_op jit(solution)/shard_map/ppermute | solution.py:377
  16.3 0.0 collective-permute-done.5.refs_8_
  16.3 0.0 copy-done.2
  16.3 3.0 %near.1 = (f32[16,4096]{1,0:T(8,128)S(1)}, f32[16,4096]{1,0:T(8,128)S(1)}) custom-call(s32[2,32]{1,0:T(2,128)} %bitcast.11, s32[2,32]{1,0:T(2,128)} %copy-done.2, bf16[16,4096]{1,0:T(8,128)(2,1)} %refs_2_.1, bf16[16,4096]{1,0:T(8,128)(2,1)S(1)} %collective-permute-done.refs_0_.refs_3_, bf16[144,128]{1,0:T(8,128)(2,1)S(1)} %collective-permute-done.2.refs_4_.refs_2_, ...), custom_call_target="tpu_custom_call" | custom-call | bytes 11070000 | tf_op jit(solution)/shard_map/near/pallas_call | solution.py:446
  19.4 1.5 %collective-permute-start.7 = (f32[16,4096]{1,0:T(8,128)S(1)}, f32[16,4096]{1,0:T(8,128)S(1)}, u32[]{:S(2)}, u32[]{:S(2)}) collective-permute-start(f32[16,4096]{1,0:T(8,128)S(1)} %get-tuple-element.32), channel_id=1, source_target_pairs={{0,2},{2,0},{1,3},{3,1},{4,6},{6,4},{5,7},{7,5},{8,10},{10,8},{9,1... | collective-permute-start | bytes 786440 | tf_op jit(solution)/shard_map/ppermute | solution.py:374
  20.9 2.5 %collective-permute-start.6 = (bf16[64,128]{1,0:T(8,128)(2,1)S(1)}, bf16[64,128]{1,0:T(8,128)(2,1)S(1)}, u32[]{:S(2)}, u32[]{:S(2)}) collective-permute-start(bf16[64,128]{1,0:T(8,128)(2,1)S(1)} %pad_maximum_fusion), channel_id=1, source_target_pairs={{0,28},{4,24},{8,20},{12,16},{16,12},{20,8},{24,4},{28,0},{1,29},{... | collective-permute-start | bytes 49160 | tf_op jit(solution)/shard_map/ppermute | solution.py:377
  23.4 0.0 copy-done
  23.4 0.0 copy-start.1
  23.4 2.1 %couple.1.local_ref = f32[16,1024]{1,0:T(8,128)S(1)} custom-call(s32[8,32]{1,0:T(8,128)} %bitcast.9, f32[16,1024]{1,0:T(8,128)S(1)} %get-tuple-element.29.coef_ref, f32[32,8,32,32]{3,2,1,0:T(8,128)S(1)} %copy-done), custom_call_target="tpu_custom_call" | custom-call | bytes 7380000 | tf_op jit(solution)/shard_map/couple/pallas_call | solution.py:470
  25.5 1.9 %collective-permute-done.6.refs_1_ = bf16[64,128]{1,0:T(8,128)(2,1)S(1)} collective-permute-done((bf16[64,128]{1,0:T(8,128)(2,1)S(1)}, bf16[64,128]{1,0:T(8,128)(2,1)S(1)}, u32[]{:S(2)}, u32[]{:S(2)}) %collective-permute-start.6) | collective-permute-done | bytes 16416 | tf_op jit(solution)/shard_map/ppermute | solution.py:377
  27.4 0.0 copy-done.1
  27.4 2.9 %far.1 = f32[16,4096]{1,0:T(8,128)S(1)} custom-call(s32[1]{0:T(128)} %bitcast.where_ref, f32[16,4096]{1,0:T(8,128)S(1)} %get-tuple-element.28.near_ref, f32[16,1024]{1,0:T(8,128)S(1)} %couple.1.local_ref, f32[32,4096]{1,0:T(8,128)S(1)} %copy-done.1, bf16[2048,128]{1,0:T(8,128)(2,1)S(1)} %get-tuple-element.30.high_ref, ...), custom_call_target="tpu_custom_call" | custom-call | bytes 7380000 | tf_op jit(solution)/shard_map/far/pallas_call | solution.py:484
  30.3 0.0 collective-permute-done.7
  30.3 0.7 %add.3 = f32[16,4096]{1,0:T(8,128)} add(f32[16,4096]{1,0:T(8,128)S(1)} %far.1, f32[16,4096]{1,0:T(8,128)S(1)} %collective-permute-done.7) | non-fusion elementwise | flops 65536 | bytes 786432 | tf_op jit(solution)/shard_map/add | solution.py:503
  (4 shorter events, 0.0 us)
Async XLA Ops:
  0.0 6.6 %collective-permute-start = (bf16[16,4096]{1,0:T(8,128)(2,1)}, bf16[16,4096]{1,0:T(8,128)(2,1)S(1)}, u32[]{:S(2)}, u32[]{:S(2)}) collective-permute-start(bf16[16,4096]{1,0:T(8,128)(2,1)} %refs_2_.1), channel_id=1, source_target_pairs={{0,2},{2,0},{1,3},{3,1},{4,6},{6,4},{5,7},{7,5},{8,10},{10,8},{9,1... | collective-permute-start | bytes 393224 | tf_op jit(solution)/shard_map/ppermute | solution.py:374
  2.9 3.5 %collective-permute-start.1 = (s32[2,32]{1,0:T(2,128)}, s32[2,32]{1,0:T(2,128)S(1)}, u32[]{:S(2)}, u32[]{:S(2)}) collective-permute-start(s32[2,32]{1,0:T(2,128)} %bitcast.10), channel_id=1, source_target_pairs={{0,1},{1,0},{2,3},{3,2},{4,5},{5,4},{6,7},{7,6},{8,9},{9,8},{10,11... | collective-permute-start | bytes 776 | tf_op jit(solution)/shard_map/ppermute | solution.py:374
  6.4 9.9 %copy-start.2 = (s32[2,32]{1,0:T(2,128)}, s32[2,32]{1,0:T(2,128)S(1)}, u32[]{:S(2)}) copy-start(s32[2,32]{1,0:T(2,128)S(1)} %collective-permute-done.1.refs_1_) | copy-start | bytes 772
  6.6 9.7 %collective-permute-start.5 = (bf16[32,2,128,128]{3,2,1,0:T(8,128)(2,1)}, bf16[32,2,128,128]{3,2,1,0:T(8,128)(2,1)S(1)}, u32[]{:S(2)}, u32[]{:S(2)}) collective-permute-start(bf16[32,2,128,128]{3,2,1,0:T(8,128)(2,1)} %refs_7_.1), channel_id=1, source_target_pairs={{0,1},{1,0},{2,3},{3,2},{4,5},{5,4},{6,7},{7,6},{8,9},{9,8},{10,11... | collective-permute-start | bytes 6291464 | tf_op jit(solution)/shard_map/ppermute | solution.py:374
  8.0 5.8 %collective-permute-start.2 = (bf16[144,128]{1,0:T(8,128)(2,1)S(1)}, bf16[144,128]{1,0:T(8,128)(2,1)S(1)}, u32[]{:S(2)}, u32[]{:S(2)}) collective-permute-start(bf16[144,128]{1,0:T(8,128)(2,1)S(1)} %get-tuple-element.24), channel_id=1, source_target_pairs={{0,4},{4,0},{8,12},{12,8},{16,20},{20,16},{24,28},{28,24},{1,5},{5... | collective-permute-start | bytes 110600 | tf_op jit(solution)/shard_map/ppermute | solution.py:377
  9.6 4.2 %collective-permute-start.3 = (bf16[144,128]{1,0:T(8,128)(2,1)S(1)}, bf16[144,128]{1,0:T(8,128)(2,1)S(1)}, u32[]{:S(2)}, u32[]{:S(2)}) collective-permute-start(bf16[144,128]{1,0:T(8,128)(2,1)S(1)} %get-tuple-element.25), channel_id=1, source_target_pairs={{0,8},{4,12},{8,0},{12,4},{16,24},{20,28},{24,16},{28,20},{1,9},{5... | collective-permute-start | bytes 110600 | tf_op jit(solution)/shard_map/ppermute | solution.py:377
  11.1 12.2 %copy-start = (f32[32,8,32,32]{3,2,1,0:T(8,128)S(1)}, f32[32,8,32,32]{3,2,1,0:T(8,128)}, u32[]{:S(2)}) copy-start(f32[32,8,32,32]{3,2,1,0:T(8,128)} %coupling_ref.1) | copy-start | bytes 3145732
  11.1 5.2 %collective-permute-start.4 = (bf16[144,128]{1,0:T(8,128)(2,1)S(1)}, bf16[144,128]{1,0:T(8,128)(2,1)S(1)}, u32[]{:S(2)}, u32[]{:S(2)}) collective-permute-start(bf16[144,128]{1,0:T(8,128)(2,1)S(1)} %get-tuple-element.26), channel_id=1, source_target_pairs={{0,16},{4,20},{8,24},{12,28},{16,0},{20,4},{24,8},{28,12},{1,17},{... | collective-permute-start | bytes 110600 | tf_op jit(solution)/shard_map/ppermute | solution.py:377
  19.4 10.9 %collective-permute-start.7 = (f32[16,4096]{1,0:T(8,128)S(1)}, f32[16,4096]{1,0:T(8,128)S(1)}, u32[]{:S(2)}, u32[]{:S(2)}) collective-permute-start(f32[16,4096]{1,0:T(8,128)S(1)} %get-tuple-element.32), channel_id=1, source_target_pairs={{0,2},{2,0},{1,3},{3,1},{4,6},{6,4},{5,7},{7,5},{8,10},{10,8},{9,1... | collective-permute-start | bytes 786440 | tf_op jit(solution)/shard_map/ppermute | solution.py:374
  20.9 6.5 %collective-permute-start.6 = (bf16[64,128]{1,0:T(8,128)(2,1)S(1)}, bf16[64,128]{1,0:T(8,128)(2,1)S(1)}, u32[]{:S(2)}, u32[]{:S(2)}) collective-permute-start(bf16[64,128]{1,0:T(8,128)(2,1)S(1)} %pad_maximum_fusion), channel_id=1, source_target_pairs={{0,28},{4,24},{8,20},{12,16},{16,12},{20,8},{24,4},{28,0},{1,29},{... | collective-permute-start | bytes 49160 | tf_op jit(solution)/shard_map/ppermute | solution.py:377
  23.4 4.0 %copy-start.1 = (f32[32,4096]{1,0:T(8,128)S(1)}, f32[32,4096]{1,0:T(8,128)}, u32[]{:S(2)}) copy-start(f32[32,4096]{1,0:T(8,128)} %bases_ref.1) | copy-start | bytes 1572868
where the time goes:
time: 31.3 us; the launch traced here: 31 us
  starting transfers between devices  13 us (42%)
  Pallas kernels  12.4 us (40%)
  waiting for transfers between devices  4.72 us (15%)
  other arithmetic  0.74 us (2%)
    ppermute x4, starting transfers between devices, crossed(): lax.ppermute(value, 'leaf', [(i, i ^ turn) for i in range(leaf_devices)])  8.24 us
    ppermute x4, starting transfers between devices, rotated(): lax.ppermute(value, axis, [(i, (i - shift) % count) for i in range(count)])  4.8 us
    ppermute x4, waiting for transfers between devices, crossed(): lax.ppermute(value, 'leaf', [(i, i ^ turn) for i in range(leaf_devices)])  4.49 us
    pallas_call x1, Pallas kernels, local(): pl.pallas_call(up_kernel, out_shape=[jax.ShapeDtypeStruct((columns, leaf_...  3.44 us
    pallas_call x1, Pallas kernels, local(): pl.pallas_call(functools.partial(near_kernel, faces, far_groups, share),...  3 us
    pallas_call x1, Pallas kernels, local(): pl.pallas_call(functools.partial(far_kernel, [tiles for tiles, _ in roots...  2.88 us
    pallas_call x1, Pallas kernels, local(): pl.pallas_call(couple_kernel, out_shape=jax.ShapeDtypeStruct(coef.shape,...  2.12 us
    pallas_call x1, Pallas kernels, local(): pl.pallas_call(functools.partial(select_kernel, faces, far_groups, share...  0.96 us
  transfers between devices with their start and end apart: 8, of which 3 were waited for; matrix products, arithmetic and copies ran while one was open for 0% of the time, Pallas kernels for 30%

commit v1 on v0

v1 whole, which is shorter than its diff:
```python
import functools

import jax
import jax.numpy as jnp
from jax import lax
from jax.experimental import pallas as pl
from jax.experimental.pallas import tpu as pltpu
from jax.sharding import Mesh
from jax.sharding import PartitionSpec as P

FACE_SIGNS = ((1, 0), (-1, 0), (1, 1), (-1, 1), (1, 2), (-1, 2))
F32 = jnp.float32
BF16 = jnp.bfloat16
LANES = 128
VMEM = pl.BlockSpec(memory_space=pltpu.VMEM)
HBM = pl.BlockSpec(memory_space=pltpu.HBM)
SMEM = pl.BlockSpec(memory_space=pltpu.SMEM)


def cube_side(device_count):
    return max((edge_len for edge_len in range(1, 65) if edge_len**3 <= device_count))


def face_offsets(device_count):
    side_len = cube_side(device_count)
    return [face_sign * side_len**axis_pos for face_sign, axis_pos in FACE_SIGNS]


def shifted(value, axis, steps):
    count = lax.axis_size(axis)
    first, last = (max(0, -steps), min(count, count - steps))
    return lax.ppermute(value, axis, [(source, source + steps) for source in range(first, last)])


def halves(value):
    high = value.astype(BF16)
    return high, (value - high.astype(F32)).astype(BF16)


def dot_nn(left, right):
    return lax.dot_general(left, right, (((1,), (0,)), ((), ())), preferred_element_type=F32)


def dot_nt(left, right):
    return lax.dot_general(left, right, (((1,), (1,)), ((), ())), preferred_element_type=F32)


def split_dot(dot, rows, right_high, right_low):
    count = rows.shape[0]
    high, low = halves(rows)
    both = jnp.concatenate([high, low], axis=0)
    out = dot(both, right_high) + dot(both, right_low)
    return out[:count] + out[count:]


def spread_bases(block, group):
    rank, lanes = block.shape
    width = lanes // group
    zero = jnp.zeros((rank, width), block.dtype)
    rows = []
    for slot in range(group):
        pieces = [zero] * group
        pieces[slot] = block[:, slot * width : (slot + 1) * width]
        rows.append(jnp.concatenate(pieces, axis=1))
    return jnp.concatenate(rows, axis=0)


def fetch(pairs, sems):
    copies = []
    for index, (source, target) in enumerate(pairs):
        copy = pltpu.make_async_copy(source, target, sems.at[index])
        copy.start()
        copies.append(copy)
    return copies


def up_kernel(
    dens_hbm, bases_hbm, maps_hbm, send_hbm, source_hbm,
    dens_ref, send_ref, source_ref, high_ref, low_ref, root_ref,
    bases_ref, maps_ref, spread_ref, chain_ref, sems,
):
    copies = fetch(
        [
            (maps_hbm, maps_ref),
            (bases_hbm, bases_ref),
            (dens_hbm, dens_ref),
            (send_hbm, send_ref),
            (source_hbm, source_ref),
        ],
        sems,
    )
    columns, points = dens_ref.shape
    rank, _, node_count = maps_ref.shape
    group = LANES // rank
    leaf_count = node_count // 2
    width = points // leaf_count
    copies[0].wait()
    node = lax.broadcasted_iota(jnp.int32, (node_count, LANES), 0)
    block = lax.broadcasted_iota(jnp.int32, (node_count, LANES), 1) // rank
    parent = node // 2 % group
    for first in range(0, rank, group):
        slab = maps_ref[first : first + group].reshape(group * rank, node_count).T
        turned = [slab] + [pltpu.roll(slab, turn * rank, 1) for turn in range(1, group)]
        for row in range(group):
            placed = jnp.zeros_like(slab)
            for place in range(group):
                here = (parent == place) & (block == place)
                placed = jnp.where(here, turned[(place - row) % group], placed)
            spread_ref[pl.ds(first + row, node_count, stride=rank), :] = placed
    tile = 2 * group * rank

    def children(parents, index):
        high, low = halves(spread_ref[index * tile : (index + 1) * tile, :])
        return split_dot(dot_nt, parents, high, low)

    row = lax.broadcasted_iota(jnp.int32, (rank, LANES), 0)
    lane = lax.broadcasted_iota(jnp.int32, (rank, LANES), 1)
    level = 1
    parents = jnp.where(lane == row + rank, 1.0, 0.0)
    while level < group:
        below = children(parents, 0)
        level *= 2
        parents = below[:, (level // group) * LANES : (level // group + 1) * LANES]
    chain_ref[:, LANES : 2 * LANES] = parents
    while level < leaf_count:
        for index in range(level // group, 2 * level // group):
            lanes = slice(index * LANES, (index + 1) * LANES)
            chain_ref[:, index * tile : (index + 1) * tile] = children(chain_ref[:, lanes], index)
        level *= 2
    for copy in copies[1:]:
        copy.wait()
    step = group * width
    root = jnp.zeros((columns, rank), F32)
    for index in range(leaf_count // group):
        spots = slice(index * step, (index + 1) * step)
        start = (leaf_count // group + index) * LANES
        high, low = halves(bases_ref[:, spots])
        basis = split_dot(
            dot_nn, chain_ref[:, start : start + LANES],
            spread_bases(high, group), spread_bases(low, group),
        )
        high, low = halves(basis)
        high_ref[:, spots] = high
        low_ref[:, spots] = low
        dens = dens_ref[:, spots]
        root += dot_nt(dens, high) + dot_nt(dens, low)
    root = jnp.concatenate([root, jnp.zeros((columns, LANES - rank), F32)], axis=1)
    high = root.astype(BF16).astype(F32)
    rest = root - high
    middle = rest.astype(BF16).astype(F32)
    last = (rest - middle).astype(BF16).astype(F32)
    packed = high + pltpu.roll(middle, rank, 1) + pltpu.roll(last, 2 * rank, 1)
    root_ref[...] = packed.astype(BF16)


def select_kernel(
    faces, far_groups, where_ref, send_vmem, dens_ref, root_ref, *refs,
):
    other_refs = refs[: far_groups - 1]
    out_refs = refs[far_groups - 1 : -2]
    send_ref, sems = refs[-2:]
    copies = fetch([(send_vmem, send_ref)], sems)
    device = where_ref[0]
    columns = dens_ref.shape[0]
    cap = send_ref.shape[1]
    copies[0].wait()
    for (directions, stride), out_ref in zip(faces, out_refs):
        direction = directions[0]
        if len(directions) > 1:
            direction = direction + device // stride % 2
        for place in range(cap):
            leaf = jnp.maximum(send_ref[direction, place, device], 0)
            for part, panel_ref in enumerate((dens_ref, *other_refs)):
                row = (place * far_groups + part) * columns
                out_ref[row : row + columns, :] = panel_ref[
                    :, pl.ds(pl.multiple_of(leaf * LANES, LANES), LANES)
                ]
        out_ref[cap * far_groups * columns :, :] = root_ref[...]


def near_kernel(
    faces, far_groups, share, *refs,
):
    source_vmems, refs = refs[:share], refs[share:]
    dens_ref, refs = refs[0], refs[1:]
    other_refs, refs = refs[: far_groups - 1], refs[far_groups - 1 :]
    got_refs, refs = refs[: len(faces)], refs[len(faces) :]
    block_hbm, refs = refs[0], refs[1:]
    mate_refs, refs = refs[: share - 1], refs[share - 1 :]
    out_refs, refs = refs[:far_groups], refs[far_groups:]
    source_refs, refs = refs[:share], refs[share:]
    block_ref, buffer_ref, small_sems, sems = refs
    columns, points = dens_ref.shape
    leaf_count, near_count, width, _ = block_ref.shape
    chunk_count = sems.shape[0]
    chunk = leaf_count // chunk_count
    copies = fetch(list(zip(source_vmems, source_refs)), small_sems)
    block_copies = fetch(
        [
            (block_hbm.at[pl.ds(index * chunk, chunk)], block_ref.at[pl.ds(index * chunk, chunk)])
            for index in range(chunk_count)
        ],
        sems,
    )
    cap = (got_refs[0].shape[0] // columns - 1) // far_groups
    for (directions, _), got_ref in zip(faces, got_refs):
        for direction in directions:
            for place in range(cap):
                row = place * far_groups * columns
                buffer_ref[leaf_count + direction * cap + place] = got_ref[
                    row : row + far_groups * columns, :
                ]
    for part, panel_ref in enumerate((dens_ref, *other_refs)):
        rows = slice(part * columns, (part + 1) * columns)
        for leaf in range(leaf_count):
            buffer_ref[leaf, rows, :] = panel_ref[:, leaf * width : (leaf + 1) * width]
    for copy in copies:
        copy.wait()
    tables = list(zip(source_refs[1:], mate_refs)) + [(source_refs[0], block_ref)]
    for turn, (source_ref, blocks_ref) in enumerate(tables):
        for leaf in range(leaf_count):
            if blocks_ref is block_ref and leaf % chunk == 0:
                block_copies[leaf // chunk].wait()
            panels = [buffer_ref[source_ref[block, leaf]] for block in range(near_count)]
            blocks = [blocks_ref[leaf, block] for block in range(near_count)]
            total = dot_nt(jnp.concatenate(panels, axis=1), jnp.concatenate(blocks, axis=1))
            lanes = slice(leaf * width, (leaf + 1) * width)
            for part, out_ref in enumerate(out_refs):
                term = total[part * columns : (part + 1) * columns]
                out_ref[:, lanes] = term if turn == 0 else out_ref[:, lanes] + term


def couple_kernel(
    far_hbm, dens_ref, bases_ref, coupling_ref, near_ref, out_ref, far_ref, turned_ref, sems,
):
    copies = fetch([(far_hbm, far_ref)], sems)
    columns, points = dens_ref.shape
    leaf_count, far_count, rank = coupling_ref.shape[:3]
    width = points // leaf_count
    group = LANES // rank
    upper = lax.broadcasted_iota(jnp.int32, (rank, 2 * columns), 1) < columns
    for leaf in range(leaf_count):
        spots = slice(leaf * width, (leaf + 1) * width)
        rows = jnp.concatenate(halves(bases_ref[:, spots]), axis=0)
        dens = dens_ref[:, spots]
        twice = dot_nt(rows, jnp.concatenate([dens, dens], axis=0))
        high, low = halves(twice[:rank] + twice[rank:])
        turned_ref[leaf * rank : (leaf + 1) * rank, :] = jnp.where(
            upper, high.astype(F32), low.astype(F32)
        ).astype(BF16)
    copies[0].wait()
    parts = []
    for leaf in range(leaf_count):
        maps = jnp.concatenate([coupling_ref[leaf, j] for j in range(far_count)], axis=1)
        maps = jnp.concatenate(halves(maps), axis=0)
        picked = jnp.concatenate(
            [
                turned_ref[pl.ds(pl.multiple_of(far_ref[j, leaf] * rank, rank), rank), :]
                for j in range(far_count)
            ],
            axis=0,
        )
        out = dot_nn(maps, picked)
        parts.append(out[:rank] + out[rank:])
        if len(parts) == group:
            turned = jnp.concatenate(parts, axis=0).T
            field = turned[:columns] + turned[columns:]
            spots = slice((leaf + 1 - group) * width, (leaf + 1) * width)
            high, low = halves(bases_ref[:, spots])
            out_ref[:, spots] = near_ref[:, spots] + split_dot(
                dot_nn, field, spread_bases(high, group), spread_bases(low, group)
            )
            parts = []


def far_kernel(
    roots, added, where_ref, upper_ref, cross_ref, high_ref, low_ref, *refs,
):
    term_refs, refs = refs[:added], refs[added:]
    root_refs, refs = refs[: len(roots)], refs[len(roots) :]
    out_hbm, tile_ref, tree_ref, sum_ref, sems = refs
    device = where_ref[0]
    columns, points = sum_ref.shape
    rank = upper_ref.shape[1]
    device_count = upper_ref.shape[0] // 2
    for tiles, root_ref in zip(roots, root_refs):
        if tiles is None:
            for index in range(device_count):
                tile_ref[index] = root_ref[index]
        else:
            for turn, row in tiles:
                tile_ref[device ^ turn] = root_ref[row : row + columns, :]
    zero = jnp.zeros((LANES - 3 * rank, rank), BF16)

    def lifted(child):
        if child >= device_count:
            high, low = (
                jnp.concatenate([half] * 3 + [zero], axis=0) for half in halves(upper_ref[child])
            )
            tile = tile_ref[child - device_count]
            return dot_nn(tile, high) + dot_nn(tile, low)
        return split_dot(dot_nn, tree_ref[child], *halves(upper_ref[child]))

    level = device_count // 2
    while level >= 4:
        for node in range(level, 2 * level):
            tree_ref[node] = lifted(2 * node) + lifted(2 * node + 1)
        level //= 2
    lane = lax.broadcasted_iota(jnp.int32, (LANES, rank), 0)
    column = lax.broadcasted_iota(jnp.int32, (LANES, rank), 1)
    gather = jnp.where((lane % rank == column) & (lane < 3 * rank), 1.0, 0.0).astype(BF16)
    field = None
    level = 4
    while level <= device_count:
        place = device // (device_count // level)
        node = level + place
        third = jnp.where(place % 2 == 0, place + 3, place - 3)
        total = None
        for slot, other in enumerate((place - 2, place + 2, third)):
            inside = (other >= 0) & (other < level)
            other = jnp.clip(other, 0, level - 1)
            if level == device_count:
                value = dot_nn(tile_ref[other], gather)
            else:
                value = tree_ref[level + other]
            value = jnp.where(inside, value, 0.0)
            term = split_dot(dot_nt, value, *halves(cross_ref[node, slot]))
            total = term if total is None else total + term
        if field is not None:
            total = total + split_dot(dot_nt, field, *halves(upper_ref[node]))
        field = total
        level *= 2
    chunk_count = sems.shape[0]
    step = points // chunk_count
    copies = []
    for index in range(chunk_count):
        spots = slice(index * step, (index + 1) * step)
        total = split_dot(dot_nn, field, high_ref[:, spots], low_ref[:, spots])
        for term_ref in term_refs:
            total = total + term_ref[:, spots]
        sum_ref[:, spots] = total
        copy = pltpu.make_async_copy(
            sum_ref.at[:, pl.ds(index * step, step)],
            out_hbm.at[:, pl.ds(index * step, step)],
            sems.at[index],
        )
        copy.start()
        copies.append(copy)
    for copy in copies:
        copy.wait()


def hbm(value):
    return pltpu.with_memory_space_constraint(value, pltpu.HBM)


def hint(micros):
    return pl.CostEstimate(flops=0, bytes_accessed=int(micros * 3.69e6), transcendentals=0)


def local(
    densities,
    bases,
    near_blocks,
    near_src,
    send_leaf,
    far_src,
    leaf_coupling,
    local_transfer,
    upper_transfer,
    up_coupling,
):
    leaf_devices = lax.axis_size("leaf")
    far_groups = lax.axis_size("far")
    share = lax.axis_size("mate")
    side = cube_side(leaf_devices)
    offsets = face_offsets(leaf_devices)
    columns, points = densities.shape
    leaf_count, near_count, width, _ = near_blocks.shape
    rank = bases.shape[0]
    cap = send_leaf.shape[2]
    node_count = local_transfer.shape[1]
    where = lax.axis_index("leaf").astype(jnp.int32).reshape(1)
    params = pltpu.CompilerParams(vmem_limit_bytes=16 * 2**20)
    dma = pltpu.SemaphoreType.DMA

    def rotated(value, axis, shift):
        count = lax.axis_size(axis)
        return lax.ppermute(value, axis, [(i, (i - shift) % count) for i in range(count)])

    def crossed(value, turn):
        return lax.ppermute(value, "leaf", [(i, i ^ turn) for i in range(leaf_devices)])

    sources = near_src.T
    others = [rotated(densities, "far", part) for part in range(1, far_groups)]
    all_sources = [sources] + [rotated(sources, "mate", part) for part in range(1, share)]
    send = send_leaf.transpose(1, 2, 0)
    dens, send, sources, high, low, root = pl.pallas_call(
        up_kernel,
        out_shape=[
            jax.ShapeDtypeStruct(densities.shape, BF16),
            jax.ShapeDtypeStruct(send.shape, jnp.int32),
            jax.ShapeDtypeStruct(sources.shape, jnp.int32),
            jax.ShapeDtypeStruct((rank, points), BF16),
            jax.ShapeDtypeStruct((rank, points), BF16),
            jax.ShapeDtypeStruct((columns, LANES), BF16),
        ],
        in_specs=[HBM] * 5,
        out_specs=[VMEM] * 6,
        scratch_shapes=[
            pltpu.VMEM(bases.shape, F32),
            pltpu.VMEM((rank, rank, node_count), F32),
            pltpu.VMEM((node_count * rank, LANES), F32),
            pltpu.VMEM((rank, node_count * rank), F32),
            dma((5,)),
        ],
        compiler_params=params,
        cost_estimate=hint(3.5),
        name="up",
    )(
        hbm(densities), hbm(bases), hbm(local_transfer[0].transpose(1, 2, 0)), hbm(send),
        hbm(sources),
    )
    all_sources[0] = sources

    later_blocks, others, all_sources, root = lax.optimization_barrier(
        (near_blocks, others, all_sources, root)
    )
    mate_blocks = [rotated(later_blocks, "mate", part) for part in range(1, share)]

    if side == 2:
        faces = [((2 * axis, 2 * axis + 1), 2**axis) for axis in range(3)]
    else:
        faces = [((direction,), offset) for direction, offset in enumerate(offsets)]
    chunk = (cap * far_groups + 1) * columns
    outgoing = pl.pallas_call(
        functools.partial(select_kernel, faces, far_groups),
        out_shape=[jax.ShapeDtypeStruct((chunk, LANES), BF16)] * len(faces),
        in_specs=[SMEM] + [VMEM] * (2 + far_groups),
        out_specs=[VMEM] * len(faces),
        scratch_shapes=[
            pltpu.SMEM(send.shape, jnp.int32),
            dma((1,)),
        ],
        compiler_params=params,
        cost_estimate=hint(1),
        name="select",
    )(where, send, dens, root, *others)
    tail = cap * far_groups * columns
    if side == 2:
        arrived = [crossed(value, stride) for (_, stride), value in zip(faces, outgoing)]
        held = jnp.concatenate([root] + [value[tail:] for value in arrived], axis=0)
        whole = leaf_devices - 1
        opposite = crossed(held, whole)
        turns = [0] + [stride for _, stride in faces]
        roots = [
            ([(0, 0)], root),
            ([(turn ^ whole, row * columns) for row, turn in enumerate(turns)], opposite),
        ]
        roots += [([(stride, tail)], value) for (_, stride), value in zip(faces, arrived)]
    else:
        arrived = [shifted(value, "leaf", stride) for (_, stride), value in zip(faces, outgoing)]
        roots = [(None, lax.all_gather(root, "leaf", axis=0))]

    slots = leaf_count + len(offsets) * cap
    partials = pl.pallas_call(
        functools.partial(near_kernel, faces, far_groups, share),
        out_shape=[jax.ShapeDtypeStruct((columns, points), F32)] * far_groups,
        in_specs=[VMEM] * (share + far_groups + len(faces))
        + [HBM]
        + [VMEM] * (share - 1),
        out_specs=[VMEM] * far_groups,
        scratch_shapes=[pltpu.SMEM(sources.shape, jnp.int32)] * share
        + [
            pltpu.VMEM(near_blocks.shape, BF16),
            pltpu.VMEM((slots, far_groups * columns, width), BF16),
            dma((share,)),
            dma((4,)),
        ],
        compiler_params=params,
        cost_estimate=hint(3),
        name="near",
    )(
        *all_sources, dens, *others, *arrived, hbm(near_blocks), *mate_blocks,
    )
    received = [rotated(partials[part], "far", -part) for part in range(1, far_groups)]
    far_table = far_src.T
    partial = pl.pallas_call(
        couple_kernel,
        out_shape=jax.ShapeDtypeStruct((columns, points), F32),
        in_specs=[HBM] + [VMEM] * 4,
        out_specs=VMEM,
        scratch_shapes=[
            pltpu.SMEM(far_table.shape, jnp.int32),
            pltpu.VMEM((leaf_count * rank, 2 * columns), BF16),
            dma((1,)),
        ],
        compiler_params=params,
        cost_estimate=hint(3),
        name="couple",
    )(hbm(far_table), dens, bases, leaf_coupling, partials[0])
    terms = [partial] + received
    return pl.pallas_call(
        functools.partial(far_kernel, [tiles for tiles, _ in roots], len(terms)),
        out_shape=jax.ShapeDtypeStruct((columns, points), F32),
        in_specs=[SMEM] + [VMEM] * (4 + len(terms) + len(roots)),
        out_specs=HBM,
        scratch_shapes=[
            pltpu.VMEM((leaf_devices, columns, LANES), BF16),
            pltpu.VMEM((2 * leaf_devices, columns, rank), F32),
            pltpu.VMEM((columns, points), F32),
            dma((4,)),
        ],
        compiler_params=params,
        cost_estimate=hint(2),
        name="far",
    )(where, upper_transfer, up_coupling, high, low, *terms, *[value for _, value in roots])


def solution(mesh):
    leaf_devices, rhs_devices = mesh.shape["leaf"], mesh.shape["rhs"]
    share = 2 if rhs_devices % 2 == 0 else 1
    split = Mesh(
        mesh.devices.reshape(leaf_devices, rhs_devices // share, share), ("leaf", "far", "mate")
    )
    rhs = ("far", "mate")
    in_specs = (
        P(rhs, "leaf"),
        P(None, "leaf"),
        P("leaf", rhs, None, None),
        P("leaf", rhs),
        P(),
        P("leaf", None),
        P("leaf", None, None, None),
        P("leaf", None, None, None),
        P(),
        P(),
    )
    return jax.shard_map(
        local, mesh=split, in_specs=in_specs, out_specs=P(rhs, "leaf"), check_vma=False
    )
```

time: 31.3 us -> 28.4 us (0.907)
  waiting for transfers between devices: 4.72 us -> 3.4 us
  other arithmetic: 0.74 us -> 0.01 us
  Pallas kernels: 12.4 us -> 12 us
    pallas_call x3, Pallas kernels: 6.53 us -> 7.93 us  [the longest x1 3.92 us: local(): pl.pallas_call(up_kernel, out_shape=[jax.ShapeDtypeStruct(densities.shape...]
    pallas_call x1, Pallas kernels: 2.88 us -> 1.62 us  [local(): pl.pallas_call(functools.partial(far_kernel, [tiles for tiles, _ in roots...]
    ppermute x4, waiting for transfers between devices: 4.49 us -> 3.39 us  [crossed(): lax.ppermute(value, 'leaf', [(i, i ^ turn) for i in range(leaf_devices)])]
    add x1 -> x0, other arithmetic: 0.73 us -> none  [local(): total = total + value]
    pallas_call x1, Pallas kernels: 3 us -> 2.43 us  [local(): pl.pallas_call(functools.partial(near_kernel, faces, far_groups, share),...]
  transfers between devices with their start and end apart: 8 -> 8, of which waited for: 3 -> 2; matrix products, arithmetic and copies ran while one was open for 0% -> 0% of each run, Pallas kernels for 30% -> 28%
where the time goes in v1:
time: 28.4 us; the launch traced here: 28.3 us
  starting transfers between devices  12.8 us (45%)
  Pallas kernels  12 us (42%)
  waiting for transfers between devices  3.4 us (12%)
    ppermute x4, starting transfers between devices, crossed(): lax.ppermute(value, 'leaf', [(i, i ^ turn) for i in range(leaf_devices)])  8.23 us
    ppermute x4, starting transfers between devices, rotated(): lax.ppermute(value, axis, [(i, (i - shift) % count) for i in range(count)])  4.56 us
    pallas_call x1, Pallas kernels, local(): pl.pallas_call(up_kernel, out_shape=[jax.ShapeDtypeStruct(densities.shape...  3.92 us
    ppermute x4, waiting for transfers between devices, crossed(): lax.ppermute(value, 'leaf', [(i, i ^ turn) for i in range(leaf_devices)])  3.39 us
    pallas_call x1, Pallas kernels, local(): pl.pallas_call(couple_kernel, out_shape=jax.ShapeDtypeStruct((columns, po...  3.21 us
    pallas_call x1, Pallas kernels, local(): pl.pallas_call(functools.partial(near_kernel, faces, far_groups, share),...  2.43 us
    pallas_call x1, Pallas kernels, local(): pl.pallas_call(functools.partial(far_kernel, [tiles for tiles, _ in roots...  1.62 us
    pallas_call x1, Pallas kernels, local(): pl.pallas_call(functools.partial(select_kernel, faces, far_groups), out_s...  0.8 us
  transfers between devices with their start and end apart: 8, of which 2 were waited for; matrix products, arithmetic and copies ran while one was open for 0% of the time, Pallas kernels for 28%

profile of v1, /device:TPU:0, one launch (start us, length us, event | category | flops | bytes accessed | tf_op | source)
XLA Modules:
  0.0 28.3 jit_solution(8387555253067641388)
XLA Ops:
  0.0 2.9 %collective-permute-start = (bf16[16,4096]{1,0:T(8,128)(2,1)}, bf16[16,4096]{1,0:T(8,128)(2,1)S(1)}, u32[]{:S(2)}, u32[]{:S(2)}) collective-permute-start(bf16[16,4096]{1,0:T(8,128)(2,1)} %dens_hbm.1), channel_id=1, source_target_pairs={{0,2},{2,0},{1,3},{3,1},{4,6},{6,4},{5,7},{7,5},{8,10},{10,8},{9,1... | collective-permute-start | bytes 393224 | tf_op jit(solution)/shard_map/ppermute | solution.py:389
  2.9 0.0 collective-permute-start.1
  2.9 3.9 %up.1 = (bf16[16,4096]{1,0:T(8,128)(2,1)S(1)}, s32[6,4,8]{2,1,0:T(4,128)S(1)}, s32[2,32]{1,0:T(2,128)S(1)}, bf16[32,4096]{1,0:T(8,128)(2,1)S(1)}, bf16[32,4096]{...) custom-call(bf16[16,4096]{1,0:T(8,128)(2,1)} %dens_hbm.1, f32[32,4096]{1,0:T(8,128)} %bases_ref.1, f32[32,32,64]{2,1,0:T(8,128)} %bitcast.7, ...), custom_call_target="tpu_custom_call" | custom-call | bytes 12915000 | tf_op jit(solution)/shard_map/up/pallas_call | solution.py:398
  6.9 0.0 collective-permute-done.1.refs_1_
  6.9 0.0 collective-permute-done.refs_0_.refs_3_
  6.9 0.6 %collective-permute-start.5 = (bf16[32,2,128,128]{3,2,1,0:T(8,128)(2,1)}, bf16[32,2,128,128]{3,2,1,0:T(8,128)(2,1)S(1)}, u32[]{:S(2)}, u32[]{:S(2)}) collective-permute-start(bf16[32,2,128,128]{3,2,1,0:T(8,128)(2,1)} %refs_7_.1), channel_id=1, source_target_pairs={{0,1},{1,0},{2,3},{3,2},{4,5},{5,4},{6,7},{7,6},{8,9},{9,8},{10,11... | collective-permute-start | bytes 6291464 | tf_op jit(solution)/shard_map/ppermute | solution.py:389
  7.5 0.0 copy-start.1
  7.5 0.8 %select.1 = (bf16[144,128]{1,0:T(8,128)(2,1)S(1)}, bf16[144,128]{1,0:T(8,128)(2,1)S(1)}, bf16[144,128]{1,0:T(8,128)(2,1)S(1)}) custom-call(s32[1]{0:T(128)} %bitcast.where_ref, s32[6,4,8]{2,1,0:T(4,128)S(1)} %get-tuple-element.29.send_vmem, bf16[16,4096]{1,0:T(8,128)(2,1)S(1)} %get-tuple-element.23.dens_ref.refs_2_, ...), custom_call_target="tpu_custom_call" | custom-call | bytes 3690000 | tf_op jit(solution)/shard_map/select/pallas_call | solution.py:436
  8.3 1.6 %collective-permute-start.2 = (bf16[144,128]{1,0:T(8,128)(2,1)S(1)}, bf16[144,128]{1,0:T(8,128)(2,1)S(1)}, u32[]{:S(2)}, u32[]{:S(2)}) collective-permute-start(bf16[144,128]{1,0:T(8,128)(2,1)S(1)} %get-tuple-element.31), channel_id=1, source_target_pairs={{0,4},{4,0},{8,12},{12,8},{16,20},{20,16},{24,28},{28,24},{1,5},{5... | collective-permute-start | bytes 110600 | tf_op jit(solution)/shard_map/ppermute | solution.py:392
  9.9 1.6 %collective-permute-start.3 = (bf16[144,128]{1,0:T(8,128)(2,1)S(1)}, bf16[144,128]{1,0:T(8,128)(2,1)S(1)}, u32[]{:S(2)}, u32[]{:S(2)}) collective-permute-start(bf16[144,128]{1,0:T(8,128)(2,1)S(1)} %get-tuple-element.32), channel_id=1, source_target_pairs={{0,8},{4,12},{8,0},{12,4},{16,24},{20,28},{24,16},{28,20},{1,9},{5... | collective-permute-start | bytes 110600 | tf_op jit(solution)/shard_map/ppermute | solution.py:392
  11.4 0.0 copy-start
  11.4 2.6 %collective-permute-start.4 = (bf16[144,128]{1,0:T(8,128)(2,1)S(1)}, bf16[144,128]{1,0:T(8,128)(2,1)S(1)}, u32[]{:S(2)}, u32[]{:S(2)}) collective-permute-start(bf16[144,128]{1,0:T(8,128)(2,1)S(1)} %get-tuple-element.33), channel_id=1, source_target_pairs={{0,16},{4,20},{8,24},{12,28},{16,0},{20,4},{24,8},{28,12},{1,17},{... | collective-permute-start | bytes 110600 | tf_op jit(solution)/shard_map/ppermute | solution.py:392
  14.0 0.0 collective-permute-done.2.refs_4_
  14.0 0.0 collective-permute-done.3.refs_5_
  14.0 2.6 %collective-permute-done.4.refs_6_ = bf16[144,128]{1,0:T(8,128)(2,1)S(1)} collective-permute-done((bf16[144,128]{1,0:T(8,128)(2,1)S(1)}, bf16[144,128]{1,0:T(8,128)(2,1)S(1)}, u32[]{:S(2)}, u32[]{:S(2)}) %collective-permute-start.4) | collective-permute-done | bytes 36896 | tf_op jit(solution)/shard_map/ppermute | solution.py:392
  16.6 0.0 collective-permute-done.5.refs_8_
  16.6 2.4 %near.1 = (f32[16,4096]{1,0:T(8,128)S(1)}, f32[16,4096]{1,0:T(8,128)S(1)}) custom-call(s32[2,32]{1,0:T(2,128)S(1)} %get-tuple-element.26.refs_0_, s32[2,32]{1,0:T(2,128)S(1)} %collective-permute-done.1.refs_1_, bf16[16,4096]{1,0:T(8,128)(2,1)S(1)} %get-tuple-element.23.dens_ref.refs_2_, bf16[16,4096]{1,0:T(8,128)(2,1)S(1)} %collective-permute-done.refs_0_.refs_3_, ...), custom_call_target="tpu_custom_call" | custom-call | bytes 11070000 | tf_op jit(solution)/shard_map/near/pallas_call | solution.py:466
  19.1 1.0 %collective-permute-start.6 = (f32[16,4096]{1,0:T(8,128)S(1)}, f32[16,4096]{1,0:T(8,128)S(1)}, u32[]{:S(2)}, u32[]{:S(2)}) collective-permute-start(f32[16,4096]{1,0:T(8,128)S(1)} %get-tuple-element.36), channel_id=1, source_target_pairs={{0,2},{2,0},{1,3},{3,1},{4,6},{6,4},{5,7},{7,5},{8,10},{10,8},{9,1... | collective-permute-start | bytes 786440 | tf_op jit(solution)/shard_map/ppermute | solution.py:389
  20.1 2.5 %collective-permute-start.7 = (bf16[64,128]{1,0:T(8,128)(2,1)S(1)}, bf16[64,128]{1,0:T(8,128)(2,1)S(1)}, u32[]{:S(2)}, u32[]{:S(2)}) collective-permute-start(bf16[64,128]{1,0:T(8,128)(2,1)S(1)} %pad_maximum_fusion), channel_id=1, source_target_pairs={{0,28},{4,24},{8,20},{12,16},{16,12},{20,8},{24,4},{28,0},{1,29},{... | collective-permute-start | bytes 49160 | tf_op jit(solution)/shard_map/ppermute | solution.py:392
  22.6 0.0 copy-done.1
  22.6 0.0 copy-done
  22.6 0.0 copy-start.2
  22.6 0.0 copy-start.3
  22.6 3.2 %couple.1.refs_0_ = f32[16,4096]{1,0:T(8,128)S(1)} custom-call(s32[8,32]{1,0:T(8,128)} %bitcast.9, bf16[16,4096]{1,0:T(8,128)(2,1)S(1)} %get-tuple-element.23.dens_ref.refs_2_, f32[32,4096]{1,0:T(8,128)S(1)} %copy-done.1, f32[32,8,32,32]{3,2,1,0:T(8,128)S(1)} %copy-done, f32[16,4096]{1,0:T(8,128)S(1)} %get-tuple-element.35.near_ref), custom_call_target="tpu_custom_call" | custom-call | bytes 11070000 | tf_op jit(solution)/shard_map/couple/pallas_call | solution.py:488
  25.8 0.8 %collective-permute-done.7.refs_3_ = bf16[64,128]{1,0:T(8,128)(2,1)S(1)} collective-permute-done((bf16[64,128]{1,0:T(8,128)(2,1)S(1)}, bf16[64,128]{1,0:T(8,128)(2,1)S(1)}, u32[]{:S(2)}, u32[]{:S(2)}) %collective-permute-start.7) | collective-permute-done | bytes 16416 | tf_op jit(solution)/shard_map/ppermute | solution.py:392
  26.6 0.0 collective-permute-done.6.refs_1_
  26.6 0.0 copy-done.2
  26.6 0.0 copy-done.3
  26.6 1.6 %far.1 = f32[16,4096]{1,0:T(8,128)} custom-call(s32[1]{0:T(128)} %bitcast.where_ref, f32[16,32,32]{2,1,0:T(8,128)S(1)} %copy-done.3, f32[16,3,32,32]{3,2,1,0:T(8,128)S(1)} %copy-done.2, bf16[32,4096]{1,0:T(8,128)(2,1)S(1)} %get-tuple-element.21.high_ref, bf16[32,4096]{1,0:T(8,128)(2,1)S(1)} %get-tuple-element.22.low_ref, f32[16,4096]{1,0:T(8,128)S(1)} %couple.1.refs_0_, ...), custom_call_target="tpu_custom_call" | custom-call | bytes 7380000 | tf_op jit(solution)/shard_map/far/pallas_call | solution.py:503
  (4 shorter events, 0.0 us)
Async XLA Ops:
  0.0 6.9 %collective-permute-start = (bf16[16,4096]{1,0:T(8,128)(2,1)}, bf16[16,4096]{1,0:T(8,128)(2,1)S(1)}, u32[]{:S(2)}, u32[]{:S(2)}) collective-permute-start(bf16[16,4096]{1,0:T(8,128)(2,1)} %dens_hbm.1), channel_id=1, source_target_pairs={{0,2},{2,0},{1,3},{3,1},{4,6},{6,4},{5,7},{7,5},{8,10},{10,8},{9,1... | collective-permute-start | bytes 393224 | tf_op jit(solution)/shard_map/ppermute | solution.py:389
  2.9 3.9 %collective-permute-start.1 = (s32[2,32]{1,0:T(2,128)}, s32[2,32]{1,0:T(2,128)S(1)}, u32[]{:S(2)}, u32[]{:S(2)}) collective-permute-start(s32[2,32]{1,0:T(2,128)} %bitcast.10), channel_id=1, source_target_pairs={{0,1},{1,0},{2,3},{3,2},{4,5},{5,4},{6,7},{7,6},{8,9},{9,8},{10,11... | collective-permute-start | bytes 776 | tf_op jit(solution)/shard_map/ppermute | solution.py:389
  6.9 9.7 %collective-permute-start.5 = (bf16[32,2,128,128]{3,2,1,0:T(8,128)(2,1)}, bf16[32,2,128,128]{3,2,1,0:T(8,128)(2,1)S(1)}, u32[]{:S(2)}, u32[]{:S(2)}) collective-permute-start(bf16[32,2,128,128]{3,2,1,0:T(8,128)(2,1)} %refs_7_.1), channel_id=1, source_target_pairs={{0,1},{1,0},{2,3},{3,2},{4,5},{5,4},{6,7},{7,6},{8,9},{9,8},{10,11... | collective-permute-start | bytes 6291464 | tf_op jit(solution)/shard_map/ppermute | solution.py:389
  7.5 15.1 %copy-start.1 = (f32[32,4096]{1,0:T(8,128)S(1)}, f32[32,4096]{1,0:T(8,128)}, u32[]{:S(2)}) copy-start(f32[32,4096]{1,0:T(8,128)} %bases_ref.1) | copy-start | bytes 1572868
  8.3 5.8 %collective-permute-start.2 = (bf16[144,128]{1,0:T(8,128)(2,1)S(1)}, bf16[144,128]{1,0:T(8,128)(2,1)S(1)}, u32[]{:S(2)}, u32[]{:S(2)}) collective-permute-start(bf16[144,128]{1,0:T(8,128)(2,1)S(1)} %get-tuple-element.31), channel_id=1, source_target_pairs={{0,4},{4,0},{8,12},{12,8},{16,20},{20,16},{24,28},{28,24},{1,5},{5... | collective-permute-start | bytes 110600 | tf_op jit(solution)/shard_map/ppermute | solution.py:392
  9.9 4.2 %collective-permute-start.3 = (bf16[144,128]{1,0:T(8,128)(2,1)S(1)}, bf16[144,128]{1,0:T(8,128)(2,1)S(1)}, u32[]{:S(2)}, u32[]{:S(2)}) collective-permute-start(bf16[144,128]{1,0:T(8,128)(2,1)S(1)} %get-tuple-element.32), channel_id=1, source_target_pairs={{0,8},{4,12},{8,0},{12,4},{16,24},{20,28},{24,16},{28,20},{1,9},{5... | collective-permute-start | bytes 110600 | tf_op jit(solution)/shard_map/ppermute | solution.py:392
  11.4 11.2 %copy-start = (f32[32,8,32,32]{3,2,1,0:T(8,128)S(1)}, f32[32,8,32,32]{3,2,1,0:T(8,128)}, u32[]{:S(2)}) copy-start(f32[32,8,32,32]{3,2,1,0:T(8,128)} %coupling_ref.1) | copy-start | bytes 3145732
  11.4 5.2 %collective-permute-start.4 = (bf16[144,128]{1,0:T(8,128)(2,1)S(1)}, bf16[144,128]{1,0:T(8,128)(2,1)S(1)}, u32[]{:S(2)}, u32[]{:S(2)}) collective-permute-start(bf16[144,128]{1,0:T(8,128)(2,1)S(1)} %get-tuple-element.33), channel_id=1, source_target_pairs={{0,16},{4,20},{8,24},{12,28},{16,0},{20,4},{24,8},{28,12},{1,17},{... | collective-permute-start | bytes 110600 | tf_op jit(solution)/shard_map/ppermute | solution.py:392
  19.1 7.6 %collective-permute-start.6 = (f32[16,4096]{1,0:T(8,128)S(1)}, f32[16,4096]{1,0:T(8,128)S(1)}, u32[]{:S(2)}, u32[]{:S(2)}) collective-permute-start(f32[16,4096]{1,0:T(8,128)S(1)} %get-tuple-element.36), channel_id=1, source_target_pairs={{0,2},{2,0},{1,3},{3,1},{4,6},{6,4},{5,7},{7,5},{8,10},{10,8},{9,1... | collective-permute-start | bytes 786440 | tf_op jit(solution)/shard_map/ppermute | solution.py:389
  20.1 6.5 %collective-permute-start.7 = (bf16[64,128]{1,0:T(8,128)(2,1)S(1)}, bf16[64,128]{1,0:T(8,128)(2,1)S(1)}, u32[]{:S(2)}, u32[]{:S(2)}) collective-permute-start(bf16[64,128]{1,0:T(8,128)(2,1)S(1)} %pad_maximum_fusion), channel_id=1, source_target_pairs={{0,28},{4,24},{8,20},{12,16},{16,12},{20,8},{24,4},{28,0},{1,29},{... | collective-permute-start | bytes 49160 | tf_op jit(solution)/shard_map/ppermute | solution.py:392
  22.6 4.0 %copy-start.2 = (f32[16,3,32,32]{3,2,1,0:T(8,128)S(1)}, f32[16,3,32,32]{3,2,1,0:T(8,128)}, u32[]{:S(2)}) copy-start(f32[16,3,32,32]{3,2,1,0:T(8,128)} %cross_ref.1) | copy-start | bytes 589828
  22.6 4.0 %copy-start.3 = (f32[16,32,32]{2,1,0:T(8,128)S(1)}, f32[16,32,32]{2,1,0:T(8,128)}, u32[]{:S(2)}) copy-start(f32[16,32,32]{2,1,0:T(8,128)} %upper_ref.1) | copy-start | bytes 196612

commit v2 on v1

--- a/solution.py
+++ b/solution.py
@@ -76,8 +76,8 @@
 
 def up_kernel(
     dens_hbm, bases_hbm, maps_hbm, send_hbm, source_hbm,
-    dens_ref, send_ref, source_ref, high_ref, low_ref, root_ref,
-    bases_ref, maps_ref, spread_ref, chain_ref, sems,
+    dens_ref, bases_ref, send_ref, source_ref, high_ref, low_ref, root_ref,
+    maps_ref, spread_ref, chain_ref, sems,
 ):
     copies = fetch(
         [
@@ -154,13 +154,13 @@
 
 
 def select_kernel(
-    faces, far_groups, where_ref, send_vmem, dens_ref, root_ref, *refs,
+    faces, far_groups, send_vmem, dens_ref, root_ref, *refs,
 ):
     other_refs = refs[: far_groups - 1]
     out_refs = refs[far_groups - 1 : -2]
     send_ref, sems = refs[-2:]
     copies = fetch([(send_vmem, send_ref)], sems)
-    device = where_ref[0]
+    device = lax.axis_index("leaf")
     columns = dens_ref.shape[0]
     cap = send_ref.shape[1]
     copies[0].wait()
@@ -187,6 +187,7 @@
     got_refs, refs = refs[: len(faces)], refs[len(faces) :]
     block_hbm, refs = refs[0], refs[1:]
     mate_refs, refs = refs[: share - 1], refs[share - 1 :]
+    refs = refs[1:]
     out_refs, refs = refs[:far_groups], refs[far_groups:]
     source_refs, refs = refs[:share], refs[share:]
     block_ref, buffer_ref, small_sems, sems = refs
@@ -202,7 +203,7 @@
         ],
         sems,
     )
-    cap = (got_refs[0].shape[0] // columns - 1) // far_groups
+    cap = (buffer_ref.shape[0] - leaf_count) // len(FACE_SIGNS)
     for (directions, _), got_ref in zip(faces, got_refs):
         for direction in directions:
             for place in range(cap):
@@ -231,9 +232,18 @@
 
 
 def couple_kernel(
-    far_hbm, dens_ref, bases_ref, coupling_ref, near_ref, out_ref, far_ref, turned_ref, sems,
+    far_hbm, coupling_hbm, dens_ref, bases_ref, out_ref, far_ref, coupling_ref, turned_ref, sems,
 ):
-    copies = fetch([(far_hbm, far_ref)], sems)
+    chunk_count = sems.shape[0] - 1
+    chunk = coupling_ref.shape[0] // chunk_count
+    copies = fetch(
+        [(far_hbm, far_ref)]
+        + [
+            (coupling_hbm.at[pl.ds(index * chunk, chunk)], coupling_ref.at[pl.ds(index * chunk, chunk)])
+            for index in range(chunk_count)
+        ],
+        sems,
+    )
     columns, points = dens_ref.shape
     leaf_count, far_count, rank = coupling_ref.shape[:3]
     width = points // leaf_count
@@ -251,6 +261,8 @@
     copies[0].wait()
     parts = []
     for leaf in range(leaf_count):
+        if leaf % chunk == 0:
+            copies[1 + leaf // chunk].wait()
         maps = jnp.concatenate([coupling_ref[leaf, j] for j in range(far_count)], axis=1)
         maps = jnp.concatenate(halves(maps), axis=0)
         picked = jnp.concatenate(
@@ -264,22 +276,31 @@
         parts.append(out[:rank] + out[rank:])
         if len(parts) == group:
             turned = jnp.concatenate(parts, axis=0).T
-            field = turned[:columns] + turned[columns:]
-            spots = slice((leaf + 1 - group) * width, (leaf + 1) * width)
-            high, low = halves(bases_ref[:, spots])
-            out_ref[:, spots] = near_ref[:, spots] + split_dot(
-                dot_nn, field, spread_bases(high, group), spread_bases(low, group)
-            )
+            spot = (leaf + 1 - group) * rank
+            out_ref[:, spot : spot + LANES] = turned[:columns] + turned[columns:]
             parts = []
 
 
+def project_kernel(leaf_count, local_ref, bases_ref, near_ref, out_ref):
+    rank, points = bases_ref.shape
+    group = LANES // rank
+    step = group * points // leaf_count
+    for index in range(leaf_count // group):
+        spots = slice(index * step, (index + 1) * step)
+        high, low = halves(bases_ref[:, spots])
+        out_ref[:, spots] = near_ref[:, spots] + split_dot(
+            dot_nn, local_ref[:, index * LANES : (index + 1) * LANES],
+            spread_bases(high, group), spread_bases(low, group),
+        )
+
+
 def far_kernel(
-    roots, added, where_ref, upper_ref, cross_ref, high_ref, low_ref, *refs,
+    roots, added, upper_ref, cross_ref, high_ref, low_ref, *refs,
 ):
     term_refs, refs = refs[:added], refs[added:]
     root_refs, refs = refs[: len(roots)], refs[len(roots) :]
     out_hbm, tile_ref, tree_ref, sum_ref, sems = refs
-    device = where_ref[0]
+    device = lax.axis_index("leaf")
     columns, points = sum_ref.shape
     rank = upper_ref.shape[1]
     device_count = upper_ref.shape[0] // 2
@@ -380,7 +401,6 @@
     rank = bases.shape[0]
     cap = send_leaf.shape[2]
     node_count = local_transfer.shape[1]
-    where = lax.axis_index("leaf").astype(jnp.int32).reshape(1)
     params = pltpu.CompilerParams(vmem_limit_bytes=16 * 2**20)
     dma = pltpu.SemaphoreType.DMA
 
@@ -395,10 +415,11 @@
     others = [rotated(densities, "far", part) for part in range(1, far_groups)]
     all_sources = [sources] + [rotated(sources, "mate", part) for part in range(1, share)]
     send = send_leaf.transpose(1, 2, 0)
-    dens, send, sources, high, low, root = pl.pallas_call(
+    dens, basis, send, sources, high, low, root = pl.pallas_call(
         up_kernel,
         out_shape=[
             jax.ShapeDtypeStruct(densities.shape, BF16),
+            jax.ShapeDtypeStruct(bases.shape, F32),
             jax.ShapeDtypeStruct(send.shape, jnp.int32),
             jax.ShapeDtypeStruct(sources.shape, jnp.int32),
             jax.ShapeDtypeStruct((rank, points), BF16),
@@ -406,9 +427,8 @@
             jax.ShapeDtypeStruct((columns, LANES), BF16),
         ],
         in_specs=[HBM] * 5,
-        out_specs=[VMEM] * 6,
+        out_specs=[VMEM] * 7,
         scratch_shapes=[
-            pltpu.VMEM(bases.shape, F32),
             pltpu.VMEM((rank, rank, node_count), F32),
             pltpu.VMEM((node_count * rank, LANES), F32),
             pltpu.VMEM((rank, node_count * rank), F32),
@@ -436,7 +456,7 @@
     outgoing = pl.pallas_call(
         functools.partial(select_kernel, faces, far_groups),
         out_shape=[jax.ShapeDtypeStruct((chunk, LANES), BF16)] * len(faces),
-        in_specs=[SMEM] + [VMEM] * (2 + far_groups),
+        in_specs=[VMEM] * (2 + far_groups),
         out_specs=[VMEM] * len(faces),
         scratch_shapes=[
             pltpu.SMEM(send.shape, jnp.int32),
@@ -445,19 +465,39 @@
         compiler_params=params,
         cost_estimate=hint(1),
         name="select",
-    )(where, send, dens, root, *others)
+    )(send, dens, root, *others)
+    outgoing, dens = lax.optimization_barrier((outgoing, dens))
+    far_table = far_src.T
+    leaf_local = pl.pallas_call(
+        couple_kernel,
+        out_shape=jax.ShapeDtypeStruct((columns, leaf_count * rank), F32),
+        in_specs=[HBM] * 2 + [VMEM] * 2,
+        out_specs=VMEM,
+        scratch_shapes=[
+            pltpu.SMEM(far_table.shape, jnp.int32),
+            pltpu.VMEM(leaf_coupling.shape, F32),
+            pltpu.VMEM((leaf_count * rank, 2 * columns), BF16),
+            dma((5,)),
+        ],
+        compiler_params=params,
+        cost_estimate=hint(2.3),
+        name="couple",
+    )(hbm(far_table), hbm(leaf_coupling), dens, basis)
     tail = cap * far_groups * columns
     if side == 2:
-        arrived = [crossed(value, stride) for (_, stride), value in zip(faces, outgoing)]
-        held = jnp.concatenate([root] + [value[tail:] for value in arrived], axis=0)
-        whole = leaf_devices - 1
-        opposite = crossed(held, whole)
-        turns = [0] + [stride for _, stride in faces]
+        first, second, third = (stride for _, stride in faces)
+        arrived = [crossed(outgoing[0], first), crossed(outgoing[1], second)]
+        last = jnp.concatenate([outgoing[2], arrived[0][tail:]], axis=0)
+        arrived.append(crossed(last, third))
+        held = jnp.concatenate([root, arrived[0][tail:], arrived[2][tail:]], axis=0)
+        beside = crossed(held, second)
+        turns = [0, first, third, third ^ first]
         roots = [
             ([(0, 0)], root),
-            ([(turn ^ whole, row * columns) for row, turn in enumerate(turns)], opposite),
+            ([(first, tail)], arrived[0]),
+            ([(third, tail), (third ^ first, tail + columns)], arrived[2]),
+            ([(turn ^ second, row * columns) for row, turn in enumerate(turns)], beside),
         ]
-        roots += [([(stride, tail)], value) for (_, stride), value in zip(faces, arrived)]
     else:
         arrived = [shifted(value, "leaf", stride) for (_, stride), value in zip(faces, outgoing)]
         roots = [(None, lax.all_gather(root, "leaf", axis=0))]
@@ -468,7 +508,7 @@
         out_shape=[jax.ShapeDtypeStruct((columns, points), F32)] * far_groups,
         in_specs=[VMEM] * (share + far_groups + len(faces))
         + [HBM]
-        + [VMEM] * (share - 1),
+        + [VMEM] * share,
         out_specs=[VMEM] * far_groups,
         scratch_shapes=[pltpu.SMEM(sources.shape, jnp.int32)] * share
         + [
@@ -481,29 +521,23 @@
         cost_estimate=hint(3),
         name="near",
     )(
-        *all_sources, dens, *others, *arrived, hbm(near_blocks), *mate_blocks,
+        *all_sources, dens, *others, *arrived, hbm(near_blocks), *mate_blocks, leaf_local,
     )
     received = [rotated(partials[part], "far", -part) for part in range(1, far_groups)]
-    far_table = far_src.T
     partial = pl.pallas_call(
-        couple_kernel,
+        functools.partial(project_kernel, leaf_count),
         out_shape=jax.ShapeDtypeStruct((columns, points), F32),
-        in_specs=[HBM] + [VMEM] * 4,
+        in_specs=[VMEM] * 3,
         out_specs=VMEM,
-        scratch_shapes=[
-            pltpu.SMEM(far_table.shape, jnp.int32),
-            pltpu.VMEM((leaf_count * rank, 2 * columns), BF16),
-            dma((1,)),
-        ],
         compiler_params=params,
-        cost_estimate=hint(3),
-        name="couple",
-    )(hbm(far_table), dens, bases, leaf_coupling, partials[0])
+        cost_estimate=hint(1),
+        name="project",
+    )(leaf_local, basis, partials[0])
     terms = [partial] + received
     return pl.pallas_call(
         functools.partial(far_kernel, [tiles for tiles, _ in roots], len(terms)),
         out_shape=jax.ShapeDtypeStruct((columns, points), F32),
-        in_specs=[SMEM] + [VMEM] * (4 + len(terms) + len(roots)),
+        in_specs=[VMEM] * (4 + len(terms) + len(roots)),
         out_specs=HBM,
         scratch_shapes=[
             pltpu.VMEM((leaf_devices, columns, LANES), BF16),
@@ -514,7 +548,7 @@
         compiler_params=params,
         cost_estimate=hint(2),
         name="far",
-    )(where, upper_transfer, up_coupling, high, low, *terms, *[value for _, value in roots])
+    )(upper_transfer, up_coupling, high, low, *terms, *[value for _, value in roots])
 
 
 def solution(mesh):

time: 28.4 us -> 30.7 us (1.081)
  waiting for transfers between devices: 3.4 us -> 7.09 us
  starting transfers between devices: 12.8 us -> 10.8 us
  Pallas kernels: 12 us -> 12.4 us
    ppermute x4, starting transfers between devices: 8.23 us -> 6.32 us  [crossed(): lax.ppermute(value, 'leaf', [(i, i ^ turn) for i in range(leaf_devices)])]
    ppermute x4, waiting for transfers between devices: 3.39 us -> 5.25 us  [crossed(): lax.ppermute(value, 'leaf', [(i, i ^ turn) for i in range(leaf_devices)])]
    ppermute x4, waiting for transfers between devices: 0.01 us -> 1.85 us  [rotated(): lax.ppermute(value, axis, [(i, (i - shift) % count) for i in range(count)])]
    pallas_call x1 -> x2, Pallas kernels: 3.21 us -> 3.68 us  [the longest x1 3.32 us: local(): pl.pallas_call(couple_kernel, out_shape=jax.ShapeDtypeStruct((columns, le...]
  transfers between devices with their start and end apart: 8 -> 8, of which waited for: 2 -> 3; matrix products, arithmetic and copies ran while one was open for 0% -> 0% of each run, Pallas kernels for 28% -> 28%
where the time goes in v2:
time: 30.7 us; the launch traced here: 30.5 us
  Pallas kernels  12.4 us (40%)
  starting transfers between devices  10.8 us (35%)
  waiting for transfers between devices  7.09 us (23%)
    ppermute x4, starting transfers between devices, crossed(): lax.ppermute(value, 'leaf', [(i, i ^ turn) for i in range(leaf_devices)])  6.32 us
    ppermute x4, waiting for transfers between devices, crossed(): lax.ppermute(value, 'leaf', [(i, i ^ turn) for i in range(leaf_devices)])  5.25 us
    ppermute x4, starting transfers between devices, rotated(): lax.ppermute(value, axis, [(i, (i - shift) % count) for i in range(count)])  4.52 us
    pallas_call x1, Pallas kernels, local(): pl.pallas_call(up_kernel, out_shape=[jax.ShapeDtypeStruct(densities.shape...  3.92 us
    pallas_call x1, Pallas kernels, local(): pl.pallas_call(couple_kernel, out_shape=jax.ShapeDtypeStruct((columns, le...  3.32 us
    pallas_call x1, Pallas kernels, local(): pl.pallas_call(functools.partial(near_kernel, faces, far_groups, share),...  2.43 us
    ppermute x4, waiting for transfers between devices, rotated(): lax.ppermute(value, axis, [(i, (i - shift) % count) for i in range(count)])  1.85 us
    pallas_call x1, Pallas kernels, local(): pl.pallas_call(functools.partial(far_kernel, [tiles for tiles, _ in roots...  1.61 us
  transfers between devices with their start and end apart: 8, of which 3 were waited for; matrix products, arithmetic and copies ran while one was open for 0% of the time, Pallas kernels for 28%

profile of v2, /device:TPU:0, one launch (start us, length us, event | category | flops | bytes accessed | tf_op | source)
XLA Modules:
  0.0 30.5 jit_solution(4241622369360981301)
XLA Ops:
  0.0 2.9 %collective-permute-start = (bf16[16,4096]{1,0:T(8,128)(2,1)}, bf16[16,4096]{1,0:T(8,128)(2,1)S(1)}, u32[]{:S(2)}, u32[]{:S(2)}) collective-permute-start(bf16[16,4096]{1,0:T(8,128)(2,1)} %dens_hbm.1), channel_id=1, source_target_pairs={{0,2},{2,0},{1,3},{3,1},{4,6},{6,4},{5,7},{7,5},{8,10},{10,8},{9,1... | collective-permute-start | bytes 393224 | tf_op jit(solution)/shard_map/ppermute | solution.py:409
  2.9 0.0 collective-permute-start.1
  2.9 3.9 %up.1 = (bf16[16,4096]{1,0:T(8,128)(2,1)S(1)}, f32[32,4096]{1,0:T(8,128)S(1)}, s32[6,4,8]{2,1,0:T(4,128)S(1)}, s32[2,32]{1,0:T(2,128)S(1)}, bf16[32,4096]{1,0:T(...) custom-call(bf16[16,4096]{1,0:T(8,128)(2,1)} %dens_hbm.1, f32[32,4096]{1,0:T(8,128)} %bases_hbm.1, ...), custom_call_target="tpu_custom_call" | custom-call | bytes 12915000 | tf_op jit(solution)/shard_map/up/pallas_call | solution.py:418
  6.9 0.0 collective-permute-done.1.refs_1_
  6.9 0.0 collective-permute-done.refs_0_.refs_3_
  6.9 0.6 %collective-permute-start.5 = (bf16[32,2,128,128]{3,2,1,0:T(8,128)(2,1)}, bf16[32,2,128,128]{3,2,1,0:T(8,128)(2,1)S(1)}, u32[]{:S(2)}, u32[]{:S(2)}) collective-permute-start(bf16[32,2,128,128]{3,2,1,0:T(8,128)(2,1)} %refs_7_.1), channel_id=1, source_target_pairs={{0,1},{1,0},{2,3},{3,2},{4,5},{5,4},{6,7},{7,6},{8,9},{9,8},{10,11... | collective-permute-start | bytes 6291464 | tf_op jit(solution)/shard_map/ppermute | solution.py:409
  7.5 0.8 %select.1 = (bf16[144,128]{1,0:T(8,128)(2,1)S(1)}, bf16[144,128]{1,0:T(8,128)(2,1)S(1)}, bf16[144,128]{1,0:T(8,128)(2,1)S(1)}) custom-call(s32[6,4,8]{2,1,0:T(4,128)S(1)} %get-tuple-element.28.send_vmem, bf16[16,4096]{1,0:T(8,128)(2,1)S(1)} %get-tuple-element.37.dens_ref.refs_2_, bf16[16,128]{1,0:T(8,128)(2,1)S(1)} %get-tuple-element.32.root_ref.refs_2_, ...), custom_call_target="tpu_custom_call" | custom-call | bytes 3690000 | tf_op jit(solution)/shard_map/select/pallas_call | solution.py:456
  8.3 1.6 %collective-permute-start.2 = (bf16[144,128]{1,0:T(8,128)(2,1)S(1)}, bf16[144,128]{1,0:T(8,128)(2,1)S(1)}, u32[]{:S(2)}, u32[]{:S(2)}) collective-permute-start(bf16[144,128]{1,0:T(8,128)(2,1)S(1)} %get-tuple-element.41), channel_id=1, source_target_pairs={{0,4},{4,0},{8,12},{12,8},{16,20},{20,16},{24,28},{28,24},{1,5},{5... | collective-permute-start | bytes 110600 | tf_op jit(solution)/shard_map/ppermute | solution.py:412
  9.9 2.4 %collective-permute-done.2.refs_4_.refs_3_ = bf16[144,128]{1,0:T(8,128)(2,1)S(1)} collective-permute-done((bf16[144,128]{1,0:T(8,128)(2,1)S(1)}, bf16[144,128]{1,0:T(8,128)(2,1)S(1)}, u32[]{:S(2)}, u32[]{:S(2)}) %collective-permute-start.2) | collective-permute-done | bytes 36896 | tf_op jit(solution)/shard_map/ppermute | solution.py:412
  12.3 2.6 %collective-permute-start.4 = (bf16[160,128]{1,0:T(8,128)(2,1)S(1)}, bf16[160,128]{1,0:T(8,128)(2,1)S(1)}, u32[]{:S(2)}, u32[]{:S(2)}) collective-permute-start(bf16[160,128]{1,0:T(8,128)(2,1)S(1)} %pad_maximum_fusion), channel_id=1, source_target_pairs={{0,16},{4,20},{8,24},{12,28},{16,0},{20,4},{24,8},{28,12},{1,17},{... | collective-permute-start | bytes 122888 | tf_op jit(solution)/shard_map/ppermute | solution.py:412
  14.9 1.6 %collective-permute-start.3 = (bf16[144,128]{1,0:T(8,128)(2,1)S(1)}, bf16[144,128]{1,0:T(8,128)(2,1)S(1)}, u32[]{:S(2)}, u32[]{:S(2)}) collective-permute-start(bf16[144,128]{1,0:T(8,128)(2,1)S(1)} %get-tuple-element.42), channel_id=1, source_target_pairs={{0,8},{4,12},{8,0},{12,4},{16,24},{20,28},{24,16},{28,20},{1,9},{5... | collective-permute-start | bytes 110600 | tf_op jit(solution)/shard_map/ppermute | solution.py:412
  16.5 3.3 %couple.1.refs_9_.local_ref = f32[16,1024]{1,0:T(8,128)S(1)} custom-call(s32[8,32]{1,0:T(8,128)} %bitcast.8, f32[32,8,32,32]{3,2,1,0:T(8,128)} %coupling_hbm.1, bf16[16,4096]{1,0:T(8,128)(2,1)S(1)} %get-tuple-element.37.dens_ref.refs_2_, f32[32,4096]{1,0:T(8,128)S(1)} %get-tuple-element.38.bases_ref), custom_call_target="tpu_custom_call" | custom-call | bytes 8487000 | tf_op jit(solution)/shard_map/couple/pallas_call | solution.py:471
  19.8 0.0 copy-start
  19.8 0.0 copy-start.1
  19.8 0.0 collective-permute-done.3.refs_5_
  19.8 0.0 collective-permute-done.4.refs_6_.refs_4_
  19.8 0.0 collective-permute-done.5.refs_8_
  19.9 2.4 %near.1 = (f32[16,4096]{1,0:T(8,128)S(1)}, f32[16,4096]{1,0:T(8,128)S(1)}) custom-call(s32[2,32]{1,0:T(2,128)S(1)} %get-tuple-element.39.refs_0_, s32[2,32]{1,0:T(2,128)S(1)} %collective-permute-done.1.refs_1_, bf16[16,4096]{1,0:T(8,128)(2,1)S(1)} %get-tuple-element.37.dens_ref.refs_2_, bf16[16,4096]{1,0:T(8,128)(2,1)S(1)} %collective-permute-done.refs_0_.refs_3_, ...), custom_call_target="tpu_custom_call" | custom-call | bytes 11070000 | tf_op jit(solution)/shard_map/near/pallas_call | solution.py:506
  22.3 1.0 %collective-permute-start.6 = (f32[16,4096]{1,0:T(8,128)S(1)}, f32[16,4096]{1,0:T(8,128)S(1)}, u32[]{:S(2)}, u32[]{:S(2)}) collective-permute-start(f32[16,4096]{1,0:T(8,128)S(1)} %get-tuple-element.46), channel_id=1, source_target_pairs={{0,2},{2,0},{1,3},{3,1},{4,6},{6,4},{5,7},{7,5},{8,10},{10,8},{9,1... | collective-permute-start | bytes 786440 | tf_op jit(solution)/shard_map/ppermute | solution.py:409
  23.3 0.6 %collective-permute-start.7 = (bf16[64,128]{1,0:T(8,128)(2,1)S(1)}, bf16[64,128]{1,0:T(8,128)(2,1)S(1)}, u32[]{:S(2)}, u32[]{:S(2)}) collective-permute-start(bf16[64,128]{1,0:T(8,128)(2,1)S(1)} %pad_maximum_fusion.1), channel_id=1, source_target_pairs={{0,8},{4,12},{8,0},{12,4},{16,24},{20,28},{24,16},{28,20},{1,9},{5... | collective-permute-start | bytes 49160 | tf_op jit(solution)/shard_map/ppermute | solution.py:412
  23.9 0.4 %project.1.refs_0_ = f32[16,4096]{1,0:T(8,128)S(1)} custom-call(f32[16,1024]{1,0:T(8,128)S(1)} %couple.1.refs_9_.local_ref, f32[32,4096]{1,0:T(8,128)S(1)} %get-tuple-element.38.bases_ref, f32[16,4096]{1,0:T(8,128)S(1)} %get-tuple-element.45.near_ref), custom_call_target="tpu_custom_call" | custom-call | bytes 3690000 | tf_op jit(solution)/shard_map/project/pallas_call | solution.py:527
  24.2 2.8 %collective-permute-done.7.refs_5_ = bf16[64,128]{1,0:T(8,128)(2,1)S(1)} collective-permute-done((bf16[64,128]{1,0:T(8,128)(2,1)S(1)}, bf16[64,128]{1,0:T(8,128)(2,1)S(1)}, u32[]{:S(2)}, u32[]{:S(2)}) %collective-permute-start.7) | collective-permute-done | bytes 16416 | tf_op jit(solution)/shard_map/ppermute | solution.py:412
  27.0 1.8 %collective-permute-done.6.refs_1_ = f32[16,4096]{1,0:T(8,128)S(1)} collective-permute-done((f32[16,4096]{1,0:T(8,128)S(1)}, f32[16,4096]{1,0:T(8,128)S(1)}, u32[]{:S(2)}, u32[]{:S(2)}) %collective-permute-start.6) | collective-permute-done | bytes 262176 | tf_op jit(solution)/shard_map/ppermute | solution.py:409
  28.9 0.0 copy-done
  28.9 0.0 copy-done.1
  28.9 1.6 %far.1 = f32[16,4096]{1,0:T(8,128)} custom-call(f32[16,32,32]{2,1,0:T(8,128)S(1)} %copy-done.1, f32[16,3,32,32]{3,2,1,0:T(8,128)S(1)} %copy-done, bf16[32,4096]{1,0:T(8,128)(2,1)S(1)} %get-tuple-element.26.high_ref, bf16[32,4096]{1,0:T(8,128)(2,1)S(1)} %get-tuple-element.27.low_ref, f32[16,4096]{1,0:T(8,128)S(1)} %project.1.refs_0_, ...), custom_call_target="tpu_custom_call" | custom-call | bytes 7380000 | tf_op jit(solution)/shard_map/far/pallas_call | solution.py:537
  (4 shorter events, 0.0 us)
Async XLA Ops:
  0.0 6.9 %collective-permute-start = (bf16[16,4096]{1,0:T(8,128)(2,1)}, bf16[16,4096]{1,0:T(8,128)(2,1)S(1)}, u32[]{:S(2)}, u32[]{:S(2)}) collective-permute-start(bf16[16,4096]{1,0:T(8,128)(2,1)} %dens_hbm.1), channel_id=1, source_target_pairs={{0,2},{2,0},{1,3},{3,1},{4,6},{6,4},{5,7},{7,5},{8,10},{10,8},{9,1... | collective-permute-start | bytes 393224 | tf_op jit(solution)/shard_map/ppermute | solution.py:409
  2.9 3.9 %collective-permute-start.1 = (s32[2,32]{1,0:T(2,128)}, s32[2,32]{1,0:T(2,128)S(1)}, u32[]{:S(2)}, u32[]{:S(2)}) collective-permute-start(s32[2,32]{1,0:T(2,128)} %bitcast.9), channel_id=1, source_target_pairs={{0,1},{1,0},{2,3},{3,2},{4,5},{5,4},{6,7},{7,6},{8,9},{9,8},{10,11... | collective-permute-start | bytes 776 | tf_op jit(solution)/shard_map/ppermute | solution.py:409
  6.9 13.0 %collective-permute-start.5 = (bf16[32,2,128,128]{3,2,1,0:T(8,128)(2,1)}, bf16[32,2,128,128]{3,2,1,0:T(8,128)(2,1)S(1)}, u32[]{:S(2)}, u32[]{:S(2)}) collective-permute-start(bf16[32,2,128,128]{3,2,1,0:T(8,128)(2,1)} %refs_7_.1), channel_id=1, source_target_pairs={{0,1},{1,0},{2,3},{3,2},{4,5},{5,4},{6,7},{7,6},{8,9},{9,8},{10,11... | collective-permute-start | bytes 6291464 | tf_op jit(solution)/shard_map/ppermute | solution.py:409
  8.3 4.0 %collective-permute-start.2 = (bf16[144,128]{1,0:T(8,128)(2,1)S(1)}, bf16[144,128]{1,0:T(8,128)(2,1)S(1)}, u32[]{:S(2)}, u32[]{:S(2)}) collective-permute-start(bf16[144,128]{1,0:T(8,128)(2,1)S(1)} %get-tuple-element.41), channel_id=1, source_target_pairs={{0,4},{4,0},{8,12},{12,8},{16,20},{20,16},{24,28},{28,24},{1,5},{5... | collective-permute-start | bytes 110600 | tf_op jit(solution)/shard_map/ppermute | solution.py:412
  12.3 7.5 %collective-permute-start.4 = (bf16[160,128]{1,0:T(8,128)(2,1)S(1)}, bf16[160,128]{1,0:T(8,128)(2,1)S(1)}, u32[]{:S(2)}, u32[]{:S(2)}) collective-permute-start(bf16[160,128]{1,0:T(8,128)(2,1)S(1)} %pad_maximum_fusion), channel_id=1, source_target_pairs={{0,16},{4,20},{8,24},{12,28},{16,0},{20,4},{24,8},{28,12},{1,17},{... | collective-permute-start | bytes 122888 | tf_op jit(solution)/shard_map/ppermute | solution.py:412
  14.9 4.9 %collective-permute-start.3 = (bf16[144,128]{1,0:T(8,128)(2,1)S(1)}, bf16[144,128]{1,0:T(8,128)(2,1)S(1)}, u32[]{:S(2)}, u32[]{:S(2)}) collective-permute-start(bf16[144,128]{1,0:T(8,128)(2,1)S(1)} %get-tuple-element.42), channel_id=1, source_target_pairs={{0,8},{4,12},{8,0},{12,4},{16,24},{20,28},{24,16},{28,20},{1,9},{5... | collective-permute-start | bytes 110600 | tf_op jit(solution)/shard_map/ppermute | solution.py:412
  19.8 9.1 %copy-start = (f32[16,3,32,32]{3,2,1,0:T(8,128)S(1)}, f32[16,3,32,32]{3,2,1,0:T(8,128)}, u32[]{:S(2)}) copy-start(f32[16,3,32,32]{3,2,1,0:T(8,128)} %cross_ref.1) | copy-start | bytes 589828
  19.8 9.1 %copy-start.1 = (f32[16,32,32]{2,1,0:T(8,128)S(1)}, f32[16,32,32]{2,1,0:T(8,128)}, u32[]{:S(2)}) copy-start(f32[16,32,32]{2,1,0:T(8,128)} %upper_ref.1) | copy-start | bytes 196612
  22.3 6.6 %collective-permute-start.6 = (f32[16,4096]{1,0:T(8,128)S(1)}, f32[16,4096]{1,0:T(8,128)S(1)}, u32[]{:S(2)}, u32[]{:S(2)}) collective-permute-start(f32[16,4096]{1,0:T(8,128)S(1)} %get-tuple-element.46), channel_id=1, source_target_pairs={{0,2},{2,0},{1,3},{3,1},{4,6},{6,4},{5,7},{7,5},{8,10},{10,8},{9,1... | collective-permute-start | bytes 786440 | tf_op jit(solution)/shard_map/ppermute | solution.py:409
  23.3 3.7 %collective-permute-start.7 = (bf16[64,128]{1,0:T(8,128)(2,1)S(1)}, bf16[64,128]{1,0:T(8,128)(2,1)S(1)}, u32[]{:S(2)}, u32[]{:S(2)}) collective-permute-start(bf16[64,128]{1,0:T(8,128)(2,1)S(1)} %pad_maximum_fusion.1), channel_id=1, source_target_pairs={{0,8},{4,12},{8,0},{12,4},{16,24},{20,28},{24,16},{28,20},{1,9},{5... | collective-permute-start | bytes 49160 | tf_op jit(solution)/shard_map/ppermute | solution.py:412

commit v3 on v2

--- a/solution.py
+++ b/solution.py
@@ -231,38 +231,12 @@
                 out_ref[:, lanes] = term if turn == 0 else out_ref[:, lanes] + term
 
 
-def couple_kernel(
-    far_hbm, coupling_hbm, dens_ref, bases_ref, out_ref, far_ref, coupling_ref, turned_ref, sems,
-):
-    chunk_count = sems.shape[0] - 1
-    chunk = coupling_ref.shape[0] // chunk_count
-    copies = fetch(
-        [(far_hbm, far_ref)]
-        + [
-            (coupling_hbm.at[pl.ds(index * chunk, chunk)], coupling_ref.at[pl.ds(index * chunk, chunk)])
-            for index in range(chunk_count)
-        ],
-        sems,
-    )
-    columns, points = dens_ref.shape
-    leaf_count, far_count, rank = coupling_ref.shape[:3]
-    width = points // leaf_count
+def coupled(leaves, far_ref, coupling_ref, turned_ref):
+    far_count, rank = coupling_ref.shape[1:3]
+    columns = turned_ref.shape[1] // 2
     group = LANES // rank
-    upper = lax.broadcasted_iota(jnp.int32, (rank, 2 * columns), 1) < columns
-    for leaf in range(leaf_count):
-        spots = slice(leaf * width, (leaf + 1) * width)
-        rows = jnp.concatenate(halves(bases_ref[:, spots]), axis=0)
-        dens = dens_ref[:, spots]
-        twice = dot_nt(rows, jnp.concatenate([dens, dens], axis=0))
-        high, low = halves(twice[:rank] + twice[rank:])
-        turned_ref[leaf * rank : (leaf + 1) * rank, :] = jnp.where(
-            upper, high.astype(F32), low.astype(F32)
-        ).astype(BF16)
-    copies[0].wait()
     parts = []
-    for leaf in range(leaf_count):
-        if leaf % chunk == 0:
-            copies[1 + leaf // chunk].wait()
+    for leaf in leaves:
         maps = jnp.concatenate([coupling_ref[leaf, j] for j in range(far_count)], axis=1)
         maps = jnp.concatenate(halves(maps), axis=0)
         picked = jnp.concatenate(
@@ -276,32 +250,75 @@
         parts.append(out[:rank] + out[rank:])
         if len(parts) == group:
             turned = jnp.concatenate(parts, axis=0).T
-            spot = (leaf + 1 - group) * rank
-            out_ref[:, spot : spot + LANES] = turned[:columns] + turned[columns:]
+            yield turned[:columns] + turned[columns:]
             parts = []
 
 
-def project_kernel(leaf_count, local_ref, bases_ref, near_ref, out_ref):
+def couple_kernel(
+    far_hbm, coupling_hbm, dens_ref, bases_ref,
+    table_ref, coupling_ref, turned_ref, out_ref, far_ref, sems, chunk_sems,
+):
+    copies = fetch([(far_hbm, far_ref), (far_hbm, table_ref)], sems)
+    chunk_count = chunk_sems.shape[0]
+    chunk = coupling_ref.shape[0] // chunk_count
+    chunks = [pl.ds(index * chunk, chunk) for index in range(chunk_count)]
+    block_copies = fetch([(coupling_hbm.at[c], coupling_ref.at[c]) for c in chunks], chunk_sems)
+    columns, points = dens_ref.shape
+    leaf_count, _, rank = coupling_ref.shape[:3]
+    width = points // leaf_count
+    upper = lax.broadcasted_iota(jnp.int32, (rank, 2 * columns), 1) < columns
+    for leaf in range(leaf_count):
+        spots = slice(leaf * width, (leaf + 1) * width)
+        rows = jnp.concatenate(halves(bases_ref[:, spots]), axis=0)
+        dens = dens_ref[:, spots]
+        twice = dot_nt(rows, jnp.concatenate([dens, dens], axis=0))
+        high, low = halves(twice[:rank] + twice[rank:])
+        turned_ref[leaf * rank : (leaf + 1) * rank, :] = jnp.where(
+            upper, high.astype(F32), low.astype(F32)
+        ).astype(BF16)
+    for copy in copies:
+        copy.wait()
+    done = out_ref.shape[1] // rank
+    for index in range(chunk_count):
+        block_copies[index].wait()
+        leaves = range(index * chunk, min((index + 1) * chunk, done))
+        for turn, field in enumerate(coupled(leaves, far_ref, coupling_ref, turned_ref)):
+            spot = index * chunk * rank + turn * LANES
+            out_ref[:, spot : spot + LANES] = field
+
+
+def project_kernel(
+    table_ref, coupling_ref, turned_ref, first_ref, bases_ref, near_ref, out_ref, far_ref, sems,
+):
+    copies = fetch([(table_ref, far_ref)], sems)
     rank, points = bases_ref.shape
+    leaf_count = coupling_ref.shape[0]
     group = LANES // rank
     step = group * points // leaf_count
-    for index in range(leaf_count // group):
+
+    def project(index, field):
         spots = slice(index * step, (index + 1) * step)
         high, low = halves(bases_ref[:, spots])
         out_ref[:, spots] = near_ref[:, spots] + split_dot(
-            dot_nn, local_ref[:, index * LANES : (index + 1) * LANES],
-            spread_bases(high, group), spread_bases(low, group),
+            dot_nn, field, spread_bases(high, group), spread_bases(low, group)
         )
 
+    done = first_ref.shape[1] // LANES
+    for index in range(done):
+        project(index, first_ref[:, index * LANES : (index + 1) * LANES])
+    copies[0].wait()
+    leaves = range(done * group, leaf_count)
+    for index, field in enumerate(coupled(leaves, far_ref, coupling_ref, turned_ref)):
+        project(done + index, field)
+
 
 def far_kernel(
-    roots, added, upper_ref, cross_ref, high_ref, low_ref, *refs,
+    roots, upper_ref, cross_ref, high_ref, low_ref, term_ref, *refs,
 ):
-    term_refs, refs = refs[:added], refs[added:]
     root_refs, refs = refs[: len(roots)], refs[len(roots) :]
-    out_hbm, tile_ref, tree_ref, sum_ref, sems = refs
+    out_ref, tile_ref, tree_ref = refs
     device = lax.axis_index("leaf")
-    columns, points = sum_ref.shape
+    columns, points = out_ref.shape
     rank = upper_ref.shape[1]
     device_count = upper_ref.shape[0] // 2
     for tiles, root_ref in zip(roots, root_refs):
@@ -351,22 +368,29 @@
             total = total + split_dot(dot_nt, field, *halves(upper_ref[node]))
         field = total
         level *= 2
+    step = 4 * LANES
+    for first in range(0, points, step):
+        spots = slice(first, first + step)
+        out_ref[:, spots] = term_ref[:, spots] + split_dot(
+            dot_nn, field, high_ref[:, spots], low_ref[:, spots]
+        )
+
+
+def add_kernel(*refs):
+    term_refs, (out_hbm, sum_ref, sems) = refs[:-3], refs[-3:]
     chunk_count = sems.shape[0]
-    step = points // chunk_count
+    step = sum_ref.shape[1] // chunk_count
     copies = []
     for index in range(chunk_count):
         spots = slice(index * step, (index + 1) * step)
-        total = split_dot(dot_nn, field, high_ref[:, spots], low_ref[:, spots])
-        for term_ref in term_refs:
+        total = term_refs[0][:, spots]
+        for term_ref in term_refs[1:]:
             total = total + term_ref[:, spots]
         sum_ref[:, spots] = total
-        copy = pltpu.make_async_copy(
-            sum_ref.at[:, pl.ds(index * step, step)],
-            out_hbm.at[:, pl.ds(index * step, step)],
-            sems.at[index],
+        copies += fetch(
+            [(sum_ref.at[:, pl.ds(index * step, step)], out_hbm.at[:, pl.ds(index * step, step)])],
+            sems.at[pl.ds(index, 1)],
         )
-        copy.start()
-        copies.append(copy)
     for copy in copies:
         copy.wait()
 
@@ -468,36 +492,34 @@
     )(send, dens, root, *others)
     outgoing, dens = lax.optimization_barrier((outgoing, dens))
     far_table = far_src.T
-    leaf_local = pl.pallas_call(
+    first_leaves = leaf_count // 2
+    *coupling, leaf_local = pl.pallas_call(
         couple_kernel,
-        out_shape=jax.ShapeDtypeStruct((columns, leaf_count * rank), F32),
+        out_shape=[
+            jax.ShapeDtypeStruct(far_table.shape, jnp.int32),
+            jax.ShapeDtypeStruct(leaf_coupling.shape, F32),
+            jax.ShapeDtypeStruct((leaf_count * rank, 2 * columns), BF16),
+            jax.ShapeDtypeStruct((columns, first_leaves * rank), F32),
+        ],
         in_specs=[HBM] * 2 + [VMEM] * 2,
-        out_specs=VMEM,
-        scratch_shapes=[
-            pltpu.SMEM(far_table.shape, jnp.int32),
-            pltpu.VMEM(leaf_coupling.shape, F32),
-            pltpu.VMEM((leaf_count * rank, 2 * columns), BF16),
-            dma((5,)),
-        ],
+        out_specs=[VMEM] * 4,
+        scratch_shapes=[pltpu.SMEM(far_table.shape, jnp.int32), dma((2,)), dma((4,))],
         compiler_params=params,
-        cost_estimate=hint(2.3),
+        cost_estimate=hint(2),
         name="couple",
     )(hbm(far_table), hbm(leaf_coupling), dens, basis)
     tail = cap * far_groups * columns
     if side == 2:
-        first, second, third = (stride for _, stride in faces)
-        arrived = [crossed(outgoing[0], first), crossed(outgoing[1], second)]
-        last = jnp.concatenate([outgoing[2], arrived[0][tail:]], axis=0)
-        arrived.append(crossed(last, third))
-        held = jnp.concatenate([root, arrived[0][tail:], arrived[2][tail:]], axis=0)
-        beside = crossed(held, second)
-        turns = [0, first, third, third ^ first]
+        arrived = [crossed(value, stride) for (_, stride), value in zip(faces, outgoing)]
+        held = jnp.concatenate([root] + [value[tail:] for value in arrived], axis=0)
+        whole = leaf_devices - 1
+        opposite = crossed(held, whole)
+        turns = [0] + [stride for _, stride in faces]
         roots = [
             ([(0, 0)], root),
-            ([(first, tail)], arrived[0]),
-            ([(third, tail), (third ^ first, tail + columns)], arrived[2]),
-            ([(turn ^ second, row * columns) for row, turn in enumerate(turns)], beside),
+            ([(turn ^ whole, row * columns) for row, turn in enumerate(turns)], opposite),
         ]
+        roots += [([(stride, tail)], value) for (_, stride), value in zip(faces, arrived)]
     else:
         arrived = [shifted(value, "leaf", stride) for (_, stride), value in zip(faces, outgoing)]
         roots = [(None, lax.all_gather(root, "leaf", axis=0))]
@@ -525,30 +547,38 @@
     )
     received = [rotated(partials[part], "far", -part) for part in range(1, far_groups)]
     partial = pl.pallas_call(
-        functools.partial(project_kernel, leaf_count),
+        project_kernel,
         out_shape=jax.ShapeDtypeStruct((columns, points), F32),
-        in_specs=[VMEM] * 3,
+        in_specs=[VMEM] * 6,
         out_specs=VMEM,
+        scratch_shapes=[pltpu.SMEM(far_table.shape, jnp.int32), dma((1,))],
         compiler_params=params,
-        cost_estimate=hint(1),
+        cost_estimate=hint(1.5),
         name="project",
-    )(leaf_local, basis, partials[0])
-    terms = [partial] + received
-    return pl.pallas_call(
-        functools.partial(far_kernel, [tiles for tiles, _ in roots], len(terms)),
+    )(*coupling, leaf_local, basis, partials[0])
+    total = pl.pallas_call(
+        functools.partial(far_kernel, [tiles for tiles, _ in roots]),
         out_shape=jax.ShapeDtypeStruct((columns, points), F32),
-        in_specs=[VMEM] * (4 + len(terms) + len(roots)),
-        out_specs=HBM,
+        in_specs=[VMEM] * (5 + len(roots)),
+        out_specs=VMEM,
         scratch_shapes=[
             pltpu.VMEM((leaf_devices, columns, LANES), BF16),
             pltpu.VMEM((2 * leaf_devices, columns, rank), F32),
-            pltpu.VMEM((columns, points), F32),
-            dma((4,)),
         ],
         compiler_params=params,
-        cost_estimate=hint(2),
+        cost_estimate=hint(1.5),
         name="far",
-    )(upper_transfer, up_coupling, high, low, *terms, *[value for _, value in roots])
+    )(upper_transfer, up_coupling, high, low, partial, *[value for _, value in roots])
+    return pl.pallas_call(
+        add_kernel,
+        out_shape=jax.ShapeDtypeStruct((columns, points), F32),
+        in_specs=[VMEM] * (1 + len(received)),
+        out_specs=HBM,
+        scratch_shapes=[pltpu.VMEM((columns, points), F32), dma((4,))],
+        compiler_params=params,
+        cost_estimate=hint(0.5),
+        name="add",
+    )(total, *received)
 
 
 def solution(mesh):

time: 30.7 us -> 28.6 us (0.932)
  waiting for transfers between devices: 7.09 us -> 2.24 us
  starting transfers between devices: 10.8 us -> 12.7 us
  Pallas kernels: 12.4 us -> 13.4 us
    ppermute x4, waiting for transfers between devices: 5.25 us -> 2.23 us  [crossed(): lax.ppermute(value, 'leaf', [(i, i ^ turn) for i in range(leaf_devices)])]
    ppermute x4, waiting for transfers between devices: 1.85 us -> 0.01 us  [rotated(): lax.ppermute(value, axis, [(i, (i - shift) % count) for i in range(count)])]
    ppermute x4, starting transfers between devices: 6.32 us -> 8.13 us  [crossed(): lax.ppermute(value, 'leaf', [(i, i ^ turn) for i in range(leaf_devices)])]
    pallas_call x2 -> x3, Pallas kernels: 3.68 us -> 5.32 us  [the longest x1 2.67 us: local(): pl.pallas_call(couple_kernel, out_shape=[jax.ShapeDtypeStruct(far_table.s...]
    pallas_call x1, Pallas kernels: 1.61 us -> 0.95 us  [local(): pl.pallas_call(functools.partial(far_kernel, [tiles for tiles, _ in roots...]
  transfers between devices with their start and end apart: 8 -> 8, of which waited for: 3 -> 1; matrix products, arithmetic and copies ran while one was open for 0% -> 0% of each run, Pallas kernels for 28% -> 36%
where the time goes in v3:
time: 28.6 us; the launch traced here: 28.4 us
  Pallas kernels  13.4 us (47%)
  starting transfers between devices  12.7 us (44%)
  waiting for transfers between devices  2.24 us (8%)
    ppermute x4, starting transfers between devices, crossed(): lax.ppermute(value, 'leaf', [(i, i ^ turn) for i in range(leaf_devices)])  8.13 us
    ppermute x4, starting transfers between devices, rotated(): lax.ppermute(value, axis, [(i, (i - shift) % count) for i in range(count)])  4.52 us
    pallas_call x1, Pallas kernels, local(): pl.pallas_call(up_kernel, out_shape=[jax.ShapeDtypeStruct(densities.shape...  3.92 us
    pallas_call x1, Pallas kernels, local(): pl.pallas_call(couple_kernel, out_shape=[jax.ShapeDtypeStruct(far_table.s...  2.67 us
    pallas_call x1, Pallas kernels, local(): pl.pallas_call(functools.partial(near_kernel, faces, far_groups, share),...  2.43 us
    ppermute x4, waiting for transfers between devices, crossed(): lax.ppermute(value, 'leaf', [(i, i ^ turn) for i in range(leaf_devices)])  2.23 us
    pallas_call x1, Pallas kernels, local(): pl.pallas_call(project_kernel, out_shape=jax.ShapeDtypeStruct((columns, p...  1.89 us
    pallas_call x1, Pallas kernels, local(): pl.pallas_call(functools.partial(far_kernel, [tiles for tiles, _ in roots...  0.95 us
  transfers between devices with their start and end apart: 8, of which 1 were waited for; matrix products, arithmetic and copies ran while one was open for 0% of the time, Pallas kernels for 36%

profile of v3, /device:TPU:0, one launch (start us, length us, event | category | flops | bytes accessed | tf_op | source)
XLA Modules:
  0.0 28.4 jit_solution(16899682520534617919)
XLA Ops:
  0.0 2.9 %collective-permute-start = (bf16[16,4096]{1,0:T(8,128)(2,1)}, bf16[16,4096]{1,0:T(8,128)(2,1)S(1)}, u32[]{:S(2)}, u32[]{:S(2)}) collective-permute-start(bf16[16,4096]{1,0:T(8,128)(2,1)} %dens_hbm.1), channel_id=1, source_target_pairs={{0,2},{2,0},{1,3},{3,1},{4,6},{6,4},{5,7},{7,5},{8,10},{10,8},{9,1... | collective-permute-start | bytes 393224 | tf_op jit(solution)/shard_map/ppermute | solution.py:433
  2.9 0.0 collective-permute-start.1
  2.9 3.9 %up.1 = (bf16[16,4096]{1,0:T(8,128)(2,1)S(1)}, f32[32,4096]{1,0:T(8,128)S(1)}, s32[6,4,8]{2,1,0:T(4,128)S(1)}, s32[2,32]{1,0:T(2,128)S(1)}, bf16[32,4096]{1,0:T(...) custom-call(bf16[16,4096]{1,0:T(8,128)(2,1)} %dens_hbm.1, f32[32,4096]{1,0:T(8,128)} %bases_hbm.1, ...), custom_call_target="tpu_custom_call" | custom-call | bytes 12915000 | tf_op jit(solution)/shard_map/up/pallas_call | solution.py:442
  6.9 0.0 collective-permute-done.1.refs_1_
  6.9 0.0 collective-permute-done.refs_0_.refs_3_
  6.9 0.6 %collective-permute-start.5 = (bf16[32,2,128,128]{3,2,1,0:T(8,128)(2,1)}, bf16[32,2,128,128]{3,2,1,0:T(8,128)(2,1)S(1)}, u32[]{:S(2)}, u32[]{:S(2)}) collective-permute-start(bf16[32,2,128,128]{3,2,1,0:T(8,128)(2,1)} %refs_7_.1), channel_id=1, source_target_pairs={{0,1},{1,0},{2,3},{3,2},{4,5},{5,4},{6,7},{7,6},{8,9},{9,8},{10,11... | collective-permute-start | bytes 6291464 | tf_op jit(solution)/shard_map/ppermute | solution.py:433
  7.5 0.8 %select.1 = (bf16[144,128]{1,0:T(8,128)(2,1)S(1)}, bf16[144,128]{1,0:T(8,128)(2,1)S(1)}, bf16[144,128]{1,0:T(8,128)(2,1)S(1)}) custom-call(s32[6,4,8]{2,1,0:T(4,128)S(1)} %get-tuple-element.32.send_vmem, bf16[16,4096]{1,0:T(8,128)(2,1)S(1)} %get-tuple-element.41.dens_ref.refs_2_, bf16[16,128]{1,0:T(8,128)(2,1)S(1)} %get-tuple-element.36.root_ref.refs_0_, ...), custom_call_target="tpu_custom_call" | custom-call | bytes 3690000 | tf_op jit(solution)/shard_map/select/pallas_call | solution.py:480
  8.3 1.6 %collective-permute-start.2 = (bf16[144,128]{1,0:T(8,128)(2,1)S(1)}, bf16[144,128]{1,0:T(8,128)(2,1)S(1)}, u32[]{:S(2)}, u32[]{:S(2)}) collective-permute-start(bf16[144,128]{1,0:T(8,128)(2,1)S(1)} %get-tuple-element.49), channel_id=1, source_target_pairs={{0,4},{4,0},{8,12},{12,8},{16,20},{20,16},{24,28},{28,24},{1,5},{5... | collective-permute-start | bytes 110600 | tf_op jit(solution)/shard_map/ppermute | solution.py:436
  9.9 1.6 %collective-permute-start.3 = (bf16[144,128]{1,0:T(8,128)(2,1)S(1)}, bf16[144,128]{1,0:T(8,128)(2,1)S(1)}, u32[]{:S(2)}, u32[]{:S(2)}) collective-permute-start(bf16[144,128]{1,0:T(8,128)(2,1)S(1)} %get-tuple-element.50), channel_id=1, source_target_pairs={{0,8},{4,12},{8,0},{12,4},{16,24},{20,28},{24,16},{28,20},{1,9},{5... | collective-permute-start | bytes 110600 | tf_op jit(solution)/shard_map/ppermute | solution.py:436
  11.4 2.6 %collective-permute-start.4 = (bf16[144,128]{1,0:T(8,128)(2,1)S(1)}, bf16[144,128]{1,0:T(8,128)(2,1)S(1)}, u32[]{:S(2)}, u32[]{:S(2)}) collective-permute-start(bf16[144,128]{1,0:T(8,128)(2,1)S(1)} %get-tuple-element.51), channel_id=1, source_target_pairs={{0,16},{4,20},{8,24},{12,28},{16,0},{20,4},{24,8},{28,12},{1,17},{... | collective-permute-start | bytes 110600 | tf_op jit(solution)/shard_map/ppermute | solution.py:436
  14.0 2.7 %couple.1 = (s32[8,32]{1,0:T(8,128)S(1)}, f32[32,8,32,32]{3,2,1,0:T(8,128)S(1)}, bf16[1024,32]{1,0:T(8,128)(2,1)S(1)}, f32[16,512]{1,0:T(8,128)S(1)}) custom-call(s32[8,32]{1,0:T(8,128)} %bitcast.8, f32[32,8,32,32]{3,2,1,0:T(8,128)} %coupling_hbm.1, bf16[16,4096]{1,0:T(8,128)(2,1)S(1)} %get-tuple-element.41.dens_ref.refs_2_, ...), custom_call_target="tpu_custom_call" | custom-call | bytes 7380000 | tf_op jit(solution)/shard_map/couple/pallas_call | solution.py:496
  16.7 0.0 collective-permute-done.2.refs_4_.refs_2_
  16.7 0.0 collective-permute-done.3.refs_5_.refs_3_
  16.7 0.0 collective-permute-done.4.refs_6_.refs_4_
  16.7 0.0 collective-permute-done.5.refs_8_
  16.7 0.0 copy-start
  16.8 0.0 copy-start.1
  16.8 2.4 %near.1 = (f32[16,4096]{1,0:T(8,128)S(1)}, f32[16,4096]{1,0:T(8,128)S(1)}) custom-call(s32[2,32]{1,0:T(2,128)S(1)} %get-tuple-element.47.refs_0_, s32[2,32]{1,0:T(2,128)S(1)} %collective-permute-done.1.refs_1_, bf16[16,4096]{1,0:T(8,128)(2,1)S(1)} %get-tuple-element.41.dens_ref.refs_2_, bf16[16,4096]{1,0:T(8,128)(2,1)S(1)} %collective-permute-done.refs_0_.refs_3_, ...), custom_call_target="tpu_custom_call" | custom-call | bytes 11070000 | tf_op jit(solution)/shard_map/near/pallas_call | solution.py:528
  19.2 1.0 %collective-permute-start.7 = (f32[16,4096]{1,0:T(8,128)S(1)}, f32[16,4096]{1,0:T(8,128)S(1)}, u32[]{:S(2)}, u32[]{:S(2)}) collective-permute-start(f32[16,4096]{1,0:T(8,128)S(1)} %get-tuple-element.54), channel_id=1, source_target_pairs={{0,2},{2,0},{1,3},{3,1},{4,6},{6,4},{5,7},{7,5},{8,10},{10,8},{9,1... | collective-permute-start | bytes 786440 | tf_op jit(solution)/shard_map/ppermute | solution.py:433
  20.2 2.4 %collective-permute-start.6 = (bf16[64,128]{1,0:T(8,128)(2,1)S(1)}, bf16[64,128]{1,0:T(8,128)(2,1)S(1)}, u32[]{:S(2)}, u32[]{:S(2)}) collective-permute-start(bf16[64,128]{1,0:T(8,128)(2,1)S(1)} %pad_maximum_fusion), channel_id=1, source_target_pairs={{0,28},{4,24},{8,20},{12,16},{16,12},{20,8},{24,4},{28,0},{1,29},{... | collective-permute-start | bytes 49160 | tf_op jit(solution)/shard_map/ppermute | solution.py:436
  22.6 1.9 %project.1.term_ref = f32[16,4096]{1,0:T(8,128)S(1)} custom-call(s32[8,32]{1,0:T(8,128)S(1)} %get-tuple-element.43.table_ref, f32[32,8,32,32]{3,2,1,0:T(8,128)S(1)} %get-tuple-element.44.coupling_ref, bf16[1024,32]{1,0:T(8,128)(2,1)S(1)} %get-tuple-element.45.turned_ref, f32[16,512]{1,0:T(8,128)S(1)} %get-tuple-element.46.refs_9_.first_ref, ...), custom_call_target="tpu_custom_call" | custom-call | bytes 5535000 | tf_op jit(solution)/shard_map/project/pallas_call | solution.py:549
  24.5 2.2 %collective-permute-done.6.refs_1_ = bf16[64,128]{1,0:T(8,128)(2,1)S(1)} collective-permute-done((bf16[64,128]{1,0:T(8,128)(2,1)S(1)}, bf16[64,128]{1,0:T(8,128)(2,1)S(1)}, u32[]{:S(2)}, u32[]{:S(2)}) %collective-permute-start.6) | collective-permute-done | bytes 16416 | tf_op jit(solution)/shard_map/ppermute | solution.py:436
  26.7 0.0 copy-done
  26.7 0.0 copy-done.1
  26.7 1.0 %far.1.refs_0_ = f32[16,4096]{1,0:T(8,128)S(1)} custom-call(f32[16,32,32]{2,1,0:T(8,128)S(1)} %copy-done.1, f32[16,3,32,32]{3,2,1,0:T(8,128)S(1)} %copy-done, bf16[32,4096]{1,0:T(8,128)(2,1)S(1)} %get-tuple-element.30.high_ref, bf16[32,4096]{1,0:T(8,128)(2,1)S(1)} %get-tuple-element.31.low_ref, f32[16,4096]{1,0:T(8,128)S(1)} %project.1.term_ref, ...), custom_call_target="tpu_custom_call" | custom-call | bytes 5535000 | tf_op jit(solution)/shard_map/far/pallas_call | solution.py:559
  27.7 0.0 collective-permute-done.7.refs_1_
  27.7 0.8 %add.1 = f32[16,4096]{1,0:T(8,128)} custom-call(f32[16,4096]{1,0:T(8,128)S(1)} %far.1.refs_0_, f32[16,4096]{1,0:T(8,128)S(1)} %collective-permute-done.7.refs_1_), custom_call_target="tpu_custom_call" | custom-call | bytes 1845000 | tf_op jit(solution)/shard_map/add/pallas_call | solution.py:572
  (4 shorter events, 0.0 us)
Async XLA Ops:
  0.0 6.9 %collective-permute-start = (bf16[16,4096]{1,0:T(8,128)(2,1)}, bf16[16,4096]{1,0:T(8,128)(2,1)S(1)}, u32[]{:S(2)}, u32[]{:S(2)}) collective-permute-start(bf16[16,4096]{1,0:T(8,128)(2,1)} %dens_hbm.1), channel_id=1, source_target_pairs={{0,2},{2,0},{1,3},{3,1},{4,6},{6,4},{5,7},{7,5},{8,10},{10,8},{9,1... | collective-permute-start | bytes 393224 | tf_op jit(solution)/shard_map/ppermute | solution.py:433
  2.9 3.9 %collective-permute-start.1 = (s32[2,32]{1,0:T(2,128)}, s32[2,32]{1,0:T(2,128)S(1)}, u32[]{:S(2)}, u32[]{:S(2)}) collective-permute-start(s32[2,32]{1,0:T(2,128)} %bitcast.9), channel_id=1, source_target_pairs={{0,1},{1,0},{2,3},{3,2},{4,5},{5,4},{6,7},{7,6},{8,9},{9,8},{10,11... | collective-permute-start | bytes 776 | tf_op jit(solution)/shard_map/ppermute | solution.py:433
  6.9 9.8 %collective-permute-start.5 = (bf16[32,2,128,128]{3,2,1,0:T(8,128)(2,1)}, bf16[32,2,128,128]{3,2,1,0:T(8,128)(2,1)S(1)}, u32[]{:S(2)}, u32[]{:S(2)}) collective-permute-start(bf16[32,2,128,128]{3,2,1,0:T(8,128)(2,1)} %refs_7_.1), channel_id=1, source_target_pairs={{0,1},{1,0},{2,3},{3,2},{4,5},{5,4},{6,7},{7,6},{8,9},{9,8},{10,11... | collective-permute-start | bytes 6291464 | tf_op jit(solution)/shard_map/ppermute | solution.py:433
  8.3 8.4 %collective-permute-start.2 = (bf16[144,128]{1,0:T(8,128)(2,1)S(1)}, bf16[144,128]{1,0:T(8,128)(2,1)S(1)}, u32[]{:S(2)}, u32[]{:S(2)}) collective-permute-start(bf16[144,128]{1,0:T(8,128)(2,1)S(1)} %get-tuple-element.49), channel_id=1, source_target_pairs={{0,4},{4,0},{8,12},{12,8},{16,20},{20,16},{24,28},{28,24},{1,5},{5... | collective-permute-start | bytes 110600 | tf_op jit(solution)/shard_map/ppermute | solution.py:436
  9.9 6.9 %collective-permute-start.3 = (bf16[144,128]{1,0:T(8,128)(2,1)S(1)}, bf16[144,128]{1,0:T(8,128)(2,1)S(1)}, u32[]{:S(2)}, u32[]{:S(2)}) collective-permute-start(bf16[144,128]{1,0:T(8,128)(2,1)S(1)} %get-tuple-element.50), channel_id=1, source_target_pairs={{0,8},{4,12},{8,0},{12,4},{16,24},{20,28},{24,16},{28,20},{1,9},{5... | collective-permute-start | bytes 110600 | tf_op jit(solution)/shard_map/ppermute | solution.py:436
  11.4 5.3 %collective-permute-start.4 = (bf16[144,128]{1,0:T(8,128)(2,1)S(1)}, bf16[144,128]{1,0:T(8,128)(2,1)S(1)}, u32[]{:S(2)}, u32[]{:S(2)}) collective-permute-start(bf16[144,128]{1,0:T(8,128)(2,1)S(1)} %get-tuple-element.51), channel_id=1, source_target_pairs={{0,16},{4,20},{8,24},{12,28},{16,0},{20,4},{24,8},{28,12},{1,17},{... | collective-permute-start | bytes 110600 | tf_op jit(solution)/shard_map/ppermute | solution.py:436
  16.7 10.0 %copy-start = (f32[16,3,32,32]{3,2,1,0:T(8,128)S(1)}, f32[16,3,32,32]{3,2,1,0:T(8,128)}, u32[]{:S(2)}) copy-start(f32[16,3,32,32]{3,2,1,0:T(8,128)} %cross_ref.1) | copy-start | bytes 589828
  16.8 10.0 %copy-start.1 = (f32[16,32,32]{2,1,0:T(8,128)S(1)}, f32[16,32,32]{2,1,0:T(8,128)}, u32[]{:S(2)}) copy-start(f32[16,32,32]{2,1,0:T(8,128)} %upper_ref.1) | copy-start | bytes 196612
  19.2 8.5 %collective-permute-start.7 = (f32[16,4096]{1,0:T(8,128)S(1)}, f32[16,4096]{1,0:T(8,128)S(1)}, u32[]{:S(2)}, u32[]{:S(2)}) collective-permute-start(f32[16,4096]{1,0:T(8,128)S(1)} %get-tuple-element.54), channel_id=1, source_target_pairs={{0,2},{2,0},{1,3},{3,1},{4,6},{6,4},{5,7},{7,5},{8,10},{10,8},{9,1... | collective-permute-start | bytes 786440 | tf_op jit(solution)/shard_map/ppermute | solution.py:433
  20.2 6.5 %collective-permute-start.6 = (bf16[64,128]{1,0:T(8,128)(2,1)S(1)}, bf16[64,128]{1,0:T(8,128)(2,1)S(1)}, u32[]{:S(2)}, u32[]{:S(2)}) collective-permute-start(bf16[64,128]{1,0:T(8,128)(2,1)S(1)} %pad_maximum_fusion), channel_id=1, source_target_pairs={{0,28},{4,24},{8,20},{12,16},{16,12},{20,8},{24,4},{28,0},{1,29},{... | collective-permute-start | bytes 49160 | tf_op jit(solution)/shard_map/ppermute | solution.py:436

commit v4 on v3

--- a/solution.py
+++ b/solution.py
@@ -175,7 +175,8 @@
                 out_ref[row : row + columns, :] = panel_ref[
                     :, pl.ds(pl.multiple_of(leaf * LANES, LANES), LANES)
                 ]
-        out_ref[cap * far_groups * columns :, :] = root_ref[...]
+        for row in range(cap * far_groups * columns, out_ref.shape[0], columns):
+            out_ref[row : row + columns, :] = root_ref[...]
 
 
 def near_kernel(
@@ -467,6 +468,7 @@
     )
     all_sources[0] = sources
 
+    beside = crossed(root, 1) if side == 2 else None
     later_blocks, others, all_sources, root = lax.optimization_barrier(
         (near_blocks, others, all_sources, root)
     )
@@ -476,10 +478,10 @@
         faces = [((2 * axis, 2 * axis + 1), 2**axis) for axis in range(3)]
     else:
         faces = [((direction,), offset) for direction, offset in enumerate(offsets)]
-    chunk = (cap * far_groups + 1) * columns
+    chunks = [(cap * far_groups + (1 if stride > 1 else 4)) * columns for _, stride in faces]
     outgoing = pl.pallas_call(
         functools.partial(select_kernel, faces, far_groups),
-        out_shape=[jax.ShapeDtypeStruct((chunk, LANES), BF16)] * len(faces),
+        out_shape=[jax.ShapeDtypeStruct((chunk, LANES), BF16) for chunk in chunks],
         in_specs=[VMEM] * (2 + far_groups),
         out_specs=[VMEM] * len(faces),
         scratch_shapes=[
@@ -510,16 +512,19 @@
     )(hbm(far_table), hbm(leaf_coupling), dens, basis)
     tail = cap * far_groups * columns
     if side == 2:
-        arrived = [crossed(value, stride) for (_, stride), value in zip(faces, outgoing)]
-        held = jnp.concatenate([root] + [value[tail:] for value in arrived], axis=0)
-        whole = leaf_devices - 1
-        opposite = crossed(held, whole)
-        turns = [0] + [stride for _, stride in faces]
-        roots = [
-            ([(0, 0)], root),
-            ([(turn ^ whole, row * columns) for row, turn in enumerate(turns)], opposite),
+        payloads = [outgoing[0]] + [
+            jnp.concatenate([value, beside], axis=0) for value in outgoing[1:]
         ]
-        roots += [([(stride, tail)], value) for (_, stride), value in zip(faces, arrived)]
+        arrived = [crossed(value, stride) for (_, stride), value in zip(faces, payloads)]
+        first, second, third = (stride for _, stride in faces)
+        far_pair = crossed(arrived[2][tail:], second)
+        roots = [([(0, 0)], root), ([(first, 0)], beside)]
+        for stride, value, row in (
+            (second, arrived[1], tail),
+            (third, arrived[2], tail),
+            (second ^ third, far_pair, 0),
+        ):
+            roots.append(([(stride, row), (stride ^ first, row + columns)], value))
     else:
         arrived = [shifted(value, "leaf", stride) for (_, stride), value in zip(faces, outgoing)]
         roots = [(None, lax.all_gather(root, "leaf", axis=0))]

time: 28.6 us -> 28 us (0.979)
  starting transfers between devices: 12.7 us -> 11.2 us
  waiting for transfers between devices: 2.24 us -> 3.14 us
    ppermute x4 -> x5, starting transfers between devices: 8.13 us -> 6.69 us  [crossed(): lax.ppermute(value, 'leaf', [(i, i ^ turn) for i in range(leaf_devices)])]
    ppermute x4, waiting for transfers between devices: 0.01 us -> 1.06 us  [rotated(): lax.ppermute(value, axis, [(i, (i - shift) % count) for i in range(count)])]
    ppermute x4 -> x5, waiting for transfers between devices: 2.23 us -> 2.08 us  [crossed(): lax.ppermute(value, 'leaf', [(i, i ^ turn) for i in range(leaf_devices)])]
  transfers between devices with their start and end apart: 8 -> 9, of which waited for: 1 -> 3; matrix products, arithmetic and copies ran while one was open for 0% -> 0% of each run, Pallas kernels for 36% -> 37%
where the time goes in v4:
time: 28 us; the launch traced here: 27.9 us
  Pallas kernels  13.4 us (48%)
  starting transfers between devices  11.2 us (40%)
  waiting for transfers between devices  3.14 us (11%)
    ppermute x5, starting transfers between devices, crossed(): lax.ppermute(value, 'leaf', [(i, i ^ turn) for i in range(leaf_devices)])  6.69 us
    ppermute x4, starting transfers between devices, rotated(): lax.ppermute(value, axis, [(i, (i - shift) % count) for i in range(count)])  4.51 us
    pallas_call x1, Pallas kernels, local(): pl.pallas_call(up_kernel, out_shape=[jax.ShapeDtypeStruct(densities.shape...  3.92 us
    pallas_call x1, Pallas kernels, local(): pl.pallas_call(couple_kernel, out_shape=[jax.ShapeDtypeStruct(far_table.s...  2.67 us
    pallas_call x1, Pallas kernels, local(): pl.pallas_call(functools.partial(near_kernel, faces, far_groups, share),...  2.44 us
    ppermute x5, waiting for transfers between devices, crossed(): lax.ppermute(value, 'leaf', [(i, i ^ turn) for i in range(leaf_devices)])  2.08 us
    pallas_call x1, Pallas kernels, local(): pl.pallas_call(project_kernel, out_shape=jax.ShapeDtypeStruct((columns, p...  1.89 us
    ppermute x4, waiting for transfers between devices, rotated(): lax.ppermute(value, axis, [(i, (i - shift) % count) for i in range(count)])  1.06 us
  transfers between devices with their start and end apart: 9, of which 3 were waited for; matrix products, arithmetic and copies ran while one was open for 0% of the time, Pallas kernels for 37%

profile of v4, /device:TPU:0, one launch (start us, length us, event | category | flops | bytes accessed | tf_op | source)
XLA Modules:
  0.0 27.9 jit_solution(13353468183193165339)
XLA Ops:
  0.0 2.9 %collective-permute-start = (bf16[16,4096]{1,0:T(8,128)(2,1)}, bf16[16,4096]{1,0:T(8,128)(2,1)S(1)}, u32[]{:S(2)}, u32[]{:S(2)}) collective-permute-start(bf16[16,4096]{1,0:T(8,128)(2,1)} %dens_hbm.1), channel_id=1, source_target_pairs={{0,2},{2,0},{1,3},{3,1},{4,6},{6,4},{5,7},{7,5},{8,10},{10,8},{9,1... | collective-permute-start | bytes 393224 | tf_op jit(solution)/shard_map/ppermute | solution.py:434
  2.9 0.0 collective-permute-start.1
  2.9 3.9 %up.1 = (bf16[16,4096]{1,0:T(8,128)(2,1)S(1)}, f32[32,4096]{1,0:T(8,128)S(1)}, s32[6,4,8]{2,1,0:T(4,128)S(1)}, s32[2,32]{1,0:T(2,128)S(1)}, bf16[32,4096]{1,0:T(...) custom-call(bf16[16,4096]{1,0:T(8,128)(2,1)} %dens_hbm.1, f32[32,4096]{1,0:T(8,128)} %bases_hbm.1, ...), custom_call_target="tpu_custom_call" | custom-call | bytes 12915000 | tf_op jit(solution)/shard_map/up/pallas_call | solution.py:443
  6.9 0.0 collective-permute-done.1.refs_1_
  6.9 0.0 collective-permute-done.refs_0_.refs_3_
  6.9 0.6 %collective-permute-start.6 = (bf16[32,2,128,128]{3,2,1,0:T(8,128)(2,1)}, bf16[32,2,128,128]{3,2,1,0:T(8,128)(2,1)S(1)}, u32[]{:S(2)}, u32[]{:S(2)}) collective-permute-start(bf16[32,2,128,128]{3,2,1,0:T(8,128)(2,1)} %refs_7_.1), channel_id=1, source_target_pairs={{0,1},{1,0},{2,3},{3,2},{4,5},{5,4},{6,7},{7,6},{8,9},{9,8},{10,11... | collective-permute-start | bytes 6291464 | tf_op jit(solution)/shard_map/ppermute | solution.py:434
  7.5 1.5 %collective-permute-start.3 = (bf16[16,128]{1,0:T(8,128)(2,1)S(1)}, bf16[16,128]{1,0:T(8,128)(2,1)S(1)}, u32[]{:S(2)}, u32[]{:S(2)}) collective-permute-start(bf16[16,128]{1,0:T(8,128)(2,1)S(1)} %get-tuple-element.36.root_ref.refs_0_), channel_id=1, source_target_pairs={{0,4},{4,0},{8,12},{12,8},{16,20},{20,16},{24,28},{28,24},{1,5},{5... | collective-permute-start | bytes 12296 | tf_op jit(solution)/shard_map/ppermute | solution.py:437
  9.0 0.8 %select.1 = (bf16[192,128]{1,0:T(8,128)(2,1)S(1)}, bf16[144,128]{1,0:T(8,128)(2,1)S(1)}, bf16[144,128]{1,0:T(8,128)(2,1)S(1)}) custom-call(s32[6,4,8]{2,1,0:T(4,128)S(1)} %get-tuple-element.32.send_vmem, bf16[16,4096]{1,0:T(8,128)(2,1)S(1)} %get-tuple-element.41.dens_ref.refs_2_, bf16[16,128]{1,0:T(8,128)(2,1)S(1)} %get-tuple-element.36.root_ref.refs_0_, ...), custom_call_target="tpu_custom_call" | custom-call | bytes 3690000 | tf_op jit(solution)/shard_map/select/pallas_call | solution.py:482
  9.8 0.6 %collective-permute-start.2 = (bf16[192,128]{1,0:T(8,128)(2,1)S(1)}, bf16[192,128]{1,0:T(8,128)(2,1)S(1)}, u32[]{:S(2)}, u32[]{:S(2)}) collective-permute-start(bf16[192,128]{1,0:T(8,128)(2,1)S(1)} %get-tuple-element.49), channel_id=1, source_target_pairs={{0,4},{4,0},{8,12},{12,8},{16,20},{20,16},{24,28},{28,24},{1,5},{5... | collective-permute-start | bytes 147464 | tf_op jit(solution)/shard_map/ppermute | solution.py:437
  10.4 0.7 %collective-permute-done.3.refs_1_ = bf16[16,128]{1,0:T(8,128)(2,1)S(1)} collective-permute-done((bf16[16,128]{1,0:T(8,128)(2,1)S(1)}, bf16[16,128]{1,0:T(8,128)(2,1)S(1)}, u32[]{:S(2)}, u32[]{:S(2)}) %collective-permute-start.3) | collective-permute-done | bytes 4128 | tf_op jit(solution)/shard_map/ppermute | solution.py:437
  11.1 1.6 %collective-permute-start.4 = (bf16[160,128]{1,0:T(8,128)(2,1)S(1)}, bf16[160,128]{1,0:T(8,128)(2,1)S(1)}, u32[]{:S(2)}, u32[]{:S(2)}) collective-permute-start(bf16[160,128]{1,0:T(8,128)(2,1)S(1)} %get-tuple-element.56), channel_id=1, source_target_pairs={{0,8},{4,12},{8,0},{12,4},{16,24},{20,28},{24,16},{28,20},{1,9},{5... | collective-permute-start | bytes 122888 | tf_op jit(solution)/shard_map/ppermute | solution.py:437
  12.6 2.6 %collective-permute-start.5 = (bf16[160,128]{1,0:T(8,128)(2,1)S(1)}, bf16[160,128]{1,0:T(8,128)(2,1)S(1)}, u32[]{:S(2)}, u32[]{:S(2)}) collective-permute-start(bf16[160,128]{1,0:T(8,128)(2,1)S(1)} %get-tuple-element.55), channel_id=1, source_target_pairs={{0,16},{4,20},{8,24},{12,28},{16,0},{20,4},{24,8},{28,12},{1,17},{... | collective-permute-start | bytes 122888 | tf_op jit(solution)/shard_map/ppermute | solution.py:437
  15.2 2.7 %couple.1 = (s32[8,32]{1,0:T(8,128)S(1)}, f32[32,8,32,32]{3,2,1,0:T(8,128)S(1)}, bf16[1024,32]{1,0:T(8,128)(2,1)S(1)}, f32[16,512]{1,0:T(8,128)S(1)}) custom-call(s32[8,32]{1,0:T(8,128)} %bitcast.8, f32[32,8,32,32]{3,2,1,0:T(8,128)} %coupling_hbm.1, bf16[16,4096]{1,0:T(8,128)(2,1)S(1)} %get-tuple-element.41.dens_ref.refs_2_, ...), custom_call_target="tpu_custom_call" | custom-call | bytes 7380000 | tf_op jit(solution)/shard_map/couple/pallas_call | solution.py:498
  17.9 0.0 collective-permute-done.4.refs_5_.refs_2_
  17.9 0.0 collective-permute-done.5.refs_6_.refs_3_
  18.0 0.0 collective-permute-done.2.refs_4_
  18.0 0.0 collective-permute-done.6.refs_8_
  18.0 0.0 copy-start
  18.0 0.0 copy-start.1
  18.0 2.4 %near.1 = (f32[16,4096]{1,0:T(8,128)S(1)}, f32[16,4096]{1,0:T(8,128)S(1)}) custom-call(s32[2,32]{1,0:T(2,128)S(1)} %get-tuple-element.47.refs_0_, s32[2,32]{1,0:T(2,128)S(1)} %collective-permute-done.1.refs_1_, bf16[16,4096]{1,0:T(8,128)(2,1)S(1)} %get-tuple-element.41.dens_ref.refs_2_, bf16[16,4096]{1,0:T(8,128)(2,1)S(1)} %collective-permute-done.refs_0_.refs_3_, ...), custom_call_target="tpu_custom_call" | custom-call | bytes 11070000 | tf_op jit(solution)/shard_map/near/pallas_call | solution.py:533
  20.4 1.0 %collective-permute-start.8 = (f32[16,4096]{1,0:T(8,128)S(1)}, f32[16,4096]{1,0:T(8,128)S(1)}, u32[]{:S(2)}, u32[]{:S(2)}) collective-permute-start(f32[16,4096]{1,0:T(8,128)S(1)} %get-tuple-element.54), channel_id=1, source_target_pairs={{0,2},{2,0},{1,3},{3,1},{4,6},{6,4},{5,7},{7,5},{8,10},{10,8},{9,1... | collective-permute-start | bytes 786440 | tf_op jit(solution)/shard_map/ppermute | solution.py:434
  21.5 0.4 %collective-permute-start.7 = (bf16[32,128]{1,0:T(8,128)(2,1)S(1)}, bf16[32,128]{1,0:T(8,128)(2,1)S(1)}, u32[]{:S(2)}, u32[]{:S(2)}) collective-permute-start(bf16[32,128]{1,0:T(8,128)(2,1)S(1)} %slice.4), channel_id=1, source_target_pairs={{0,8},{4,12},{8,0},{12,4},{16,24},{20,28},{24,16},{28,20},{1,9},{5... | collective-permute-start | bytes 24584 | tf_op jit(solution)/shard_map/ppermute | solution.py:437
  21.9 1.9 %project.1.term_ref = f32[16,4096]{1,0:T(8,128)S(1)} custom-call(s32[8,32]{1,0:T(8,128)S(1)} %get-tuple-element.43.table_ref, f32[32,8,32,32]{3,2,1,0:T(8,128)S(1)} %get-tuple-element.44.coupling_ref, bf16[1024,32]{1,0:T(8,128)(2,1)S(1)} %get-tuple-element.45.turned_ref, f32[16,512]{1,0:T(8,128)S(1)} %get-tuple-element.46.refs_9_.first_ref, ...), custom_call_target="tpu_custom_call" | custom-call | bytes 5535000 | tf_op jit(solution)/shard_map/project/pallas_call | solution.py:554
  23.8 1.3 %collective-permute-done.7.refs_4_ = bf16[32,128]{1,0:T(8,128)(2,1)S(1)} collective-permute-done((bf16[32,128]{1,0:T(8,128)(2,1)S(1)}, bf16[32,128]{1,0:T(8,128)(2,1)S(1)}, u32[]{:S(2)}, u32[]{:S(2)}) %collective-permute-start.7) | collective-permute-done | bytes 8224 | tf_op jit(solution)/shard_map/ppermute | solution.py:437
  25.1 0.0 copy-done
  25.1 0.0 copy-done.1
  25.1 1.0 %far.1.refs_0_ = f32[16,4096]{1,0:T(8,128)S(1)} custom-call(f32[16,32,32]{2,1,0:T(8,128)S(1)} %copy-done.1, f32[16,3,32,32]{3,2,1,0:T(8,128)S(1)} %copy-done, bf16[32,4096]{1,0:T(8,128)(2,1)S(1)} %get-tuple-element.30.high_ref, bf16[32,4096]{1,0:T(8,128)(2,1)S(1)} %get-tuple-element.31.low_ref, f32[16,4096]{1,0:T(8,128)S(1)} %project.1.term_ref, ...), custom_call_target="tpu_custom_call" | custom-call | bytes 5535000 | tf_op jit(solution)/shard_map/far/pallas_call | solution.py:564
  26.1 1.1 %collective-permute-done.8.refs_1_ = f32[16,4096]{1,0:T(8,128)S(1)} collective-permute-done((f32[16,4096]{1,0:T(8,128)S(1)}, f32[16,4096]{1,0:T(8,128)S(1)}, u32[]{:S(2)}, u32[]{:S(2)}) %collective-permute-start.8) | collective-permute-done | bytes 262176 | tf_op jit(solution)/shard_map/ppermute | solution.py:434
  27.1 0.7 %add.1 = f32[16,4096]{1,0:T(8,128)} custom-call(f32[16,4096]{1,0:T(8,128)S(1)} %far.1.refs_0_, f32[16,4096]{1,0:T(8,128)S(1)} %collective-permute-done.8.refs_1_), custom_call_target="tpu_custom_call" | custom-call | bytes 1845000 | tf_op jit(solution)/shard_map/add/pallas_call | solution.py:577
  (2 shorter events, 0.0 us)
Async XLA Ops:
  0.0 6.9 %collective-permute-start = (bf16[16,4096]{1,0:T(8,128)(2,1)}, bf16[16,4096]{1,0:T(8,128)(2,1)S(1)}, u32[]{:S(2)}, u32[]{:S(2)}) collective-permute-start(bf16[16,4096]{1,0:T(8,128)(2,1)} %dens_hbm.1), channel_id=1, source_target_pairs={{0,2},{2,0},{1,3},{3,1},{4,6},{6,4},{5,7},{7,5},{8,10},{10,8},{9,1... | collective-permute-start | bytes 393224 | tf_op jit(solution)/shard_map/ppermute | solution.py:434
  2.9 3.9 %collective-permute-start.1 = (s32[2,32]{1,0:T(2,128)}, s32[2,32]{1,0:T(2,128)S(1)}, u32[]{:S(2)}, u32[]{:S(2)}) collective-permute-start(s32[2,32]{1,0:T(2,128)} %bitcast.9), channel_id=1, source_target_pairs={{0,1},{1,0},{2,3},{3,2},{4,5},{5,4},{6,7},{7,6},{8,9},{9,8},{10,11... | collective-permute-start | bytes 776 | tf_op jit(solution)/shard_map/ppermute | solution.py:434
  6.9 11.1 %collective-permute-start.6 = (bf16[32,2,128,128]{3,2,1,0:T(8,128)(2,1)}, bf16[32,2,128,128]{3,2,1,0:T(8,128)(2,1)S(1)}, u32[]{:S(2)}, u32[]{:S(2)}) collective-permute-start(bf16[32,2,128,128]{3,2,1,0:T(8,128)(2,1)} %refs_7_.1), channel_id=1, source_target_pairs={{0,1},{1,0},{2,3},{3,2},{4,5},{5,4},{6,7},{7,6},{8,9},{9,8},{10,11... | collective-permute-start | bytes 6291464 | tf_op jit(solution)/shard_map/ppermute | solution.py:434
  7.5 3.6 %collective-permute-start.3 = (bf16[16,128]{1,0:T(8,128)(2,1)S(1)}, bf16[16,128]{1,0:T(8,128)(2,1)S(1)}, u32[]{:S(2)}, u32[]{:S(2)}) collective-permute-start(bf16[16,128]{1,0:T(8,128)(2,1)S(1)} %get-tuple-element.36.root_ref.refs_0_), channel_id=1, source_target_pairs={{0,4},{4,0},{8,12},{12,8},{16,20},{20,16},{24,28},{28,24},{1,5},{5... | collective-permute-start | bytes 12296 | tf_op jit(solution)/shard_map/ppermute | solution.py:437
  9.8 8.2 %collective-permute-start.2 = (bf16[192,128]{1,0:T(8,128)(2,1)S(1)}, bf16[192,128]{1,0:T(8,128)(2,1)S(1)}, u32[]{:S(2)}, u32[]{:S(2)}) collective-permute-start(bf16[192,128]{1,0:T(8,128)(2,1)S(1)} %get-tuple-element.49), channel_id=1, source_target_pairs={{0,4},{4,0},{8,12},{12,8},{16,20},{20,16},{24,28},{28,24},{1,5},{5... | collective-permute-start | bytes 147464 | tf_op jit(solution)/shard_map/ppermute | solution.py:437
  11.1 6.8 %collective-permute-start.4 = (bf16[160,128]{1,0:T(8,128)(2,1)S(1)}, bf16[160,128]{1,0:T(8,128)(2,1)S(1)}, u32[]{:S(2)}, u32[]{:S(2)}) collective-permute-start(bf16[160,128]{1,0:T(8,128)(2,1)S(1)} %get-tuple-element.56), channel_id=1, source_target_pairs={{0,8},{4,12},{8,0},{12,4},{16,24},{20,28},{24,16},{28,20},{1,9},{5... | collective-permute-start | bytes 122888 | tf_op jit(solution)/shard_map/ppermute | solution.py:437
  12.6 5.3 %collective-permute-start.5 = (bf16[160,128]{1,0:T(8,128)(2,1)S(1)}, bf16[160,128]{1,0:T(8,128)(2,1)S(1)}, u32[]{:S(2)}, u32[]{:S(2)}) collective-permute-start(bf16[160,128]{1,0:T(8,128)(2,1)S(1)} %get-tuple-element.55), channel_id=1, source_target_pairs={{0,16},{4,20},{8,24},{12,28},{16,0},{20,4},{24,8},{28,12},{1,17},{... | collective-permute-start | bytes 122888 | tf_op jit(solution)/shard_map/ppermute | solution.py:437
  18.0 7.1 %copy-start = (f32[16,3,32,32]{3,2,1,0:T(8,128)S(1)}, f32[16,3,32,32]{3,2,1,0:T(8,128)}, u32[]{:S(2)}) copy-start(f32[16,3,32,32]{3,2,1,0:T(8,128)} %cross_ref.1) | copy-start | bytes 589828
  18.0 7.1 %copy-start.1 = (f32[16,32,32]{2,1,0:T(8,128)S(1)}, f32[16,32,32]{2,1,0:T(8,128)}, u32[]{:S(2)}) copy-start(f32[16,32,32]{2,1,0:T(8,128)} %upper_ref.1) | copy-start | bytes 196612
  20.4 6.7 %collective-permute-start.8 = (f32[16,4096]{1,0:T(8,128)S(1)}, f32[16,4096]{1,0:T(8,128)S(1)}, u32[]{:S(2)}, u32[]{:S(2)}) collective-permute-start(f32[16,4096]{1,0:T(8,128)S(1)} %get-tuple-element.54), channel_id=1, source_target_pairs={{0,2},{2,0},{1,3},{3,1},{4,6},{6,4},{5,7},{7,5},{8,10},{10,8},{9,1... | collective-permute-start | bytes 786440 | tf_op jit(solution)/shard_map/ppermute | solution.py:434
  21.5 3.7 %collective-permute-start.7 = (bf16[32,128]{1,0:T(8,128)(2,1)S(1)}, bf16[32,128]{1,0:T(8,128)(2,1)S(1)}, u32[]{:S(2)}, u32[]{:S(2)}) collective-permute-start(bf16[32,128]{1,0:T(8,128)(2,1)S(1)} %slice.4), channel_id=1, source_target_pairs={{0,8},{4,12},{8,0},{12,4},{16,24},{20,28},{24,16},{28,20},{1,9},{5... | collective-permute-start | bytes 24584 | tf_op jit(solution)/shard_map/ppermute | solution.py:437

commit v5 on v4

--- a/solution.py
+++ b/solution.py
@@ -468,17 +468,17 @@
     )
     all_sources[0] = sources
 
-    beside = crossed(root, 1) if side == 2 else None
+    beside = crossed(root, 4) if side == 2 else None
     later_blocks, others, all_sources, root = lax.optimization_barrier(
         (near_blocks, others, all_sources, root)
     )
     mate_blocks = [rotated(later_blocks, "mate", part) for part in range(1, share)]
 
     if side == 2:
-        faces = [((2 * axis, 2 * axis + 1), 2**axis) for axis in range(3)]
+        faces = [((2 * axis, 2 * axis + 1), 2**axis) for axis in (2, 0, 1)]
     else:
         faces = [((direction,), offset) for direction, offset in enumerate(offsets)]
-    chunks = [(cap * far_groups + (1 if stride > 1 else 4)) * columns for _, stride in faces]
+    chunks = [(cap * far_groups + (1 if place else 3)) * columns for place in range(len(faces))]
     outgoing = pl.pallas_call(
         functools.partial(select_kernel, faces, far_groups),
         out_shape=[jax.ShapeDtypeStruct((chunk, LANES), BF16) for chunk in chunks],

time: 28 us -> 27.8 us (level)
  no operation moved by 1% of the time
where the time goes in v5:
time: 27.8 us; the launch traced here: 27.7 us
  Pallas kernels  13.4 us (48%)
  starting transfers between devices  11.1 us (40%)
  waiting for transfers between devices  3.05 us (11%)
    ppermute x5, starting transfers between devices, crossed(): lax.ppermute(value, 'leaf', [(i, i ^ turn) for i in range(leaf_devices)])  6.59 us
    ppermute x4, starting transfers between devices, rotated(): lax.ppermute(value, axis, [(i, (i - shift) % count) for i in range(count)])  4.51 us
    pallas_call x1, Pallas kernels, local(): pl.pallas_call(up_kernel, out_shape=[jax.ShapeDtypeStruct(densities.shape...  3.92 us
    pallas_call x1, Pallas kernels, local(): pl.pallas_call(couple_kernel, out_shape=[jax.ShapeDtypeStruct(far_table.s...  2.67 us
    pallas_call x1, Pallas kernels, local(): pl.pallas_call(functools.partial(near_kernel, faces, far_groups, share),...  2.44 us
    ppermute x5, waiting for transfers between devices, crossed(): lax.ppermute(value, 'leaf', [(i, i ^ turn) for i in range(leaf_devices)])  1.97 us
    pallas_call x1, Pallas kernels, local(): pl.pallas_call(project_kernel, out_shape=jax.ShapeDtypeStruct((columns, p...  1.89 us
    ppermute x4, waiting for transfers between devices, rotated(): lax.ppermute(value, axis, [(i, (i - shift) % count) for i in range(count)])  1.08 us
  transfers between devices with their start and end apart: 9, of which 3 were waited for; matrix products, arithmetic and copies ran while one was open for 0% of the time, Pallas kernels for 37%

profile of v5, /device:TPU:0, one launch (start us, length us, event | category | flops | bytes accessed | tf_op | source)
XLA Modules:
  0.0 27.7 jit_solution(12368058498214034228)
XLA Ops:
  0.0 2.9 %collective-permute-start = (bf16[16,4096]{1,0:T(8,128)(2,1)}, bf16[16,4096]{1,0:T(8,128)(2,1)S(1)}, u32[]{:S(2)}, u32[]{:S(2)}) collective-permute-start(bf16[16,4096]{1,0:T(8,128)(2,1)} %dens_hbm.1), channel_id=1, source_target_pairs={{0,2},{2,0},{1,3},{3,1},{4,6},{6,4},{5,7},{7,5},{8,10},{10,8},{9,1... | collective-permute-start | bytes 393224 | tf_op jit(solution)/shard_map/ppermute | solution.py:434
  2.9 0.0 collective-permute-start.1
  2.9 3.9 %up.1 = (bf16[16,4096]{1,0:T(8,128)(2,1)S(1)}, f32[32,4096]{1,0:T(8,128)S(1)}, s32[6,4,8]{2,1,0:T(4,128)S(1)}, s32[2,32]{1,0:T(2,128)S(1)}, bf16[32,4096]{1,0:T(...) custom-call(bf16[16,4096]{1,0:T(8,128)(2,1)} %dens_hbm.1, f32[32,4096]{1,0:T(8,128)} %bases_hbm.1, ...), custom_call_target="tpu_custom_call" | custom-call | bytes 12915000 | tf_op jit(solution)/shard_map/up/pallas_call | solution.py:443
  6.9 0.0 collective-permute-done.1.refs_1_
  6.9 0.0 collective-permute-done.refs_0_.refs_3_
  6.9 0.6 %collective-permute-start.6 = (bf16[32,2,128,128]{3,2,1,0:T(8,128)(2,1)}, bf16[32,2,128,128]{3,2,1,0:T(8,128)(2,1)S(1)}, u32[]{:S(2)}, u32[]{:S(2)}) collective-permute-start(bf16[32,2,128,128]{3,2,1,0:T(8,128)(2,1)} %refs_7_.1), channel_id=1, source_target_pairs={{0,1},{1,0},{2,3},{3,2},{4,5},{5,4},{6,7},{7,6},{8,9},{9,8},{10,11... | collective-permute-start | bytes 6291464 | tf_op jit(solution)/shard_map/ppermute | solution.py:434
  7.5 2.6 %collective-permute-start.3 = (bf16[16,128]{1,0:T(8,128)(2,1)S(1)}, bf16[16,128]{1,0:T(8,128)(2,1)S(1)}, u32[]{:S(2)}, u32[]{:S(2)}) collective-permute-start(bf16[16,128]{1,0:T(8,128)(2,1)S(1)} %get-tuple-element.36.root_ref.refs_0_), channel_id=1, source_target_pairs={{0,16},{4,20},{8,24},{12,28},{16,0},{20,4},{24,8},{28,12},{1,17},{... | collective-permute-start | bytes 12296 | tf_op jit(solution)/shard_map/ppermute | solution.py:437
  10.0 0.8 %select.1 = (bf16[176,128]{1,0:T(8,128)(2,1)S(1)}, bf16[144,128]{1,0:T(8,128)(2,1)S(1)}, bf16[144,128]{1,0:T(8,128)(2,1)S(1)}) custom-call(s32[6,4,8]{2,1,0:T(4,128)S(1)} %get-tuple-element.32.send_vmem, bf16[16,4096]{1,0:T(8,128)(2,1)S(1)} %get-tuple-element.41.dens_ref.refs_2_, bf16[16,128]{1,0:T(8,128)(2,1)S(1)} %get-tuple-element.36.root_ref.refs_0_, ...), custom_call_target="tpu_custom_call" | custom-call | bytes 3690000 | tf_op jit(solution)/shard_map/select/pallas_call | solution.py:482
  10.9 0.4 %collective-permute-start.2 = (bf16[176,128]{1,0:T(8,128)(2,1)S(1)}, bf16[176,128]{1,0:T(8,128)(2,1)S(1)}, u32[]{:S(2)}, u32[]{:S(2)}) collective-permute-start(bf16[176,128]{1,0:T(8,128)(2,1)S(1)} %get-tuple-element.49), channel_id=1, source_target_pairs={{0,16},{4,20},{8,24},{12,28},{16,0},{20,4},{24,8},{28,12},{1,17},{... | collective-permute-start | bytes 135176 | tf_op jit(solution)/shard_map/ppermute | solution.py:437
  11.3 0.7 %collective-permute-done.3.refs_1_ = bf16[16,128]{1,0:T(8,128)(2,1)S(1)} collective-permute-done((bf16[16,128]{1,0:T(8,128)(2,1)S(1)}, bf16[16,128]{1,0:T(8,128)(2,1)S(1)}, u32[]{:S(2)}, u32[]{:S(2)}) %collective-permute-start.3) | collective-permute-done | bytes 4128 | tf_op jit(solution)/shard_map/ppermute | solution.py:437
  12.0 1.5 %collective-permute-start.4 = (bf16[160,128]{1,0:T(8,128)(2,1)S(1)}, bf16[160,128]{1,0:T(8,128)(2,1)S(1)}, u32[]{:S(2)}, u32[]{:S(2)}) collective-permute-start(bf16[160,128]{1,0:T(8,128)(2,1)S(1)} %get-tuple-element.56), channel_id=1, source_target_pairs={{0,4},{4,0},{8,12},{12,8},{16,20},{20,16},{24,28},{28,24},{1,5},{5... | collective-permute-start | bytes 122888 | tf_op jit(solution)/shard_map/ppermute | solution.py:437
  13.5 1.6 %collective-permute-start.5 = (bf16[160,128]{1,0:T(8,128)(2,1)S(1)}, bf16[160,128]{1,0:T(8,128)(2,1)S(1)}, u32[]{:S(2)}, u32[]{:S(2)}) collective-permute-start(bf16[160,128]{1,0:T(8,128)(2,1)S(1)} %get-tuple-element.55), channel_id=1, source_target_pairs={{0,8},{4,12},{8,0},{12,4},{16,24},{20,28},{24,16},{28,20},{1,9},{5... | collective-permute-start | bytes 122888 | tf_op jit(solution)/shard_map/ppermute | solution.py:437
  15.1 2.7 %couple.1 = (s32[8,32]{1,0:T(8,128)S(1)}, f32[32,8,32,32]{3,2,1,0:T(8,128)S(1)}, bf16[1024,32]{1,0:T(8,128)(2,1)S(1)}, f32[16,512]{1,0:T(8,128)S(1)}) custom-call(s32[8,32]{1,0:T(8,128)} %bitcast.8, f32[32,8,32,32]{3,2,1,0:T(8,128)} %coupling_hbm.1, bf16[16,4096]{1,0:T(8,128)(2,1)S(1)} %get-tuple-element.41.dens_ref.refs_2_, ...), custom_call_target="tpu_custom_call" | custom-call | bytes 7380000 | tf_op jit(solution)/shard_map/couple/pallas_call | solution.py:498
  17.8 0.0 collective-permute-done.4.refs_5_.refs_2_
  17.8 0.0 collective-permute-done.5.refs_6_.refs_3_
  17.8 0.0 collective-permute-done.2.refs_4_
  17.8 0.0 collective-permute-done.6.refs_8_
  17.8 0.0 copy-start
  17.8 0.0 copy-start.1
  17.8 2.4 %near.1 = (f32[16,4096]{1,0:T(8,128)S(1)}, f32[16,4096]{1,0:T(8,128)S(1)}) custom-call(s32[2,32]{1,0:T(2,128)S(1)} %get-tuple-element.47.refs_0_, s32[2,32]{1,0:T(2,128)S(1)} %collective-permute-done.1.refs_1_, bf16[16,4096]{1,0:T(8,128)(2,1)S(1)} %get-tuple-element.41.dens_ref.refs_2_, bf16[16,4096]{1,0:T(8,128)(2,1)S(1)} %collective-permute-done.refs_0_.refs_3_, ...), custom_call_target="tpu_custom_call" | custom-call | bytes 11070000 | tf_op jit(solution)/shard_map/near/pallas_call | solution.py:533
  20.3 1.0 %collective-permute-start.8 = (f32[16,4096]{1,0:T(8,128)S(1)}, f32[16,4096]{1,0:T(8,128)S(1)}, u32[]{:S(2)}, u32[]{:S(2)}) collective-permute-start(f32[16,4096]{1,0:T(8,128)S(1)} %get-tuple-element.54), channel_id=1, source_target_pairs={{0,2},{2,0},{1,3},{3,1},{4,6},{6,4},{5,7},{7,5},{8,10},{10,8},{9,1... | collective-permute-start | bytes 786440 | tf_op jit(solution)/shard_map/ppermute | solution.py:434
  21.3 0.5 %collective-permute-start.7 = (bf16[32,128]{1,0:T(8,128)(2,1)S(1)}, bf16[32,128]{1,0:T(8,128)(2,1)S(1)}, u32[]{:S(2)}, u32[]{:S(2)}) collective-permute-start(bf16[32,128]{1,0:T(8,128)(2,1)S(1)} %slice.4), channel_id=1, source_target_pairs={{0,4},{4,0},{8,12},{12,8},{16,20},{20,16},{24,28},{28,24},{1,5},{5... | collective-permute-start | bytes 24584 | tf_op jit(solution)/shard_map/ppermute | solution.py:437
  21.8 1.9 %project.1.term_ref = f32[16,4096]{1,0:T(8,128)S(1)} custom-call(s32[8,32]{1,0:T(8,128)S(1)} %get-tuple-element.43.table_ref, f32[32,8,32,32]{3,2,1,0:T(8,128)S(1)} %get-tuple-element.44.coupling_ref, bf16[1024,32]{1,0:T(8,128)(2,1)S(1)} %get-tuple-element.45.turned_ref, f32[16,512]{1,0:T(8,128)S(1)} %get-tuple-element.46.refs_9_.first_ref, ...), custom_call_target="tpu_custom_call" | custom-call | bytes 5535000 | tf_op jit(solution)/shard_map/project/pallas_call | solution.py:554
  23.7 1.3 %collective-permute-done.7.refs_4_ = bf16[32,128]{1,0:T(8,128)(2,1)S(1)} collective-permute-done((bf16[32,128]{1,0:T(8,128)(2,1)S(1)}, bf16[32,128]{1,0:T(8,128)(2,1)S(1)}, u32[]{:S(2)}, u32[]{:S(2)}) %collective-permute-start.7) | collective-permute-done | bytes 8224 | tf_op jit(solution)/shard_map/ppermute | solution.py:437
  24.9 0.0 copy-done
  24.9 0.0 copy-done.1
  24.9 1.0 %far.1.refs_0_ = f32[16,4096]{1,0:T(8,128)S(1)} custom-call(f32[16,32,32]{2,1,0:T(8,128)S(1)} %copy-done.1, f32[16,3,32,32]{3,2,1,0:T(8,128)S(1)} %copy-done, bf16[32,4096]{1,0:T(8,128)(2,1)S(1)} %get-tuple-element.30.high_ref, bf16[32,4096]{1,0:T(8,128)(2,1)S(1)} %get-tuple-element.31.low_ref, f32[16,4096]{1,0:T(8,128)S(1)} %project.1.term_ref, ...), custom_call_target="tpu_custom_call" | custom-call | bytes 5535000 | tf_op jit(solution)/shard_map/far/pallas_call | solution.py:564
  25.9 1.1 %collective-permute-done.8.refs_1_ = f32[16,4096]{1,0:T(8,128)S(1)} collective-permute-done((f32[16,4096]{1,0:T(8,128)S(1)}, f32[16,4096]{1,0:T(8,128)S(1)}, u32[]{:S(2)}, u32[]{:S(2)}) %collective-permute-start.8) | collective-permute-done | bytes 262176 | tf_op jit(solution)/shard_map/ppermute | solution.py:434
  26.9 0.7 %add.1 = f32[16,4096]{1,0:T(8,128)} custom-call(f32[16,4096]{1,0:T(8,128)S(1)} %far.1.refs_0_, f32[16,4096]{1,0:T(8,128)S(1)} %collective-permute-done.8.refs_1_), custom_call_target="tpu_custom_call" | custom-call | bytes 1845000 | tf_op jit(solution)/shard_map/add/pallas_call | solution.py:577
  (2 shorter events, 0.0 us)
Async XLA Ops:
  0.0 6.9 %collective-permute-start = (bf16[16,4096]{1,0:T(8,128)(2,1)}, bf16[16,4096]{1,0:T(8,128)(2,1)S(1)}, u32[]{:S(2)}, u32[]{:S(2)}) collective-permute-start(bf16[16,4096]{1,0:T(8,128)(2,1)} %dens_hbm.1), channel_id=1, source_target_pairs={{0,2},{2,0},{1,3},{3,1},{4,6},{6,4},{5,7},{7,5},{8,10},{10,8},{9,1... | collective-permute-start | bytes 393224 | tf_op jit(solution)/shard_map/ppermute | solution.py:434
  2.9 3.9 %collective-permute-start.1 = (s32[2,32]{1,0:T(2,128)}, s32[2,32]{1,0:T(2,128)S(1)}, u32[]{:S(2)}, u32[]{:S(2)}) collective-permute-start(s32[2,32]{1,0:T(2,128)} %bitcast.9), channel_id=1, source_target_pairs={{0,1},{1,0},{2,3},{3,2},{4,5},{5,4},{6,7},{7,6},{8,9},{9,8},{10,11... | collective-permute-start | bytes 776 | tf_op jit(solution)/shard_map/ppermute | solution.py:434
  6.9 10.9 %collective-permute-start.6 = (bf16[32,2,128,128]{3,2,1,0:T(8,128)(2,1)}, bf16[32,2,128,128]{3,2,1,0:T(8,128)(2,1)S(1)}, u32[]{:S(2)}, u32[]{:S(2)}) collective-permute-start(bf16[32,2,128,128]{3,2,1,0:T(8,128)(2,1)} %refs_7_.1), channel_id=1, source_target_pairs={{0,1},{1,0},{2,3},{3,2},{4,5},{5,4},{6,7},{7,6},{8,9},{9,8},{10,11... | collective-permute-start | bytes 6291464 | tf_op jit(solution)/shard_map/ppermute | solution.py:434
  7.5 4.5 %collective-permute-start.3 = (bf16[16,128]{1,0:T(8,128)(2,1)S(1)}, bf16[16,128]{1,0:T(8,128)(2,1)S(1)}, u32[]{:S(2)}, u32[]{:S(2)}) collective-permute-start(bf16[16,128]{1,0:T(8,128)(2,1)S(1)} %get-tuple-element.36.root_ref.refs_0_), channel_id=1, source_target_pairs={{0,16},{4,20},{8,24},{12,28},{16,0},{20,4},{24,8},{28,12},{1,17},{... | collective-permute-start | bytes 12296 | tf_op jit(solution)/shard_map/ppermute | solution.py:437
  10.9 6.9 %collective-permute-start.2 = (bf16[176,128]{1,0:T(8,128)(2,1)S(1)}, bf16[176,128]{1,0:T(8,128)(2,1)S(1)}, u32[]{:S(2)}, u32[]{:S(2)}) collective-permute-start(bf16[176,128]{1,0:T(8,128)(2,1)S(1)} %get-tuple-element.49), channel_id=1, source_target_pairs={{0,16},{4,20},{8,24},{12,28},{16,0},{20,4},{24,8},{28,12},{1,17},{... | collective-permute-start | bytes 135176 | tf_op jit(solution)/shard_map/ppermute | solution.py:437
  12.0 5.8 %collective-permute-start.4 = (bf16[160,128]{1,0:T(8,128)(2,1)S(1)}, bf16[160,128]{1,0:T(8,128)(2,1)S(1)}, u32[]{:S(2)}, u32[]{:S(2)}) collective-permute-start(bf16[160,128]{1,0:T(8,128)(2,1)S(1)} %get-tuple-element.56), channel_id=1, source_target_pairs={{0,4},{4,0},{8,12},{12,8},{16,20},{20,16},{24,28},{28,24},{1,5},{5... | collective-permute-start | bytes 122888 | tf_op jit(solution)/shard_map/ppermute | solution.py:437
  13.5 4.3 %collective-permute-start.5 = (bf16[160,128]{1,0:T(8,128)(2,1)S(1)}, bf16[160,128]{1,0:T(8,128)(2,1)S(1)}, u32[]{:S(2)}, u32[]{:S(2)}) collective-permute-start(bf16[160,128]{1,0:T(8,128)(2,1)S(1)} %get-tuple-element.55), channel_id=1, source_target_pairs={{0,8},{4,12},{8,0},{12,4},{16,24},{20,28},{24,16},{28,20},{1,9},{5... | collective-permute-start | bytes 122888 | tf_op jit(solution)/shard_map/ppermute | solution.py:437
  17.8 7.1 %copy-start = (f32[16,3,32,32]{3,2,1,0:T(8,128)S(1)}, f32[16,3,32,32]{3,2,1,0:T(8,128)}, u32[]{:S(2)}) copy-start(f32[16,3,32,32]{3,2,1,0:T(8,128)} %cross_ref.1) | copy-start | bytes 589828
  17.8 7.1 %copy-start.1 = (f32[16,32,32]{2,1,0:T(8,128)S(1)}, f32[16,32,32]{2,1,0:T(8,128)}, u32[]{:S(2)}) copy-start(f32[16,32,32]{2,1,0:T(8,128)} %upper_ref.1) | copy-start | bytes 196612
  20.3 6.7 %collective-permute-start.8 = (f32[16,4096]{1,0:T(8,128)S(1)}, f32[16,4096]{1,0:T(8,128)S(1)}, u32[]{:S(2)}, u32[]{:S(2)}) collective-permute-start(f32[16,4096]{1,0:T(8,128)S(1)} %get-tuple-element.54), channel_id=1, source_target_pairs={{0,2},{2,0},{1,3},{3,1},{4,6},{6,4},{5,7},{7,5},{8,10},{10,8},{9,1... | collective-permute-start | bytes 786440 | tf_op jit(solution)/shard_map/ppermute | solution.py:434
  21.3 3.7 %collective-permute-start.7 = (bf16[32,128]{1,0:T(8,128)(2,1)S(1)}, bf16[32,128]{1,0:T(8,128)(2,1)S(1)}, u32[]{:S(2)}, u32[]{:S(2)}) collective-permute-start(bf16[32,128]{1,0:T(8,128)(2,1)S(1)} %slice.4), channel_id=1, source_target_pairs={{0,4},{4,0},{8,12},{12,8},{16,20},{20,16},{24,28},{28,24},{1,5},{5... | collective-permute-start | bytes 24584 | tf_op jit(solution)/shard_map/ppermute | solution.py:437

commit v6 on v4

--- a/solution.py
+++ b/solution.py
@@ -12,6 +12,7 @@
 F32 = jnp.float32
 BF16 = jnp.bfloat16
 LANES = 128
+STEPS = 32000.0
 VMEM = pl.BlockSpec(memory_space=pltpu.VMEM)
 HBM = pl.BlockSpec(memory_space=pltpu.HBM)
 SMEM = pl.BlockSpec(memory_space=pltpu.SMEM)
@@ -191,6 +192,8 @@
     refs = refs[1:]
     out_refs, refs = refs[:far_groups], refs[far_groups:]
     source_refs, refs = refs[:share], refs[share:]
+    sum_refs, refs = refs[: far_groups - 1], refs[far_groups - 1 :]
+    peak_refs, refs = refs[: far_groups - 1], refs[far_groups - 1 :]
     block_ref, buffer_ref, small_sems, sems = refs
     columns, points = dens_ref.shape
     leaf_count, near_count, width, _ = block_ref.shape
@@ -219,6 +222,8 @@
     for copy in copies:
         copy.wait()
     tables = list(zip(source_refs[1:], mate_refs)) + [(source_refs[0], block_ref)]
+    own_ref, sent_refs = out_refs[0], out_refs[1:]
+    targets = (own_ref, *sum_refs)
     for turn, (source_ref, blocks_ref) in enumerate(tables):
         for leaf in range(leaf_count):
             if blocks_ref is block_ref and leaf % chunk == 0:
@@ -227,9 +232,26 @@
             blocks = [blocks_ref[leaf, block] for block in range(near_count)]
             total = dot_nt(jnp.concatenate(panels, axis=1), jnp.concatenate(blocks, axis=1))
             lanes = slice(leaf * width, (leaf + 1) * width)
-            for part, out_ref in enumerate(out_refs):
+            for part, target_ref in enumerate(targets):
                 term = total[part * columns : (part + 1) * columns]
-                out_ref[:, lanes] = term if turn == 0 else out_ref[:, lanes] + term
+                if turn:
+                    term = target_ref[:, lanes] + term
+                target_ref[:, lanes] = term
+                if part and turn == share - 1:
+                    peak_refs[part - 1][leaf : leaf + 1, :] = jnp.max(
+                        jnp.abs(term), axis=0, keepdims=True
+                    )
+    for sum_ref, peak_ref, sent_ref in zip(sum_refs, peak_refs, sent_refs):
+        power = jnp.floor(jnp.log2(jnp.maximum(peak_ref[...], 2.0**-100))) + 1.0
+        factor = STEPS * jnp.exp2(-power)
+        for leaf in range(leaf_count):
+            lanes = slice(leaf * width, (leaf + 1) * width)
+            steps = sum_ref[:, lanes] * factor[leaf : leaf + 1, :]
+            sent_ref[:, lanes] = jnp.floor(steps + 0.5).astype(jnp.int32).astype(jnp.int16)
+        power = power.astype(jnp.int32).astype(jnp.int16)
+        for first in range(0, leaf_count, columns):
+            spot = points + first // columns * width
+            sent_ref[:, spot : spot + width] = power[first : first + columns]
 
 
 def coupled(leaves, far_ref, coupling_ref, turned_ref):
@@ -314,12 +336,21 @@
 
 
 def far_kernel(
-    roots, upper_ref, cross_ref, high_ref, low_ref, term_ref, *refs,
+    roots, leaf_count, upper_ref, cross_ref, high_ref, low_ref, term_ref, *refs,
 ):
     root_refs, refs = refs[: len(roots)], refs[len(roots) :]
-    out_ref, tile_ref, tree_ref = refs
+    sent_refs, (out_hbm, sum_ref, tile_ref, tree_ref, sems) = refs[:-5], refs[-5:]
     device = lax.axis_index("leaf")
-    columns, points = out_ref.shape
+    columns, points = sum_ref.shape
+    width = points // leaf_count
+    factors = []
+    for sent_ref in sent_refs:
+        powers = [
+            sent_ref[:, points + first // columns * width :][:, :width]
+            for first in range(0, leaf_count, columns)
+        ]
+        power = jnp.concatenate([p.astype(jnp.int32).astype(F32) for p in powers], axis=0)
+        factors.append(jnp.exp2(power) * (1.0 / STEPS))
     rank = upper_ref.shape[1]
     device_count = upper_ref.shape[0] // 2
     for tiles, root_ref in zip(roots, root_refs):
@@ -369,24 +400,19 @@
             total = total + split_dot(dot_nt, field, *halves(upper_ref[node]))
         field = total
         level *= 2
-    step = 4 * LANES
-    for first in range(0, points, step):
-        spots = slice(first, first + step)
-        out_ref[:, spots] = term_ref[:, spots] + split_dot(
-            dot_nn, field, high_ref[:, spots], low_ref[:, spots]
-        )
-
-
-def add_kernel(*refs):
-    term_refs, (out_hbm, sum_ref, sems) = refs[:-3], refs[-3:]
     chunk_count = sems.shape[0]
-    step = sum_ref.shape[1] // chunk_count
+    step = points // chunk_count
     copies = []
     for index in range(chunk_count):
         spots = slice(index * step, (index + 1) * step)
-        total = term_refs[0][:, spots]
-        for term_ref in term_refs[1:]:
-            total = total + term_ref[:, spots]
+        total = term_ref[:, spots] + split_dot(
+            dot_nn, field, high_ref[:, spots], low_ref[:, spots]
+        )
+        for sent_ref, factor in zip(sent_refs, factors):
+            steps = sent_ref[:, spots].astype(jnp.int32).astype(F32)
+            leaves = range(index * leaf_count // chunk_count, (index + 1) * leaf_count // chunk_count)
+            scale = jnp.concatenate([factor[leaf : leaf + 1] for leaf in leaves], axis=1)
+            total = total + steps * scale
         sum_ref[:, spots] = total
         copies += fetch(
             [(sum_ref.at[:, pl.ds(index * step, step)], out_hbm.at[:, pl.ds(index * step, step)])],
@@ -478,7 +504,7 @@
         faces = [((2 * axis, 2 * axis + 1), 2**axis) for axis in range(3)]
     else:
         faces = [((direction,), offset) for direction, offset in enumerate(offsets)]
-    chunks = [(cap * far_groups + (1 if stride > 1 else 4)) * columns for _, stride in faces]
+    chunks = [(cap * far_groups + (1 if place else 3)) * columns for place in range(len(faces))]
     outgoing = pl.pallas_call(
         functools.partial(select_kernel, faces, far_groups),
         out_shape=[jax.ShapeDtypeStruct((chunk, LANES), BF16) for chunk in chunks],
@@ -530,14 +556,18 @@
         roots = [(None, lax.all_gather(root, "leaf", axis=0))]
 
     slots = leaf_count + len(offsets) * cap
+    tables = -(-leaf_count // columns) * width
     partials = pl.pallas_call(
         functools.partial(near_kernel, faces, far_groups, share),
-        out_shape=[jax.ShapeDtypeStruct((columns, points), F32)] * far_groups,
+        out_shape=[jax.ShapeDtypeStruct((columns, points), F32)]
+        + [jax.ShapeDtypeStruct((columns, points + tables), jnp.int16)] * (far_groups - 1),
         in_specs=[VMEM] * (share + far_groups + len(faces))
         + [HBM]
         + [VMEM] * share,
         out_specs=[VMEM] * far_groups,
         scratch_shapes=[pltpu.SMEM(sources.shape, jnp.int32)] * share
+        + [pltpu.VMEM((columns, points), F32)] * (far_groups - 1)
+        + [pltpu.VMEM((leaf_count, width), F32)] * (far_groups - 1)
         + [
             pltpu.VMEM(near_blocks.shape, BF16),
             pltpu.VMEM((slots, far_groups * columns, width), BF16),
@@ -561,29 +591,21 @@
         cost_estimate=hint(1.5),
         name="project",
     )(*coupling, leaf_local, basis, partials[0])
-    total = pl.pallas_call(
-        functools.partial(far_kernel, [tiles for tiles, _ in roots]),
+    return pl.pallas_call(
+        functools.partial(far_kernel, [tiles for tiles, _ in roots], leaf_count),
         out_shape=jax.ShapeDtypeStruct((columns, points), F32),
-        in_specs=[VMEM] * (5 + len(roots)),
-        out_specs=VMEM,
+        in_specs=[VMEM] * (5 + len(roots) + len(received)),
+        out_specs=HBM,
         scratch_shapes=[
+            pltpu.VMEM((columns, points), F32),
             pltpu.VMEM((leaf_devices, columns, LANES), BF16),
             pltpu.VMEM((2 * leaf_devices, columns, rank), F32),
+            dma((8,)),
         ],
         compiler_params=params,
         cost_estimate=hint(1.5),
         name="far",
-    )(upper_transfer, up_coupling, high, low, partial, *[value for _, value in roots])
-    return pl.pallas_call(
-        add_kernel,
-        out_shape=jax.ShapeDtypeStruct((columns, points), F32),
-        in_specs=[VMEM] * (1 + len(received)),
-        out_specs=HBM,
-        scratch_shapes=[pltpu.VMEM((columns, points), F32), dma((4,))],
-        compiler_params=params,
-        cost_estimate=hint(0.5),
-        name="add",
-    )(total, *received)
+    )(upper_transfer, up_coupling, high, low, partial, *[value for _, value in roots], *received)
 
 
 def solution(mesh):

time: 28 us -> 27.5 us (0.982)
  waiting for transfers between devices: 3.14 us -> 2.56 us
    pallas_call x1 -> x0, Pallas kernels: 0.74 us -> none  [local(): pl.pallas_call(add_kernel, out_shape=jax.ShapeDtypeStruct((columns, point...]
    pallas_call x1, Pallas kernels: 0.95 us -> 1.67 us  [local(): pl.pallas_call(functools.partial(far_kernel, [tiles for tiles, _ in roots...]
    ppermute x4, waiting for transfers between devices: 1.06 us -> 0.48 us  [rotated(): lax.ppermute(value, axis, [(i, (i - shift) % count) for i in range(count)])]
  transfers between devices with their start and end apart: 9 -> 9, of which waited for: 3 -> 3; matrix products, arithmetic and copies ran while one was open for 0% -> 0% of each run, Pallas kernels for 37% -> 34%
where the time goes in v6:
time: 27.5 us; the launch traced here: 27.3 us
  Pallas kernels  13.5 us (49%)
  starting transfers between devices  11.2 us (41%)
  waiting for transfers between devices  2.56 us (9%)
    ppermute x5, starting transfers between devices, crossed(): lax.ppermute(value, 'leaf', [(i, i ^ turn) for i in range(leaf_devices)])  6.69 us
    ppermute x4, starting transfers between devices, rotated(): lax.ppermute(value, axis, [(i, (i - shift) % count) for i in range(count)])  4.51 us
    pallas_call x1, Pallas kernels, local(): pl.pallas_call(up_kernel, out_shape=[jax.ShapeDtypeStruct(densities.shape...  3.92 us
    pallas_call x1, Pallas kernels, local(): pl.pallas_call(couple_kernel, out_shape=[jax.ShapeDtypeStruct(far_table.s...  2.67 us
    pallas_call x1, Pallas kernels, local(): pl.pallas_call(functools.partial(near_kernel, faces, far_groups, share),...  2.51 us
    ppermute x5, waiting for transfers between devices, crossed(): lax.ppermute(value, 'leaf', [(i, i ^ turn) for i in range(leaf_devices)])  2.08 us
    pallas_call x1, Pallas kernels, local(): pl.pallas_call(project_kernel, out_shape=jax.ShapeDtypeStruct((columns, p...  1.89 us
    pallas_call x1, Pallas kernels, local(): pl.pallas_call(functools.partial(far_kernel, [tiles for tiles, _ in roots...  1.67 us
  transfers between devices with their start and end apart: 9, of which 3 were waited for; matrix products, arithmetic and copies ran while one was open for 0% of the time, Pallas kernels for 34%

profile of v6, /device:TPU:0, one launch (start us, length us, event | category | flops | bytes accessed | tf_op | source)
XLA Modules:
  0.0 27.3 jit_solution(5876920142742863842)
XLA Ops:
  0.0 2.9 %collective-permute-start = (bf16[16,4096]{1,0:T(8,128)(2,1)}, bf16[16,4096]{1,0:T(8,128)(2,1)S(1)}, u32[]{:S(2)}, u32[]{:S(2)}) collective-permute-start(bf16[16,4096]{1,0:T(8,128)(2,1)} %dens_hbm.1), channel_id=1, source_target_pairs={{0,2},{2,0},{1,3},{3,1},{4,6},{6,4},{5,7},{7,5},{8,10},{10,8},{9,1... | collective-permute-start | bytes 393224 | tf_op jit(solution)/shard_map/ppermute | solution.py:460
  2.9 0.0 collective-permute-start.1
  2.9 3.9 %up.1 = (bf16[16,4096]{1,0:T(8,128)(2,1)S(1)}, f32[32,4096]{1,0:T(8,128)S(1)}, s32[6,4,8]{2,1,0:T(4,128)S(1)}, s32[2,32]{1,0:T(2,128)S(1)}, bf16[32,4096]{1,0:T(...) custom-call(bf16[16,4096]{1,0:T(8,128)(2,1)} %dens_hbm.1, f32[32,4096]{1,0:T(8,128)} %bases_hbm.1, ...), custom_call_target="tpu_custom_call" | custom-call | bytes 12915000 | tf_op jit(solution)/shard_map/up/pallas_call | solution.py:469
  6.9 0.0 collective-permute-done.1.refs_1_
  6.9 0.0 collective-permute-done.refs_0_.refs_3_
  6.9 0.6 %collective-permute-start.6 = (bf16[32,2,128,128]{3,2,1,0:T(8,128)(2,1)}, bf16[32,2,128,128]{3,2,1,0:T(8,128)(2,1)S(1)}, u32[]{:S(2)}, u32[]{:S(2)}) collective-permute-start(bf16[32,2,128,128]{3,2,1,0:T(8,128)(2,1)} %refs_7_.1), channel_id=1, source_target_pairs={{0,1},{1,0},{2,3},{3,2},{4,5},{5,4},{6,7},{7,6},{8,9},{9,8},{10,11... | collective-permute-start | bytes 6291464 | tf_op jit(solution)/shard_map/ppermute | solution.py:460
  7.5 1.5 %collective-permute-start.3 = (bf16[16,128]{1,0:T(8,128)(2,1)S(1)}, bf16[16,128]{1,0:T(8,128)(2,1)S(1)}, u32[]{:S(2)}, u32[]{:S(2)}) collective-permute-start(bf16[16,128]{1,0:T(8,128)(2,1)S(1)} %get-tuple-element.36.root_ref.refs_0_), channel_id=1, source_target_pairs={{0,4},{4,0},{8,12},{12,8},{16,20},{20,16},{24,28},{28,24},{1,5},{5... | collective-permute-start | bytes 12296 | tf_op jit(solution)/shard_map/ppermute | solution.py:463
  9.0 0.8 %select.1 = (bf16[176,128]{1,0:T(8,128)(2,1)S(1)}, bf16[144,128]{1,0:T(8,128)(2,1)S(1)}, bf16[144,128]{1,0:T(8,128)(2,1)S(1)}) custom-call(s32[6,4,8]{2,1,0:T(4,128)S(1)} %get-tuple-element.32.send_vmem, bf16[16,4096]{1,0:T(8,128)(2,1)S(1)} %get-tuple-element.41.dens_ref.refs_2_, bf16[16,128]{1,0:T(8,128)(2,1)S(1)} %get-tuple-element.36.root_ref.refs_0_, ...), custom_call_target="tpu_custom_call" | custom-call | bytes 3690000 | tf_op jit(solution)/shard_map/select/pallas_call | solution.py:508
  9.8 0.6 %collective-permute-start.2 = (bf16[176,128]{1,0:T(8,128)(2,1)S(1)}, bf16[176,128]{1,0:T(8,128)(2,1)S(1)}, u32[]{:S(2)}, u32[]{:S(2)}) collective-permute-start(bf16[176,128]{1,0:T(8,128)(2,1)S(1)} %get-tuple-element.49), channel_id=1, source_target_pairs={{0,4},{4,0},{8,12},{12,8},{16,20},{20,16},{24,28},{28,24},{1,5},{5... | collective-permute-start | bytes 135176 | tf_op jit(solution)/shard_map/ppermute | solution.py:463
  10.4 0.7 %collective-permute-done.3.refs_1_ = bf16[16,128]{1,0:T(8,128)(2,1)S(1)} collective-permute-done((bf16[16,128]{1,0:T(8,128)(2,1)S(1)}, bf16[16,128]{1,0:T(8,128)(2,1)S(1)}, u32[]{:S(2)}, u32[]{:S(2)}) %collective-permute-start.3) | collective-permute-done | bytes 4128 | tf_op jit(solution)/shard_map/ppermute | solution.py:463
  11.1 1.6 %collective-permute-start.4 = (bf16[160,128]{1,0:T(8,128)(2,1)S(1)}, bf16[160,128]{1,0:T(8,128)(2,1)S(1)}, u32[]{:S(2)}, u32[]{:S(2)}) collective-permute-start(bf16[160,128]{1,0:T(8,128)(2,1)S(1)} %get-tuple-element.56), channel_id=1, source_target_pairs={{0,8},{4,12},{8,0},{12,4},{16,24},{20,28},{24,16},{28,20},{1,9},{5... | collective-permute-start | bytes 122888 | tf_op jit(solution)/shard_map/ppermute | solution.py:463
  12.6 2.6 %collective-permute-start.5 = (bf16[160,128]{1,0:T(8,128)(2,1)S(1)}, bf16[160,128]{1,0:T(8,128)(2,1)S(1)}, u32[]{:S(2)}, u32[]{:S(2)}) collective-permute-start(bf16[160,128]{1,0:T(8,128)(2,1)S(1)} %get-tuple-element.55), channel_id=1, source_target_pairs={{0,16},{4,20},{8,24},{12,28},{16,0},{20,4},{24,8},{28,12},{1,17},{... | collective-permute-start | bytes 122888 | tf_op jit(solution)/shard_map/ppermute | solution.py:463
  15.2 2.7 %couple.1 = (s32[8,32]{1,0:T(8,128)S(1)}, f32[32,8,32,32]{3,2,1,0:T(8,128)S(1)}, bf16[1024,32]{1,0:T(8,128)(2,1)S(1)}, f32[16,512]{1,0:T(8,128)S(1)}) custom-call(s32[8,32]{1,0:T(8,128)} %bitcast.8, f32[32,8,32,32]{3,2,1,0:T(8,128)} %coupling_hbm.1, bf16[16,4096]{1,0:T(8,128)(2,1)S(1)} %get-tuple-element.41.dens_ref.refs_2_, ...), custom_call_target="tpu_custom_call" | custom-call | bytes 7380000 | tf_op jit(solution)/shard_map/couple/pallas_call | solution.py:524
  17.9 0.0 collective-permute-done.4.refs_5_.refs_2_
  17.9 0.0 collective-permute-done.5.refs_6_.refs_3_
  18.0 0.0 collective-permute-done.2.refs_4_
  18.0 0.0 collective-permute-done.6.refs_8_
  18.0 0.0 copy-start
  18.0 0.0 copy-start.1
  18.0 2.5 %near.1 = (f32[16,4096]{1,0:T(8,128)S(1)}, s16[16,4352]{1,0:T(8,128)(2,1)S(1)}) custom-call(s32[2,32]{1,0:T(2,128)S(1)} %get-tuple-element.47.refs_0_, s32[2,32]{1,0:T(2,128)S(1)} %collective-permute-done.1.refs_1_, bf16[16,4096]{1,0:T(8,128)(2,1)S(1)} %get-tuple-element.41.dens_ref.refs_2_, bf16[16,4096]{1,0:T(8,128)(2,1)S(1)} %collective-permute-done.refs_0_.refs_3_, ...), custom_call_target="tpu_custom_call" | custom-call | bytes 11070000 | tf_op jit(solution)/shard_map/near/pallas_call | solution.py:560
  20.5 1.0 %collective-permute-start.8 = (s16[16,4352]{1,0:T(8,128)(2,1)S(1)}, s16[16,4352]{1,0:T(8,128)(2,1)S(1)}, u32[]{:S(2)}, u32[]{:S(2)}) collective-permute-start(s16[16,4352]{1,0:T(8,128)(2,1)S(1)} %get-tuple-element.54), channel_id=1, source_target_pairs={{0,2},{2,0},{1,3},{3,1},{4,6},{6,4},{5,7},{7,5},{8,10},{10,8},{9,1... | collective-permute-start | bytes 417800 | tf_op jit(solution)/shard_map/ppermute | solution.py:460
  21.5 0.4 %collective-permute-start.7 = (bf16[32,128]{1,0:T(8,128)(2,1)S(1)}, bf16[32,128]{1,0:T(8,128)(2,1)S(1)}, u32[]{:S(2)}, u32[]{:S(2)}) collective-permute-start(bf16[32,128]{1,0:T(8,128)(2,1)S(1)} %slice.4), channel_id=1, source_target_pairs={{0,8},{4,12},{8,0},{12,4},{16,24},{20,28},{24,16},{28,20},{1,9},{5... | collective-permute-start | bytes 24584 | tf_op jit(solution)/shard_map/ppermute | solution.py:463
  22.0 1.9 %project.1.term_ref = f32[16,4096]{1,0:T(8,128)S(1)} custom-call(s32[8,32]{1,0:T(8,128)S(1)} %get-tuple-element.43.table_ref, f32[32,8,32,32]{3,2,1,0:T(8,128)S(1)} %get-tuple-element.44.coupling_ref, bf16[1024,32]{1,0:T(8,128)(2,1)S(1)} %get-tuple-element.45.turned_ref, f32[16,512]{1,0:T(8,128)S(1)} %get-tuple-element.46.refs_9_.first_ref, ...), custom_call_target="tpu_custom_call" | custom-call | bytes 5535000 | tf_op jit(solution)/shard_map/project/pallas_call | solution.py:584
  23.9 1.3 %collective-permute-done.7.refs_4_ = bf16[32,128]{1,0:T(8,128)(2,1)S(1)} collective-permute-done((bf16[32,128]{1,0:T(8,128)(2,1)S(1)}, bf16[32,128]{1,0:T(8,128)(2,1)S(1)}, u32[]{:S(2)}, u32[]{:S(2)}) %collective-permute-start.7) | collective-permute-done | bytes 8224 | tf_op jit(solution)/shard_map/ppermute | solution.py:463
  25.2 0.5 %collective-permute-done.8.refs_5_ = s16[16,4352]{1,0:T(8,128)(2,1)S(1)} collective-permute-done((s16[16,4352]{1,0:T(8,128)(2,1)S(1)}, s16[16,4352]{1,0:T(8,128)(2,1)S(1)}, u32[]{:S(2)}, u32[]{:S(2)}) %collective-permute-start.8) | collective-permute-done | bytes 139296 | tf_op jit(solution)/shard_map/ppermute | solution.py:460
  25.6 0.0 copy-done
  25.6 0.0 copy-done.1
  25.6 1.7 %far.1 = f32[16,4096]{1,0:T(8,128)} custom-call(f32[16,32,32]{2,1,0:T(8,128)S(1)} %copy-done.1, f32[16,3,32,32]{3,2,1,0:T(8,128)S(1)} %copy-done, bf16[32,4096]{1,0:T(8,128)(2,1)S(1)} %get-tuple-element.30.high_ref, bf16[32,4096]{1,0:T(8,128)(2,1)S(1)} %get-tuple-element.31.low_ref, f32[16,4096]{1,0:T(8,128)S(1)} %project.1.term_ref, ...), custom_call_target="tpu_custom_call" | custom-call | bytes 5535000 | tf_op jit(solution)/shard_map/far/pallas_call | solution.py:594
  (2 shorter events, 0.0 us)
Async XLA Ops:
  0.0 6.9 %collective-permute-start = (bf16[16,4096]{1,0:T(8,128)(2,1)}, bf16[16,4096]{1,0:T(8,128)(2,1)S(1)}, u32[]{:S(2)}, u32[]{:S(2)}) collective-permute-start(bf16[16,4096]{1,0:T(8,128)(2,1)} %dens_hbm.1), channel_id=1, source_target_pairs={{0,2},{2,0},{1,3},{3,1},{4,6},{6,4},{5,7},{7,5},{8,10},{10,8},{9,1... | collective-permute-start | bytes 393224 | tf_op jit(solution)/shard_map/ppermute | solution.py:460
  2.9 3.9 %collective-permute-start.1 = (s32[2,32]{1,0:T(2,128)}, s32[2,32]{1,0:T(2,128)S(1)}, u32[]{:S(2)}, u32[]{:S(2)}) collective-permute-start(s32[2,32]{1,0:T(2,128)} %bitcast.9), channel_id=1, source_target_pairs={{0,1},{1,0},{2,3},{3,2},{4,5},{5,4},{6,7},{7,6},{8,9},{9,8},{10,11... | collective-permute-start | bytes 776 | tf_op jit(solution)/shard_map/ppermute | solution.py:460
  6.9 11.1 %collective-permute-start.6 = (bf16[32,2,128,128]{3,2,1,0:T(8,128)(2,1)}, bf16[32,2,128,128]{3,2,1,0:T(8,128)(2,1)S(1)}, u32[]{:S(2)}, u32[]{:S(2)}) collective-permute-start(bf16[32,2,128,128]{3,2,1,0:T(8,128)(2,1)} %refs_7_.1), channel_id=1, source_target_pairs={{0,1},{1,0},{2,3},{3,2},{4,5},{5,4},{6,7},{7,6},{8,9},{9,8},{10,11... | collective-permute-start | bytes 6291464 | tf_op jit(solution)/shard_map/ppermute | solution.py:460
  7.5 3.6 %collective-permute-start.3 = (bf16[16,128]{1,0:T(8,128)(2,1)S(1)}, bf16[16,128]{1,0:T(8,128)(2,1)S(1)}, u32[]{:S(2)}, u32[]{:S(2)}) collective-permute-start(bf16[16,128]{1,0:T(8,128)(2,1)S(1)} %get-tuple-element.36.root_ref.refs_0_), channel_id=1, source_target_pairs={{0,4},{4,0},{8,12},{12,8},{16,20},{20,16},{24,28},{28,24},{1,5},{5... | collective-permute-start | bytes 12296 | tf_op jit(solution)/shard_map/ppermute | solution.py:463
  9.8 8.2 %collective-permute-start.2 = (bf16[176,128]{1,0:T(8,128)(2,1)S(1)}, bf16[176,128]{1,0:T(8,128)(2,1)S(1)}, u32[]{:S(2)}, u32[]{:S(2)}) collective-permute-start(bf16[176,128]{1,0:T(8,128)(2,1)S(1)} %get-tuple-element.49), channel_id=1, source_target_pairs={{0,4},{4,0},{8,12},{12,8},{16,20},{20,16},{24,28},{28,24},{1,5},{5... | collective-permute-start | bytes 135176 | tf_op jit(solution)/shard_map/ppermute | solution.py:463
  11.1 6.8 %collective-permute-start.4 = (bf16[160,128]{1,0:T(8,128)(2,1)S(1)}, bf16[160,128]{1,0:T(8,128)(2,1)S(1)}, u32[]{:S(2)}, u32[]{:S(2)}) collective-permute-start(bf16[160,128]{1,0:T(8,128)(2,1)S(1)} %get-tuple-element.56), channel_id=1, source_target_pairs={{0,8},{4,12},{8,0},{12,4},{16,24},{20,28},{24,16},{28,20},{1,9},{5... | collective-permute-start | bytes 122888 | tf_op jit(solution)/shard_map/ppermute | solution.py:463
  12.6 5.3 %collective-permute-start.5 = (bf16[160,128]{1,0:T(8,128)(2,1)S(1)}, bf16[160,128]{1,0:T(8,128)(2,1)S(1)}, u32[]{:S(2)}, u32[]{:S(2)}) collective-permute-start(bf16[160,128]{1,0:T(8,128)(2,1)S(1)} %get-tuple-element.55), channel_id=1, source_target_pairs={{0,16},{4,20},{8,24},{12,28},{16,0},{20,4},{24,8},{28,12},{1,17},{... | collective-permute-start | bytes 122888 | tf_op jit(solution)/shard_map/ppermute | solution.py:463
  18.0 7.7 %copy-start = (f32[16,3,32,32]{3,2,1,0:T(8,128)S(1)}, f32[16,3,32,32]{3,2,1,0:T(8,128)}, u32[]{:S(2)}) copy-start(f32[16,3,32,32]{3,2,1,0:T(8,128)} %cross_ref.1) | copy-start | bytes 589828
  18.0 7.7 %copy-start.1 = (f32[16,32,32]{2,1,0:T(8,128)S(1)}, f32[16,32,32]{2,1,0:T(8,128)}, u32[]{:S(2)}) copy-start(f32[16,32,32]{2,1,0:T(8,128)} %upper_ref.1) | copy-start | bytes 196612
  20.5 5.1 %collective-permute-start.8 = (s16[16,4352]{1,0:T(8,128)(2,1)S(1)}, s16[16,4352]{1,0:T(8,128)(2,1)S(1)}, u32[]{:S(2)}, u32[]{:S(2)}) collective-permute-start(s16[16,4352]{1,0:T(8,128)(2,1)S(1)} %get-tuple-element.54), channel_id=1, source_target_pairs={{0,2},{2,0},{1,3},{3,1},{4,6},{6,4},{5,7},{7,5},{8,10},{10,8},{9,1... | collective-permute-start | bytes 417800 | tf_op jit(solution)/shard_map/ppermute | solution.py:460
  21.5 3.7 %collective-permute-start.7 = (bf16[32,128]{1,0:T(8,128)(2,1)S(1)}, bf16[32,128]{1,0:T(8,128)(2,1)S(1)}, u32[]{:S(2)}, u32[]{:S(2)}) collective-permute-start(bf16[32,128]{1,0:T(8,128)(2,1)S(1)} %slice.4), channel_id=1, source_target_pairs={{0,8},{4,12},{8,0},{12,4},{16,24},{20,28},{24,16},{28,20},{1,9},{5... | collective-permute-start | bytes 24584 | tf_op jit(solution)/shard_map/ppermute | solution.py:463

commit v7 on v6

--- a/solution.py
+++ b/solution.py
@@ -494,14 +494,13 @@
     )
     all_sources[0] = sources
 
-    beside = crossed(root, 1) if side == 2 else None
     later_blocks, others, all_sources, root = lax.optimization_barrier(
         (near_blocks, others, all_sources, root)
     )
     mate_blocks = [rotated(later_blocks, "mate", part) for part in range(1, share)]
 
     if side == 2:
-        faces = [((2 * axis, 2 * axis + 1), 2**axis) for axis in range(3)]
+        faces = [((2 * axis, 2 * axis + 1), 2**axis) for axis in (2, 0, 1)]
     else:
         faces = [((direction,), offset) for direction, offset in enumerate(offsets)]
     chunks = [(cap * far_groups + (1 if place else 3)) * columns for place in range(len(faces))]
@@ -520,7 +519,7 @@
     )(send, dens, root, *others)
     outgoing, dens = lax.optimization_barrier((outgoing, dens))
     far_table = far_src.T
-    first_leaves = leaf_count // 2
+    first_leaves = leaf_count // 4
     *coupling, leaf_local = pl.pallas_call(
         couple_kernel,
         out_shape=[
@@ -538,19 +537,14 @@
     )(hbm(far_table), hbm(leaf_coupling), dens, basis)
     tail = cap * far_groups * columns
     if side == 2:
-        payloads = [outgoing[0]] + [
-            jnp.concatenate([value, beside], axis=0) for value in outgoing[1:]
-        ]
-        arrived = [crossed(value, stride) for (_, stride), value in zip(faces, payloads)]
-        first, second, third = (stride for _, stride in faces)
-        far_pair = crossed(arrived[2][tail:], second)
-        roots = [([(0, 0)], root), ([(first, 0)], beside)]
-        for stride, value, row in (
-            (second, arrived[1], tail),
-            (third, arrived[2], tail),
-            (second ^ third, far_pair, 0),
-        ):
-            roots.append(([(stride, row), (stride ^ first, row + columns)], value))
+        arrived = [crossed(value, stride) for (_, stride), value in zip(faces, outgoing)]
+        far_one, near_one, near_two = (value[tail : tail + columns] for value in arrived)
+        later_two, leaf_local = lax.optimization_barrier((arrived[2], leaf_local))
+        third = crossed(later_two[-4 * columns :], 1)[-columns:]
+        rest = crossed(jnp.concatenate([near_one, near_two, third], axis=0), 4)
+        roots = [([(0, 0)], root), ([(3, 0)], third)]
+        roots += [([(stride, tail)], value) for (_, stride), value in zip(faces, arrived)]
+        roots.append(([(turn + 4, (turn - 1) * columns) for turn in (1, 2, 3)], rest))
     else:
         arrived = [shifted(value, "leaf", stride) for (_, stride), value in zip(faces, outgoing)]
         roots = [(None, lax.all_gather(root, "leaf", axis=0))]

time: 27.5 us -> 27 us (0.982)
  waiting for transfers between devices: 2.56 us -> 1.86 us
    pallas_call x1, Pallas kernels: 1.89 us -> 2.41 us  [local(): pl.pallas_call(project_kernel, out_shape=jax.ShapeDtypeStruct((columns, p...]
    ppermute x4, waiting for transfers between devices: 0.48 us -> 0.01 us  [rotated(): lax.ppermute(value, axis, [(i, (i - shift) % count) for i in range(count)])]
    pallas_call x1, Pallas kernels: 2.67 us -> 2.29 us  [local(): pl.pallas_call(couple_kernel, out_shape=[jax.ShapeDtypeStruct(far_table.s...]
  transfers between devices with their start and end apart: 9 -> 9, of which waited for: 3 -> 1; matrix products, arithmetic and copies ran while one was open for 0% -> 0% of each run, Pallas kernels for 34% -> 45%
where the time goes in v7:
time: 27 us; the launch traced here: 26.8 us
  Pallas kernels  13.6 us (50%)
  starting transfers between devices  11.2 us (41%)
  waiting for transfers between devices  1.86 us (7%)
    ppermute x5, starting transfers between devices, crossed(): lax.ppermute(value, 'leaf', [(i, i ^ turn) for i in range(leaf_devices)])  6.72 us
    ppermute x4, starting transfers between devices, rotated(): lax.ppermute(value, axis, [(i, (i - shift) % count) for i in range(count)])  4.51 us
    pallas_call x1, Pallas kernels, local(): pl.pallas_call(up_kernel, out_shape=[jax.ShapeDtypeStruct(densities.shape...  3.92 us
    pallas_call x1, Pallas kernels, local(): pl.pallas_call(functools.partial(near_kernel, faces, far_groups, share),...  2.51 us
    pallas_call x1, Pallas kernels, local(): pl.pallas_call(project_kernel, out_shape=jax.ShapeDtypeStruct((columns, p...  2.41 us
    pallas_call x1, Pallas kernels, local(): pl.pallas_call(couple_kernel, out_shape=[jax.ShapeDtypeStruct(far_table.s...  2.29 us
    ppermute x5, waiting for transfers between devices, crossed(): lax.ppermute(value, 'leaf', [(i, i ^ turn) for i in range(leaf_devices)])  1.85 us
    pallas_call x1, Pallas kernels, local(): pl.pallas_call(functools.partial(far_kernel, [tiles for tiles, _ in roots...  1.68 us
  transfers between devices with their start and end apart: 9, of which 1 were waited for; matrix products, arithmetic and copies ran while one was open for 0% of the time, Pallas kernels for 45%

profile of v7, /device:TPU:0, one launch (start us, length us, event | category | flops | bytes accessed | tf_op | source)
XLA Modules:
  0.0 26.8 jit_solution(18354116052254375525)
XLA Ops:
  0.0 2.9 %collective-permute-start = (bf16[16,4096]{1,0:T(8,128)(2,1)}, bf16[16,4096]{1,0:T(8,128)(2,1)S(1)}, u32[]{:S(2)}, u32[]{:S(2)}) collective-permute-start(bf16[16,4096]{1,0:T(8,128)(2,1)} %dens_hbm.1), channel_id=1, source_target_pairs={{0,2},{2,0},{1,3},{3,1},{4,6},{6,4},{5,7},{7,5},{8,10},{10,8},{9,1... | collective-permute-start | bytes 393224 | tf_op jit(solution)/shard_map/ppermute | solution.py:460
  2.9 0.0 collective-permute-start.1
  2.9 3.9 %up.1 = (bf16[16,4096]{1,0:T(8,128)(2,1)S(1)}, f32[32,4096]{1,0:T(8,128)S(1)}, s32[6,4,8]{2,1,0:T(4,128)S(1)}, s32[2,32]{1,0:T(2,128)S(1)}, bf16[32,4096]{1,0:T(...) custom-call(bf16[16,4096]{1,0:T(8,128)(2,1)} %dens_hbm.1, f32[32,4096]{1,0:T(8,128)} %bases_hbm.1, ...), custom_call_target="tpu_custom_call" | custom-call | bytes 12915000 | tf_op jit(solution)/shard_map/up/pallas_call | solution.py:469
  6.9 0.0 collective-permute-done.1.refs_1_
  6.9 0.0 collective-permute-done.refs_0_.refs_3_
  6.9 0.6 %collective-permute-start.5 = (bf16[32,2,128,128]{3,2,1,0:T(8,128)(2,1)}, bf16[32,2,128,128]{3,2,1,0:T(8,128)(2,1)S(1)}, u32[]{:S(2)}, u32[]{:S(2)}) collective-permute-start(bf16[32,2,128,128]{3,2,1,0:T(8,128)(2,1)} %refs_7_.1), channel_id=1, source_target_pairs={{0,1},{1,0},{2,3},{3,2},{4,5},{5,4},{6,7},{7,6},{8,9},{9,8},{10,11... | collective-permute-start | bytes 6291464 | tf_op jit(solution)/shard_map/ppermute | solution.py:460
  7.5 0.8 %select.1 = (bf16[176,128]{1,0:T(8,128)(2,1)S(1)}, bf16[144,128]{1,0:T(8,128)(2,1)S(1)}, bf16[144,128]{1,0:T(8,128)(2,1)S(1)}) custom-call(s32[6,4,8]{2,1,0:T(4,128)S(1)} %get-tuple-element.34.send_vmem, bf16[16,4096]{1,0:T(8,128)(2,1)S(1)} %get-tuple-element.43.dens_ref.refs_2_, bf16[16,128]{1,0:T(8,128)(2,1)S(1)} %get-tuple-element.38.root_ref.refs_0_, ...), custom_call_target="tpu_custom_call" | custom-call | bytes 3690000 | tf_op jit(solution)/shard_map/select/pallas_call | solution.py:507
  8.3 2.7 %collective-permute-start.3 = (bf16[176,128]{1,0:T(8,128)(2,1)S(1)}, bf16[176,128]{1,0:T(8,128)(2,1)S(1)}, u32[]{:S(2)}, u32[]{:S(2)}) collective-permute-start(bf16[176,128]{1,0:T(8,128)(2,1)S(1)} %get-tuple-element.53), channel_id=1, source_target_pairs={{0,16},{4,20},{8,24},{12,28},{16,0},{20,4},{24,8},{28,12},{1,17},{... | collective-permute-start | bytes 135176 | tf_op jit(solution)/shard_map/ppermute | solution.py:463
  10.9 1.6 %collective-permute-start.2 = (bf16[144,128]{1,0:T(8,128)(2,1)S(1)}, bf16[144,128]{1,0:T(8,128)(2,1)S(1)}, u32[]{:S(2)}, u32[]{:S(2)}) collective-permute-start(bf16[144,128]{1,0:T(8,128)(2,1)S(1)} %get-tuple-element.48), channel_id=1, source_target_pairs={{0,8},{4,12},{8,0},{12,4},{16,24},{20,28},{24,16},{28,20},{1,9},{5... | collective-permute-start | bytes 110600 | tf_op jit(solution)/shard_map/ppermute | solution.py:463
  12.5 1.5 %collective-permute-start.4 = (bf16[144,128]{1,0:T(8,128)(2,1)S(1)}, bf16[144,128]{1,0:T(8,128)(2,1)S(1)}, u32[]{:S(2)}, u32[]{:S(2)}) collective-permute-start(bf16[144,128]{1,0:T(8,128)(2,1)S(1)} %get-tuple-element.54), channel_id=1, source_target_pairs={{0,4},{4,0},{8,12},{12,8},{16,20},{20,16},{24,28},{28,24},{1,5},{5... | collective-permute-start | bytes 110600 | tf_op jit(solution)/shard_map/ppermute | solution.py:463
  14.0 2.3 %couple.1 = (s32[8,32]{1,0:T(8,128)S(1)}, f32[32,8,32,32]{3,2,1,0:T(8,128)S(1)}, bf16[1024,32]{1,0:T(8,128)(2,1)S(1)}, f32[16,256]{1,0:T(8,128)S(1)}) custom-call(s32[8,32]{1,0:T(8,128)} %bitcast.8, f32[32,8,32,32]{3,2,1,0:T(8,128)} %coupling_hbm.1, bf16[16,4096]{1,0:T(8,128)(2,1)S(1)} %get-tuple-element.43.dens_ref.refs_2_, ...), custom_call_target="tpu_custom_call" | custom-call | bytes 7380000 | tf_op jit(solution)/shard_map/couple/pallas_call | solution.py:523
  16.3 0.0 collective-permute-done.2.refs_6_.refs_4_
  16.3 0.0 copy-start
  16.3 0.0 copy-start.1
  16.4 0.6 %collective-permute-start.6 = (bf16[64,128]{1,0:T(8,128)(2,1)S(1)}, bf16[64,128]{1,0:T(8,128)(2,1)S(1)}, u32[]{:S(2)}, u32[]{:S(2)}) collective-permute-start(bf16[64,128]{1,0:T(8,128)(2,1)S(1)} %slice.12), channel_id=1, source_target_pairs={{0,4},{4,0},{8,12},{12,8},{16,20},{20,16},{24,28},{28,24},{1,5},{5... | collective-permute-start | bytes 49160 | tf_op jit(solution)/shard_map/ppermute | solution.py:463
  16.9 0.0 collective-permute-done.4.refs_5_.refs_3_
  16.9 0.0 collective-permute-done.3.refs_4_.refs_2_
  16.9 0.0 collective-permute-done.5.refs_8_
  16.9 2.5 %near.1 = (f32[16,4096]{1,0:T(8,128)S(1)}, s16[16,4352]{1,0:T(8,128)(2,1)S(1)}) custom-call(s32[2,32]{1,0:T(2,128)S(1)} %get-tuple-element.51.refs_0_, s32[2,32]{1,0:T(2,128)S(1)} %collective-permute-done.1.refs_1_, bf16[16,4096]{1,0:T(8,128)(2,1)S(1)} %get-tuple-element.43.dens_ref.refs_2_, bf16[16,4096]{1,0:T(8,128)(2,1)S(1)} %collective-permute-done.refs_0_.refs_3_, ...), custom_call_target="tpu_custom_call" | custom-call | bytes 11070000 | tf_op jit(solution)/shard_map/near/pallas_call | solution.py:554
  19.5 1.0 %collective-permute-start.8 = (s16[16,4352]{1,0:T(8,128)(2,1)S(1)}, s16[16,4352]{1,0:T(8,128)(2,1)S(1)}, u32[]{:S(2)}, u32[]{:S(2)}) collective-permute-start(s16[16,4352]{1,0:T(8,128)(2,1)S(1)} %get-tuple-element.58), channel_id=1, source_target_pairs={{0,2},{2,0},{1,3},{3,1},{4,6},{6,4},{5,7},{7,5},{8,10},{10,8},{9,1... | collective-permute-start | bytes 417800 | tf_op jit(solution)/shard_map/ppermute | solution.py:460
  20.5 0.0 collective-permute-done.6
  20.5 0.4 %collective-permute-start.7 = (bf16[48,128]{1,0:T(8,128)(2,1)S(1)}, bf16[48,128]{1,0:T(8,128)(2,1)S(1)}, u32[]{:S(2)}, u32[]{:S(2)}) collective-permute-start(bf16[48,128]{1,0:T(8,128)(2,1)S(1)} %pad_maximum_fusion), channel_id=1, source_target_pairs={{0,16},{4,20},{8,24},{12,28},{16,0},{20,4},{24,8},{28,12},{1,17},{... | collective-permute-start | bytes 36872 | tf_op jit(solution)/shard_map/ppermute | solution.py:463
  20.9 2.4 %project.1.term_ref = f32[16,4096]{1,0:T(8,128)S(1)} custom-call(s32[8,32]{1,0:T(8,128)S(1)} %get-tuple-element.45.table_ref, f32[32,8,32,32]{3,2,1,0:T(8,128)S(1)} %get-tuple-element.46.coupling_ref, bf16[1024,32]{1,0:T(8,128)(2,1)S(1)} %get-tuple-element.47.turned_ref, f32[16,256]{1,0:T(8,128)S(1)} %get-tuple-element.50.refs_9_.first_ref, ...), custom_call_target="tpu_custom_call" | custom-call | bytes 5535000 | tf_op jit(solution)/shard_map/project/pallas_call | solution.py:578
  23.3 1.8 %collective-permute-done.7.refs_5_ = bf16[48,128]{1,0:T(8,128)(2,1)S(1)} collective-permute-done((bf16[48,128]{1,0:T(8,128)(2,1)S(1)}, bf16[48,128]{1,0:T(8,128)(2,1)S(1)}, u32[]{:S(2)}, u32[]{:S(2)}) %collective-permute-start.7) | collective-permute-done | bytes 12320 | tf_op jit(solution)/shard_map/ppermute | solution.py:463
  25.1 0.0 collective-permute-done.8.refs_6_
  25.1 0.0 copy-done
  25.2 0.0 copy-done.1
  25.2 1.7 %far.1 = f32[16,4096]{1,0:T(8,128)} custom-call(f32[16,32,32]{2,1,0:T(8,128)S(1)} %copy-done.1, f32[16,3,32,32]{3,2,1,0:T(8,128)S(1)} %copy-done, bf16[32,4096]{1,0:T(8,128)(2,1)S(1)} %get-tuple-element.32.high_ref, bf16[32,4096]{1,0:T(8,128)(2,1)S(1)} %get-tuple-element.33.low_ref, f32[16,4096]{1,0:T(8,128)S(1)} %project.1.term_ref, ...), custom_call_target="tpu_custom_call" | custom-call | bytes 5535000 | tf_op jit(solution)/shard_map/far/pallas_call | solution.py:588
  (5 shorter events, 0.0 us)
Async XLA Ops:
  0.0 6.9 %collective-permute-start = (bf16[16,4096]{1,0:T(8,128)(2,1)}, bf16[16,4096]{1,0:T(8,128)(2,1)S(1)}, u32[]{:S(2)}, u32[]{:S(2)}) collective-permute-start(bf16[16,4096]{1,0:T(8,128)(2,1)} %dens_hbm.1), channel_id=1, source_target_pairs={{0,2},{2,0},{1,3},{3,1},{4,6},{6,4},{5,7},{7,5},{8,10},{10,8},{9,1... | collective-permute-start | bytes 393224 | tf_op jit(solution)/shard_map/ppermute | solution.py:460
  2.9 3.9 %collective-permute-start.1 = (s32[2,32]{1,0:T(2,128)}, s32[2,32]{1,0:T(2,128)S(1)}, u32[]{:S(2)}, u32[]{:S(2)}) collective-permute-start(s32[2,32]{1,0:T(2,128)} %bitcast.9), channel_id=1, source_target_pairs={{0,1},{1,0},{2,3},{3,2},{4,5},{5,4},{6,7},{7,6},{8,9},{9,8},{10,11... | collective-permute-start | bytes 776 | tf_op jit(solution)/shard_map/ppermute | solution.py:460
  6.9 10.1 %collective-permute-start.5 = (bf16[32,2,128,128]{3,2,1,0:T(8,128)(2,1)}, bf16[32,2,128,128]{3,2,1,0:T(8,128)(2,1)S(1)}, u32[]{:S(2)}, u32[]{:S(2)}) collective-permute-start(bf16[32,2,128,128]{3,2,1,0:T(8,128)(2,1)} %refs_7_.1), channel_id=1, source_target_pairs={{0,1},{1,0},{2,3},{3,2},{4,5},{5,4},{6,7},{7,6},{8,9},{9,8},{10,11... | collective-permute-start | bytes 6291464 | tf_op jit(solution)/shard_map/ppermute | solution.py:460
  8.3 8.7 %collective-permute-start.3 = (bf16[176,128]{1,0:T(8,128)(2,1)S(1)}, bf16[176,128]{1,0:T(8,128)(2,1)S(1)}, u32[]{:S(2)}, u32[]{:S(2)}) collective-permute-start(bf16[176,128]{1,0:T(8,128)(2,1)S(1)} %get-tuple-element.53), channel_id=1, source_target_pairs={{0,16},{4,20},{8,24},{12,28},{16,0},{20,4},{24,8},{28,12},{1,17},{... | collective-permute-start | bytes 135176 | tf_op jit(solution)/shard_map/ppermute | solution.py:463
  10.9 5.4 %collective-permute-start.2 = (bf16[144,128]{1,0:T(8,128)(2,1)S(1)}, bf16[144,128]{1,0:T(8,128)(2,1)S(1)}, u32[]{:S(2)}, u32[]{:S(2)}) collective-permute-start(bf16[144,128]{1,0:T(8,128)(2,1)S(1)} %get-tuple-element.48), channel_id=1, source_target_pairs={{0,8},{4,12},{8,0},{12,4},{16,24},{20,28},{24,16},{28,20},{1,9},{5... | collective-permute-start | bytes 110600 | tf_op jit(solution)/shard_map/ppermute | solution.py:463
  12.5 4.4 %collective-permute-start.4 = (bf16[144,128]{1,0:T(8,128)(2,1)S(1)}, bf16[144,128]{1,0:T(8,128)(2,1)S(1)}, u32[]{:S(2)}, u32[]{:S(2)}) collective-permute-start(bf16[144,128]{1,0:T(8,128)(2,1)S(1)} %get-tuple-element.54), channel_id=1, source_target_pairs={{0,4},{4,0},{8,12},{12,8},{16,20},{20,16},{24,28},{28,24},{1,5},{5... | collective-permute-start | bytes 110600 | tf_op jit(solution)/shard_map/ppermute | solution.py:463
  16.3 8.8 %copy-start = (f32[16,3,32,32]{3,2,1,0:T(8,128)S(1)}, f32[16,3,32,32]{3,2,1,0:T(8,128)}, u32[]{:S(2)}) copy-start(f32[16,3,32,32]{3,2,1,0:T(8,128)} %cross_ref.1) | copy-start | bytes 589828
  16.3 8.8 %copy-start.1 = (f32[16,32,32]{2,1,0:T(8,128)S(1)}, f32[16,32,32]{2,1,0:T(8,128)}, u32[]{:S(2)}) copy-start(f32[16,32,32]{2,1,0:T(8,128)} %upper_ref.1) | copy-start | bytes 196612
  16.4 4.1 %collective-permute-start.6 = (bf16[64,128]{1,0:T(8,128)(2,1)S(1)}, bf16[64,128]{1,0:T(8,128)(2,1)S(1)}, u32[]{:S(2)}, u32[]{:S(2)}) collective-permute-start(bf16[64,128]{1,0:T(8,128)(2,1)S(1)} %slice.12), channel_id=1, source_target_pairs={{0,4},{4,0},{8,12},{12,8},{16,20},{20,16},{24,28},{28,24},{1,5},{5... | collective-permute-start | bytes 49160 | tf_op jit(solution)/shard_map/ppermute | solution.py:463
  19.5 5.7 %collective-permute-start.8 = (s16[16,4352]{1,0:T(8,128)(2,1)S(1)}, s16[16,4352]{1,0:T(8,128)(2,1)S(1)}, u32[]{:S(2)}, u32[]{:S(2)}) collective-permute-start(s16[16,4352]{1,0:T(8,128)(2,1)S(1)} %get-tuple-element.58), channel_id=1, source_target_pairs={{0,2},{2,0},{1,3},{3,1},{4,6},{6,4},{5,7},{7,5},{8,10},{10,8},{9,1... | collective-permute-start | bytes 417800 | tf_op jit(solution)/shard_map/ppermute | solution.py:460
  20.5 4.7 %collective-permute-start.7 = (bf16[48,128]{1,0:T(8,128)(2,1)S(1)}, bf16[48,128]{1,0:T(8,128)(2,1)S(1)}, u32[]{:S(2)}, u32[]{:S(2)}) collective-permute-start(bf16[48,128]{1,0:T(8,128)(2,1)S(1)} %pad_maximum_fusion), channel_id=1, source_target_pairs={{0,16},{4,20},{8,24},{12,28},{16,0},{20,4},{24,8},{28,12},{1,17},{... | collective-permute-start | bytes 36872 | tf_op jit(solution)/shard_map/ppermute | solution.py:463

commit v8 on v7

--- a/solution.py
+++ b/solution.py
@@ -76,19 +76,14 @@
 
 
 def up_kernel(
-    dens_hbm, bases_hbm, maps_hbm, send_hbm, source_hbm,
-    dens_ref, bases_ref, send_ref, source_ref, high_ref, low_ref, root_ref,
-    maps_ref, spread_ref, chain_ref, sems,
-):
+    maps_hbm, bases_hbm, *refs,
+):
+    count = (len(refs) - 8) // 2
+    hbm_refs, bases_ref, vmem_refs = refs[:count], refs[count], refs[count + 1 : 2 * count + 1]
+    high_ref, low_ref, root_ref, maps_ref, spread_ref, chain_ref, sems = refs[2 * count + 1 :]
+    dens_ref = vmem_refs[0]
     copies = fetch(
-        [
-            (maps_hbm, maps_ref),
-            (bases_hbm, bases_ref),
-            (dens_hbm, dens_ref),
-            (send_hbm, send_ref),
-            (source_hbm, source_ref),
-        ],
-        sems,
+        [(maps_hbm, maps_ref), (bases_hbm, bases_ref), *zip(hbm_refs, vmem_refs)], sems
     )
     columns, points = dens_ref.shape
     rank, _, node_count = maps_ref.shape
@@ -128,8 +123,8 @@
             lanes = slice(index * LANES, (index + 1) * LANES)
             chain_ref[:, index * tile : (index + 1) * tile] = children(chain_ref[:, lanes], index)
         level *= 2
-    for copy in copies[1:]:
-        copy.wait()
+    copies[1].wait()
+    copies[2].wait()
     step = group * width
     root = jnp.zeros((columns, rank), F32)
     for index in range(leaf_count // group):
@@ -152,6 +147,8 @@
     last = (rest - middle).astype(BF16).astype(F32)
     packed = high + pltpu.roll(middle, rank, 1) + pltpu.roll(last, 2 * rank, 1)
     root_ref[...] = packed.astype(BF16)
+    for copy in copies[3:]:
+        copy.wait()
 
 
 def select_kernel(
@@ -187,26 +184,17 @@
     dens_ref, refs = refs[0], refs[1:]
     other_refs, refs = refs[: far_groups - 1], refs[far_groups - 1 :]
     got_refs, refs = refs[: len(faces)], refs[len(faces) :]
-    block_hbm, refs = refs[0], refs[1:]
+    block_ref, refs = refs[0], refs[1:]
     mate_refs, refs = refs[: share - 1], refs[share - 1 :]
     refs = refs[1:]
     out_refs, refs = refs[:far_groups], refs[far_groups:]
     source_refs, refs = refs[:share], refs[share:]
     sum_refs, refs = refs[: far_groups - 1], refs[far_groups - 1 :]
     peak_refs, refs = refs[: far_groups - 1], refs[far_groups - 1 :]
-    block_ref, buffer_ref, small_sems, sems = refs
+    buffer_ref, sems = refs
     columns, points = dens_ref.shape
     leaf_count, near_count, width, _ = block_ref.shape
-    chunk_count = sems.shape[0]
-    chunk = leaf_count // chunk_count
-    copies = fetch(list(zip(source_vmems, source_refs)), small_sems)
-    block_copies = fetch(
-        [
-            (block_hbm.at[pl.ds(index * chunk, chunk)], block_ref.at[pl.ds(index * chunk, chunk)])
-            for index in range(chunk_count)
-        ],
-        sems,
-    )
+    copies = fetch(list(zip(source_vmems, source_refs)), sems)
     cap = (buffer_ref.shape[0] - leaf_count) // len(FACE_SIGNS)
     for (directions, _), got_ref in zip(faces, got_refs):
         for direction in directions:
@@ -226,8 +214,6 @@
     targets = (own_ref, *sum_refs)
     for turn, (source_ref, blocks_ref) in enumerate(tables):
         for leaf in range(leaf_count):
-            if blocks_ref is block_ref and leaf % chunk == 0:
-                block_copies[leaf // chunk].wait()
             panels = [buffer_ref[source_ref[block, leaf]] for block in range(near_count)]
             blocks = [blocks_ref[leaf, block] for block in range(near_count)]
             total = dot_nt(jnp.concatenate(panels, axis=1), jnp.concatenate(blocks, axis=1))
@@ -278,14 +264,9 @@
 
 
 def couple_kernel(
-    far_hbm, coupling_hbm, dens_ref, bases_ref,
-    table_ref, coupling_ref, turned_ref, out_ref, far_ref, sems, chunk_sems,
-):
-    copies = fetch([(far_hbm, far_ref), (far_hbm, table_ref)], sems)
-    chunk_count = chunk_sems.shape[0]
-    chunk = coupling_ref.shape[0] // chunk_count
-    chunks = [pl.ds(index * chunk, chunk) for index in range(chunk_count)]
-    block_copies = fetch([(coupling_hbm.at[c], coupling_ref.at[c]) for c in chunks], chunk_sems)
+    table_ref, coupling_ref, dens_ref, bases_ref, turned_ref, out_ref, far_ref, sems,
+):
+    copies = fetch([(table_ref, far_ref)], sems)
     columns, points = dens_ref.shape
     leaf_count, _, rank = coupling_ref.shape[:3]
     width = points // leaf_count
@@ -299,15 +280,10 @@
         turned_ref[leaf * rank : (leaf + 1) * rank, :] = jnp.where(
             upper, high.astype(F32), low.astype(F32)
         ).astype(BF16)
-    for copy in copies:
-        copy.wait()
-    done = out_ref.shape[1] // rank
-    for index in range(chunk_count):
-        block_copies[index].wait()
-        leaves = range(index * chunk, min((index + 1) * chunk, done))
-        for turn, field in enumerate(coupled(leaves, far_ref, coupling_ref, turned_ref)):
-            spot = index * chunk * rank + turn * LANES
-            out_ref[:, spot : spot + LANES] = field
+    copies[0].wait()
+    leaves = range(out_ref.shape[1] // rank)
+    for index, field in enumerate(coupled(leaves, far_ref, coupling_ref, turned_ref)):
+        out_ref[:, index * LANES : (index + 1) * LANES] = field
 
 
 def project_kernel(
@@ -466,36 +442,31 @@
     others = [rotated(densities, "far", part) for part in range(1, far_groups)]
     all_sources = [sources] + [rotated(sources, "mate", part) for part in range(1, share)]
     send = send_leaf.transpose(1, 2, 0)
-    dens, basis, send, sources, high, low, root = pl.pallas_call(
+    moved = [densities, send, sources, far_src.T, leaf_coupling, near_blocks]
+    basis, dens, send, sources, far_table, coupling, blocks, high, low, root = pl.pallas_call(
         up_kernel,
-        out_shape=[
-            jax.ShapeDtypeStruct(densities.shape, BF16),
-            jax.ShapeDtypeStruct(bases.shape, F32),
-            jax.ShapeDtypeStruct(send.shape, jnp.int32),
-            jax.ShapeDtypeStruct(sources.shape, jnp.int32),
+        out_shape=[jax.ShapeDtypeStruct(value.shape, value.dtype) for value in (bases, *moved)]
+        + [
             jax.ShapeDtypeStruct((rank, points), BF16),
             jax.ShapeDtypeStruct((rank, points), BF16),
             jax.ShapeDtypeStruct((columns, LANES), BF16),
         ],
-        in_specs=[HBM] * 5,
-        out_specs=[VMEM] * 7,
+        in_specs=[HBM] * (2 + len(moved)),
+        out_specs=[VMEM] * (4 + len(moved)),
         scratch_shapes=[
             pltpu.VMEM((rank, rank, node_count), F32),
             pltpu.VMEM((node_count * rank, LANES), F32),
             pltpu.VMEM((rank, node_count * rank), F32),
-            dma((5,)),
+            dma((2 + len(moved),)),
         ],
         compiler_params=params,
         cost_estimate=hint(3.5),
         name="up",
-    )(
-        hbm(densities), hbm(bases), hbm(local_transfer[0].transpose(1, 2, 0)), hbm(send),
-        hbm(sources),
-    )
+    )(hbm(local_transfer[0].transpose(1, 2, 0)), hbm(bases), *map(hbm, moved))
     all_sources[0] = sources
 
     later_blocks, others, all_sources, root = lax.optimization_barrier(
-        (near_blocks, others, all_sources, root)
+        (blocks, others, all_sources, root)
     )
     mate_blocks = [rotated(later_blocks, "mate", part) for part in range(1, share)]
 
@@ -518,33 +489,31 @@
         name="select",
     )(send, dens, root, *others)
     outgoing, dens = lax.optimization_barrier((outgoing, dens))
-    far_table = far_src.T
-    first_leaves = leaf_count // 4
-    *coupling, leaf_local = pl.pallas_call(
+    first_leaves = LANES // rank
+    turned, leaf_local = pl.pallas_call(
         couple_kernel,
         out_shape=[
-            jax.ShapeDtypeStruct(far_table.shape, jnp.int32),
-            jax.ShapeDtypeStruct(leaf_coupling.shape, F32),
             jax.ShapeDtypeStruct((leaf_count * rank, 2 * columns), BF16),
             jax.ShapeDtypeStruct((columns, first_leaves * rank), F32),
         ],
-        in_specs=[HBM] * 2 + [VMEM] * 2,
-        out_specs=[VMEM] * 4,
-        scratch_shapes=[pltpu.SMEM(far_table.shape, jnp.int32), dma((2,)), dma((4,))],
+        in_specs=[VMEM] * 4,
+        out_specs=[VMEM] * 2,
+        scratch_shapes=[pltpu.SMEM(far_table.shape, jnp.int32), dma((1,))],
         compiler_params=params,
         cost_estimate=hint(2),
         name="couple",
-    )(hbm(far_table), hbm(leaf_coupling), dens, basis)
+    )(far_table, coupling, dens, basis)
     tail = cap * far_groups * columns
     if side == 2:
         arrived = [crossed(value, stride) for (_, stride), value in zip(faces, outgoing)]
-        far_one, near_one, near_two = (value[tail : tail + columns] for value in arrived)
-        later_two, leaf_local = lax.optimization_barrier((arrived[2], leaf_local))
-        third = crossed(later_two[-4 * columns :], 1)[-columns:]
-        rest = crossed(jnp.concatenate([near_one, near_two, third], axis=0), 4)
-        roots = [([(0, 0)], root), ([(3, 0)], third)]
+        far_one, near_one, _ = (value[tail : tail + columns] for value in arrived)
+        later, leaf_local = lax.optimization_barrier((arrived[0][-4 * columns :], leaf_local))
+        across = crossed(later, 1)
+        held = jnp.concatenate([near_one, far_one, across[-columns:]], axis=0)
+        beside = crossed(held, 2)
+        roots = [([(0, 0)], root), ([(5, 3 * columns)], across)]
         roots += [([(stride, tail)], value) for (_, stride), value in zip(faces, arrived)]
-        roots.append(([(turn + 4, (turn - 1) * columns) for turn in (1, 2, 3)], rest))
+        roots.append(([(3, 0), (6, columns), (7, 2 * columns)], beside))
     else:
         arrived = [shifted(value, "leaf", stride) for (_, stride), value in zip(faces, outgoing)]
         roots = [(None, lax.all_gather(root, "leaf", axis=0))]
@@ -555,24 +524,20 @@
         functools.partial(near_kernel, faces, far_groups, share),
         out_shape=[jax.ShapeDtypeStruct((columns, points), F32)]
         + [jax.ShapeDtypeStruct((columns, points + tables), jnp.int16)] * (far_groups - 1),
-        in_specs=[VMEM] * (share + far_groups + len(faces))
-        + [HBM]
-        + [VMEM] * share,
+        in_specs=[VMEM] * (2 * share + far_groups + len(faces) + 1),
         out_specs=[VMEM] * far_groups,
         scratch_shapes=[pltpu.SMEM(sources.shape, jnp.int32)] * share
         + [pltpu.VMEM((columns, points), F32)] * (far_groups - 1)
         + [pltpu.VMEM((leaf_count, width), F32)] * (far_groups - 1)
         + [
-            pltpu.VMEM(near_blocks.shape, BF16),
             pltpu.VMEM((slots, far_groups * columns, width), BF16),
             dma((share,)),
-            dma((4,)),
         ],
         compiler_params=params,
         cost_estimate=hint(3),
         name="near",
     )(
-        *all_sources, dens, *others, *arrived, hbm(near_blocks), *mate_blocks, leaf_local,
+        *all_sources, dens, *others, *arrived, blocks, *mate_blocks, leaf_local,
     )
     received = [rotated(partials[part], "far", -part) for part in range(1, far_groups)]
     partial = pl.pallas_call(
@@ -584,7 +549,7 @@
         compiler_params=params,
         cost_estimate=hint(1.5),
         name="project",
-    )(*coupling, leaf_local, basis, partials[0])
+    )(far_table, coupling, turned, leaf_local, basis, partials[0])
     return pl.pallas_call(
         functools.partial(far_kernel, [tiles for tiles, _ in roots], leaf_count),
         out_shape=jax.ShapeDtypeStruct((columns, points), F32),

time: 27 us -> 25.8 us (0.956)
  Pallas kernels: 13.6 us -> 12.2 us
  starting transfers between devices: 11.2 us -> 12.4 us
  waiting for transfers between devices: 1.86 us -> 0.84 us
    pallas_call x2, Pallas kernels: 6.2 us -> 4.9 us  [the longest x1 3.95 us: local(): pl.pallas_call(up_kernel, out_shape=[jax.ShapeDtypeStruct(value.shape, va...]
    ppermute x5, starting transfers between devices: 6.72 us -> 7.96 us  [crossed(): lax.ppermute(value, 'leaf', [(i, i ^ turn) for i in range(leaf_devices)])]
    ppermute x5, waiting for transfers between devices: 1.85 us -> 0.83 us  [crossed(): lax.ppermute(value, 'leaf', [(i, i ^ turn) for i in range(leaf_devices)])]
    pallas_call x1, Pallas kernels: 2.51 us -> 2.12 us  [local(): pl.pallas_call(functools.partial(near_kernel, faces, far_groups, share),...]
    pallas_call x1, Pallas kernels: 2.41 us -> 2.71 us  [local(): pl.pallas_call(project_kernel, out_shape=jax.ShapeDtypeStruct((columns, p...]
  transfers between devices with their start and end apart: 9 -> 9, of which waited for: 1 -> 1; matrix products, arithmetic and copies ran while one was open for 0% -> 0% of each run, Pallas kernels for 45% -> 41%
where the time goes in v8:
time: 25.8 us; the launch traced here: 25.6 us
  starting transfers between devices  12.4 us (48%)
  Pallas kernels  12.2 us (47%)
  waiting for transfers between devices  0.84 us (3%)
    ppermute x5, starting transfers between devices, crossed(): lax.ppermute(value, 'leaf', [(i, i ^ turn) for i in range(leaf_devices)])  7.96 us
    ppermute x4, starting transfers between devices, rotated(): lax.ppermute(value, axis, [(i, (i - shift) % count) for i in range(count)])  4.48 us
    pallas_call x1, Pallas kernels, local(): pl.pallas_call(up_kernel, out_shape=[jax.ShapeDtypeStruct(value.shape, va...  3.95 us
    pallas_call x1, Pallas kernels, local(): pl.pallas_call(project_kernel, out_shape=jax.ShapeDtypeStruct((columns, p...  2.71 us
    pallas_call x1, Pallas kernels, local(): pl.pallas_call(functools.partial(near_kernel, faces, far_groups, share),...  2.12 us
    pallas_call x1, Pallas kernels, local(): pl.pallas_call(functools.partial(far_kernel, [tiles for tiles, _ in roots...  1.68 us
    pallas_call x1, Pallas kernels, local(): pl.pallas_call(couple_kernel, out_shape=[jax.ShapeDtypeStruct((leaf_count...  0.96 us
    ppermute x5, waiting for transfers between devices, crossed(): lax.ppermute(value, 'leaf', [(i, i ^ turn) for i in range(leaf_devices)])  0.83 us
  transfers between devices with their start and end apart: 9, of which 1 were waited for; matrix products, arithmetic and copies ran while one was open for 0% of the time, Pallas kernels for 41%

profile of v8, /device:TPU:0, one launch (start us, length us, event | category | flops | bytes accessed | tf_op | source)
XLA Modules:
  0.0 25.6 jit_solution(16352922686309780876)
XLA Ops:
  0.0 2.9 %collective-permute-start = (bf16[16,4096]{1,0:T(8,128)(2,1)}, bf16[16,4096]{1,0:T(8,128)(2,1)S(1)}, u32[]{:S(2)}, u32[]{:S(2)}) collective-permute-start(bf16[16,4096]{1,0:T(8,128)(2,1)} %refs_0_.1), channel_id=1, source_target_pairs={{0,2},{2,0},{1,3},{3,1},{4,6},{6,4},{5,7},{7,5},{8,10},{10,8},{9,1... | collective-permute-start | bytes 393224 | tf_op jit(solution)/shard_map/ppermute | solution.py:436
  2.9 0.0 collective-permute-start.1
  2.9 3.9 %up.1 = (f32[32,4096]{1,0:T(8,128)S(1)}, bf16[16,4096]{1,0:T(8,128)(2,1)S(1)}, s32[6,4,8]{2,1,0:T(4,128)S(1)}, s32[2,32]{1,0:T(2,128)S(1)}, s32[8,32]{1,0:T(8,12...) custom-call(f32[32,32,64]{2,1,0:T(8,128)} %bitcast.6, ...), custom_call_target="tpu_custom_call" | custom-call | bytes 12915000 | tf_op jit(solution)/shard_map/up/pallas_call | solution.py:446
  6.9 0.0 collective-permute-done.1.refs_1_
  6.9 0.0 collective-permute-done.refs_0_.refs_3_
  6.9 0.6 %collective-permute-start.5 = (bf16[32,2,128,128]{3,2,1,0:T(8,128)(2,1)S(1)}, bf16[32,2,128,128]{3,2,1,0:T(8,128)(2,1)S(1)}, u32[]{:S(2)}, u32[]{:S(2)}) collective-permute-start(bf16[32,2,128,128]{3,2,1,0:T(8,128)(2,1)S(1)} %get-tuple-element.57.refs_7_), channel_id=1, source_target_pairs={{0,1},{1,0},{2,3},{3,2},{4,5},{5,4},{6,7},{7,6},{8,9},{9,8},{10,11... | collective-permute-start | bytes 6291464 | tf_op jit(solution)/shard_map/ppermute | solution.py:436
  7.5 0.8 %select.1 = (bf16[176,128]{1,0:T(8,128)(2,1)S(1)}, bf16[144,128]{1,0:T(8,128)(2,1)S(1)}, bf16[144,128]{1,0:T(8,128)(2,1)S(1)}) custom-call(s32[6,4,8]{2,1,0:T(4,128)S(1)} %get-tuple-element.37.send_vmem, bf16[16,4096]{1,0:T(8,128)(2,1)S(1)} %get-tuple-element.47.dens_ref.refs_2_, bf16[16,128]{1,0:T(8,128)(2,1)S(1)} %get-tuple-element.42.root_ref.refs_0_, ...), custom_call_target="tpu_custom_call" | custom-call | bytes 3690000 | tf_op jit(solution)/shard_map/select/pallas_call | solution.py:478
  8.3 2.7 %collective-permute-start.2 = (bf16[176,128]{1,0:T(8,128)(2,1)S(1)}, bf16[176,128]{1,0:T(8,128)(2,1)S(1)}, u32[]{:S(2)}, u32[]{:S(2)}) collective-permute-start(bf16[176,128]{1,0:T(8,128)(2,1)S(1)} %get-tuple-element.50), channel_id=1, source_target_pairs={{0,16},{4,20},{8,24},{12,28},{16,0},{20,4},{24,8},{28,12},{1,17},{... | collective-permute-start | bytes 135176 | tf_op jit(solution)/shard_map/ppermute | solution.py:439
  11.0 1.5 %collective-permute-start.3 = (bf16[144,128]{1,0:T(8,128)(2,1)S(1)}, bf16[144,128]{1,0:T(8,128)(2,1)S(1)}, u32[]{:S(2)}, u32[]{:S(2)}) collective-permute-start(bf16[144,128]{1,0:T(8,128)(2,1)S(1)} %get-tuple-element.55), channel_id=1, source_target_pairs={{0,4},{4,0},{8,12},{12,8},{16,20},{20,16},{24,28},{28,24},{1,5},{5... | collective-permute-start | bytes 110600 | tf_op jit(solution)/shard_map/ppermute | solution.py:439
  12.5 1.6 %collective-permute-start.4 = (bf16[144,128]{1,0:T(8,128)(2,1)S(1)}, bf16[144,128]{1,0:T(8,128)(2,1)S(1)}, u32[]{:S(2)}, u32[]{:S(2)}) collective-permute-start(bf16[144,128]{1,0:T(8,128)(2,1)S(1)} %get-tuple-element.56), channel_id=1, source_target_pairs={{0,8},{4,12},{8,0},{12,4},{16,24},{20,28},{24,16},{28,20},{1,9},{5... | collective-permute-start | bytes 110600 | tf_op jit(solution)/shard_map/ppermute | solution.py:439
  14.0 1.0 %couple.1 = (bf16[1024,32]{1,0:T(8,128)(2,1)S(1)}, f32[16,128]{1,0:T(8,128)S(1)}) custom-call(s32[8,32]{1,0:T(8,128)S(1)} %get-tuple-element.35.table_ref, f32[32,8,32,32]{3,2,1,0:T(8,128)S(1)} %get-tuple-element.36.coupling_ref, bf16[16,4096]{1,0:T(8,128)(2,1)S(1)} %get-tuple-element.47.dens_ref.refs_2_, f32[32,4096]{1,0:T(8,128)S(1)} %get-tuple-element.48.bases_ref), custom_call_target="tpu_custom_call" | custom-call | bytes 7380000 | tf_op jit(solution)/shard_map/couple/pallas_call | solution.py:493
  15.0 0.0 collective-permute-done.2.refs_4_.refs_2_
  15.0 0.6 %collective-permute-start.6 = (bf16[64,128]{1,0:T(8,128)(2,1)S(1)}, bf16[64,128]{1,0:T(8,128)(2,1)S(1)}, u32[]{:S(2)}, u32[]{:S(2)}) collective-permute-start(bf16[64,128]{1,0:T(8,128)(2,1)S(1)} %slice.16), channel_id=1, source_target_pairs={{0,4},{4,0},{8,12},{12,8},{16,20},{20,16},{24,28},{28,24},{1,5},{5... | collective-permute-start | bytes 49160 | tf_op jit(solution)/shard_map/ppermute | solution.py:439
  15.6 0.0 collective-permute-done.3.refs_5_.refs_3_
  15.6 0.8 %collective-permute-done.4.refs_6_.refs_4_ = bf16[144,128]{1,0:T(8,128)(2,1)S(1)} collective-permute-done((bf16[144,128]{1,0:T(8,128)(2,1)S(1)}, bf16[144,128]{1,0:T(8,128)(2,1)S(1)}, u32[]{:S(2)}, u32[]{:S(2)}) %collective-permute-start.4) | collective-permute-done | bytes 36896 | tf_op jit(solution)/shard_map/ppermute | solution.py:439
  16.4 0.0 collective-permute-done.5.refs_8_
  16.4 2.1 %near.1 = (f32[16,4096]{1,0:T(8,128)S(1)}, s16[16,4352]{1,0:T(8,128)(2,1)S(1)}) custom-call(s32[2,32]{1,0:T(2,128)S(1)} %get-tuple-element.53.refs_0_, s32[2,32]{1,0:T(2,128)S(1)} %collective-permute-done.1.refs_1_, bf16[16,4096]{1,0:T(8,128)(2,1)S(1)} %get-tuple-element.47.dens_ref.refs_2_, bf16[16,4096]{1,0:T(8,128)(2,1)S(1)} %collective-permute-done.refs_0_.refs_3_, ...), custom_call_target="tpu_custom_call" | custom-call | bytes 11070000 | tf_op jit(solution)/shard_map/near/pallas_call | solution.py:523
  18.6 1.0 %collective-permute-start.8 = (s16[16,4352]{1,0:T(8,128)(2,1)S(1)}, s16[16,4352]{1,0:T(8,128)(2,1)S(1)}, u32[]{:S(2)}, u32[]{:S(2)}) collective-permute-start(s16[16,4352]{1,0:T(8,128)(2,1)S(1)} %get-tuple-element.60), channel_id=1, source_target_pairs={{0,2},{2,0},{1,3},{3,1},{4,6},{6,4},{5,7},{7,5},{8,10},{10,8},{9,1... | collective-permute-start | bytes 417800 | tf_op jit(solution)/shard_map/ppermute | solution.py:436
  19.5 0.0 collective-permute-done.6.refs_1_
  19.6 1.6 %collective-permute-start.7 = (bf16[48,128]{1,0:T(8,128)(2,1)S(1)}, bf16[48,128]{1,0:T(8,128)(2,1)S(1)}, u32[]{:S(2)}, u32[]{:S(2)}) collective-permute-start(bf16[48,128]{1,0:T(8,128)(2,1)S(1)} %pad_maximum_fusion), channel_id=1, source_target_pairs={{0,8},{4,12},{8,0},{12,4},{16,24},{20,28},{24,16},{28,20},{1,9},{5... | collective-permute-start | bytes 36872 | tf_op jit(solution)/shard_map/ppermute | solution.py:439
  21.2 0.0 copy-start
  21.2 0.0 copy-start.1
  21.2 2.7 %project.1.term_ref = f32[16,4096]{1,0:T(8,128)S(1)} custom-call(s32[8,32]{1,0:T(8,128)S(1)} %get-tuple-element.35.table_ref, f32[32,8,32,32]{3,2,1,0:T(8,128)S(1)} %get-tuple-element.36.coupling_ref, bf16[1024,32]{1,0:T(8,128)(2,1)S(1)} %get-tuple-element.49.turned_ref, f32[16,128]{1,0:T(8,128)S(1)} %get-tuple-element.52.refs_9_.first_ref, ...), custom_call_target="tpu_custom_call" | custom-call | bytes 5535000 | tf_op jit(solution)/shard_map/project/pallas_call | solution.py:543
  23.9 0.0 collective-permute-done.7.refs_5_
  23.9 0.0 collective-permute-done.8.refs_6_
  23.9 0.0 copy-done
  23.9 0.0 copy-done.1
  24.0 1.7 %far.1 = f32[16,4096]{1,0:T(8,128)} custom-call(f32[16,32,32]{2,1,0:T(8,128)S(1)} %copy-done.1, f32[16,3,32,32]{3,2,1,0:T(8,128)S(1)} %copy-done, bf16[32,4096]{1,0:T(8,128)(2,1)S(1)} %get-tuple-element.33.high_ref, bf16[32,4096]{1,0:T(8,128)(2,1)S(1)} %get-tuple-element.34.low_ref, f32[16,4096]{1,0:T(8,128)S(1)} %project.1.term_ref, ...), custom_call_target="tpu_custom_call" | custom-call | bytes 5535000 | tf_op jit(solution)/shard_map/far/pallas_call | solution.py:553
  (5 shorter events, 0.0 us)
Async XLA Ops:
  0.0 6.9 %collective-permute-start = (bf16[16,4096]{1,0:T(8,128)(2,1)}, bf16[16,4096]{1,0:T(8,128)(2,1)S(1)}, u32[]{:S(2)}, u32[]{:S(2)}) collective-permute-start(bf16[16,4096]{1,0:T(8,128)(2,1)} %refs_0_.1), channel_id=1, source_target_pairs={{0,2},{2,0},{1,3},{3,1},{4,6},{6,4},{5,7},{7,5},{8,10},{10,8},{9,1... | collective-permute-start | bytes 393224 | tf_op jit(solution)/shard_map/ppermute | solution.py:436
  2.9 4.0 %collective-permute-start.1 = (s32[2,32]{1,0:T(2,128)}, s32[2,32]{1,0:T(2,128)S(1)}, u32[]{:S(2)}, u32[]{:S(2)}) collective-permute-start(s32[2,32]{1,0:T(2,128)} %bitcast.9), channel_id=1, source_target_pairs={{0,1},{1,0},{2,3},{3,2},{4,5},{5,4},{6,7},{7,6},{8,9},{9,8},{10,11... | collective-permute-start | bytes 776 | tf_op jit(solution)/shard_map/ppermute | solution.py:436
  6.9 9.5 %collective-permute-start.5 = (bf16[32,2,128,128]{3,2,1,0:T(8,128)(2,1)S(1)}, bf16[32,2,128,128]{3,2,1,0:T(8,128)(2,1)S(1)}, u32[]{:S(2)}, u32[]{:S(2)}) collective-permute-start(bf16[32,2,128,128]{3,2,1,0:T(8,128)(2,1)S(1)} %get-tuple-element.57.refs_7_), channel_id=1, source_target_pairs={{0,1},{1,0},{2,3},{3,2},{4,5},{5,4},{6,7},{7,6},{8,9},{9,8},{10,11... | collective-permute-start | bytes 6291464 | tf_op jit(solution)/shard_map/ppermute | solution.py:436
  8.3 6.7 %collective-permute-start.2 = (bf16[176,128]{1,0:T(8,128)(2,1)S(1)}, bf16[176,128]{1,0:T(8,128)(2,1)S(1)}, u32[]{:S(2)}, u32[]{:S(2)}) collective-permute-start(bf16[176,128]{1,0:T(8,128)(2,1)S(1)} %get-tuple-element.50), channel_id=1, source_target_pairs={{0,16},{4,20},{8,24},{12,28},{16,0},{20,4},{24,8},{28,12},{1,17},{... | collective-permute-start | bytes 135176 | tf_op jit(solution)/shard_map/ppermute | solution.py:439
  11.0 4.7 %collective-permute-start.3 = (bf16[144,128]{1,0:T(8,128)(2,1)S(1)}, bf16[144,128]{1,0:T(8,128)(2,1)S(1)}, u32[]{:S(2)}, u32[]{:S(2)}) collective-permute-start(bf16[144,128]{1,0:T(8,128)(2,1)S(1)} %get-tuple-element.55), channel_id=1, source_target_pairs={{0,4},{4,0},{8,12},{12,8},{16,20},{20,16},{24,28},{28,24},{1,5},{5... | collective-permute-start | bytes 110600 | tf_op jit(solution)/shard_map/ppermute | solution.py:439
  12.5 4.0 %collective-permute-start.4 = (bf16[144,128]{1,0:T(8,128)(2,1)S(1)}, bf16[144,128]{1,0:T(8,128)(2,1)S(1)}, u32[]{:S(2)}, u32[]{:S(2)}) collective-permute-start(bf16[144,128]{1,0:T(8,128)(2,1)S(1)} %get-tuple-element.56), channel_id=1, source_target_pairs={{0,8},{4,12},{8,0},{12,4},{16,24},{20,28},{24,16},{28,20},{1,9},{5... | collective-permute-start | bytes 110600 | tf_op jit(solution)/shard_map/ppermute | solution.py:439
  15.0 4.5 %collective-permute-start.6 = (bf16[64,128]{1,0:T(8,128)(2,1)S(1)}, bf16[64,128]{1,0:T(8,128)(2,1)S(1)}, u32[]{:S(2)}, u32[]{:S(2)}) collective-permute-start(bf16[64,128]{1,0:T(8,128)(2,1)S(1)} %slice.16), channel_id=1, source_target_pairs={{0,4},{4,0},{8,12},{12,8},{16,20},{20,16},{24,28},{28,24},{1,5},{5... | collective-permute-start | bytes 49160 | tf_op jit(solution)/shard_map/ppermute | solution.py:439
  18.6 5.4 %collective-permute-start.8 = (s16[16,4352]{1,0:T(8,128)(2,1)S(1)}, s16[16,4352]{1,0:T(8,128)(2,1)S(1)}, u32[]{:S(2)}, u32[]{:S(2)}) collective-permute-start(s16[16,4352]{1,0:T(8,128)(2,1)S(1)} %get-tuple-element.60), channel_id=1, source_target_pairs={{0,2},{2,0},{1,3},{3,1},{4,6},{6,4},{5,7},{7,5},{8,10},{10,8},{9,1... | collective-permute-start | bytes 417800 | tf_op jit(solution)/shard_map/ppermute | solution.py:436
  19.6 4.4 %collective-permute-start.7 = (bf16[48,128]{1,0:T(8,128)(2,1)S(1)}, bf16[48,128]{1,0:T(8,128)(2,1)S(1)}, u32[]{:S(2)}, u32[]{:S(2)}) collective-permute-start(bf16[48,128]{1,0:T(8,128)(2,1)S(1)} %pad_maximum_fusion), channel_id=1, source_target_pairs={{0,8},{4,12},{8,0},{12,4},{16,24},{20,28},{24,16},{28,20},{1,9},{5... | collective-permute-start | bytes 36872 | tf_op jit(solution)/shard_map/ppermute | solution.py:439
  21.2 2.7 %copy-start = (f32[16,3,32,32]{3,2,1,0:T(8,128)S(1)}, f32[16,3,32,32]{3,2,1,0:T(8,128)}, u32[]{:S(2)}) copy-start(f32[16,3,32,32]{3,2,1,0:T(8,128)} %cross_ref.1) | copy-start | bytes 589828
  21.2 2.8 %copy-start.1 = (f32[16,32,32]{2,1,0:T(8,128)S(1)}, f32[16,32,32]{2,1,0:T(8,128)}, u32[]{:S(2)}) copy-start(f32[16,32,32]{2,1,0:T(8,128)} %upper_ref.1) | copy-start | bytes 196612

commit v9 on v8

--- a/solution.py
+++ b/solution.py
@@ -152,29 +152,26 @@
 
 
 def select_kernel(
-    faces, far_groups, send_vmem, dens_ref, root_ref, *refs,
-):
-    other_refs = refs[: far_groups - 1]
-    out_refs = refs[far_groups - 1 : -2]
-    send_ref, sems = refs[-2:]
-    copies = fetch([(send_vmem, send_ref)], sems)
+    faces, far_groups, send_ref, dens_ref, root_ref, *refs,
+):
+    other_refs, out_refs = refs[: far_groups - 1], refs[far_groups - 1 :]
     device = lax.axis_index("leaf")
     columns = dens_ref.shape[0]
-    cap = send_ref.shape[1]
-    copies[0].wait()
+    cap, device_count = send_ref.shape[1:]
+    own = lax.broadcasted_iota(jnp.int32, (cap, device_count), 1) == device
     for (directions, stride), out_ref in zip(faces, out_refs):
-        direction = directions[0]
+        table = send_ref[directions[0]]
         if len(directions) > 1:
-            direction = direction + device // stride % 2
+            table = jnp.where(device // stride % 2 == 0, table, send_ref[directions[1]])
+        picks = jnp.max(jnp.where(own, table.astype(F32), 0.0), axis=1, keepdims=True)
         for place in range(cap):
-            leaf = jnp.maximum(send_ref[direction, place, device], 0)
+            leaf = picks[place, 0].astype(jnp.int32)
             for part, panel_ref in enumerate((dens_ref, *other_refs)):
                 row = (place * far_groups + part) * columns
                 out_ref[row : row + columns, :] = panel_ref[
                     :, pl.ds(pl.multiple_of(leaf * LANES, LANES), LANES)
                 ]
-        for row in range(cap * far_groups * columns, out_ref.shape[0], columns):
-            out_ref[row : row + columns, :] = root_ref[...]
+        out_ref[cap * far_groups * columns :, :] = root_ref[...]
 
 
 def near_kernel(
@@ -474,22 +471,18 @@
         faces = [((2 * axis, 2 * axis + 1), 2**axis) for axis in (2, 0, 1)]
     else:
         faces = [((direction,), offset) for direction, offset in enumerate(offsets)]
-    chunks = [(cap * far_groups + (1 if place else 3)) * columns for place in range(len(faces))]
+    chunk = (cap * far_groups + 1) * columns
     outgoing = pl.pallas_call(
         functools.partial(select_kernel, faces, far_groups),
-        out_shape=[jax.ShapeDtypeStruct((chunk, LANES), BF16) for chunk in chunks],
+        out_shape=[jax.ShapeDtypeStruct((chunk, LANES), BF16)] * len(faces),
         in_specs=[VMEM] * (2 + far_groups),
         out_specs=[VMEM] * len(faces),
-        scratch_shapes=[
-            pltpu.SMEM(send.shape, jnp.int32),
-            dma((1,)),
-        ],
         compiler_params=params,
         cost_estimate=hint(1),
         name="select",
     )(send, dens, root, *others)
     outgoing, dens = lax.optimization_barrier((outgoing, dens))
-    first_leaves = LANES // rank
+    first_leaves = leaf_count // 2
     turned, leaf_local = pl.pallas_call(
         couple_kernel,
         out_shape=[

time: 25.8 us -> 24.9 us (0.965)
  Pallas kernels: 12.2 us -> 11.2 us
    pallas_call x1, Pallas kernels: 2.71 us -> 1.9 us  [local(): pl.pallas_call(project_kernel, out_shape=jax.ShapeDtypeStruct((columns, p...]
    pallas_call x1, Pallas kernels: 0.8 us -> 0.16 us  [local(): pl.pallas_call(functools.partial(select_kernel, faces, far_groups), out_s...]
    pallas_call x1, Pallas kernels: 0.96 us -> 1.38 us  [local(): pl.pallas_call(couple_kernel, out_shape=[jax.ShapeDtypeStruct((leaf_count...]
    ppermute x4, waiting for transfers between devices: 0.01 us -> 0.37 us  [rotated(): lax.ppermute(value, axis, [(i, (i - shift) % count) for i in range(count)])]
  transfers between devices with their start and end apart: 9 -> 9, of which waited for: 1 -> 3; matrix products, arithmetic and copies ran while one was open for 0% -> 0% of each run, Pallas kernels for 41% -> 38%
where the time goes in v9:
time: 24.9 us; the launch traced here: 24.7 us
  starting transfers between devices  12.4 us (50%)
  Pallas kernels  11.2 us (45%)
  waiting for transfers between devices  0.99 us (4%)
    ppermute x5, starting transfers between devices, crossed(): lax.ppermute(value, 'leaf', [(i, i ^ turn) for i in range(leaf_devices)])  7.95 us
    ppermute x4, starting transfers between devices, rotated(): lax.ppermute(value, axis, [(i, (i - shift) % count) for i in range(count)])  4.49 us
    pallas_call x1, Pallas kernels, local(): pl.pallas_call(up_kernel, out_shape=[jax.ShapeDtypeStruct(value.shape, va...  3.95 us
    pallas_call x1, Pallas kernels, local(): pl.pallas_call(functools.partial(near_kernel, faces, far_groups, share),...  2.13 us
    pallas_call x1, Pallas kernels, local(): pl.pallas_call(project_kernel, out_shape=jax.ShapeDtypeStruct((columns, p...  1.9 us
    pallas_call x1, Pallas kernels, local(): pl.pallas_call(functools.partial(far_kernel, [tiles for tiles, _ in roots...  1.67 us
    pallas_call x1, Pallas kernels, local(): pl.pallas_call(couple_kernel, out_shape=[jax.ShapeDtypeStruct((leaf_count...  1.38 us
    ppermute x5, waiting for transfers between devices, crossed(): lax.ppermute(value, 'leaf', [(i, i ^ turn) for i in range(leaf_devices)])  0.62 us
  transfers between devices with their start and end apart: 9, of which 3 were waited for; matrix products, arithmetic and copies ran while one was open for 0% of the time, Pallas kernels for 38%

profile of v9, /device:TPU:0, one launch (start us, length us, event | category | flops | bytes accessed | tf_op | source)
XLA Modules:
  0.0 24.7 jit_solution(8690091714728484798)
XLA Ops:
  0.0 2.9 %collective-permute-start = (bf16[16,4096]{1,0:T(8,128)(2,1)}, bf16[16,4096]{1,0:T(8,128)(2,1)S(1)}, u32[]{:S(2)}, u32[]{:S(2)}) collective-permute-start(bf16[16,4096]{1,0:T(8,128)(2,1)} %refs_0_.1), channel_id=1, source_target_pairs={{0,2},{2,0},{1,3},{3,1},{4,6},{6,4},{5,7},{7,5},{8,10},{10,8},{9,1... | collective-permute-start | bytes 393224 | tf_op jit(solution)/shard_map/ppermute | solution.py:433
  2.9 0.0 collective-permute-start.1
  2.9 3.9 %up.1 = (f32[32,4096]{1,0:T(8,128)S(1)}, bf16[16,4096]{1,0:T(8,128)(2,1)S(1)}, s32[6,4,8]{2,1,0:T(4,128)S(1)}, s32[2,32]{1,0:T(2,128)S(1)}, s32[8,32]{1,0:T(8,12...) custom-call(f32[32,32,64]{2,1,0:T(8,128)} %bitcast.6, ...), custom_call_target="tpu_custom_call" | custom-call | bytes 12915000 | tf_op jit(solution)/shard_map/up/pallas_call | solution.py:443
  6.9 0.0 collective-permute-done.1.refs_1_
  6.9 0.0 collective-permute-done.refs_0_.refs_3_
  6.9 0.6 %collective-permute-start.5 = (bf16[32,2,128,128]{3,2,1,0:T(8,128)(2,1)S(1)}, bf16[32,2,128,128]{3,2,1,0:T(8,128)(2,1)S(1)}, u32[]{:S(2)}, u32[]{:S(2)}) collective-permute-start(bf16[32,2,128,128]{3,2,1,0:T(8,128)(2,1)S(1)} %get-tuple-element.57.refs_7_), channel_id=1, source_target_pairs={{0,1},{1,0},{2,3},{3,2},{4,5},{5,4},{6,7},{7,6},{8,9},{9,8},{10,11... | collective-permute-start | bytes 6291464 | tf_op jit(solution)/shard_map/ppermute | solution.py:433
  7.5 0.2 select.1
  7.7 2.7 %collective-permute-start.2 = (bf16[144,128]{1,0:T(8,128)(2,1)S(1)}, bf16[144,128]{1,0:T(8,128)(2,1)S(1)}, u32[]{:S(2)}, u32[]{:S(2)}) collective-permute-start(bf16[144,128]{1,0:T(8,128)(2,1)S(1)} %get-tuple-element.50), channel_id=1, source_target_pairs={{0,16},{4,20},{8,24},{12,28},{16,0},{20,4},{24,8},{28,12},{1,17},{... | collective-permute-start | bytes 110600 | tf_op jit(solution)/shard_map/ppermute | solution.py:436
  10.3 1.5 %collective-permute-start.3 = (bf16[144,128]{1,0:T(8,128)(2,1)S(1)}, bf16[144,128]{1,0:T(8,128)(2,1)S(1)}, u32[]{:S(2)}, u32[]{:S(2)}) collective-permute-start(bf16[144,128]{1,0:T(8,128)(2,1)S(1)} %get-tuple-element.55), channel_id=1, source_target_pairs={{0,4},{4,0},{8,12},{12,8},{16,20},{20,16},{24,28},{28,24},{1,5},{5... | collective-permute-start | bytes 110600 | tf_op jit(solution)/shard_map/ppermute | solution.py:436
  11.8 1.6 %collective-permute-start.4 = (bf16[144,128]{1,0:T(8,128)(2,1)S(1)}, bf16[144,128]{1,0:T(8,128)(2,1)S(1)}, u32[]{:S(2)}, u32[]{:S(2)}) collective-permute-start(bf16[144,128]{1,0:T(8,128)(2,1)S(1)} %get-tuple-element.56), channel_id=1, source_target_pairs={{0,8},{4,12},{8,0},{12,4},{16,24},{20,28},{24,16},{28,20},{1,9},{5... | collective-permute-start | bytes 110600 | tf_op jit(solution)/shard_map/ppermute | solution.py:436
  13.4 1.4 %couple.1 = (bf16[1024,32]{1,0:T(8,128)(2,1)S(1)}, f32[16,512]{1,0:T(8,128)S(1)}) custom-call(s32[8,32]{1,0:T(8,128)S(1)} %get-tuple-element.35.table_ref, f32[32,8,32,32]{3,2,1,0:T(8,128)S(1)} %get-tuple-element.36.coupling_ref, bf16[16,4096]{1,0:T(8,128)(2,1)S(1)} %get-tuple-element.47.dens_ref.refs_2_, f32[32,4096]{1,0:T(8,128)S(1)} %get-tuple-element.48.bases_ref), custom_call_target="tpu_custom_call" | custom-call | bytes 7380000 | tf_op jit(solution)/shard_map/couple/pallas_call | solution.py:486
  14.8 0.0 collective-permute-done.2.refs_4_.refs_2_
  14.8 0.6 %collective-permute-start.6 = (bf16[64,128]{1,0:T(8,128)(2,1)S(1)}, bf16[64,128]{1,0:T(8,128)(2,1)S(1)}, u32[]{:S(2)}, u32[]{:S(2)}) collective-permute-start(bf16[64,128]{1,0:T(8,128)(2,1)S(1)} %slice.16), channel_id=1, source_target_pairs={{0,4},{4,0},{8,12},{12,8},{16,20},{20,16},{24,28},{28,24},{1,5},{5... | collective-permute-start | bytes 49160 | tf_op jit(solution)/shard_map/ppermute | solution.py:436
  15.4 0.0 collective-permute-done.3.refs_5_.refs_3_
  15.4 0.4 %collective-permute-done.4.refs_6_.refs_4_ = bf16[144,128]{1,0:T(8,128)(2,1)S(1)} collective-permute-done((bf16[144,128]{1,0:T(8,128)(2,1)S(1)}, bf16[144,128]{1,0:T(8,128)(2,1)S(1)}, u32[]{:S(2)}, u32[]{:S(2)}) %collective-permute-start.4) | collective-permute-done | bytes 36896 | tf_op jit(solution)/shard_map/ppermute | solution.py:436
  15.8 0.0 collective-permute-done.5.refs_8_
  15.8 2.1 %near.1 = (f32[16,4096]{1,0:T(8,128)S(1)}, s16[16,4352]{1,0:T(8,128)(2,1)S(1)}) custom-call(s32[2,32]{1,0:T(2,128)S(1)} %get-tuple-element.53.refs_0_, s32[2,32]{1,0:T(2,128)S(1)} %collective-permute-done.1.refs_1_, bf16[16,4096]{1,0:T(8,128)(2,1)S(1)} %get-tuple-element.47.dens_ref.refs_2_, bf16[16,4096]{1,0:T(8,128)(2,1)S(1)} %collective-permute-done.refs_0_.refs_3_, ...), custom_call_target="tpu_custom_call" | custom-call | bytes 11070000 | tf_op jit(solution)/shard_map/near/pallas_call | solution.py:516
  17.9 1.0 %collective-permute-start.8 = (s16[16,4352]{1,0:T(8,128)(2,1)S(1)}, s16[16,4352]{1,0:T(8,128)(2,1)S(1)}, u32[]{:S(2)}, u32[]{:S(2)}) collective-permute-start(s16[16,4352]{1,0:T(8,128)(2,1)S(1)} %get-tuple-element.60), channel_id=1, source_target_pairs={{0,2},{2,0},{1,3},{3,1},{4,6},{6,4},{5,7},{7,5},{8,10},{10,8},{9,1... | collective-permute-start | bytes 417800 | tf_op jit(solution)/shard_map/ppermute | solution.py:433
  18.9 0.0 collective-permute-done.6.refs_1_
  18.9 1.6 %collective-permute-start.7 = (bf16[48,128]{1,0:T(8,128)(2,1)S(1)}, bf16[48,128]{1,0:T(8,128)(2,1)S(1)}, u32[]{:S(2)}, u32[]{:S(2)}) collective-permute-start(bf16[48,128]{1,0:T(8,128)(2,1)S(1)} %pad_maximum_fusion), channel_id=1, source_target_pairs={{0,8},{4,12},{8,0},{12,4},{16,24},{20,28},{24,16},{28,20},{1,9},{5... | collective-permute-start | bytes 36872 | tf_op jit(solution)/shard_map/ppermute | solution.py:436
  20.6 0.0 copy-start
  20.6 0.0 copy-start.1
  20.6 1.9 %project.1.term_ref = f32[16,4096]{1,0:T(8,128)S(1)} custom-call(s32[8,32]{1,0:T(8,128)S(1)} %get-tuple-element.35.table_ref, f32[32,8,32,32]{3,2,1,0:T(8,128)S(1)} %get-tuple-element.36.coupling_ref, bf16[1024,32]{1,0:T(8,128)(2,1)S(1)} %get-tuple-element.49.turned_ref, f32[16,512]{1,0:T(8,128)S(1)} %get-tuple-element.52.refs_9_.first_ref, ...), custom_call_target="tpu_custom_call" | custom-call | bytes 5535000 | tf_op jit(solution)/shard_map/project/pallas_call | solution.py:536
  22.5 0.2 collective-permute-done.7.refs_5_
  22.7 0.4 %collective-permute-done.8.refs_6_ = s16[16,4352]{1,0:T(8,128)(2,1)S(1)} collective-permute-done((s16[16,4352]{1,0:T(8,128)(2,1)S(1)}, s16[16,4352]{1,0:T(8,128)(2,1)S(1)}, u32[]{:S(2)}, u32[]{:S(2)}) %collective-permute-start.8) | collective-permute-done | bytes 139296 | tf_op jit(solution)/shard_map/ppermute | solution.py:433
  23.0 0.0 copy-done
  23.0 0.0 copy-done.1
  23.1 1.7 %far.1 = f32[16,4096]{1,0:T(8,128)} custom-call(f32[16,32,32]{2,1,0:T(8,128)S(1)} %copy-done.1, f32[16,3,32,32]{3,2,1,0:T(8,128)S(1)} %copy-done, bf16[32,4096]{1,0:T(8,128)(2,1)S(1)} %get-tuple-element.33.high_ref, bf16[32,4096]{1,0:T(8,128)(2,1)S(1)} %get-tuple-element.34.low_ref, f32[16,4096]{1,0:T(8,128)S(1)} %project.1.term_ref, ...), custom_call_target="tpu_custom_call" | custom-call | bytes 5535000 | tf_op jit(solution)/shard_map/far/pallas_call | solution.py:546
  (5 shorter events, 0.0 us)
Async XLA Ops:
  0.0 6.9 %collective-permute-start = (bf16[16,4096]{1,0:T(8,128)(2,1)}, bf16[16,4096]{1,0:T(8,128)(2,1)S(1)}, u32[]{:S(2)}, u32[]{:S(2)}) collective-permute-start(bf16[16,4096]{1,0:T(8,128)(2,1)} %refs_0_.1), channel_id=1, source_target_pairs={{0,2},{2,0},{1,3},{3,1},{4,6},{6,4},{5,7},{7,5},{8,10},{10,8},{9,1... | collective-permute-start | bytes 393224 | tf_op jit(solution)/shard_map/ppermute | solution.py:433
  2.9 4.0 %collective-permute-start.1 = (s32[2,32]{1,0:T(2,128)}, s32[2,32]{1,0:T(2,128)S(1)}, u32[]{:S(2)}, u32[]{:S(2)}) collective-permute-start(s32[2,32]{1,0:T(2,128)} %bitcast.9), channel_id=1, source_target_pairs={{0,1},{1,0},{2,3},{3,2},{4,5},{5,4},{6,7},{7,6},{8,9},{9,8},{10,11... | collective-permute-start | bytes 776 | tf_op jit(solution)/shard_map/ppermute | solution.py:433
  6.9 8.9 %collective-permute-start.5 = (bf16[32,2,128,128]{3,2,1,0:T(8,128)(2,1)S(1)}, bf16[32,2,128,128]{3,2,1,0:T(8,128)(2,1)S(1)}, u32[]{:S(2)}, u32[]{:S(2)}) collective-permute-start(bf16[32,2,128,128]{3,2,1,0:T(8,128)(2,1)S(1)} %get-tuple-element.57.refs_7_), channel_id=1, source_target_pairs={{0,1},{1,0},{2,3},{3,2},{4,5},{5,4},{6,7},{7,6},{8,9},{9,8},{10,11... | collective-permute-start | bytes 6291464 | tf_op jit(solution)/shard_map/ppermute | solution.py:433
  7.7 7.1 %collective-permute-start.2 = (bf16[144,128]{1,0:T(8,128)(2,1)S(1)}, bf16[144,128]{1,0:T(8,128)(2,1)S(1)}, u32[]{:S(2)}, u32[]{:S(2)}) collective-permute-start(bf16[144,128]{1,0:T(8,128)(2,1)S(1)} %get-tuple-element.50), channel_id=1, source_target_pairs={{0,16},{4,20},{8,24},{12,28},{16,0},{20,4},{24,8},{28,12},{1,17},{... | collective-permute-start | bytes 110600 | tf_op jit(solution)/shard_map/ppermute | solution.py:436
  10.3 5.1 %collective-permute-start.3 = (bf16[144,128]{1,0:T(8,128)(2,1)S(1)}, bf16[144,128]{1,0:T(8,128)(2,1)S(1)}, u32[]{:S(2)}, u32[]{:S(2)}) collective-permute-start(bf16[144,128]{1,0:T(8,128)(2,1)S(1)} %get-tuple-element.55), channel_id=1, source_target_pairs={{0,4},{4,0},{8,12},{12,8},{16,20},{20,16},{24,28},{28,24},{1,5},{5... | collective-permute-start | bytes 110600 | tf_op jit(solution)/shard_map/ppermute | solution.py:436
  11.8 4.0 %collective-permute-start.4 = (bf16[144,128]{1,0:T(8,128)(2,1)S(1)}, bf16[144,128]{1,0:T(8,128)(2,1)S(1)}, u32[]{:S(2)}, u32[]{:S(2)}) collective-permute-start(bf16[144,128]{1,0:T(8,128)(2,1)S(1)} %get-tuple-element.56), channel_id=1, source_target_pairs={{0,8},{4,12},{8,0},{12,4},{16,24},{20,28},{24,16},{28,20},{1,9},{5... | collective-permute-start | bytes 110600 | tf_op jit(solution)/shard_map/ppermute | solution.py:436
  14.8 4.1 %collective-permute-start.6 = (bf16[64,128]{1,0:T(8,128)(2,1)S(1)}, bf16[64,128]{1,0:T(8,128)(2,1)S(1)}, u32[]{:S(2)}, u32[]{:S(2)}) collective-permute-start(bf16[64,128]{1,0:T(8,128)(2,1)S(1)} %slice.16), channel_id=1, source_target_pairs={{0,4},{4,0},{8,12},{12,8},{16,20},{20,16},{24,28},{28,24},{1,5},{5... | collective-permute-start | bytes 49160 | tf_op jit(solution)/shard_map/ppermute | solution.py:436
  17.9 5.1 %collective-permute-start.8 = (s16[16,4352]{1,0:T(8,128)(2,1)S(1)}, s16[16,4352]{1,0:T(8,128)(2,1)S(1)}, u32[]{:S(2)}, u32[]{:S(2)}) collective-permute-start(s16[16,4352]{1,0:T(8,128)(2,1)S(1)} %get-tuple-element.60), channel_id=1, source_target_pairs={{0,2},{2,0},{1,3},{3,1},{4,6},{6,4},{5,7},{7,5},{8,10},{10,8},{9,1... | collective-permute-start | bytes 417800 | tf_op jit(solution)/shard_map/ppermute | solution.py:433
  18.9 3.8 %collective-permute-start.7 = (bf16[48,128]{1,0:T(8,128)(2,1)S(1)}, bf16[48,128]{1,0:T(8,128)(2,1)S(1)}, u32[]{:S(2)}, u32[]{:S(2)}) collective-permute-start(bf16[48,128]{1,0:T(8,128)(2,1)S(1)} %pad_maximum_fusion), channel_id=1, source_target_pairs={{0,8},{4,12},{8,0},{12,4},{16,24},{20,28},{24,16},{28,20},{1,9},{5... | collective-permute-start | bytes 36872 | tf_op jit(solution)/shard_map/ppermute | solution.py:436
  20.6 2.5 %copy-start = (f32[16,3,32,32]{3,2,1,0:T(8,128)S(1)}, f32[16,3,32,32]{3,2,1,0:T(8,128)}, u32[]{:S(2)}) copy-start(f32[16,3,32,32]{3,2,1,0:T(8,128)} %cross_ref.1) | copy-start | bytes 589828
  20.6 2.5 %copy-start.1 = (f32[16,32,32]{2,1,0:T(8,128)S(1)}, f32[16,32,32]{2,1,0:T(8,128)}, u32[]{:S(2)}) copy-start(f32[16,32,32]{2,1,0:T(8,128)} %upper_ref.1) | copy-start | bytes 196612

commit v10 on v9

--- a/solution.py
+++ b/solution.py
@@ -15,7 +15,6 @@
 STEPS = 32000.0
 VMEM = pl.BlockSpec(memory_space=pltpu.VMEM)
 HBM = pl.BlockSpec(memory_space=pltpu.HBM)
-SMEM = pl.BlockSpec(memory_space=pltpu.SMEM)
 
 
 def cube_side(device_count):
@@ -64,6 +63,21 @@
         pieces[slot] = block[:, slot * width : (slot + 1) * width]
         rows.append(jnp.concatenate(pieces, axis=1))
     return jnp.concatenate(rows, axis=0)
+
+
+def packed_words(table):
+    words = []
+    for first in range(0, table.shape[0], 4):
+        word = table[first : first + 1]
+        for row in range(first + 1, min(first + 4, table.shape[0])):
+            word = word + (table[row : row + 1] << (8 * (row - first)))
+        words.append(word)
+    return words
+
+
+def unpacked(words, count, place):
+    values = [word[0, place] for word in words]
+    return [(values[row // 4] >> (8 * (row % 4))) & 255 for row in range(count)]
 
 
 def fetch(pairs, sems):
@@ -177,7 +191,7 @@
 def near_kernel(
     faces, far_groups, share, *refs,
 ):
-    source_vmems, refs = refs[:share], refs[share:]
+    source_refs, refs = refs[:share], refs[share:]
     dens_ref, refs = refs[0], refs[1:]
     other_refs, refs = refs[: far_groups - 1], refs[far_groups - 1 :]
     got_refs, refs = refs[: len(faces)], refs[len(faces) :]
@@ -185,13 +199,11 @@
     mate_refs, refs = refs[: share - 1], refs[share - 1 :]
     refs = refs[1:]
     out_refs, refs = refs[:far_groups], refs[far_groups:]
-    source_refs, refs = refs[:share], refs[share:]
     sum_refs, refs = refs[: far_groups - 1], refs[far_groups - 1 :]
     peak_refs, refs = refs[: far_groups - 1], refs[far_groups - 1 :]
-    buffer_ref, sems = refs
+    (buffer_ref,) = refs
     columns, points = dens_ref.shape
     leaf_count, near_count, width, _ = block_ref.shape
-    copies = fetch(list(zip(source_vmems, source_refs)), sems)
     cap = (buffer_ref.shape[0] - leaf_count) // len(FACE_SIGNS)
     for (directions, _), got_ref in zip(faces, got_refs):
         for direction in directions:
@@ -204,14 +216,13 @@
         rows = slice(part * columns, (part + 1) * columns)
         for leaf in range(leaf_count):
             buffer_ref[leaf, rows, :] = panel_ref[:, leaf * width : (leaf + 1) * width]
-    for copy in copies:
-        copy.wait()
     tables = list(zip(source_refs[1:], mate_refs)) + [(source_refs[0], block_ref)]
     own_ref, sent_refs = out_refs[0], out_refs[1:]
     targets = (own_ref, *sum_refs)
     for turn, (source_ref, blocks_ref) in enumerate(tables):
+        words = packed_words(source_ref[...])
         for leaf in range(leaf_count):
-            panels = [buffer_ref[source_ref[block, leaf]] for block in range(near_count)]
+            panels = [buffer_ref[slot] for slot in unpacked(words, near_count, leaf)]
             blocks = [blocks_ref[leaf, block] for block in range(near_count)]
             total = dot_nt(jnp.concatenate(panels, axis=1), jnp.concatenate(blocks, axis=1))
             lanes = slice(leaf * width, (leaf + 1) * width)
@@ -237,18 +248,19 @@
             sent_ref[:, spot : spot + width] = power[first : first + columns]
 
 
-def coupled(leaves, far_ref, coupling_ref, turned_ref):
+def coupled(leaves, table_ref, coupling_ref, turned_ref):
     far_count, rank = coupling_ref.shape[1:3]
     columns = turned_ref.shape[1] // 2
     group = LANES // rank
+    words = packed_words(table_ref[...])
     parts = []
     for leaf in leaves:
         maps = jnp.concatenate([coupling_ref[leaf, j] for j in range(far_count)], axis=1)
         maps = jnp.concatenate(halves(maps), axis=0)
         picked = jnp.concatenate(
             [
-                turned_ref[pl.ds(pl.multiple_of(far_ref[j, leaf] * rank, rank), rank), :]
-                for j in range(far_count)
+                turned_ref[pl.ds(pl.multiple_of(source * rank, rank), rank), :]
+                for source in unpacked(words, far_count, leaf)
             ],
             axis=0,
         )
@@ -261,9 +273,8 @@
 
 
 def couple_kernel(
-    table_ref, coupling_ref, dens_ref, bases_ref, turned_ref, out_ref, far_ref, sems,
+    table_ref, coupling_ref, dens_ref, bases_ref, turned_ref, out_ref,
 ):
-    copies = fetch([(table_ref, far_ref)], sems)
     columns, points = dens_ref.shape
     leaf_count, _, rank = coupling_ref.shape[:3]
     width = points // leaf_count
@@ -277,16 +288,14 @@
         turned_ref[leaf * rank : (leaf + 1) * rank, :] = jnp.where(
             upper, high.astype(F32), low.astype(F32)
         ).astype(BF16)
-    copies[0].wait()
     leaves = range(out_ref.shape[1] // rank)
-    for index, field in enumerate(coupled(leaves, far_ref, coupling_ref, turned_ref)):
+    for index, field in enumerate(coupled(leaves, table_ref, coupling_ref, turned_ref)):
         out_ref[:, index * LANES : (index + 1) * LANES] = field
 
 
 def project_kernel(
-    table_ref, coupling_ref, turned_ref, first_ref, bases_ref, near_ref, out_ref, far_ref, sems,
+    table_ref, coupling_ref, turned_ref, first_ref, bases_ref, near_ref, out_ref,
 ):
-    copies = fetch([(table_ref, far_ref)], sems)
     rank, points = bases_ref.shape
     leaf_count = coupling_ref.shape[0]
     group = LANES // rank
@@ -302,28 +311,18 @@
     done = first_ref.shape[1] // LANES
     for index in range(done):
         project(index, first_ref[:, index * LANES : (index + 1) * LANES])
-    copies[0].wait()
     leaves = range(done * group, leaf_count)
-    for index, field in enumerate(coupled(leaves, far_ref, coupling_ref, turned_ref)):
+    for index, field in enumerate(coupled(leaves, table_ref, coupling_ref, turned_ref)):
         project(done + index, field)
 
 
 def far_kernel(
-    roots, leaf_count, upper_ref, cross_ref, high_ref, low_ref, term_ref, *refs,
+    roots, upper_ref, cross_ref, high_ref, low_ref, term_ref, *refs,
 ):
     root_refs, refs = refs[: len(roots)], refs[len(roots) :]
-    sent_refs, (out_hbm, sum_ref, tile_ref, tree_ref, sems) = refs[:-5], refs[-5:]
+    out_ref, tile_ref, tree_ref = refs
     device = lax.axis_index("leaf")
-    columns, points = sum_ref.shape
-    width = points // leaf_count
-    factors = []
-    for sent_ref in sent_refs:
-        powers = [
-            sent_ref[:, points + first // columns * width :][:, :width]
-            for first in range(0, leaf_count, columns)
-        ]
-        power = jnp.concatenate([p.astype(jnp.int32).astype(F32) for p in powers], axis=0)
-        factors.append(jnp.exp2(power) * (1.0 / STEPS))
+    columns, points = out_ref.shape
     rank = upper_ref.shape[1]
     device_count = upper_ref.shape[0] // 2
     for tiles, root_ref in zip(roots, root_refs):
@@ -373,14 +372,32 @@
             total = total + split_dot(dot_nt, field, *halves(upper_ref[node]))
         field = total
         level *= 2
+    step = 4 * LANES
+    for first in range(0, points, step):
+        spots = slice(first, first + step)
+        out_ref[:, spots] = term_ref[:, spots] + split_dot(
+            dot_nn, field, high_ref[:, spots], low_ref[:, spots]
+        )
+
+
+def add_kernel(leaf_count, term_ref, *refs):
+    sent_refs, (out_hbm, sum_ref, sems) = refs[:-3], refs[-3:]
+    columns, points = sum_ref.shape
+    width = points // leaf_count
+    factors = []
+    for sent_ref in sent_refs:
+        powers = [
+            sent_ref[:, points + first // columns * width :][:, :width]
+            for first in range(0, leaf_count, columns)
+        ]
+        power = jnp.concatenate([p.astype(jnp.int32).astype(F32) for p in powers], axis=0)
+        factors.append(jnp.exp2(power) * (1.0 / STEPS))
     chunk_count = sems.shape[0]
     step = points // chunk_count
     copies = []
     for index in range(chunk_count):
         spots = slice(index * step, (index + 1) * step)
-        total = term_ref[:, spots] + split_dot(
-            dot_nn, field, high_ref[:, spots], low_ref[:, spots]
-        )
+        total = term_ref[:, spots]
         for sent_ref, factor in zip(sent_refs, factors):
             steps = sent_ref[:, spots].astype(jnp.int32).astype(F32)
             leaves = range(index * leaf_count // chunk_count, (index + 1) * leaf_count // chunk_count)
@@ -491,7 +508,6 @@
         ],
         in_specs=[VMEM] * 4,
         out_specs=[VMEM] * 2,
-        scratch_shapes=[pltpu.SMEM(far_table.shape, jnp.int32), dma((1,))],
         compiler_params=params,
         cost_estimate=hint(2),
         name="couple",
@@ -519,12 +535,10 @@
         + [jax.ShapeDtypeStruct((columns, points + tables), jnp.int16)] * (far_groups - 1),
         in_specs=[VMEM] * (2 * share + far_groups + len(faces) + 1),
         out_specs=[VMEM] * far_groups,
-        scratch_shapes=[pltpu.SMEM(sources.shape, jnp.int32)] * share
-        + [pltpu.VMEM((columns, points), F32)] * (far_groups - 1)
+        scratch_shapes=[pltpu.VMEM((columns, points), F32)] * (far_groups - 1)
         + [pltpu.VMEM((leaf_count, width), F32)] * (far_groups - 1)
         + [
             pltpu.VMEM((slots, far_groups * columns, width), BF16),
-            dma((share,)),
         ],
         compiler_params=params,
         cost_estimate=hint(3),
@@ -538,26 +552,33 @@
         out_shape=jax.ShapeDtypeStruct((columns, points), F32),
         in_specs=[VMEM] * 6,
         out_specs=VMEM,
-        scratch_shapes=[pltpu.SMEM(far_table.shape, jnp.int32), dma((1,))],
         compiler_params=params,
         cost_estimate=hint(1.5),
         name="project",
     )(far_table, coupling, turned, leaf_local, basis, partials[0])
-    return pl.pallas_call(
-        functools.partial(far_kernel, [tiles for tiles, _ in roots], leaf_count),
+    total = pl.pallas_call(
+        functools.partial(far_kernel, [tiles for tiles, _ in roots]),
         out_shape=jax.ShapeDtypeStruct((columns, points), F32),
-        in_specs=[VMEM] * (5 + len(roots) + len(received)),
-        out_specs=HBM,
+        in_specs=[VMEM] * (5 + len(roots)),
+        out_specs=VMEM,
         scratch_shapes=[
-            pltpu.VMEM((columns, points), F32),
             pltpu.VMEM((leaf_devices, columns, LANES), BF16),
             pltpu.VMEM((2 * leaf_devices, columns, rank), F32),
-            dma((8,)),
         ],
         compiler_params=params,
-        cost_estimate=hint(1.5),
+        cost_estimate=hint(1),
         name="far",
-    )(upper_transfer, up_coupling, high, low, partial, *[value for _, value in roots], *received)
+    )(upper_transfer, up_coupling, high, low, partial, *[value for _, value in roots])
+    return pl.pallas_call(
+        functools.partial(add_kernel, leaf_count),
+        out_shape=jax.ShapeDtypeStruct((columns, points), F32),
+        in_specs=[VMEM] * (1 + len(received)),
+        out_specs=HBM,
+        scratch_shapes=[pltpu.VMEM((columns, points), F32), dma((4,))],
+        compiler_params=params,
+        cost_estimate=hint(0.5),
+        name="add",
+    )(total, *received)
 
 
 def solution(mesh):

time: 24.9 us -> 23.9 us (0.960)
  Pallas kernels: 11.2 us -> 9.5 us
  waiting for transfers between devices: 0.99 us -> 1.75 us
    ppermute x5, waiting for transfers between devices: 0.62 us -> 1.74 us  [crossed(): lax.ppermute(value, 'leaf', [(i, i ^ turn) for i in range(leaf_devices)])]
    pallas_call x0 -> x1, Pallas kernels: none -> 0.77 us  [local(): pl.pallas_call(functools.partial(add_kernel, leaf_count), out_shape=jax.S...]
    pallas_call x1, Pallas kernels: 1.67 us -> 0.95 us  [local(): pl.pallas_call(functools.partial(far_kernel, [tiles for tiles, _ in roots...]
    pallas_call x1, Pallas kernels: 2.13 us -> 1.51 us  [local(): pl.pallas_call(functools.partial(near_kernel, faces, far_groups, share),...]
    pallas_call x1, Pallas kernels: 1.9 us -> 1.31 us  [local(): pl.pallas_call(project_kernel, out_shape=jax.ShapeDtypeStruct((columns, p...]
    pallas_call x1, Pallas kernels: 1.38 us -> 0.86 us  [local(): pl.pallas_call(couple_kernel, out_shape=[jax.ShapeDtypeStruct((leaf_count...]
    ppermute x4, waiting for transfers between devices: 0.37 us -> 0.01 us  [rotated(): lax.ppermute(value, axis, [(i, (i - shift) % count) for i in range(count)])]
  transfers between devices with their start and end apart: 9 -> 9, of which waited for: 3 -> 2; matrix products, arithmetic and copies ran while one was open for 0% -> 0% of each run, Pallas kernels for 38% -> 37%
where the time goes in v10:
time: 23.9 us; the launch traced here: 23.8 us
  starting transfers between devices  12.5 us (52%)
  Pallas kernels  9.5 us (40%)
  waiting for transfers between devices  1.75 us (7%)
    ppermute x5, starting transfers between devices, crossed(): lax.ppermute(value, 'leaf', [(i, i ^ turn) for i in range(leaf_devices)])  7.97 us
    ppermute x4, starting transfers between devices, rotated(): lax.ppermute(value, axis, [(i, (i - shift) % count) for i in range(count)])  4.49 us
    pallas_call x1, Pallas kernels, local(): pl.pallas_call(up_kernel, out_shape=[jax.ShapeDtypeStruct(value.shape, va...  3.95 us
    ppermute x5, waiting for transfers between devices, crossed(): lax.ppermute(value, 'leaf', [(i, i ^ turn) for i in range(leaf_devices)])  1.74 us
    pallas_call x1, Pallas kernels, local(): pl.pallas_call(functools.partial(near_kernel, faces, far_groups, share),...  1.51 us
    pallas_call x1, Pallas kernels, local(): pl.pallas_call(project_kernel, out_shape=jax.ShapeDtypeStruct((columns, p...  1.31 us
    pallas_call x1, Pallas kernels, local(): pl.pallas_call(functools.partial(far_kernel, [tiles for tiles, _ in roots...  0.95 us
    pallas_call x1, Pallas kernels, local(): pl.pallas_call(couple_kernel, out_shape=[jax.ShapeDtypeStruct((leaf_count...  0.86 us
  transfers between devices with their start and end apart: 9, of which 2 were waited for; matrix products, arithmetic and copies ran while one was open for 0% of the time, Pallas kernels for 37%

profile of v10, /device:TPU:0, one launch (start us, length us, event | category | flops | bytes accessed | tf_op | source)
XLA Modules:
  0.0 23.8 jit_solution(9795443159477288376)
XLA Ops:
  0.0 2.9 %collective-permute-start = (bf16[16,4096]{1,0:T(8,128)(2,1)}, bf16[16,4096]{1,0:T(8,128)(2,1)S(1)}, u32[]{:S(2)}, u32[]{:S(2)}) collective-permute-start(bf16[16,4096]{1,0:T(8,128)(2,1)} %refs_0_.1), channel_id=1, source_target_pairs={{0,2},{2,0},{1,3},{3,1},{4,6},{6,4},{5,7},{7,5},{8,10},{10,8},{9,1... | collective-permute-start | bytes 393224 | tf_op jit(solution)/shard_map/ppermute | solution.py:450
  2.9 0.0 collective-permute-start.1
  2.9 3.9 %up.1 = (f32[32,4096]{1,0:T(8,128)S(1)}, bf16[16,4096]{1,0:T(8,128)(2,1)S(1)}, s32[6,4,8]{2,1,0:T(4,128)S(1)}, s32[2,32]{1,0:T(2,128)S(1)}, s32[8,32]{1,0:T(8,12...) custom-call(f32[32,32,64]{2,1,0:T(8,128)} %bitcast.6, ...), custom_call_target="tpu_custom_call" | custom-call | bytes 12915000 | tf_op jit(solution)/shard_map/up/pallas_call | solution.py:460
  6.9 0.0 collective-permute-done.1.refs_1_
  6.9 0.0 collective-permute-done.refs_0_.refs_3_
  6.9 0.6 %collective-permute-start.5 = (bf16[32,2,128,128]{3,2,1,0:T(8,128)(2,1)S(1)}, bf16[32,2,128,128]{3,2,1,0:T(8,128)(2,1)S(1)}, u32[]{:S(2)}, u32[]{:S(2)}) collective-permute-start(bf16[32,2,128,128]{3,2,1,0:T(8,128)(2,1)S(1)} %get-tuple-element.57.refs_7_), channel_id=1, source_target_pairs={{0,1},{1,0},{2,3},{3,2},{4,5},{5,4},{6,7},{7,6},{8,9},{9,8},{10,11... | collective-permute-start | bytes 6291464 | tf_op jit(solution)/shard_map/ppermute | solution.py:450
  7.5 0.2 select.1
  7.7 2.7 %collective-permute-start.2 = (bf16[144,128]{1,0:T(8,128)(2,1)S(1)}, bf16[144,128]{1,0:T(8,128)(2,1)S(1)}, u32[]{:S(2)}, u32[]{:S(2)}) collective-permute-start(bf16[144,128]{1,0:T(8,128)(2,1)S(1)} %get-tuple-element.50), channel_id=1, source_target_pairs={{0,16},{4,20},{8,24},{12,28},{16,0},{20,4},{24,8},{28,12},{1,17},{... | collective-permute-start | bytes 110600 | tf_op jit(solution)/shard_map/ppermute | solution.py:453
  10.3 1.5 %collective-permute-start.3 = (bf16[144,128]{1,0:T(8,128)(2,1)S(1)}, bf16[144,128]{1,0:T(8,128)(2,1)S(1)}, u32[]{:S(2)}, u32[]{:S(2)}) collective-permute-start(bf16[144,128]{1,0:T(8,128)(2,1)S(1)} %get-tuple-element.55), channel_id=1, source_target_pairs={{0,4},{4,0},{8,12},{12,8},{16,20},{20,16},{24,28},{28,24},{1,5},{5... | collective-permute-start | bytes 110600 | tf_op jit(solution)/shard_map/ppermute | solution.py:453
  11.8 1.6 %collective-permute-start.4 = (bf16[144,128]{1,0:T(8,128)(2,1)S(1)}, bf16[144,128]{1,0:T(8,128)(2,1)S(1)}, u32[]{:S(2)}, u32[]{:S(2)}) collective-permute-start(bf16[144,128]{1,0:T(8,128)(2,1)S(1)} %get-tuple-element.56), channel_id=1, source_target_pairs={{0,8},{4,12},{8,0},{12,4},{16,24},{20,28},{24,16},{28,20},{1,9},{5... | collective-permute-start | bytes 110600 | tf_op jit(solution)/shard_map/ppermute | solution.py:453
  13.4 0.9 %couple.1 = (bf16[1024,32]{1,0:T(8,128)(2,1)S(1)}, f32[16,512]{1,0:T(8,128)S(1)}) custom-call(s32[8,32]{1,0:T(8,128)S(1)} %get-tuple-element.35.table_ref, f32[32,8,32,32]{3,2,1,0:T(8,128)S(1)} %get-tuple-element.36.coupling_ref, bf16[16,4096]{1,0:T(8,128)(2,1)S(1)} %get-tuple-element.47.dens_ref.refs_2_, f32[32,4096]{1,0:T(8,128)S(1)} %get-tuple-element.48.bases_ref), custom_call_target="tpu_custom_call" | custom-call | bytes 7380000 | tf_op jit(solution)/shard_map/couple/pallas_call | solution.py:503
  14.3 0.0 collective-permute-done.2.refs_4_.refs_2_
  14.3 0.6 %collective-permute-start.6 = (bf16[64,128]{1,0:T(8,128)(2,1)S(1)}, bf16[64,128]{1,0:T(8,128)(2,1)S(1)}, u32[]{:S(2)}, u32[]{:S(2)}) collective-permute-start(bf16[64,128]{1,0:T(8,128)(2,1)S(1)} %slice.16), channel_id=1, source_target_pairs={{0,4},{4,0},{8,12},{12,8},{16,20},{20,16},{24,28},{28,24},{1,5},{5... | collective-permute-start | bytes 49160 | tf_op jit(solution)/shard_map/ppermute | solution.py:453
  14.9 0.0 collective-permute-done.3.refs_5_.refs_3_
  14.9 0.9 %collective-permute-done.4.refs_6_.refs_4_ = bf16[144,128]{1,0:T(8,128)(2,1)S(1)} collective-permute-done((bf16[144,128]{1,0:T(8,128)(2,1)S(1)}, bf16[144,128]{1,0:T(8,128)(2,1)S(1)}, u32[]{:S(2)}, u32[]{:S(2)}) %collective-permute-start.4) | collective-permute-done | bytes 36896 | tf_op jit(solution)/shard_map/ppermute | solution.py:453
  15.8 0.0 collective-permute-done.5.refs_8_
  15.8 1.5 %near.1 = (f32[16,4096]{1,0:T(8,128)S(1)}, s16[16,4352]{1,0:T(8,128)(2,1)S(1)}) custom-call(s32[2,32]{1,0:T(2,128)S(1)} %get-tuple-element.53.refs_0_, s32[2,32]{1,0:T(2,128)S(1)} %collective-permute-done.1.refs_1_, bf16[16,4096]{1,0:T(8,128)(2,1)S(1)} %get-tuple-element.47.dens_ref.refs_2_, bf16[16,4096]{1,0:T(8,128)(2,1)S(1)} %collective-permute-done.refs_0_.refs_3_, ...), custom_call_target="tpu_custom_call" | custom-call | bytes 11070000 | tf_op jit(solution)/shard_map/near/pallas_call | solution.py:532
  17.3 1.0 %collective-permute-start.8 = (s16[16,4352]{1,0:T(8,128)(2,1)S(1)}, s16[16,4352]{1,0:T(8,128)(2,1)S(1)}, u32[]{:S(2)}, u32[]{:S(2)}) collective-permute-start(s16[16,4352]{1,0:T(8,128)(2,1)S(1)} %get-tuple-element.60), channel_id=1, source_target_pairs={{0,2},{2,0},{1,3},{3,1},{4,6},{6,4},{5,7},{7,5},{8,10},{10,8},{9,1... | collective-permute-start | bytes 417800 | tf_op jit(solution)/shard_map/ppermute | solution.py:450
  18.3 0.0 collective-permute-done.6.refs_1_
  18.3 1.6 %collective-permute-start.7 = (bf16[48,128]{1,0:T(8,128)(2,1)S(1)}, bf16[48,128]{1,0:T(8,128)(2,1)S(1)}, u32[]{:S(2)}, u32[]{:S(2)}) collective-permute-start(bf16[48,128]{1,0:T(8,128)(2,1)S(1)} %pad_maximum_fusion), channel_id=1, source_target_pairs={{0,8},{4,12},{8,0},{12,4},{16,24},{20,28},{24,16},{28,20},{1,9},{5... | collective-permute-start | bytes 36872 | tf_op jit(solution)/shard_map/ppermute | solution.py:453
  20.0 0.0 copy-start
  20.0 0.0 copy-start.1
  20.0 1.3 %project.1.term_ref = f32[16,4096]{1,0:T(8,128)S(1)} custom-call(s32[8,32]{1,0:T(8,128)S(1)} %get-tuple-element.35.table_ref, f32[32,8,32,32]{3,2,1,0:T(8,128)S(1)} %get-tuple-element.36.coupling_ref, bf16[1024,32]{1,0:T(8,128)(2,1)S(1)} %get-tuple-element.49.turned_ref, f32[16,512]{1,0:T(8,128)S(1)} %get-tuple-element.52.refs_9_.first_ref, ...), custom_call_target="tpu_custom_call" | custom-call | bytes 5535000 | tf_op jit(solution)/shard_map/project/pallas_call | solution.py:550
  21.3 0.8 %collective-permute-done.7.refs_5_ = bf16[48,128]{1,0:T(8,128)(2,1)S(1)} collective-permute-done((bf16[48,128]{1,0:T(8,128)(2,1)S(1)}, bf16[48,128]{1,0:T(8,128)(2,1)S(1)}, u32[]{:S(2)}, u32[]{:S(2)}) %collective-permute-start.7) | collective-permute-done | bytes 12320 | tf_op jit(solution)/shard_map/ppermute | solution.py:453
  22.1 0.0 copy-done
  22.1 0.0 copy-done.1
  22.1 1.0 %far.1.term_ref = f32[16,4096]{1,0:T(8,128)S(1)} custom-call(f32[16,32,32]{2,1,0:T(8,128)S(1)} %copy-done.1, f32[16,3,32,32]{3,2,1,0:T(8,128)S(1)} %copy-done, bf16[32,4096]{1,0:T(8,128)(2,1)S(1)} %get-tuple-element.33.high_ref, bf16[32,4096]{1,0:T(8,128)(2,1)S(1)} %get-tuple-element.34.low_ref, f32[16,4096]{1,0:T(8,128)S(1)} %project.1.term_ref, ...), custom_call_target="tpu_custom_call" | custom-call | bytes 3690000 | tf_op jit(solution)/shard_map/far/pallas_call | solution.py:559
  23.0 0.0 collective-permute-done.8.refs_0_
  23.0 0.8 %add.1 = f32[16,4096]{1,0:T(8,128)} custom-call(f32[16,4096]{1,0:T(8,128)S(1)} %far.1.term_ref, s16[16,4352]{1,0:T(8,128)(2,1)S(1)} %collective-permute-done.8.refs_0_), custom_call_target="tpu_custom_call" | custom-call | bytes 1845000 | tf_op jit(solution)/shard_map/add/pallas_call | solution.py:572
  (5 shorter events, 0.0 us)
Async XLA Ops:
  0.0 6.9 %collective-permute-start = (bf16[16,4096]{1,0:T(8,128)(2,1)}, bf16[16,4096]{1,0:T(8,128)(2,1)S(1)}, u32[]{:S(2)}, u32[]{:S(2)}) collective-permute-start(bf16[16,4096]{1,0:T(8,128)(2,1)} %refs_0_.1), channel_id=1, source_target_pairs={{0,2},{2,0},{1,3},{3,1},{4,6},{6,4},{5,7},{7,5},{8,10},{10,8},{9,1... | collective-permute-start | bytes 393224 | tf_op jit(solution)/shard_map/ppermute | solution.py:450
  2.9 4.0 %collective-permute-start.1 = (s32[2,32]{1,0:T(2,128)}, s32[2,32]{1,0:T(2,128)S(1)}, u32[]{:S(2)}, u32[]{:S(2)}) collective-permute-start(s32[2,32]{1,0:T(2,128)} %bitcast.9), channel_id=1, source_target_pairs={{0,1},{1,0},{2,3},{3,2},{4,5},{5,4},{6,7},{7,6},{8,9},{9,8},{10,11... | collective-permute-start | bytes 776 | tf_op jit(solution)/shard_map/ppermute | solution.py:450
  6.9 8.9 %collective-permute-start.5 = (bf16[32,2,128,128]{3,2,1,0:T(8,128)(2,1)S(1)}, bf16[32,2,128,128]{3,2,1,0:T(8,128)(2,1)S(1)}, u32[]{:S(2)}, u32[]{:S(2)}) collective-permute-start(bf16[32,2,128,128]{3,2,1,0:T(8,128)(2,1)S(1)} %get-tuple-element.57.refs_7_), channel_id=1, source_target_pairs={{0,1},{1,0},{2,3},{3,2},{4,5},{5,4},{6,7},{7,6},{8,9},{9,8},{10,11... | collective-permute-start | bytes 6291464 | tf_op jit(solution)/shard_map/ppermute | solution.py:450
  7.7 6.6 %collective-permute-start.2 = (bf16[144,128]{1,0:T(8,128)(2,1)S(1)}, bf16[144,128]{1,0:T(8,128)(2,1)S(1)}, u32[]{:S(2)}, u32[]{:S(2)}) collective-permute-start(bf16[144,128]{1,0:T(8,128)(2,1)S(1)} %get-tuple-element.50), channel_id=1, source_target_pairs={{0,16},{4,20},{8,24},{12,28},{16,0},{20,4},{24,8},{28,12},{1,17},{... | collective-permute-start | bytes 110600 | tf_op jit(solution)/shard_map/ppermute | solution.py:453
  10.3 4.6 %collective-permute-start.3 = (bf16[144,128]{1,0:T(8,128)(2,1)S(1)}, bf16[144,128]{1,0:T(8,128)(2,1)S(1)}, u32[]{:S(2)}, u32[]{:S(2)}) collective-permute-start(bf16[144,128]{1,0:T(8,128)(2,1)S(1)} %get-tuple-element.55), channel_id=1, source_target_pairs={{0,4},{4,0},{8,12},{12,8},{16,20},{20,16},{24,28},{28,24},{1,5},{5... | collective-permute-start | bytes 110600 | tf_op jit(solution)/shard_map/ppermute | solution.py:453
  11.8 4.0 %collective-permute-start.4 = (bf16[144,128]{1,0:T(8,128)(2,1)S(1)}, bf16[144,128]{1,0:T(8,128)(2,1)S(1)}, u32[]{:S(2)}, u32[]{:S(2)}) collective-permute-start(bf16[144,128]{1,0:T(8,128)(2,1)S(1)} %get-tuple-element.56), channel_id=1, source_target_pairs={{0,8},{4,12},{8,0},{12,4},{16,24},{20,28},{24,16},{28,20},{1,9},{5... | collective-permute-start | bytes 110600 | tf_op jit(solution)/shard_map/ppermute | solution.py:453
  14.3 4.0 %collective-permute-start.6 = (bf16[64,128]{1,0:T(8,128)(2,1)S(1)}, bf16[64,128]{1,0:T(8,128)(2,1)S(1)}, u32[]{:S(2)}, u32[]{:S(2)}) collective-permute-start(bf16[64,128]{1,0:T(8,128)(2,1)S(1)} %slice.16), channel_id=1, source_target_pairs={{0,4},{4,0},{8,12},{12,8},{16,20},{20,16},{24,28},{28,24},{1,5},{5... | collective-permute-start | bytes 49160 | tf_op jit(solution)/shard_map/ppermute | solution.py:453
  17.3 5.7 %collective-permute-start.8 = (s16[16,4352]{1,0:T(8,128)(2,1)S(1)}, s16[16,4352]{1,0:T(8,128)(2,1)S(1)}, u32[]{:S(2)}, u32[]{:S(2)}) collective-permute-start(s16[16,4352]{1,0:T(8,128)(2,1)S(1)} %get-tuple-element.60), channel_id=1, source_target_pairs={{0,2},{2,0},{1,3},{3,1},{4,6},{6,4},{5,7},{7,5},{8,10},{10,8},{9,1... | collective-permute-start | bytes 417800 | tf_op jit(solution)/shard_map/ppermute | solution.py:450
  18.3 3.8 %collective-permute-start.7 = (bf16[48,128]{1,0:T(8,128)(2,1)S(1)}, bf16[48,128]{1,0:T(8,128)(2,1)S(1)}, u32[]{:S(2)}, u32[]{:S(2)}) collective-permute-start(bf16[48,128]{1,0:T(8,128)(2,1)S(1)} %pad_maximum_fusion), channel_id=1, source_target_pairs={{0,8},{4,12},{8,0},{12,4},{16,24},{20,28},{24,16},{28,20},{1,9},{5... | collective-permute-start | bytes 36872 | tf_op jit(solution)/shard_map/ppermute | solution.py:453
  20.0 2.1 %copy-start = (f32[16,3,32,32]{3,2,1,0:T(8,128)S(1)}, f32[16,3,32,32]{3,2,1,0:T(8,128)}, u32[]{:S(2)}) copy-start(f32[16,3,32,32]{3,2,1,0:T(8,128)} %cross_ref.1) | copy-start | bytes 589828
  20.0 2.1 %copy-start.1 = (f32[16,32,32]{2,1,0:T(8,128)S(1)}, f32[16,32,32]{2,1,0:T(8,128)}, u32[]{:S(2)}) copy-start(f32[16,32,32]{2,1,0:T(8,128)} %upper_ref.1) | copy-start | bytes 196612

commit v11 on v10

--- a/solution.py
+++ b/solution.py
@@ -197,7 +197,7 @@
     got_refs, refs = refs[: len(faces)], refs[len(faces) :]
     block_ref, refs = refs[0], refs[1:]
     mate_refs, refs = refs[: share - 1], refs[share - 1 :]
-    refs = refs[1:]
+    refs = refs[2:]
     out_refs, refs = refs[:far_groups], refs[far_groups:]
     sum_refs, refs = refs[: far_groups - 1], refs[far_groups - 1 :]
     peak_refs, refs = refs[: far_groups - 1], refs[far_groups - 1 :]
@@ -216,25 +216,23 @@
         rows = slice(part * columns, (part + 1) * columns)
         for leaf in range(leaf_count):
             buffer_ref[leaf, rows, :] = panel_ref[:, leaf * width : (leaf + 1) * width]
-    tables = list(zip(source_refs[1:], mate_refs)) + [(source_refs[0], block_ref)]
+    words = [packed_words(source_ref[...]) for source_ref in source_refs]
     own_ref, sent_refs = out_refs[0], out_refs[1:]
     targets = (own_ref, *sum_refs)
-    for turn, (source_ref, blocks_ref) in enumerate(tables):
-        words = packed_words(source_ref[...])
-        for leaf in range(leaf_count):
-            panels = [buffer_ref[slot] for slot in unpacked(words, near_count, leaf)]
-            blocks = [blocks_ref[leaf, block] for block in range(near_count)]
-            total = dot_nt(jnp.concatenate(panels, axis=1), jnp.concatenate(blocks, axis=1))
-            lanes = slice(leaf * width, (leaf + 1) * width)
-            for part, target_ref in enumerate(targets):
-                term = total[part * columns : (part + 1) * columns]
-                if turn:
-                    term = target_ref[:, lanes] + term
-                target_ref[:, lanes] = term
-                if part and turn == share - 1:
-                    peak_refs[part - 1][leaf : leaf + 1, :] = jnp.max(
-                        jnp.abs(term), axis=0, keepdims=True
-                    )
+    for leaf in range(leaf_count):
+        panels, blocks = [], []
+        for word, blocks_ref in zip(words, (block_ref, *mate_refs)):
+            panels += [buffer_ref[slot] for slot in unpacked(word, near_count, leaf)]
+            blocks += [blocks_ref[leaf, block] for block in range(near_count)]
+        total = dot_nt(jnp.concatenate(panels, axis=1), jnp.concatenate(blocks, axis=1))
+        lanes = slice(leaf * width, (leaf + 1) * width)
+        for part, target_ref in enumerate(targets):
+            term = total[part * columns : (part + 1) * columns]
+            target_ref[:, lanes] = term
+            if part:
+                peak_refs[part - 1][leaf : leaf + 1, :] = jnp.max(
+                    jnp.abs(term), axis=0, keepdims=True
+                )
     for sum_ref, peak_ref, sent_ref in zip(sum_refs, peak_refs, sent_refs):
         power = jnp.floor(jnp.log2(jnp.maximum(peak_ref[...], 2.0**-100))) + 1.0
         factor = STEPS * jnp.exp2(-power)
@@ -316,62 +314,55 @@
         project(done + index, field)
 
 
-def far_kernel(
-    roots, upper_ref, cross_ref, high_ref, low_ref, term_ref, *refs,
-):
-    root_refs, refs = refs[: len(roots)], refs[len(roots) :]
-    out_ref, tile_ref, tree_ref = refs
+def paths_kernel(turns, exchanged, upper_ref, cross_ref, high_ref, low_ref, map_ref):
     device = lax.axis_index("leaf")
-    columns, points = out_ref.shape
     rank = upper_ref.shape[1]
     device_count = upper_ref.shape[0] // 2
-    for tiles, root_ref in zip(roots, root_refs):
-        if tiles is None:
-            for index in range(device_count):
-                tile_ref[index] = root_ref[index]
-        else:
-            for turn, row in tiles:
-                tile_ref[device ^ turn] = root_ref[row : row + columns, :]
-    zero = jnp.zeros((LANES - 3 * rank, rank), BF16)
-
-    def lifted(child):
-        if child >= device_count:
-            high, low = (
-                jnp.concatenate([half] * 3 + [zero], axis=0) for half in halves(upper_ref[child])
-            )
-            tile = tile_ref[child - device_count]
-            return dot_nn(tile, high) + dot_nn(tile, low)
-        return split_dot(dot_nn, tree_ref[child], *halves(upper_ref[child]))
-
-    level = device_count // 2
-    while level >= 4:
-        for node in range(level, 2 * level):
-            tree_ref[node] = lifted(2 * node) + lifted(2 * node + 1)
+    downs = {device_count: None}
+    level = device_count
+    while level > 4:
+        node = level + device // (device_count // level)
+        below = downs[level]
+        matrix = upper_ref[node]
+        downs[level // 2] = matrix if below is None else split_dot(dot_nn, below, *halves(matrix))
         level //= 2
-    lane = lax.broadcasted_iota(jnp.int32, (LANES, rank), 0)
-    column = lax.broadcasted_iota(jnp.int32, (LANES, rank), 1)
-    gather = jnp.where((lane % rank == column) & (lane < 3 * rank), 1.0, 0.0).astype(BF16)
-    field = None
-    level = 4
-    while level <= device_count:
+    for level in sorted(downs):
         place = device // (device_count // level)
-        node = level + place
+        for index in range(level):
+            if level == 4:
+                map_ref[level + index] = jnp.zeros((rank, rank), F32)
+            else:
+                above = map_ref[(level + index) // 2]
+                map_ref[level + index] = split_dot(
+                    dot_nt, above, *halves(upper_ref[level + index])
+                )
         third = jnp.where(place % 2 == 0, place + 3, place - 3)
-        total = None
         for slot, other in enumerate((place - 2, place + 2, third)):
             inside = (other >= 0) & (other < level)
-            other = jnp.clip(other, 0, level - 1)
-            if level == device_count:
-                value = dot_nn(tile_ref[other], gather)
-            else:
-                value = tree_ref[level + other]
-            value = jnp.where(inside, value, 0.0)
-            term = split_dot(dot_nt, value, *halves(cross_ref[node, slot]))
-            total = term if total is None else total + term
-        if field is not None:
-            total = total + split_dot(dot_nt, field, *halves(upper_ref[node]))
-        field = total
-        level *= 2
+            matrix = cross_ref[level + place, slot]
+            if downs[level] is not None:
+                matrix = split_dot(dot_nn, downs[level], *halves(matrix))
+            node = level + jnp.clip(other, 0, level - 1)
+            map_ref[node] = map_ref[node] + jnp.where(inside, matrix, 0.0)
+    zero = jnp.zeros((rank, LANES - 3 * rank), F32)
+    for place, turn in enumerate(turns):
+        matrix = map_ref[device_count + (device ^ turn if exchanged else turn)]
+        matrix = jnp.concatenate([matrix] * 3 + [zero], axis=1)
+        high, low = halves(matrix)
+        high_ref[:, place * LANES : (place + 1) * LANES] = high
+        low_ref[:, place * LANES : (place + 1) * LANES] = low
+
+
+def far_kernel(
+    tiles, path_high_ref, path_low_ref, high_ref, low_ref, term_ref, *refs,
+):
+    root_refs, out_ref = refs[:-1], refs[-1]
+    columns, points = out_ref.shape
+    pieces = []
+    for rows, root_ref in zip(tiles, root_refs):
+        pieces += [root_ref[row : row + columns, :] for row in rows]
+    roots = jnp.concatenate(pieces, axis=1)
+    field = dot_nt(roots, path_high_ref[...]) + dot_nt(roots, path_low_ref[...])
     step = 4 * LANES
     for first in range(0, points, step):
         spots = slice(first, first + step)
@@ -456,8 +447,12 @@
     others = [rotated(densities, "far", part) for part in range(1, far_groups)]
     all_sources = [sources] + [rotated(sources, "mate", part) for part in range(1, share)]
     send = send_leaf.transpose(1, 2, 0)
-    moved = [densities, send, sources, far_src.T, leaf_coupling, near_blocks]
-    basis, dens, send, sources, far_table, coupling, blocks, high, low, root = pl.pallas_call(
+    moved = [
+        densities, send, sources, far_src.T, upper_transfer, up_coupling, leaf_coupling, near_blocks,
+    ]
+    (
+        basis, dens, send, sources, far_table, upper, cross, coupling, blocks, high, low, root,
+    ) = pl.pallas_call(
         up_kernel,
         out_shape=[jax.ShapeDtypeStruct(value.shape, value.dtype) for value in (bases, *moved)]
         + [
@@ -515,17 +510,29 @@
     tail = cap * far_groups * columns
     if side == 2:
         arrived = [crossed(value, stride) for (_, stride), value in zip(faces, outgoing)]
-        far_one, near_one, _ = (value[tail : tail + columns] for value in arrived)
+        far_one, _, near_two = (value[tail : tail + columns] for value in arrived)
         later, leaf_local = lax.optimization_barrier((arrived[0][-4 * columns :], leaf_local))
-        across = crossed(later, 1)
-        held = jnp.concatenate([near_one, far_one, across[-columns:]], axis=0)
-        beside = crossed(held, 2)
-        roots = [([(0, 0)], root), ([(5, 3 * columns)], across)]
-        roots += [([(stride, tail)], value) for (_, stride), value in zip(faces, arrived)]
-        roots.append(([(3, 0), (6, columns), (7, 2 * columns)], beside))
+        across = crossed(later, 2)
+        held = jnp.concatenate([near_two, far_one, across[-columns:]], axis=0)
+        beside = crossed(held, 1)
+        turns = [0] + [stride for _, stride in faces] + [6, 3, 5, 7]
+        roots = [([0], root)] + [([tail], value) for value in arrived]
+        roots += [([3 * columns], across), ([0, columns, 2 * columns], beside)]
     else:
         arrived = [shifted(value, "leaf", stride) for (_, stride), value in zip(faces, outgoing)]
-        roots = [(None, lax.all_gather(root, "leaf", axis=0))]
+        turns = list(range(leaf_devices))
+        everyone = lax.all_gather(root, "leaf", axis=0, tiled=True)
+        roots = [([turn * columns for turn in turns], everyone)]
+    paths = pl.pallas_call(
+        functools.partial(paths_kernel, turns, side == 2),
+        out_shape=[jax.ShapeDtypeStruct((rank, leaf_devices * LANES), BF16)] * 2,
+        in_specs=[VMEM] * 2,
+        out_specs=[VMEM] * 2,
+        scratch_shapes=[pltpu.VMEM((2 * leaf_devices, rank, rank), F32)],
+        compiler_params=params,
+        cost_estimate=hint(0.7),
+        name="paths",
+    )(upper, cross)
 
     slots = leaf_count + len(offsets) * cap
     tables = -(-leaf_count // columns) * width
@@ -533,7 +540,7 @@
         functools.partial(near_kernel, faces, far_groups, share),
         out_shape=[jax.ShapeDtypeStruct((columns, points), F32)]
         + [jax.ShapeDtypeStruct((columns, points + tables), jnp.int16)] * (far_groups - 1),
-        in_specs=[VMEM] * (2 * share + far_groups + len(faces) + 1),
+        in_specs=[VMEM] * (2 * share + far_groups + len(faces) + 2),
         out_specs=[VMEM] * far_groups,
         scratch_shapes=[pltpu.VMEM((columns, points), F32)] * (far_groups - 1)
         + [pltpu.VMEM((leaf_count, width), F32)] * (far_groups - 1)
@@ -544,7 +551,7 @@
         cost_estimate=hint(3),
         name="near",
     )(
-        *all_sources, dens, *others, *arrived, blocks, *mate_blocks, leaf_local,
+        *all_sources, dens, *others, *arrived, blocks, *mate_blocks, leaf_local, paths[0],
     )
     received = [rotated(partials[part], "far", -part) for part in range(1, far_groups)]
     partial = pl.pallas_call(
@@ -557,18 +564,14 @@
         name="project",
     )(far_table, coupling, turned, leaf_local, basis, partials[0])
     total = pl.pallas_call(
-        functools.partial(far_kernel, [tiles for tiles, _ in roots]),
+        functools.partial(far_kernel, [rows for rows, _ in roots]),
         out_shape=jax.ShapeDtypeStruct((columns, points), F32),
         in_specs=[VMEM] * (5 + len(roots)),
         out_specs=VMEM,
-        scratch_shapes=[
-            pltpu.VMEM((leaf_devices, columns, LANES), BF16),
-            pltpu.VMEM((2 * leaf_devices, columns, rank), F32),
-        ],
-        compiler_params=params,
-        cost_estimate=hint(1),
+        compiler_params=params,
+        cost_estimate=hint(0.6),
         name="far",
-    )(upper_transfer, up_coupling, high, low, partial, *[value for _, value in roots])
+    )(*paths, high, low, partial, *[value for _, value in roots])
     return pl.pallas_call(
         functools.partial(add_kernel, leaf_count),
         out_shape=jax.ShapeDtypeStruct((columns, points), F32),

time: 23.9 us -> 23.6 us (0.987)
  starting transfers between devices: 12.5 us -> 11.6 us
  waiting for transfers between devices: 1.75 us -> 2.01 us
    ppermute x5, starting transfers between devices: 7.97 us -> 7.13 us  [crossed(): lax.ppermute(value, 'leaf', [(i, i ^ turn) for i in range(leaf_devices)])]
    ppermute x5, waiting for transfers between devices: 1.74 us -> 2 us  [crossed(): lax.ppermute(value, 'leaf', [(i, i ^ turn) for i in range(leaf_devices)])]
    pallas_call x1 -> x2, Pallas kernels: 0.95 us -> 1.08 us  [the longest x1 0.54 us: local(): pl.pallas_call(functools.partial(far_kernel, [rows for rows, _ in roots])...]
  transfers between devices with their start and end apart: 9 -> 9, of which waited for: 2 -> 2; matrix products, arithmetic and copies ran while one was open for 0% -> 0% of each run, Pallas kernels for 37% -> 38%
where the time goes in v11:
time: 23.6 us; the launch traced here: 23.4 us
  starting transfers between devices  11.6 us (49%)
  Pallas kernels  9.71 us (41%)
  waiting for transfers between devices  2.01 us (9%)
    ppermute x5, starting transfers between devices, crossed(): lax.ppermute(value, 'leaf', [(i, i ^ turn) for i in range(leaf_devices)])  7.13 us
    ppermute x4, starting transfers between devices, rotated(): lax.ppermute(value, axis, [(i, (i - shift) % count) for i in range(count)])  4.47 us
    pallas_call x1, Pallas kernels, local(): pl.pallas_call(up_kernel, out_shape=[jax.ShapeDtypeStruct(value.shape, va...  3.97 us
    ppermute x5, waiting for transfers between devices, crossed(): lax.ppermute(value, 'leaf', [(i, i ^ turn) for i in range(leaf_devices)])  2 us
    pallas_call x1, Pallas kernels, local(): pl.pallas_call(functools.partial(near_kernel, faces, far_groups, share),...  1.56 us
    pallas_call x1, Pallas kernels, local(): pl.pallas_call(project_kernel, out_shape=jax.ShapeDtypeStruct((columns, p...  1.31 us
    pallas_call x1, Pallas kernels, local(): pl.pallas_call(couple_kernel, out_shape=[jax.ShapeDtypeStruct((leaf_count...  0.87 us
    pallas_call x1, Pallas kernels, local(): pl.pallas_call(functools.partial(add_kernel, leaf_count), out_shape=jax.S...  0.76 us
  transfers between devices with their start and end apart: 9, of which 2 were waited for; matrix products, arithmetic and copies ran while one was open for 0% of the time, Pallas kernels for 38%

profile of v11, /device:TPU:0, one launch (start us, length us, event | category | flops | bytes accessed | tf_op | source)
XLA Modules:
  0.0 23.4 jit_solution(12000919640655334187)
XLA Ops:
  0.0 2.9 %collective-permute-start = (bf16[16,4096]{1,0:T(8,128)(2,1)}, bf16[16,4096]{1,0:T(8,128)(2,1)S(1)}, u32[]{:S(2)}, u32[]{:S(2)}) collective-permute-start(bf16[16,4096]{1,0:T(8,128)(2,1)} %refs_0_.1), channel_id=1, source_target_pairs={{0,2},{2,0},{1,3},{3,1},{4,6},{6,4},{5,7},{7,5},{8,10},{10,8},{9,1... | collective-permute-start | bytes 393224 | tf_op jit(solution)/shard_map/ppermute | solution.py:441
  2.9 0.0 collective-permute-start.1
  2.9 4.0 %up.1 = (f32[32,4096]{1,0:T(8,128)S(1)}, bf16[16,4096]{1,0:T(8,128)(2,1)S(1)}, s32[6,4,8]{2,1,0:T(4,128)S(1)}, s32[2,32]{1,0:T(2,128)S(1)}, s32[8,32]{1,0:T(8,12...) custom-call(f32[32,32,64]{2,1,0:T(8,128)} %bitcast.6, ...), custom_call_target="tpu_custom_call" | custom-call | bytes 12915000 | tf_op jit(solution)/shard_map/up/pallas_call | solution.py:455
  6.9 0.0 collective-permute-done.1.refs_1_
  6.9 0.0 collective-permute-done.refs_0_.refs_3_
  6.9 0.6 %collective-permute-start.5 = (bf16[32,2,128,128]{3,2,1,0:T(8,128)(2,1)S(1)}, bf16[32,2,128,128]{3,2,1,0:T(8,128)(2,1)S(1)}, u32[]{:S(2)}, u32[]{:S(2)}) collective-permute-start(bf16[32,2,128,128]{3,2,1,0:T(8,128)(2,1)S(1)} %get-tuple-element.65.refs_7_), channel_id=1, source_target_pairs={{0,1},{1,0},{2,3},{3,2},{4,5},{5,4},{6,7},{7,6},{8,9},{9,8},{10,11... | collective-permute-start | bytes 6291464 | tf_op jit(solution)/shard_map/ppermute | solution.py:441
  7.5 0.2 select.1
  7.7 2.7 %collective-permute-start.2 = (bf16[144,128]{1,0:T(8,128)(2,1)S(1)}, bf16[144,128]{1,0:T(8,128)(2,1)S(1)}, u32[]{:S(2)}, u32[]{:S(2)}) collective-permute-start(bf16[144,128]{1,0:T(8,128)(2,1)S(1)} %get-tuple-element.58), channel_id=1, source_target_pairs={{0,16},{4,20},{8,24},{12,28},{16,0},{20,4},{24,8},{28,12},{1,17},{... | collective-permute-start | bytes 110600 | tf_op jit(solution)/shard_map/ppermute | solution.py:444
  10.3 1.5 %collective-permute-start.3 = (bf16[144,128]{1,0:T(8,128)(2,1)S(1)}, bf16[144,128]{1,0:T(8,128)(2,1)S(1)}, u32[]{:S(2)}, u32[]{:S(2)}) collective-permute-start(bf16[144,128]{1,0:T(8,128)(2,1)S(1)} %get-tuple-element.63), channel_id=1, source_target_pairs={{0,4},{4,0},{8,12},{12,8},{16,20},{20,16},{24,28},{28,24},{1,5},{5... | collective-permute-start | bytes 110600 | tf_op jit(solution)/shard_map/ppermute | solution.py:444
  11.8 1.6 %collective-permute-start.4 = (bf16[144,128]{1,0:T(8,128)(2,1)S(1)}, bf16[144,128]{1,0:T(8,128)(2,1)S(1)}, u32[]{:S(2)}, u32[]{:S(2)}) collective-permute-start(bf16[144,128]{1,0:T(8,128)(2,1)S(1)} %get-tuple-element.64), channel_id=1, source_target_pairs={{0,8},{4,12},{8,0},{12,4},{16,24},{20,28},{24,16},{28,20},{1,9},{5... | collective-permute-start | bytes 110600 | tf_op jit(solution)/shard_map/ppermute | solution.py:444
  13.4 0.9 %couple.1 = (bf16[1024,32]{1,0:T(8,128)(2,1)S(1)}, f32[16,512]{1,0:T(8,128)S(1)}) custom-call(s32[8,32]{1,0:T(8,128)S(1)} %get-tuple-element.43.table_ref, f32[32,8,32,32]{3,2,1,0:T(8,128)S(1)} %get-tuple-element.44.coupling_ref, bf16[16,4096]{1,0:T(8,128)(2,1)S(1)} %get-tuple-element.55.dens_ref.refs_2_, f32[32,4096]{1,0:T(8,128)S(1)} %get-tuple-element.56.bases_ref), custom_call_target="tpu_custom_call" | custom-call | bytes 7380000 | tf_op jit(solution)/shard_map/couple/pallas_call | solution.py:498
  14.3 0.0 collective-permute-done.2.refs_4_.refs_1_
  14.3 0.5 %collective-permute-start.6 = (bf16[64,128]{1,0:T(8,128)(2,1)S(1)}, bf16[64,128]{1,0:T(8,128)(2,1)S(1)}, u32[]{:S(2)}, u32[]{:S(2)}) collective-permute-start(bf16[64,128]{1,0:T(8,128)(2,1)S(1)} %slice.16), channel_id=1, source_target_pairs={{0,8},{4,12},{8,0},{12,4},{16,24},{20,28},{24,16},{28,20},{1,9},{5... | collective-permute-start | bytes 49160 | tf_op jit(solution)/shard_map/ppermute | solution.py:444
  14.8 0.5 %paths.1 = (bf16[32,1024]{1,0:T(8,128)(2,1)S(1)}, bf16[32,1024]{1,0:T(8,128)(2,1)S(1)}) custom-call(f32[16,32,32]{2,1,0:T(8,128)S(1)} %get-tuple-element.37.upper_ref, f32[16,3,32,32]{3,2,1,0:T(8,128)S(1)} %get-tuple-element.38.cross_ref), custom_call_target="tpu_custom_call" | custom-call | bytes 2583000 | tf_op jit(solution)/shard_map/paths/pallas_call | solution.py:526
  15.4 0.0 collective-permute-done.3.refs_5_.refs_2_
  15.4 0.4 %collective-permute-done.4.refs_6_.refs_3_ = bf16[144,128]{1,0:T(8,128)(2,1)S(1)} collective-permute-done((bf16[144,128]{1,0:T(8,128)(2,1)S(1)}, bf16[144,128]{1,0:T(8,128)(2,1)S(1)}, u32[]{:S(2)}, u32[]{:S(2)}) %collective-permute-start.4) | collective-permute-done | bytes 36896 | tf_op jit(solution)/shard_map/ppermute | solution.py:444
  15.8 0.0 collective-permute-done.5.refs_8_
  15.8 1.6 %near.1 = (f32[16,4096]{1,0:T(8,128)S(1)}, s16[16,4352]{1,0:T(8,128)(2,1)S(1)}) custom-call(s32[2,32]{1,0:T(2,128)S(1)} %get-tuple-element.61.refs_0_, s32[2,32]{1,0:T(2,128)S(1)} %collective-permute-done.1.refs_1_, bf16[16,4096]{1,0:T(8,128)(2,1)S(1)} %get-tuple-element.55.dens_ref.refs_2_, bf16[16,4096]{1,0:T(8,128)(2,1)S(1)} %collective-permute-done.refs_0_.refs_3_, ...), custom_call_target="tpu_custom_call" | custom-call | bytes 11070000 | tf_op jit(solution)/shard_map/near/pallas_call | solution.py:539
  17.4 1.0 %collective-permute-start.8 = (s16[16,4352]{1,0:T(8,128)(2,1)S(1)}, s16[16,4352]{1,0:T(8,128)(2,1)S(1)}, u32[]{:S(2)}, u32[]{:S(2)}) collective-permute-start(s16[16,4352]{1,0:T(8,128)(2,1)S(1)} %get-tuple-element.68), channel_id=1, source_target_pairs={{0,2},{2,0},{1,3},{3,1},{4,6},{6,4},{5,7},{7,5},{8,10},{10,8},{9,1... | collective-permute-start | bytes 417800 | tf_op jit(solution)/shard_map/ppermute | solution.py:441
  18.3 0.0 collective-permute-done.6.refs_4_
  18.4 0.9 %collective-permute-start.7 = (bf16[48,128]{1,0:T(8,128)(2,1)S(1)}, bf16[48,128]{1,0:T(8,128)(2,1)S(1)}, u32[]{:S(2)}, u32[]{:S(2)}) collective-permute-start(bf16[48,128]{1,0:T(8,128)(2,1)S(1)} %pad_maximum_fusion), channel_id=1, source_target_pairs={{0,4},{4,0},{8,12},{12,8},{16,20},{20,16},{24,28},{28,24},{1,5},{5... | collective-permute-start | bytes 36872 | tf_op jit(solution)/shard_map/ppermute | solution.py:444
  19.2 1.3 %project.1.term_ref = f32[16,4096]{1,0:T(8,128)S(1)} custom-call(s32[8,32]{1,0:T(8,128)S(1)} %get-tuple-element.43.table_ref, f32[32,8,32,32]{3,2,1,0:T(8,128)S(1)} %get-tuple-element.44.coupling_ref, bf16[1024,32]{1,0:T(8,128)(2,1)S(1)} %get-tuple-element.57.turned_ref, f32[16,512]{1,0:T(8,128)S(1)} %get-tuple-element.60.refs_9_.first_ref, ...), custom_call_target="tpu_custom_call" | custom-call | bytes 5535000 | tf_op jit(solution)/shard_map/project/pallas_call | solution.py:557
  20.5 1.6 %collective-permute-done.7.refs_5_ = bf16[48,128]{1,0:T(8,128)(2,1)S(1)} collective-permute-done((bf16[48,128]{1,0:T(8,128)(2,1)S(1)}, bf16[48,128]{1,0:T(8,128)(2,1)S(1)}, u32[]{:S(2)}, u32[]{:S(2)}) %collective-permute-start.7) | collective-permute-done | bytes 12320 | tf_op jit(solution)/shard_map/ppermute | solution.py:444
  22.1 0.5 %far.1.term_ref = f32[16,4096]{1,0:T(8,128)S(1)} custom-call(bf16[32,1024]{1,0:T(8,128)(2,1)S(1)} %get-tuple-element.39.refs_10_.path_high_ref, bf16[32,1024]{1,0:T(8,128)(2,1)S(1)} %get-tuple-element.40.path_low_ref, bf16[32,4096]{1,0:T(8,128)(2,1)S(1)} %get-tuple-element.41.high_ref, bf16[32,4096]{1,0:T(8,128)(2,1)S(1)} %get-tuple-element.42.low_ref, ...), custom_call_target="tpu_custom_call" | custom-call | bytes 2214000 | tf_op jit(solution)/shard_map/far/pallas_call | solution.py:566
  22.7 0.0 collective-permute-done.8.refs_0_
  22.7 0.8 %add.1 = f32[16,4096]{1,0:T(8,128)} custom-call(f32[16,4096]{1,0:T(8,128)S(1)} %far.1.term_ref, s16[16,4352]{1,0:T(8,128)(2,1)S(1)} %collective-permute-done.8.refs_0_), custom_call_target="tpu_custom_call" | custom-call | bytes 1845000 | tf_op jit(solution)/shard_map/add/pallas_call | solution.py:575
  (5 shorter events, 0.0 us)
Async XLA Ops:
  0.0 6.9 %collective-permute-start = (bf16[16,4096]{1,0:T(8,128)(2,1)}, bf16[16,4096]{1,0:T(8,128)(2,1)S(1)}, u32[]{:S(2)}, u32[]{:S(2)}) collective-permute-start(bf16[16,4096]{1,0:T(8,128)(2,1)} %refs_0_.1), channel_id=1, source_target_pairs={{0,2},{2,0},{1,3},{3,1},{4,6},{6,4},{5,7},{7,5},{8,10},{10,8},{9,1... | collective-permute-start | bytes 393224 | tf_op jit(solution)/shard_map/ppermute | solution.py:441
  2.9 4.0 %collective-permute-start.1 = (s32[2,32]{1,0:T(2,128)}, s32[2,32]{1,0:T(2,128)S(1)}, u32[]{:S(2)}, u32[]{:S(2)}) collective-permute-start(s32[2,32]{1,0:T(2,128)} %bitcast.9), channel_id=1, source_target_pairs={{0,1},{1,0},{2,3},{3,2},{4,5},{5,4},{6,7},{7,6},{8,9},{9,8},{10,11... | collective-permute-start | bytes 776 | tf_op jit(solution)/shard_map/ppermute | solution.py:441
  6.9 8.9 %collective-permute-start.5 = (bf16[32,2,128,128]{3,2,1,0:T(8,128)(2,1)S(1)}, bf16[32,2,128,128]{3,2,1,0:T(8,128)(2,1)S(1)}, u32[]{:S(2)}, u32[]{:S(2)}) collective-permute-start(bf16[32,2,128,128]{3,2,1,0:T(8,128)(2,1)S(1)} %get-tuple-element.65.refs_7_), channel_id=1, source_target_pairs={{0,1},{1,0},{2,3},{3,2},{4,5},{5,4},{6,7},{7,6},{8,9},{9,8},{10,11... | collective-permute-start | bytes 6291464 | tf_op jit(solution)/shard_map/ppermute | solution.py:441
  7.7 6.6 %collective-permute-start.2 = (bf16[144,128]{1,0:T(8,128)(2,1)S(1)}, bf16[144,128]{1,0:T(8,128)(2,1)S(1)}, u32[]{:S(2)}, u32[]{:S(2)}) collective-permute-start(bf16[144,128]{1,0:T(8,128)(2,1)S(1)} %get-tuple-element.58), channel_id=1, source_target_pairs={{0,16},{4,20},{8,24},{12,28},{16,0},{20,4},{24,8},{28,12},{1,17},{... | collective-permute-start | bytes 110600 | tf_op jit(solution)/shard_map/ppermute | solution.py:444
  10.3 5.0 %collective-permute-start.3 = (bf16[144,128]{1,0:T(8,128)(2,1)S(1)}, bf16[144,128]{1,0:T(8,128)(2,1)S(1)}, u32[]{:S(2)}, u32[]{:S(2)}) collective-permute-start(bf16[144,128]{1,0:T(8,128)(2,1)S(1)} %get-tuple-element.63), channel_id=1, source_target_pairs={{0,4},{4,0},{8,12},{12,8},{16,20},{20,16},{24,28},{28,24},{1,5},{5... | collective-permute-start | bytes 110600 | tf_op jit(solution)/shard_map/ppermute | solution.py:444
  11.8 4.0 %collective-permute-start.4 = (bf16[144,128]{1,0:T(8,128)(2,1)S(1)}, bf16[144,128]{1,0:T(8,128)(2,1)S(1)}, u32[]{:S(2)}, u32[]{:S(2)}) collective-permute-start(bf16[144,128]{1,0:T(8,128)(2,1)S(1)} %get-tuple-element.64), channel_id=1, source_target_pairs={{0,8},{4,12},{8,0},{12,4},{16,24},{20,28},{24,16},{28,20},{1,9},{5... | collective-permute-start | bytes 110600 | tf_op jit(solution)/shard_map/ppermute | solution.py:444
  14.3 4.0 %collective-permute-start.6 = (bf16[64,128]{1,0:T(8,128)(2,1)S(1)}, bf16[64,128]{1,0:T(8,128)(2,1)S(1)}, u32[]{:S(2)}, u32[]{:S(2)}) collective-permute-start(bf16[64,128]{1,0:T(8,128)(2,1)S(1)} %slice.16), channel_id=1, source_target_pairs={{0,8},{4,12},{8,0},{12,4},{16,24},{20,28},{24,16},{28,20},{1,9},{5... | collective-permute-start | bytes 49160 | tf_op jit(solution)/shard_map/ppermute | solution.py:444
  17.4 5.3 %collective-permute-start.8 = (s16[16,4352]{1,0:T(8,128)(2,1)S(1)}, s16[16,4352]{1,0:T(8,128)(2,1)S(1)}, u32[]{:S(2)}, u32[]{:S(2)}) collective-permute-start(s16[16,4352]{1,0:T(8,128)(2,1)S(1)} %get-tuple-element.68), channel_id=1, source_target_pairs={{0,2},{2,0},{1,3},{3,1},{4,6},{6,4},{5,7},{7,5},{8,10},{10,8},{9,1... | collective-permute-start | bytes 417800 | tf_op jit(solution)/shard_map/ppermute | solution.py:441
  18.4 3.8 %collective-permute-start.7 = (bf16[48,128]{1,0:T(8,128)(2,1)S(1)}, bf16[48,128]{1,0:T(8,128)(2,1)S(1)}, u32[]{:S(2)}, u32[]{:S(2)}) collective-permute-start(bf16[48,128]{1,0:T(8,128)(2,1)S(1)} %pad_maximum_fusion), channel_id=1, source_target_pairs={{0,4},{4,0},{8,12},{12,8},{16,20},{20,16},{24,28},{28,24},{1,5},{5... | collective-permute-start | bytes 36872 | tf_op jit(solution)/shard_map/ppermute | solution.py:444

commit v12 on v11

--- a/solution.py
+++ b/solution.py
@@ -197,10 +197,9 @@
     got_refs, refs = refs[: len(faces)], refs[len(faces) :]
     block_ref, refs = refs[0], refs[1:]
     mate_refs, refs = refs[: share - 1], refs[share - 1 :]
-    refs = refs[2:]
+    refs = refs[1:]
     out_refs, refs = refs[:far_groups], refs[far_groups:]
-    sum_refs, refs = refs[: far_groups - 1], refs[far_groups - 1 :]
-    peak_refs, refs = refs[: far_groups - 1], refs[far_groups - 1 :]
+    power_refs, refs = refs[: far_groups - 1], refs[far_groups - 1 :]
     (buffer_ref,) = refs
     columns, points = dens_ref.shape
     leaf_count, near_count, width, _ = block_ref.shape
@@ -218,7 +217,6 @@
             buffer_ref[leaf, rows, :] = panel_ref[:, leaf * width : (leaf + 1) * width]
     words = [packed_words(source_ref[...]) for source_ref in source_refs]
     own_ref, sent_refs = out_refs[0], out_refs[1:]
-    targets = (own_ref, *sum_refs)
     for leaf in range(leaf_count):
         panels, blocks = [], []
         for word, blocks_ref in zip(words, (block_ref, *mate_refs)):
@@ -226,21 +224,16 @@
             blocks += [blocks_ref[leaf, block] for block in range(near_count)]
         total = dot_nt(jnp.concatenate(panels, axis=1), jnp.concatenate(blocks, axis=1))
         lanes = slice(leaf * width, (leaf + 1) * width)
-        for part, target_ref in enumerate(targets):
+        own_ref[:, lanes] = total[:columns]
+        for part, (sent_ref, power_ref) in enumerate(zip(sent_refs, power_refs), 1):
             term = total[part * columns : (part + 1) * columns]
-            target_ref[:, lanes] = term
-            if part:
-                peak_refs[part - 1][leaf : leaf + 1, :] = jnp.max(
-                    jnp.abs(term), axis=0, keepdims=True
-                )
-    for sum_ref, peak_ref, sent_ref in zip(sum_refs, peak_refs, sent_refs):
-        power = jnp.floor(jnp.log2(jnp.maximum(peak_ref[...], 2.0**-100))) + 1.0
-        factor = STEPS * jnp.exp2(-power)
-        for leaf in range(leaf_count):
-            lanes = slice(leaf * width, (leaf + 1) * width)
-            steps = sum_ref[:, lanes] * factor[leaf : leaf + 1, :]
-            sent_ref[:, lanes] = jnp.floor(steps + 0.5).astype(jnp.int32).astype(jnp.int16)
-        power = power.astype(jnp.int32).astype(jnp.int16)
+            peak = jnp.max(jnp.abs(term), axis=0, keepdims=True)
+            power = jnp.floor(jnp.log2(jnp.maximum(peak, 2.0**-100))) + 1.0
+            steps = jnp.floor(term * (STEPS * jnp.exp2(-power)) + 0.5)
+            sent_ref[:, lanes] = steps.astype(jnp.int32).astype(jnp.int16)
+            power_ref[leaf : leaf + 1, :] = power
+    for sent_ref, power_ref in zip(sent_refs, power_refs):
+        power = power_ref[...].astype(jnp.int32).astype(jnp.int16)
         for first in range(0, leaf_count, columns):
             spot = points + first // columns * width
             sent_ref[:, spot : spot + width] = power[first : first + columns]
@@ -523,6 +516,25 @@
         turns = list(range(leaf_devices))
         everyone = lax.all_gather(root, "leaf", axis=0, tiled=True)
         roots = [([turn * columns for turn in turns], everyone)]
+    slots = leaf_count + len(offsets) * cap
+    tables = -(-leaf_count // columns) * width
+    partials = pl.pallas_call(
+        functools.partial(near_kernel, faces, far_groups, share),
+        out_shape=[jax.ShapeDtypeStruct((columns, points), F32)]
+        + [jax.ShapeDtypeStruct((columns, points + tables), jnp.int16)] * (far_groups - 1),
+        in_specs=[VMEM] * (2 * share + far_groups + len(faces) + 1),
+        out_specs=[VMEM] * far_groups,
+        scratch_shapes=[pltpu.VMEM((leaf_count, width), F32)] * (far_groups - 1)
+        + [
+            pltpu.VMEM((slots, far_groups * columns, width), BF16),
+        ],
+        compiler_params=params,
+        cost_estimate=hint(3),
+        name="near",
+    )(
+        *all_sources, dens, *others, *arrived, blocks, *mate_blocks, leaf_local,
+    )
+    upper, cross, near_own = lax.optimization_barrier((upper, cross, partials[0]))
     paths = pl.pallas_call(
         functools.partial(paths_kernel, turns, side == 2),
         out_shape=[jax.ShapeDtypeStruct((rank, leaf_devices * LANES), BF16)] * 2,
@@ -533,26 +545,6 @@
         cost_estimate=hint(0.7),
         name="paths",
     )(upper, cross)
-
-    slots = leaf_count + len(offsets) * cap
-    tables = -(-leaf_count // columns) * width
-    partials = pl.pallas_call(
-        functools.partial(near_kernel, faces, far_groups, share),
-        out_shape=[jax.ShapeDtypeStruct((columns, points), F32)]
-        + [jax.ShapeDtypeStruct((columns, points + tables), jnp.int16)] * (far_groups - 1),
-        in_specs=[VMEM] * (2 * share + far_groups + len(faces) + 2),
-        out_specs=[VMEM] * far_groups,
-        scratch_shapes=[pltpu.VMEM((columns, points), F32)] * (far_groups - 1)
-        + [pltpu.VMEM((leaf_count, width), F32)] * (far_groups - 1)
-        + [
-            pltpu.VMEM((slots, far_groups * columns, width), BF16),
-        ],
-        compiler_params=params,
-        cost_estimate=hint(3),
-        name="near",
-    )(
-        *all_sources, dens, *others, *arrived, blocks, *mate_blocks, leaf_local, paths[0],
-    )
     received = [rotated(partials[part], "far", -part) for part in range(1, far_groups)]
     partial = pl.pallas_call(
         project_kernel,
@@ -562,7 +554,7 @@
         compiler_params=params,
         cost_estimate=hint(1.5),
         name="project",
-    )(far_table, coupling, turned, leaf_local, basis, partials[0])
+    )(far_table, coupling, turned, leaf_local, basis, near_own)
     total = pl.pallas_call(
         functools.partial(far_kernel, [rows for rows, _ in roots]),
         out_shape=jax.ShapeDtypeStruct((columns, points), F32),

time: 23.6 us -> 23.5 us (level)
  waiting for transfers between devices: 2.01 us -> 2.32 us
  starting transfers between devices: 11.6 us -> 11.3 us
    ppermute x5, starting transfers between devices: 7.13 us -> 6.83 us  [crossed(): lax.ppermute(value, 'leaf', [(i, i ^ turn) for i in range(leaf_devices)])]
    ppermute x5, waiting for transfers between devices: 2 us -> 2.31 us  [crossed(): lax.ppermute(value, 'leaf', [(i, i ^ turn) for i in range(leaf_devices)])]
where the time goes in v12:
time: 23.5 us; the launch traced here: 23.3 us
  starting transfers between devices  11.3 us (48%)
  Pallas kernels  9.62 us (41%)
  waiting for transfers between devices  2.32 us (10%)
    ppermute x5, starting transfers between devices, crossed(): lax.ppermute(value, 'leaf', [(i, i ^ turn) for i in range(leaf_devices)])  6.83 us
    ppermute x4, starting transfers between devices, rotated(): lax.ppermute(value, axis, [(i, (i - shift) % count) for i in range(count)])  4.47 us
    pallas_call x1, Pallas kernels, local(): pl.pallas_call(up_kernel, out_shape=[jax.ShapeDtypeStruct(value.shape, va...  3.97 us
    ppermute x5, waiting for transfers between devices, crossed(): lax.ppermute(value, 'leaf', [(i, i ^ turn) for i in range(leaf_devices)])  2.31 us
    pallas_call x1, Pallas kernels, local(): pl.pallas_call(functools.partial(near_kernel, faces, far_groups, share),...  1.46 us
    pallas_call x1, Pallas kernels, local(): pl.pallas_call(project_kernel, out_shape=jax.ShapeDtypeStruct((columns, p...  1.31 us
    pallas_call x1, Pallas kernels, local(): pl.pallas_call(couple_kernel, out_shape=[jax.ShapeDtypeStruct((leaf_count...  0.88 us
    pallas_call x1, Pallas kernels, local(): pl.pallas_call(functools.partial(add_kernel, leaf_count), out_shape=jax.S...  0.76 us
  transfers between devices with their start and end apart: 9, of which 2 were waited for; matrix products, arithmetic and copies ran while one was open for 0% of the time, Pallas kernels for 38%

profile of v12, /device:TPU:0, one launch (start us, length us, event | category | flops | bytes accessed | tf_op | source)
XLA Modules:
  0.0 23.3 jit_solution(4907497833936325654)
XLA Ops:
  0.0 2.9 %collective-permute-start = (bf16[16,4096]{1,0:T(8,128)(2,1)}, bf16[16,4096]{1,0:T(8,128)(2,1)S(1)}, u32[]{:S(2)}, u32[]{:S(2)}) collective-permute-start(bf16[16,4096]{1,0:T(8,128)(2,1)} %refs_0_.1), channel_id=1, source_target_pairs={{0,2},{2,0},{1,3},{3,1},{4,6},{6,4},{5,7},{7,5},{8,10},{10,8},{9,1... | collective-permute-start | bytes 393224 | tf_op jit(solution)/shard_map/ppermute | solution.py:434
  2.9 0.0 collective-permute-start.1
  2.9 4.0 %up.1 = (f32[32,4096]{1,0:T(8,128)S(1)}, bf16[16,4096]{1,0:T(8,128)(2,1)S(1)}, s32[6,4,8]{2,1,0:T(4,128)S(1)}, s32[2,32]{1,0:T(2,128)S(1)}, s32[8,32]{1,0:T(8,12...) custom-call(f32[32,32,64]{2,1,0:T(8,128)} %bitcast.6, ...), custom_call_target="tpu_custom_call" | custom-call | bytes 12915000 | tf_op jit(solution)/shard_map/up/pallas_call | solution.py:448
  6.9 0.0 collective-permute-done.1.refs_1_
  6.9 0.0 collective-permute-done.refs_0_.refs_3_
  6.9 0.6 %collective-permute-start.5 = (bf16[32,2,128,128]{3,2,1,0:T(8,128)(2,1)S(1)}, bf16[32,2,128,128]{3,2,1,0:T(8,128)(2,1)S(1)}, u32[]{:S(2)}, u32[]{:S(2)}) collective-permute-start(bf16[32,2,128,128]{3,2,1,0:T(8,128)(2,1)S(1)} %get-tuple-element.58.refs_7_), channel_id=1, source_target_pairs={{0,1},{1,0},{2,3},{3,2},{4,5},{5,4},{6,7},{7,6},{8,9},{9,8},{10,11... | collective-permute-start | bytes 6291464 | tf_op jit(solution)/shard_map/ppermute | solution.py:434
  7.5 0.2 select.1
  7.7 2.7 %collective-permute-start.2 = (bf16[144,128]{1,0:T(8,128)(2,1)S(1)}, bf16[144,128]{1,0:T(8,128)(2,1)S(1)}, u32[]{:S(2)}, u32[]{:S(2)}) collective-permute-start(bf16[144,128]{1,0:T(8,128)(2,1)S(1)} %get-tuple-element.55), channel_id=1, source_target_pairs={{0,16},{4,20},{8,24},{12,28},{16,0},{20,4},{24,8},{28,12},{1,17},{... | collective-permute-start | bytes 110600 | tf_op jit(solution)/shard_map/ppermute | solution.py:437
  10.3 1.5 %collective-permute-start.3 = (bf16[144,128]{1,0:T(8,128)(2,1)S(1)}, bf16[144,128]{1,0:T(8,128)(2,1)S(1)}, u32[]{:S(2)}, u32[]{:S(2)}) collective-permute-start(bf16[144,128]{1,0:T(8,128)(2,1)S(1)} %get-tuple-element.56), channel_id=1, source_target_pairs={{0,4},{4,0},{8,12},{12,8},{16,20},{20,16},{24,28},{28,24},{1,5},{5... | collective-permute-start | bytes 110600 | tf_op jit(solution)/shard_map/ppermute | solution.py:437
  11.8 1.6 %collective-permute-start.4 = (bf16[144,128]{1,0:T(8,128)(2,1)S(1)}, bf16[144,128]{1,0:T(8,128)(2,1)S(1)}, u32[]{:S(2)}, u32[]{:S(2)}) collective-permute-start(bf16[144,128]{1,0:T(8,128)(2,1)S(1)} %get-tuple-element.57), channel_id=1, source_target_pairs={{0,8},{4,12},{8,0},{12,4},{16,24},{20,28},{24,16},{28,20},{1,9},{5... | collective-permute-start | bytes 110600 | tf_op jit(solution)/shard_map/ppermute | solution.py:437
  13.4 0.9 %couple.1 = (bf16[1024,32]{1,0:T(8,128)(2,1)S(1)}, f32[16,512]{1,0:T(8,128)S(1)}) custom-call(s32[8,32]{1,0:T(8,128)S(1)} %get-tuple-element.59.table_ref, f32[32,8,32,32]{3,2,1,0:T(8,128)S(1)} %get-tuple-element.60.coupling_ref, bf16[16,4096]{1,0:T(8,128)(2,1)S(1)} %get-tuple-element.54.dens_ref.refs_2_, f32[32,4096]{1,0:T(8,128)S(1)} %get-tuple-element.61.bases_ref), custom_call_target="tpu_custom_call" | custom-call | bytes 7380000 | tf_op jit(solution)/shard_map/couple/pallas_call | solution.py:491
  14.3 0.0 collective-permute-done.2.refs_4_.refs_1_
  14.3 0.5 %collective-permute-start.6 = (bf16[64,128]{1,0:T(8,128)(2,1)S(1)}, bf16[64,128]{1,0:T(8,128)(2,1)S(1)}, u32[]{:S(2)}, u32[]{:S(2)}) collective-permute-start(bf16[64,128]{1,0:T(8,128)(2,1)S(1)} %slice.16), channel_id=1, source_target_pairs={{0,8},{4,12},{8,0},{12,4},{16,24},{20,28},{24,16},{28,20},{1,9},{5... | collective-permute-start | bytes 49160 | tf_op jit(solution)/shard_map/ppermute | solution.py:437
  14.8 0.0 collective-permute-done.3.refs_5_.refs_2_
  14.8 1.0 %collective-permute-done.4.refs_6_.refs_3_ = bf16[144,128]{1,0:T(8,128)(2,1)S(1)} collective-permute-done((bf16[144,128]{1,0:T(8,128)(2,1)S(1)}, bf16[144,128]{1,0:T(8,128)(2,1)S(1)}, u32[]{:S(2)}, u32[]{:S(2)}) %collective-permute-start.4) | collective-permute-done | bytes 36896 | tf_op jit(solution)/shard_map/ppermute | solution.py:437
  15.8 0.0 collective-permute-done.5.refs_8_
  15.8 1.5 %near.1 = (f32[16,4096]{1,0:T(8,128)S(1)}, s16[16,4352]{1,0:T(8,128)(2,1)S(1)}) custom-call(s32[2,32]{1,0:T(2,128)S(1)} %get-tuple-element.45.refs_0_, s32[2,32]{1,0:T(2,128)S(1)} %collective-permute-done.1.refs_1_, bf16[16,4096]{1,0:T(8,128)(2,1)S(1)} %get-tuple-element.54.dens_ref.refs_2_, bf16[16,4096]{1,0:T(8,128)(2,1)S(1)} %collective-permute-done.refs_0_.refs_3_, ...), custom_call_target="tpu_custom_call" | custom-call | bytes 11070000 | tf_op jit(solution)/shard_map/near/pallas_call | solution.py:521
  17.3 0.9 %collective-permute-start.8 = (s16[16,4352]{1,0:T(8,128)(2,1)S(1)}, s16[16,4352]{1,0:T(8,128)(2,1)S(1)}, u32[]{:S(2)}, u32[]{:S(2)}) collective-permute-start(s16[16,4352]{1,0:T(8,128)(2,1)S(1)} %get-tuple-element.74), channel_id=1, source_target_pairs={{0,2},{2,0},{1,3},{3,1},{4,6},{6,4},{5,7},{7,5},{8,10},{10,8},{9,1... | collective-permute-start | bytes 417800 | tf_op jit(solution)/shard_map/ppermute | solution.py:434
  18.2 0.0 collective-permute-done.6.refs_4_
  18.3 0.6 %collective-permute-start.7 = (bf16[48,128]{1,0:T(8,128)(2,1)S(1)}, bf16[48,128]{1,0:T(8,128)(2,1)S(1)}, u32[]{:S(2)}, u32[]{:S(2)}) collective-permute-start(bf16[48,128]{1,0:T(8,128)(2,1)S(1)} %pad_maximum_fusion), channel_id=1, source_target_pairs={{0,4},{4,0},{8,12},{12,8},{16,20},{20,16},{24,28},{28,24},{1,5},{5... | collective-permute-start | bytes 36872 | tf_op jit(solution)/shard_map/ppermute | solution.py:437
  18.8 0.5 %paths.1 = (bf16[32,1024]{1,0:T(8,128)(2,1)S(1)}, bf16[32,1024]{1,0:T(8,128)(2,1)S(1)}) custom-call(f32[16,32,32]{2,1,0:T(8,128)S(1)} %get-tuple-element.65.upper_ref, f32[16,3,32,32]{3,2,1,0:T(8,128)S(1)} %get-tuple-element.66.cross_ref), custom_call_target="tpu_custom_call" | custom-call | bytes 2583000 | tf_op jit(solution)/shard_map/paths/pallas_call | solution.py:538
  19.4 1.3 %project.1.term_ref = f32[16,4096]{1,0:T(8,128)S(1)} custom-call(s32[8,32]{1,0:T(8,128)S(1)} %get-tuple-element.59.table_ref, f32[32,8,32,32]{3,2,1,0:T(8,128)S(1)} %get-tuple-element.60.coupling_ref, bf16[1024,32]{1,0:T(8,128)(2,1)S(1)} %get-tuple-element.71.turned_ref, f32[16,512]{1,0:T(8,128)S(1)} %get-tuple-element.63.refs_9_.first_ref, ...), custom_call_target="tpu_custom_call" | custom-call | bytes 5535000 | tf_op jit(solution)/shard_map/project/pallas_call | solution.py:549
  20.7 1.3 %collective-permute-done.7.refs_5_ = bf16[48,128]{1,0:T(8,128)(2,1)S(1)} collective-permute-done((bf16[48,128]{1,0:T(8,128)(2,1)S(1)}, bf16[48,128]{1,0:T(8,128)(2,1)S(1)}, u32[]{:S(2)}, u32[]{:S(2)}) %collective-permute-start.7) | collective-permute-done | bytes 12320 | tf_op jit(solution)/shard_map/ppermute | solution.py:437
  22.0 0.5 %far.1.term_ref = f32[16,4096]{1,0:T(8,128)S(1)} custom-call(bf16[32,1024]{1,0:T(8,128)(2,1)S(1)} %get-tuple-element.67.path_high_ref, bf16[32,1024]{1,0:T(8,128)(2,1)S(1)} %get-tuple-element.68.path_low_ref, bf16[32,4096]{1,0:T(8,128)(2,1)S(1)} %get-tuple-element.69.high_ref, bf16[32,4096]{1,0:T(8,128)(2,1)S(1)} %get-tuple-element.70.low_ref, ...), custom_call_target="tpu_custom_call" | custom-call | bytes 2214000 | tf_op jit(solution)/shard_map/far/pallas_call | solution.py:558
  22.6 0.0 collective-permute-done.8.refs_0_
  22.6 0.8 %add.1 = f32[16,4096]{1,0:T(8,128)} custom-call(f32[16,4096]{1,0:T(8,128)S(1)} %far.1.term_ref, s16[16,4352]{1,0:T(8,128)(2,1)S(1)} %collective-permute-done.8.refs_0_), custom_call_target="tpu_custom_call" | custom-call | bytes 1845000 | tf_op jit(solution)/shard_map/add/pallas_call | solution.py:567
  (5 shorter events, 0.0 us)
Async XLA Ops:
  0.0 6.9 %collective-permute-start = (bf16[16,4096]{1,0:T(8,128)(2,1)}, bf16[16,4096]{1,0:T(8,128)(2,1)S(1)}, u32[]{:S(2)}, u32[]{:S(2)}) collective-permute-start(bf16[16,4096]{1,0:T(8,128)(2,1)} %refs_0_.1), channel_id=1, source_target_pairs={{0,2},{2,0},{1,3},{3,1},{4,6},{6,4},{5,7},{7,5},{8,10},{10,8},{9,1... | collective-permute-start | bytes 393224 | tf_op jit(solution)/shard_map/ppermute | solution.py:434
  2.9 4.0 %collective-permute-start.1 = (s32[2,32]{1,0:T(2,128)}, s32[2,32]{1,0:T(2,128)S(1)}, u32[]{:S(2)}, u32[]{:S(2)}) collective-permute-start(s32[2,32]{1,0:T(2,128)} %bitcast.9), channel_id=1, source_target_pairs={{0,1},{1,0},{2,3},{3,2},{4,5},{5,4},{6,7},{7,6},{8,9},{9,8},{10,11... | collective-permute-start | bytes 776 | tf_op jit(solution)/shard_map/ppermute | solution.py:434
  6.9 8.9 %collective-permute-start.5 = (bf16[32,2,128,128]{3,2,1,0:T(8,128)(2,1)S(1)}, bf16[32,2,128,128]{3,2,1,0:T(8,128)(2,1)S(1)}, u32[]{:S(2)}, u32[]{:S(2)}) collective-permute-start(bf16[32,2,128,128]{3,2,1,0:T(8,128)(2,1)S(1)} %get-tuple-element.58.refs_7_), channel_id=1, source_target_pairs={{0,1},{1,0},{2,3},{3,2},{4,5},{5,4},{6,7},{7,6},{8,9},{9,8},{10,11... | collective-permute-start | bytes 6291464 | tf_op jit(solution)/shard_map/ppermute | solution.py:434
  7.7 6.6 %collective-permute-start.2 = (bf16[144,128]{1,0:T(8,128)(2,1)S(1)}, bf16[144,128]{1,0:T(8,128)(2,1)S(1)}, u32[]{:S(2)}, u32[]{:S(2)}) collective-permute-start(bf16[144,128]{1,0:T(8,128)(2,1)S(1)} %get-tuple-element.55), channel_id=1, source_target_pairs={{0,16},{4,20},{8,24},{12,28},{16,0},{20,4},{24,8},{28,12},{1,17},{... | collective-permute-start | bytes 110600 | tf_op jit(solution)/shard_map/ppermute | solution.py:437
  10.3 4.5 %collective-permute-start.3 = (bf16[144,128]{1,0:T(8,128)(2,1)S(1)}, bf16[144,128]{1,0:T(8,128)(2,1)S(1)}, u32[]{:S(2)}, u32[]{:S(2)}) collective-permute-start(bf16[144,128]{1,0:T(8,128)(2,1)S(1)} %get-tuple-element.56), channel_id=1, source_target_pairs={{0,4},{4,0},{8,12},{12,8},{16,20},{20,16},{24,28},{28,24},{1,5},{5... | collective-permute-start | bytes 110600 | tf_op jit(solution)/shard_map/ppermute | solution.py:437
  11.8 4.0 %collective-permute-start.4 = (bf16[144,128]{1,0:T(8,128)(2,1)S(1)}, bf16[144,128]{1,0:T(8,128)(2,1)S(1)}, u32[]{:S(2)}, u32[]{:S(2)}) collective-permute-start(bf16[144,128]{1,0:T(8,128)(2,1)S(1)} %get-tuple-element.57), channel_id=1, source_target_pairs={{0,8},{4,12},{8,0},{12,4},{16,24},{20,28},{24,16},{28,20},{1,9},{5... | collective-permute-start | bytes 110600 | tf_op jit(solution)/shard_map/ppermute | solution.py:437
  14.3 3.9 %collective-permute-start.6 = (bf16[64,128]{1,0:T(8,128)(2,1)S(1)}, bf16[64,128]{1,0:T(8,128)(2,1)S(1)}, u32[]{:S(2)}, u32[]{:S(2)}) collective-permute-start(bf16[64,128]{1,0:T(8,128)(2,1)S(1)} %slice.16), channel_id=1, source_target_pairs={{0,8},{4,12},{8,0},{12,4},{16,24},{20,28},{24,16},{28,20},{1,9},{5... | collective-permute-start | bytes 49160 | tf_op jit(solution)/shard_map/ppermute | solution.py:437
  17.3 5.3 %collective-permute-start.8 = (s16[16,4352]{1,0:T(8,128)(2,1)S(1)}, s16[16,4352]{1,0:T(8,128)(2,1)S(1)}, u32[]{:S(2)}, u32[]{:S(2)}) collective-permute-start(s16[16,4352]{1,0:T(8,128)(2,1)S(1)} %get-tuple-element.74), channel_id=1, source_target_pairs={{0,2},{2,0},{1,3},{3,1},{4,6},{6,4},{5,7},{7,5},{8,10},{10,8},{9,1... | collective-permute-start | bytes 417800 | tf_op jit(solution)/shard_map/ppermute | solution.py:434
  18.3 3.8 %collective-permute-start.7 = (bf16[48,128]{1,0:T(8,128)(2,1)S(1)}, bf16[48,128]{1,0:T(8,128)(2,1)S(1)}, u32[]{:S(2)}, u32[]{:S(2)}) collective-permute-start(bf16[48,128]{1,0:T(8,128)(2,1)S(1)} %pad_maximum_fusion), channel_id=1, source_target_pairs={{0,4},{4,0},{8,12},{12,8},{16,20},{20,16},{24,28},{28,24},{1,5},{5... | collective-permute-start | bytes 36872 | tf_op jit(solution)/shard_map/ppermute | solution.py:437

commit v13 on v12

--- a/solution.py
+++ b/solution.py
@@ -222,7 +222,7 @@
         for word, blocks_ref in zip(words, (block_ref, *mate_refs)):
             panels += [buffer_ref[slot] for slot in unpacked(word, near_count, leaf)]
             blocks += [blocks_ref[leaf, block] for block in range(near_count)]
-        total = dot_nt(jnp.concatenate(panels, axis=1), jnp.concatenate(blocks, axis=1))
+        total = dot_nt(jnp.concatenate(blocks, axis=1), jnp.concatenate(panels, axis=1)).T
         lanes = slice(leaf * width, (leaf + 1) * width)
         own_ref[:, lanes] = total[:columns]
         for part, (sent_ref, power_ref) in enumerate(zip(sent_refs, power_refs), 1):

time: 23.5 us -> 23.5 us (level)
  no operation moved by 1% of the time
where the time goes in v13:
time: 23.5 us; the launch traced here: 23.4 us
  starting transfers between devices  11.3 us (48%)
  Pallas kernels  9.67 us (41%)
  waiting for transfers between devices  2.33 us (10%)
    ppermute x5, starting transfers between devices, crossed(): lax.ppermute(value, 'leaf', [(i, i ^ turn) for i in range(leaf_devices)])  6.83 us
    ppermute x4, starting transfers between devices, rotated(): lax.ppermute(value, axis, [(i, (i - shift) % count) for i in range(count)])  4.47 us
    pallas_call x1, Pallas kernels, local(): pl.pallas_call(up_kernel, out_shape=[jax.ShapeDtypeStruct(value.shape, va...  3.97 us
    ppermute x5, waiting for transfers between devices, crossed(): lax.ppermute(value, 'leaf', [(i, i ^ turn) for i in range(leaf_devices)])  2.32 us
    pallas_call x1, Pallas kernels, local(): pl.pallas_call(functools.partial(near_kernel, faces, far_groups, share),...  1.53 us
    pallas_call x1, Pallas kernels, local(): pl.pallas_call(project_kernel, out_shape=jax.ShapeDtypeStruct((columns, p...  1.31 us
    pallas_call x1, Pallas kernels, local(): pl.pallas_call(couple_kernel, out_shape=[jax.ShapeDtypeStruct((leaf_count...  0.86 us
    pallas_call x1, Pallas kernels, local(): pl.pallas_call(functools.partial(add_kernel, leaf_count), out_shape=jax.S...  0.76 us
  transfers between devices with their start and end apart: 9, of which 2 were waited for; matrix products, arithmetic and copies ran while one was open for 0% of the time, Pallas kernels for 38%

profile of v13, /device:TPU:0, one launch (start us, length us, event | category | flops | bytes accessed | tf_op | source)
XLA Modules:
  0.0 23.4 jit_solution(6493651350549861665)
XLA Ops:
  0.0 2.9 %collective-permute-start = (bf16[16,4096]{1,0:T(8,128)(2,1)}, bf16[16,4096]{1,0:T(8,128)(2,1)S(1)}, u32[]{:S(2)}, u32[]{:S(2)}) collective-permute-start(bf16[16,4096]{1,0:T(8,128)(2,1)} %refs_0_.1), channel_id=1, source_target_pairs={{0,2},{2,0},{1,3},{3,1},{4,6},{6,4},{5,7},{7,5},{8,10},{10,8},{9,1... | collective-permute-start | bytes 393224 | tf_op jit(solution)/shard_map/ppermute | solution.py:434
  2.9 0.0 collective-permute-start.1
  2.9 4.0 %up.1 = (f32[32,4096]{1,0:T(8,128)S(1)}, bf16[16,4096]{1,0:T(8,128)(2,1)S(1)}, s32[6,4,8]{2,1,0:T(4,128)S(1)}, s32[2,32]{1,0:T(2,128)S(1)}, s32[8,32]{1,0:T(8,12...) custom-call(f32[32,32,64]{2,1,0:T(8,128)} %bitcast.6, ...), custom_call_target="tpu_custom_call" | custom-call | bytes 12915000 | tf_op jit(solution)/shard_map/up/pallas_call | solution.py:448
  6.9 0.0 collective-permute-done.1.refs_1_
  6.9 0.0 collective-permute-done.refs_0_.refs_3_
  6.9 0.6 %collective-permute-start.5 = (bf16[32,2,128,128]{3,2,1,0:T(8,128)(2,1)S(1)}, bf16[32,2,128,128]{3,2,1,0:T(8,128)(2,1)S(1)}, u32[]{:S(2)}, u32[]{:S(2)}) collective-permute-start(bf16[32,2,128,128]{3,2,1,0:T(8,128)(2,1)S(1)} %get-tuple-element.58.refs_7_), channel_id=1, source_target_pairs={{0,1},{1,0},{2,3},{3,2},{4,5},{5,4},{6,7},{7,6},{8,9},{9,8},{10,11... | collective-permute-start | bytes 6291464 | tf_op jit(solution)/shard_map/ppermute | solution.py:434
  7.5 0.2 select.1
  7.7 2.7 %collective-permute-start.2 = (bf16[144,128]{1,0:T(8,128)(2,1)S(1)}, bf16[144,128]{1,0:T(8,128)(2,1)S(1)}, u32[]{:S(2)}, u32[]{:S(2)}) collective-permute-start(bf16[144,128]{1,0:T(8,128)(2,1)S(1)} %get-tuple-element.55), channel_id=1, source_target_pairs={{0,16},{4,20},{8,24},{12,28},{16,0},{20,4},{24,8},{28,12},{1,17},{... | collective-permute-start | bytes 110600 | tf_op jit(solution)/shard_map/ppermute | solution.py:437
  10.3 1.5 %collective-permute-start.3 = (bf16[144,128]{1,0:T(8,128)(2,1)S(1)}, bf16[144,128]{1,0:T(8,128)(2,1)S(1)}, u32[]{:S(2)}, u32[]{:S(2)}) collective-permute-start(bf16[144,128]{1,0:T(8,128)(2,1)S(1)} %get-tuple-element.56), channel_id=1, source_target_pairs={{0,4},{4,0},{8,12},{12,8},{16,20},{20,16},{24,28},{28,24},{1,5},{5... | collective-permute-start | bytes 110600 | tf_op jit(solution)/shard_map/ppermute | solution.py:437
  11.8 1.6 %collective-permute-start.4 = (bf16[144,128]{1,0:T(8,128)(2,1)S(1)}, bf16[144,128]{1,0:T(8,128)(2,1)S(1)}, u32[]{:S(2)}, u32[]{:S(2)}) collective-permute-start(bf16[144,128]{1,0:T(8,128)(2,1)S(1)} %get-tuple-element.57), channel_id=1, source_target_pairs={{0,8},{4,12},{8,0},{12,4},{16,24},{20,28},{24,16},{28,20},{1,9},{5... | collective-permute-start | bytes 110600 | tf_op jit(solution)/shard_map/ppermute | solution.py:437
  13.4 0.9 %couple.1 = (bf16[1024,32]{1,0:T(8,128)(2,1)S(1)}, f32[16,512]{1,0:T(8,128)S(1)}) custom-call(s32[8,32]{1,0:T(8,128)S(1)} %get-tuple-element.59.table_ref, f32[32,8,32,32]{3,2,1,0:T(8,128)S(1)} %get-tuple-element.60.coupling_ref, bf16[16,4096]{1,0:T(8,128)(2,1)S(1)} %get-tuple-element.54.dens_ref.refs_2_, f32[32,4096]{1,0:T(8,128)S(1)} %get-tuple-element.61.bases_ref), custom_call_target="tpu_custom_call" | custom-call | bytes 7380000 | tf_op jit(solution)/shard_map/couple/pallas_call | solution.py:491
  14.3 0.0 collective-permute-done.2.refs_4_.refs_1_
  14.3 0.5 %collective-permute-start.6 = (bf16[64,128]{1,0:T(8,128)(2,1)S(1)}, bf16[64,128]{1,0:T(8,128)(2,1)S(1)}, u32[]{:S(2)}, u32[]{:S(2)}) collective-permute-start(bf16[64,128]{1,0:T(8,128)(2,1)S(1)} %slice.16), channel_id=1, source_target_pairs={{0,8},{4,12},{8,0},{12,4},{16,24},{20,28},{24,16},{28,20},{1,9},{5... | collective-permute-start | bytes 49160 | tf_op jit(solution)/shard_map/ppermute | solution.py:437
  14.8 0.0 collective-permute-done.3.refs_5_.refs_2_
  14.8 1.0 %collective-permute-done.4.refs_6_.refs_3_ = bf16[144,128]{1,0:T(8,128)(2,1)S(1)} collective-permute-done((bf16[144,128]{1,0:T(8,128)(2,1)S(1)}, bf16[144,128]{1,0:T(8,128)(2,1)S(1)}, u32[]{:S(2)}, u32[]{:S(2)}) %collective-permute-start.4) | collective-permute-done | bytes 36896 | tf_op jit(solution)/shard_map/ppermute | solution.py:437
  15.8 0.0 collective-permute-done.5.refs_8_
  15.8 1.5 %near.1 = (f32[16,4096]{1,0:T(8,128)S(1)}, s16[16,4352]{1,0:T(8,128)(2,1)S(1)}) custom-call(s32[2,32]{1,0:T(2,128)S(1)} %get-tuple-element.45.refs_0_, s32[2,32]{1,0:T(2,128)S(1)} %collective-permute-done.1.refs_1_, bf16[16,4096]{1,0:T(8,128)(2,1)S(1)} %get-tuple-element.54.dens_ref.refs_2_, bf16[16,4096]{1,0:T(8,128)(2,1)S(1)} %collective-permute-done.refs_0_.refs_3_, ...), custom_call_target="tpu_custom_call" | custom-call | bytes 11070000 | tf_op jit(solution)/shard_map/near/pallas_call | solution.py:521
  17.3 1.0 %collective-permute-start.8 = (s16[16,4352]{1,0:T(8,128)(2,1)S(1)}, s16[16,4352]{1,0:T(8,128)(2,1)S(1)}, u32[]{:S(2)}, u32[]{:S(2)}) collective-permute-start(s16[16,4352]{1,0:T(8,128)(2,1)S(1)} %get-tuple-element.74), channel_id=1, source_target_pairs={{0,2},{2,0},{1,3},{3,1},{4,6},{6,4},{5,7},{7,5},{8,10},{10,8},{9,1... | collective-permute-start | bytes 417800 | tf_op jit(solution)/shard_map/ppermute | solution.py:434
  18.3 0.0 collective-permute-done.6.refs_4_
  18.3 0.6 %collective-permute-start.7 = (bf16[48,128]{1,0:T(8,128)(2,1)S(1)}, bf16[48,128]{1,0:T(8,128)(2,1)S(1)}, u32[]{:S(2)}, u32[]{:S(2)}) collective-permute-start(bf16[48,128]{1,0:T(8,128)(2,1)S(1)} %pad_maximum_fusion), channel_id=1, source_target_pairs={{0,4},{4,0},{8,12},{12,8},{16,20},{20,16},{24,28},{28,24},{1,5},{5... | collective-permute-start | bytes 36872 | tf_op jit(solution)/shard_map/ppermute | solution.py:437
  18.9 0.5 %paths.1 = (bf16[32,1024]{1,0:T(8,128)(2,1)S(1)}, bf16[32,1024]{1,0:T(8,128)(2,1)S(1)}) custom-call(f32[16,32,32]{2,1,0:T(8,128)S(1)} %get-tuple-element.65.upper_ref, f32[16,3,32,32]{3,2,1,0:T(8,128)S(1)} %get-tuple-element.66.cross_ref), custom_call_target="tpu_custom_call" | custom-call | bytes 2583000 | tf_op jit(solution)/shard_map/paths/pallas_call | solution.py:538
  19.4 1.3 %project.1.term_ref = f32[16,4096]{1,0:T(8,128)S(1)} custom-call(s32[8,32]{1,0:T(8,128)S(1)} %get-tuple-element.59.table_ref, f32[32,8,32,32]{3,2,1,0:T(8,128)S(1)} %get-tuple-element.60.coupling_ref, bf16[1024,32]{1,0:T(8,128)(2,1)S(1)} %get-tuple-element.71.turned_ref, f32[16,512]{1,0:T(8,128)S(1)} %get-tuple-element.63.refs_9_.first_ref, ...), custom_call_target="tpu_custom_call" | custom-call | bytes 5535000 | tf_op jit(solution)/shard_map/project/pallas_call | solution.py:549
  20.8 1.3 %collective-permute-done.7.refs_5_ = bf16[48,128]{1,0:T(8,128)(2,1)S(1)} collective-permute-done((bf16[48,128]{1,0:T(8,128)(2,1)S(1)}, bf16[48,128]{1,0:T(8,128)(2,1)S(1)}, u32[]{:S(2)}, u32[]{:S(2)}) %collective-permute-start.7) | collective-permute-done | bytes 12320 | tf_op jit(solution)/shard_map/ppermute | solution.py:437
  22.1 0.5 %far.1.term_ref = f32[16,4096]{1,0:T(8,128)S(1)} custom-call(bf16[32,1024]{1,0:T(8,128)(2,1)S(1)} %get-tuple-element.67.path_high_ref, bf16[32,1024]{1,0:T(8,128)(2,1)S(1)} %get-tuple-element.68.path_low_ref, bf16[32,4096]{1,0:T(8,128)(2,1)S(1)} %get-tuple-element.69.high_ref, bf16[32,4096]{1,0:T(8,128)(2,1)S(1)} %get-tuple-element.70.low_ref, ...), custom_call_target="tpu_custom_call" | custom-call | bytes 2214000 | tf_op jit(solution)/shard_map/far/pallas_call | solution.py:558
  22.6 0.0 collective-permute-done.8.refs_0_
  22.6 0.8 %add.1 = f32[16,4096]{1,0:T(8,128)} custom-call(f32[16,4096]{1,0:T(8,128)S(1)} %far.1.term_ref, s16[16,4352]{1,0:T(8,128)(2,1)S(1)} %collective-permute-done.8.refs_0_), custom_call_target="tpu_custom_call" | custom-call | bytes 1845000 | tf_op jit(solution)/shard_map/add/pallas_call | solution.py:567
  (5 shorter events, 0.0 us)
Async XLA Ops:
  0.0 6.9 %collective-permute-start = (bf16[16,4096]{1,0:T(8,128)(2,1)}, bf16[16,4096]{1,0:T(8,128)(2,1)S(1)}, u32[]{:S(2)}, u32[]{:S(2)}) collective-permute-start(bf16[16,4096]{1,0:T(8,128)(2,1)} %refs_0_.1), channel_id=1, source_target_pairs={{0,2},{2,0},{1,3},{3,1},{4,6},{6,4},{5,7},{7,5},{8,10},{10,8},{9,1... | collective-permute-start | bytes 393224 | tf_op jit(solution)/shard_map/ppermute | solution.py:434
  2.9 4.0 %collective-permute-start.1 = (s32[2,32]{1,0:T(2,128)}, s32[2,32]{1,0:T(2,128)S(1)}, u32[]{:S(2)}, u32[]{:S(2)}) collective-permute-start(s32[2,32]{1,0:T(2,128)} %bitcast.9), channel_id=1, source_target_pairs={{0,1},{1,0},{2,3},{3,2},{4,5},{5,4},{6,7},{7,6},{8,9},{9,8},{10,11... | collective-permute-start | bytes 776 | tf_op jit(solution)/shard_map/ppermute | solution.py:434
  6.9 8.9 %collective-permute-start.5 = (bf16[32,2,128,128]{3,2,1,0:T(8,128)(2,1)S(1)}, bf16[32,2,128,128]{3,2,1,0:T(8,128)(2,1)S(1)}, u32[]{:S(2)}, u32[]{:S(2)}) collective-permute-start(bf16[32,2,128,128]{3,2,1,0:T(8,128)(2,1)S(1)} %get-tuple-element.58.refs_7_), channel_id=1, source_target_pairs={{0,1},{1,0},{2,3},{3,2},{4,5},{5,4},{6,7},{7,6},{8,9},{9,8},{10,11... | collective-permute-start | bytes 6291464 | tf_op jit(solution)/shard_map/ppermute | solution.py:434
  7.7 6.6 %collective-permute-start.2 = (bf16[144,128]{1,0:T(8,128)(2,1)S(1)}, bf16[144,128]{1,0:T(8,128)(2,1)S(1)}, u32[]{:S(2)}, u32[]{:S(2)}) collective-permute-start(bf16[144,128]{1,0:T(8,128)(2,1)S(1)} %get-tuple-element.55), channel_id=1, source_target_pairs={{0,16},{4,20},{8,24},{12,28},{16,0},{20,4},{24,8},{28,12},{1,17},{... | collective-permute-start | bytes 110600 | tf_op jit(solution)/shard_map/ppermute | solution.py:437
  10.3 4.5 %collective-permute-start.3 = (bf16[144,128]{1,0:T(8,128)(2,1)S(1)}, bf16[144,128]{1,0:T(8,128)(2,1)S(1)}, u32[]{:S(2)}, u32[]{:S(2)}) collective-permute-start(bf16[144,128]{1,0:T(8,128)(2,1)S(1)} %get-tuple-element.56), channel_id=1, source_target_pairs={{0,4},{4,0},{8,12},{12,8},{16,20},{20,16},{24,28},{28,24},{1,5},{5... | collective-permute-start | bytes 110600 | tf_op jit(solution)/shard_map/ppermute | solution.py:437
  11.8 4.0 %collective-permute-start.4 = (bf16[144,128]{1,0:T(8,128)(2,1)S(1)}, bf16[144,128]{1,0:T(8,128)(2,1)S(1)}, u32[]{:S(2)}, u32[]{:S(2)}) collective-permute-start(bf16[144,128]{1,0:T(8,128)(2,1)S(1)} %get-tuple-element.57), channel_id=1, source_target_pairs={{0,8},{4,12},{8,0},{12,4},{16,24},{20,28},{24,16},{28,20},{1,9},{5... | collective-permute-start | bytes 110600 | tf_op jit(solution)/shard_map/ppermute | solution.py:437
  14.3 4.0 %collective-permute-start.6 = (bf16[64,128]{1,0:T(8,128)(2,1)S(1)}, bf16[64,128]{1,0:T(8,128)(2,1)S(1)}, u32[]{:S(2)}, u32[]{:S(2)}) collective-permute-start(bf16[64,128]{1,0:T(8,128)(2,1)S(1)} %slice.16), channel_id=1, source_target_pairs={{0,8},{4,12},{8,0},{12,4},{16,24},{20,28},{24,16},{28,20},{1,9},{5... | collective-permute-start | bytes 49160 | tf_op jit(solution)/shard_map/ppermute | solution.py:437
  17.3 5.3 %collective-permute-start.8 = (s16[16,4352]{1,0:T(8,128)(2,1)S(1)}, s16[16,4352]{1,0:T(8,128)(2,1)S(1)}, u32[]{:S(2)}, u32[]{:S(2)}) collective-permute-start(s16[16,4352]{1,0:T(8,128)(2,1)S(1)} %get-tuple-element.74), channel_id=1, source_target_pairs={{0,2},{2,0},{1,3},{3,1},{4,6},{6,4},{5,7},{7,5},{8,10},{10,8},{9,1... | collective-permute-start | bytes 417800 | tf_op jit(solution)/shard_map/ppermute | solution.py:434
  18.3 3.8 %collective-permute-start.7 = (bf16[48,128]{1,0:T(8,128)(2,1)S(1)}, bf16[48,128]{1,0:T(8,128)(2,1)S(1)}, u32[]{:S(2)}, u32[]{:S(2)}) collective-permute-start(bf16[48,128]{1,0:T(8,128)(2,1)S(1)} %pad_maximum_fusion), channel_id=1, source_target_pairs={{0,4},{4,0},{8,12},{12,8},{16,20},{20,16},{24,28},{28,24},{1,5},{5... | collective-permute-start | bytes 36872 | tf_op jit(solution)/shard_map/ppermute | solution.py:437

commit v14 on v12

--- a/solution.py
+++ b/solution.py
@@ -200,9 +200,10 @@
     refs = refs[1:]
     out_refs, refs = refs[:far_groups], refs[far_groups:]
     power_refs, refs = refs[: far_groups - 1], refs[far_groups - 1 :]
-    (buffer_ref,) = refs
+    smem_refs, (buffer_ref, sems) = refs[:share], refs[share:]
     columns, points = dens_ref.shape
     leaf_count, near_count, width, _ = block_ref.shape
+    copies = fetch([(source_ref, smem) for source_ref, smem in zip(source_refs, smem_refs)], sems)
     cap = (buffer_ref.shape[0] - leaf_count) // len(FACE_SIGNS)
     for (directions, _), got_ref in zip(faces, got_refs):
         for direction in directions:
@@ -215,13 +216,23 @@
         rows = slice(part * columns, (part + 1) * columns)
         for leaf in range(leaf_count):
             buffer_ref[leaf, rows, :] = panel_ref[:, leaf * width : (leaf + 1) * width]
-    words = [packed_words(source_ref[...]) for source_ref in source_refs]
+    words = packed_words(jnp.concatenate([source_ref[...] for source_ref in source_refs], axis=0))
+    early = 3 * leaf_count // 8
     own_ref, sent_refs = out_refs[0], out_refs[1:]
     for leaf in range(leaf_count):
-        panels, blocks = [], []
-        for word, blocks_ref in zip(words, (block_ref, *mate_refs)):
-            panels += [buffer_ref[slot] for slot in unpacked(word, near_count, leaf)]
-            blocks += [blocks_ref[leaf, block] for block in range(near_count)]
+        if leaf < early:
+            slots = unpacked(words, near_count * share, leaf)
+        else:
+            if leaf == early:
+                for copy in copies:
+                    copy.wait()
+            slots = [smem[block, leaf] for smem in smem_refs for block in range(near_count)]
+        panels = [buffer_ref[slot] for slot in slots]
+        blocks = [
+            blocks_ref[leaf, block]
+            for blocks_ref in (block_ref, *mate_refs)
+            for block in range(near_count)
+        ]
         total = dot_nt(jnp.concatenate(panels, axis=1), jnp.concatenate(blocks, axis=1))
         lanes = slice(leaf * width, (leaf + 1) * width)
         own_ref[:, lanes] = total[:columns]
@@ -525,9 +536,8 @@
         in_specs=[VMEM] * (2 * share + far_groups + len(faces) + 1),
         out_specs=[VMEM] * far_groups,
         scratch_shapes=[pltpu.VMEM((leaf_count, width), F32)] * (far_groups - 1)
-        + [
-            pltpu.VMEM((slots, far_groups * columns, width), BF16),
-        ],
+        + [pltpu.SMEM(sources.shape, jnp.int32)] * share
+        + [pltpu.VMEM((slots, far_groups * columns, width), BF16), dma((share,))],
         compiler_params=params,
         cost_estimate=hint(3),
         name="near",

time: 23.5 us -> 24.2 us (1.030)
  Pallas kernels: 9.62 us -> 10.3 us
    pallas_call x1, Pallas kernels: 1.46 us -> 2.16 us  [local(): pl.pallas_call(functools.partial(near_kernel, faces, far_groups, share),...]
  transfers between devices with their start and end apart: 9 -> 9, of which waited for: 2 -> 2; matrix products, arithmetic and copies ran while one was open for 0% -> 0% of each run, Pallas kernels for 38% -> 40%
where the time goes in v14:
time: 24.2 us; the launch traced here: 24 us
  starting transfers between devices  11.3 us (47%)
  Pallas kernels  10.3 us (43%)
  waiting for transfers between devices  2.33 us (10%)
    ppermute x5, starting transfers between devices, crossed(): lax.ppermute(value, 'leaf', [(i, i ^ turn) for i in range(leaf_devices)])  6.81 us
    ppermute x4, starting transfers between devices, rotated(): lax.ppermute(value, axis, [(i, (i - shift) % count) for i in range(count)])  4.46 us
    pallas_call x1, Pallas kernels, local(): pl.pallas_call(up_kernel, out_shape=[jax.ShapeDtypeStruct(value.shape, va...  3.97 us
    ppermute x5, waiting for transfers between devices, crossed(): lax.ppermute(value, 'leaf', [(i, i ^ turn) for i in range(leaf_devices)])  2.32 us
    pallas_call x1, Pallas kernels, local(): pl.pallas_call(functools.partial(near_kernel, faces, far_groups, share),...  2.16 us
    pallas_call x1, Pallas kernels, local(): pl.pallas_call(project_kernel, out_shape=jax.ShapeDtypeStruct((columns, p...  1.31 us
    pallas_call x1, Pallas kernels, local(): pl.pallas_call(couple_kernel, out_shape=[jax.ShapeDtypeStruct((leaf_count...  0.88 us
    pallas_call x1, Pallas kernels, local(): pl.pallas_call(functools.partial(add_kernel, leaf_count), out_shape=jax.S...  0.76 us
  transfers between devices with their start and end apart: 9, of which 2 were waited for; matrix products, arithmetic and copies ran while one was open for 0% of the time, Pallas kernels for 40%

profile of v14, /device:TPU:0, one launch (start us, length us, event | category | flops | bytes accessed | tf_op | source)
XLA Modules:
  0.0 24.0 jit_solution(14083427041232344363)
XLA Ops:
  0.0 2.9 %collective-permute-start = (bf16[16,4096]{1,0:T(8,128)(2,1)}, bf16[16,4096]{1,0:T(8,128)(2,1)S(1)}, u32[]{:S(2)}, u32[]{:S(2)}) collective-permute-start(bf16[16,4096]{1,0:T(8,128)(2,1)} %refs_0_.1), channel_id=1, source_target_pairs={{0,2},{2,0},{1,3},{3,1},{4,6},{6,4},{5,7},{7,5},{8,10},{10,8},{9,1... | collective-permute-start | bytes 393224 | tf_op jit(solution)/shard_map/ppermute | solution.py:445
  2.9 0.0 collective-permute-start.1
  2.9 4.0 %up.1 = (f32[32,4096]{1,0:T(8,128)S(1)}, bf16[16,4096]{1,0:T(8,128)(2,1)S(1)}, s32[6,4,8]{2,1,0:T(4,128)S(1)}, s32[2,32]{1,0:T(2,128)S(1)}, s32[8,32]{1,0:T(8,12...) custom-call(f32[32,32,64]{2,1,0:T(8,128)} %bitcast.6, ...), custom_call_target="tpu_custom_call" | custom-call | bytes 12915000 | tf_op jit(solution)/shard_map/up/pallas_call | solution.py:459
  6.9 0.0 collective-permute-done.1.refs_1_
  6.9 0.0 collective-permute-done.refs_0_.refs_3_
  6.9 0.6 %collective-permute-start.5 = (bf16[32,2,128,128]{3,2,1,0:T(8,128)(2,1)S(1)}, bf16[32,2,128,128]{3,2,1,0:T(8,128)(2,1)S(1)}, u32[]{:S(2)}, u32[]{:S(2)}) collective-permute-start(bf16[32,2,128,128]{3,2,1,0:T(8,128)(2,1)S(1)} %get-tuple-element.58.refs_7_), channel_id=1, source_target_pairs={{0,1},{1,0},{2,3},{3,2},{4,5},{5,4},{6,7},{7,6},{8,9},{9,8},{10,11... | collective-permute-start | bytes 6291464 | tf_op jit(solution)/shard_map/ppermute | solution.py:445
  7.5 0.2 select.1
  7.7 2.7 %collective-permute-start.2 = (bf16[144,128]{1,0:T(8,128)(2,1)S(1)}, bf16[144,128]{1,0:T(8,128)(2,1)S(1)}, u32[]{:S(2)}, u32[]{:S(2)}) collective-permute-start(bf16[144,128]{1,0:T(8,128)(2,1)S(1)} %get-tuple-element.55), channel_id=1, source_target_pairs={{0,16},{4,20},{8,24},{12,28},{16,0},{20,4},{24,8},{28,12},{1,17},{... | collective-permute-start | bytes 110600 | tf_op jit(solution)/shard_map/ppermute | solution.py:448
  10.3 1.5 %collective-permute-start.3 = (bf16[144,128]{1,0:T(8,128)(2,1)S(1)}, bf16[144,128]{1,0:T(8,128)(2,1)S(1)}, u32[]{:S(2)}, u32[]{:S(2)}) collective-permute-start(bf16[144,128]{1,0:T(8,128)(2,1)S(1)} %get-tuple-element.56), channel_id=1, source_target_pairs={{0,4},{4,0},{8,12},{12,8},{16,20},{20,16},{24,28},{28,24},{1,5},{5... | collective-permute-start | bytes 110600 | tf_op jit(solution)/shard_map/ppermute | solution.py:448
  11.8 1.6 %collective-permute-start.4 = (bf16[144,128]{1,0:T(8,128)(2,1)S(1)}, bf16[144,128]{1,0:T(8,128)(2,1)S(1)}, u32[]{:S(2)}, u32[]{:S(2)}) collective-permute-start(bf16[144,128]{1,0:T(8,128)(2,1)S(1)} %get-tuple-element.57), channel_id=1, source_target_pairs={{0,8},{4,12},{8,0},{12,4},{16,24},{20,28},{24,16},{28,20},{1,9},{5... | collective-permute-start | bytes 110600 | tf_op jit(solution)/shard_map/ppermute | solution.py:448
  13.4 0.9 %couple.1 = (bf16[1024,32]{1,0:T(8,128)(2,1)S(1)}, f32[16,512]{1,0:T(8,128)S(1)}) custom-call(s32[8,32]{1,0:T(8,128)S(1)} %get-tuple-element.59.table_ref, f32[32,8,32,32]{3,2,1,0:T(8,128)S(1)} %get-tuple-element.60.coupling_ref, bf16[16,4096]{1,0:T(8,128)(2,1)S(1)} %get-tuple-element.54.dens_ref.refs_2_, f32[32,4096]{1,0:T(8,128)S(1)} %get-tuple-element.61.bases_ref), custom_call_target="tpu_custom_call" | custom-call | bytes 7380000 | tf_op jit(solution)/shard_map/couple/pallas_call | solution.py:502
  14.3 0.0 collective-permute-done.2.refs_4_.refs_1_
  14.3 0.5 %collective-permute-start.6 = (bf16[64,128]{1,0:T(8,128)(2,1)S(1)}, bf16[64,128]{1,0:T(8,128)(2,1)S(1)}, u32[]{:S(2)}, u32[]{:S(2)}) collective-permute-start(bf16[64,128]{1,0:T(8,128)(2,1)S(1)} %slice.16), channel_id=1, source_target_pairs={{0,8},{4,12},{8,0},{12,4},{16,24},{20,28},{24,16},{28,20},{1,9},{5... | collective-permute-start | bytes 49160 | tf_op jit(solution)/shard_map/ppermute | solution.py:448
  14.8 0.0 collective-permute-done.3.refs_5_.refs_2_
  14.8 1.0 %collective-permute-done.4.refs_6_.refs_3_ = bf16[144,128]{1,0:T(8,128)(2,1)S(1)} collective-permute-done((bf16[144,128]{1,0:T(8,128)(2,1)S(1)}, bf16[144,128]{1,0:T(8,128)(2,1)S(1)}, u32[]{:S(2)}, u32[]{:S(2)}) %collective-permute-start.4) | collective-permute-done | bytes 36896 | tf_op jit(solution)/shard_map/ppermute | solution.py:448
  15.8 0.0 collective-permute-done.5.refs_8_
  15.8 2.2 %near.1 = (f32[16,4096]{1,0:T(8,128)S(1)}, s16[16,4352]{1,0:T(8,128)(2,1)S(1)}) custom-call(s32[2,32]{1,0:T(2,128)S(1)} %get-tuple-element.45.refs_0_, s32[2,32]{1,0:T(2,128)S(1)} %collective-permute-done.1.refs_1_, bf16[16,4096]{1,0:T(8,128)(2,1)S(1)} %get-tuple-element.54.dens_ref.refs_2_, bf16[16,4096]{1,0:T(8,128)(2,1)S(1)} %collective-permute-done.refs_0_.refs_3_, ...), custom_call_target="tpu_custom_call" | custom-call | bytes 11070000 | tf_op jit(solution)/shard_map/near/pallas_call | solution.py:532
  18.0 0.9 %collective-permute-start.8 = (s16[16,4352]{1,0:T(8,128)(2,1)S(1)}, s16[16,4352]{1,0:T(8,128)(2,1)S(1)}, u32[]{:S(2)}, u32[]{:S(2)}) collective-permute-start(s16[16,4352]{1,0:T(8,128)(2,1)S(1)} %get-tuple-element.74), channel_id=1, source_target_pairs={{0,2},{2,0},{1,3},{3,1},{4,6},{6,4},{5,7},{7,5},{8,10},{10,8},{9,1... | collective-permute-start | bytes 417800 | tf_op jit(solution)/shard_map/ppermute | solution.py:445
  18.9 0.0 collective-permute-done.6.refs_4_
  19.0 0.6 %collective-permute-start.7 = (bf16[48,128]{1,0:T(8,128)(2,1)S(1)}, bf16[48,128]{1,0:T(8,128)(2,1)S(1)}, u32[]{:S(2)}, u32[]{:S(2)}) collective-permute-start(bf16[48,128]{1,0:T(8,128)(2,1)S(1)} %pad_maximum_fusion), channel_id=1, source_target_pairs={{0,4},{4,0},{8,12},{12,8},{16,20},{20,16},{24,28},{28,24},{1,5},{5... | collective-permute-start | bytes 36872 | tf_op jit(solution)/shard_map/ppermute | solution.py:448
  19.5 0.5 %paths.1 = (bf16[32,1024]{1,0:T(8,128)(2,1)S(1)}, bf16[32,1024]{1,0:T(8,128)(2,1)S(1)}) custom-call(f32[16,32,32]{2,1,0:T(8,128)S(1)} %get-tuple-element.65.upper_ref, f32[16,3,32,32]{3,2,1,0:T(8,128)S(1)} %get-tuple-element.66.cross_ref), custom_call_target="tpu_custom_call" | custom-call | bytes 2583000 | tf_op jit(solution)/shard_map/paths/pallas_call | solution.py:548
  20.1 1.3 %project.1.term_ref = f32[16,4096]{1,0:T(8,128)S(1)} custom-call(s32[8,32]{1,0:T(8,128)S(1)} %get-tuple-element.59.table_ref, f32[32,8,32,32]{3,2,1,0:T(8,128)S(1)} %get-tuple-element.60.coupling_ref, bf16[1024,32]{1,0:T(8,128)(2,1)S(1)} %get-tuple-element.71.turned_ref, f32[16,512]{1,0:T(8,128)S(1)} %get-tuple-element.63.refs_9_.first_ref, ...), custom_call_target="tpu_custom_call" | custom-call | bytes 5535000 | tf_op jit(solution)/shard_map/project/pallas_call | solution.py:559
  21.4 1.3 %collective-permute-done.7.refs_5_ = bf16[48,128]{1,0:T(8,128)(2,1)S(1)} collective-permute-done((bf16[48,128]{1,0:T(8,128)(2,1)S(1)}, bf16[48,128]{1,0:T(8,128)(2,1)S(1)}, u32[]{:S(2)}, u32[]{:S(2)}) %collective-permute-start.7) | collective-permute-done | bytes 12320 | tf_op jit(solution)/shard_map/ppermute | solution.py:448
  22.7 0.5 %far.1.term_ref = f32[16,4096]{1,0:T(8,128)S(1)} custom-call(bf16[32,1024]{1,0:T(8,128)(2,1)S(1)} %get-tuple-element.67.path_high_ref, bf16[32,1024]{1,0:T(8,128)(2,1)S(1)} %get-tuple-element.68.path_low_ref, bf16[32,4096]{1,0:T(8,128)(2,1)S(1)} %get-tuple-element.69.high_ref, bf16[32,4096]{1,0:T(8,128)(2,1)S(1)} %get-tuple-element.70.low_ref, ...), custom_call_target="tpu_custom_call" | custom-call | bytes 2214000 | tf_op jit(solution)/shard_map/far/pallas_call | solution.py:568
  23.3 0.0 collective-permute-done.8.refs_0_
  23.3 0.8 %add.1 = f32[16,4096]{1,0:T(8,128)} custom-call(f32[16,4096]{1,0:T(8,128)S(1)} %far.1.term_ref, s16[16,4352]{1,0:T(8,128)(2,1)S(1)} %collective-permute-done.8.refs_0_), custom_call_target="tpu_custom_call" | custom-call | bytes 1845000 | tf_op jit(solution)/shard_map/add/pallas_call | solution.py:577
  (5 shorter events, 0.0 us)
Async XLA Ops:
  0.0 6.9 %collective-permute-start = (bf16[16,4096]{1,0:T(8,128)(2,1)}, bf16[16,4096]{1,0:T(8,128)(2,1)S(1)}, u32[]{:S(2)}, u32[]{:S(2)}) collective-permute-start(bf16[16,4096]{1,0:T(8,128)(2,1)} %refs_0_.1), channel_id=1, source_target_pairs={{0,2},{2,0},{1,3},{3,1},{4,6},{6,4},{5,7},{7,5},{8,10},{10,8},{9,1... | collective-permute-start | bytes 393224 | tf_op jit(solution)/shard_map/ppermute | solution.py:445
  2.9 4.0 %collective-permute-start.1 = (s32[2,32]{1,0:T(2,128)}, s32[2,32]{1,0:T(2,128)S(1)}, u32[]{:S(2)}, u32[]{:S(2)}) collective-permute-start(s32[2,32]{1,0:T(2,128)} %bitcast.9), channel_id=1, source_target_pairs={{0,1},{1,0},{2,3},{3,2},{4,5},{5,4},{6,7},{7,6},{8,9},{9,8},{10,11... | collective-permute-start | bytes 776 | tf_op jit(solution)/shard_map/ppermute | solution.py:445
  6.9 8.9 %collective-permute-start.5 = (bf16[32,2,128,128]{3,2,1,0:T(8,128)(2,1)S(1)}, bf16[32,2,128,128]{3,2,1,0:T(8,128)(2,1)S(1)}, u32[]{:S(2)}, u32[]{:S(2)}) collective-permute-start(bf16[32,2,128,128]{3,2,1,0:T(8,128)(2,1)S(1)} %get-tuple-element.58.refs_7_), channel_id=1, source_target_pairs={{0,1},{1,0},{2,3},{3,2},{4,5},{5,4},{6,7},{7,6},{8,9},{9,8},{10,11... | collective-permute-start | bytes 6291464 | tf_op jit(solution)/shard_map/ppermute | solution.py:445
  7.7 6.6 %collective-permute-start.2 = (bf16[144,128]{1,0:T(8,128)(2,1)S(1)}, bf16[144,128]{1,0:T(8,128)(2,1)S(1)}, u32[]{:S(2)}, u32[]{:S(2)}) collective-permute-start(bf16[144,128]{1,0:T(8,128)(2,1)S(1)} %get-tuple-element.55), channel_id=1, source_target_pairs={{0,16},{4,20},{8,24},{12,28},{16,0},{20,4},{24,8},{28,12},{1,17},{... | collective-permute-start | bytes 110600 | tf_op jit(solution)/shard_map/ppermute | solution.py:448
  10.3 4.5 %collective-permute-start.3 = (bf16[144,128]{1,0:T(8,128)(2,1)S(1)}, bf16[144,128]{1,0:T(8,128)(2,1)S(1)}, u32[]{:S(2)}, u32[]{:S(2)}) collective-permute-start(bf16[144,128]{1,0:T(8,128)(2,1)S(1)} %get-tuple-element.56), channel_id=1, source_target_pairs={{0,4},{4,0},{8,12},{12,8},{16,20},{20,16},{24,28},{28,24},{1,5},{5... | collective-permute-start | bytes 110600 | tf_op jit(solution)/shard_map/ppermute | solution.py:448
  11.8 4.0 %collective-permute-start.4 = (bf16[144,128]{1,0:T(8,128)(2,1)S(1)}, bf16[144,128]{1,0:T(8,128)(2,1)S(1)}, u32[]{:S(2)}, u32[]{:S(2)}) collective-permute-start(bf16[144,128]{1,0:T(8,128)(2,1)S(1)} %get-tuple-element.57), channel_id=1, source_target_pairs={{0,8},{4,12},{8,0},{12,4},{16,24},{20,28},{24,16},{28,20},{1,9},{5... | collective-permute-start | bytes 110600 | tf_op jit(solution)/shard_map/ppermute | solution.py:448
  14.3 4.6 %collective-permute-start.6 = (bf16[64,128]{1,0:T(8,128)(2,1)S(1)}, bf16[64,128]{1,0:T(8,128)(2,1)S(1)}, u32[]{:S(2)}, u32[]{:S(2)}) collective-permute-start(bf16[64,128]{1,0:T(8,128)(2,1)S(1)} %slice.16), channel_id=1, source_target_pairs={{0,8},{4,12},{8,0},{12,4},{16,24},{20,28},{24,16},{28,20},{1,9},{5... | collective-permute-start | bytes 49160 | tf_op jit(solution)/shard_map/ppermute | solution.py:448
  18.0 5.3 %collective-permute-start.8 = (s16[16,4352]{1,0:T(8,128)(2,1)S(1)}, s16[16,4352]{1,0:T(8,128)(2,1)S(1)}, u32[]{:S(2)}, u32[]{:S(2)}) collective-permute-start(s16[16,4352]{1,0:T(8,128)(2,1)S(1)} %get-tuple-element.74), channel_id=1, source_target_pairs={{0,2},{2,0},{1,3},{3,1},{4,6},{6,4},{5,7},{7,5},{8,10},{10,8},{9,1... | collective-permute-start | bytes 417800 | tf_op jit(solution)/shard_map/ppermute | solution.py:445
  19.0 3.8 %collective-permute-start.7 = (bf16[48,128]{1,0:T(8,128)(2,1)S(1)}, bf16[48,128]{1,0:T(8,128)(2,1)S(1)}, u32[]{:S(2)}, u32[]{:S(2)}) collective-permute-start(bf16[48,128]{1,0:T(8,128)(2,1)S(1)} %pad_maximum_fusion), channel_id=1, source_target_pairs={{0,4},{4,0},{8,12},{12,8},{16,20},{20,16},{24,28},{28,24},{1,5},{5... | collective-permute-start | bytes 36872 | tf_op jit(solution)/shard_map/ppermute | solution.py:448

commit v15 on v12

--- a/solution.py
+++ b/solution.py
@@ -92,9 +92,9 @@
 def up_kernel(
     maps_hbm, bases_hbm, *refs,
 ):
-    count = (len(refs) - 8) // 2
+    count = (len(refs) - 7) // 2
     hbm_refs, bases_ref, vmem_refs = refs[:count], refs[count], refs[count + 1 : 2 * count + 1]
-    high_ref, low_ref, root_ref, maps_ref, spread_ref, chain_ref, sems = refs[2 * count + 1 :]
+    halves_ref, root_ref, maps_ref, spread_ref, chain_ref, sems = refs[2 * count + 1 :]
     dens_ref = vmem_refs[0]
     copies = fetch(
         [(maps_hbm, maps_ref), (bases_hbm, bases_ref), *zip(hbm_refs, vmem_refs)], sems
@@ -150,8 +150,8 @@
             spread_bases(high, group), spread_bases(low, group),
         )
         high, low = halves(basis)
-        high_ref[:, spots] = high
-        low_ref[:, spots] = low
+        halves_ref[:rank, spots] = high
+        halves_ref[rank:, spots] = low
         dens = dens_ref[:, spots]
         root += dot_nt(dens, high) + dot_nt(dens, low)
     root = jnp.concatenate([root, jnp.zeros((columns, LANES - rank), F32)], axis=1)
@@ -215,13 +215,15 @@
         rows = slice(part * columns, (part + 1) * columns)
         for leaf in range(leaf_count):
             buffer_ref[leaf, rows, :] = panel_ref[:, leaf * width : (leaf + 1) * width]
-    words = [packed_words(source_ref[...]) for source_ref in source_refs]
+    words = packed_words(jnp.concatenate([source_ref[...] for source_ref in source_refs], axis=0))
     own_ref, sent_refs = out_refs[0], out_refs[1:]
     for leaf in range(leaf_count):
-        panels, blocks = [], []
-        for word, blocks_ref in zip(words, (block_ref, *mate_refs)):
-            panels += [buffer_ref[slot] for slot in unpacked(word, near_count, leaf)]
-            blocks += [blocks_ref[leaf, block] for block in range(near_count)]
+        panels = [buffer_ref[slot] for slot in unpacked(words, near_count * share, leaf)]
+        blocks = [
+            blocks_ref[leaf, block]
+            for blocks_ref in (block_ref, *mate_refs)
+            for block in range(near_count)
+        ]
         total = dot_nt(jnp.concatenate(panels, axis=1), jnp.concatenate(blocks, axis=1))
         lanes = slice(leaf * width, (leaf + 1) * width)
         own_ref[:, lanes] = total[:columns]
@@ -347,7 +349,7 @@
 
 
 def far_kernel(
-    tiles, path_high_ref, path_low_ref, high_ref, low_ref, term_ref, *refs,
+    tiles, path_high_ref, path_low_ref, halves_ref, term_ref, *refs,
 ):
     root_refs, out_ref = refs[:-1], refs[-1]
     columns, points = out_ref.shape
@@ -356,12 +358,13 @@
         pieces += [root_ref[row : row + columns, :] for row in rows]
     roots = jnp.concatenate(pieces, axis=1)
     field = dot_nt(roots, path_high_ref[...]) + dot_nt(roots, path_low_ref[...])
+    rows = jnp.concatenate(halves(field), axis=0)
+    rows = jnp.concatenate([rows, rows], axis=1)
     step = 4 * LANES
     for first in range(0, points, step):
         spots = slice(first, first + step)
-        out_ref[:, spots] = term_ref[:, spots] + split_dot(
-            dot_nn, field, high_ref[:, spots], low_ref[:, spots]
-        )
+        out = dot_nn(rows, halves_ref[:, spots])
+        out_ref[:, spots] = term_ref[:, spots] + (out[:columns] + out[columns:])
 
 
 def add_kernel(leaf_count, term_ref, *refs):
@@ -444,17 +447,16 @@
         densities, send, sources, far_src.T, upper_transfer, up_coupling, leaf_coupling, near_blocks,
     ]
     (
-        basis, dens, send, sources, far_table, upper, cross, coupling, blocks, high, low, root,
+        basis, dens, send, sources, far_table, upper, cross, coupling, blocks, subtree, root,
     ) = pl.pallas_call(
         up_kernel,
         out_shape=[jax.ShapeDtypeStruct(value.shape, value.dtype) for value in (bases, *moved)]
         + [
-            jax.ShapeDtypeStruct((rank, points), BF16),
-            jax.ShapeDtypeStruct((rank, points), BF16),
+            jax.ShapeDtypeStruct((2 * rank, points), BF16),
             jax.ShapeDtypeStruct((columns, LANES), BF16),
         ],
         in_specs=[HBM] * (2 + len(moved)),
-        out_specs=[VMEM] * (4 + len(moved)),
+        out_specs=[VMEM] * (3 + len(moved)),
         scratch_shapes=[
             pltpu.VMEM((rank, rank, node_count), F32),
             pltpu.VMEM((node_count * rank, LANES), F32),
@@ -473,7 +475,7 @@
     mate_blocks = [rotated(later_blocks, "mate", part) for part in range(1, share)]
 
     if side == 2:
-        faces = [((2 * axis, 2 * axis + 1), 2**axis) for axis in (2, 0, 1)]
+        faces = [((2 * axis, 2 * axis + 1), 2**axis) for axis in (2, 1, 0)]
     else:
         faces = [((direction,), offset) for direction, offset in enumerate(offsets)]
     chunk = (cap * far_groups + 1) * columns
@@ -503,7 +505,7 @@
     tail = cap * far_groups * columns
     if side == 2:
         arrived = [crossed(value, stride) for (_, stride), value in zip(faces, outgoing)]
-        far_one, _, near_two = (value[tail : tail + columns] for value in arrived)
+        far_one, near_two, _ = (value[tail : tail + columns] for value in arrived)
         later, leaf_local = lax.optimization_barrier((arrived[0][-4 * columns :], leaf_local))
         across = crossed(later, 2)
         held = jnp.concatenate([near_two, far_one, across[-columns:]], axis=0)
@@ -558,12 +560,12 @@
     total = pl.pallas_call(
         functools.partial(far_kernel, [rows for rows, _ in roots]),
         out_shape=jax.ShapeDtypeStruct((columns, points), F32),
-        in_specs=[VMEM] * (5 + len(roots)),
+        in_specs=[VMEM] * (4 + len(roots)),
         out_specs=VMEM,
         compiler_params=params,
         cost_estimate=hint(0.6),
         name="far",
-    )(*paths, high, low, partial, *[value for _, value in roots])
+    )(*paths, subtree, partial, *[value for _, value in roots])
     return pl.pallas_call(
         functools.partial(add_kernel, leaf_count),
         out_shape=jax.ShapeDtypeStruct((columns, points), F32),

time: 23.5 us -> 23.5 us (level)
  starting transfers between devices: 11.3 us -> 12.3 us
  waiting for transfers between devices: 2.32 us -> 1.4 us
    ppermute x5, starting transfers between devices: 6.83 us -> 7.84 us  [crossed(): lax.ppermute(value, 'leaf', [(i, i ^ turn) for i in range(leaf_devices)])]
    ppermute x5, waiting for transfers between devices: 2.31 us -> 1.39 us  [crossed(): lax.ppermute(value, 'leaf', [(i, i ^ turn) for i in range(leaf_devices)])]
where the time goes in v15:
time: 23.5 us; the launch traced here: 23.4 us
  starting transfers between devices  12.3 us (52%)
  Pallas kernels  9.57 us (41%)
  waiting for transfers between devices  1.4 us (6%)
    ppermute x5, starting transfers between devices, crossed(): lax.ppermute(value, 'leaf', [(i, i ^ turn) for i in range(leaf_devices)])  7.84 us
    ppermute x4, starting transfers between devices, rotated(): lax.ppermute(value, axis, [(i, (i - shift) % count) for i in range(count)])  4.47 us
    pallas_call x1, Pallas kernels, local(): pl.pallas_call(up_kernel, out_shape=[jax.ShapeDtypeStruct(value.shape, va...  3.97 us
    pallas_call x1, Pallas kernels, local(): pl.pallas_call(functools.partial(near_kernel, faces, far_groups, share),...  1.49 us
    ppermute x5, waiting for transfers between devices, crossed(): lax.ppermute(value, 'leaf', [(i, i ^ turn) for i in range(leaf_devices)])  1.39 us
    pallas_call x1, Pallas kernels, local(): pl.pallas_call(project_kernel, out_shape=jax.ShapeDtypeStruct((columns, p...  1.3 us
    pallas_call x1, Pallas kernels, local(): pl.pallas_call(couple_kernel, out_shape=[jax.ShapeDtypeStruct((leaf_count...  0.85 us
    pallas_call x1, Pallas kernels, local(): pl.pallas_call(functools.partial(add_kernel, leaf_count), out_shape=jax.S...  0.75 us
  transfers between devices with their start and end apart: 9, of which 2 were waited for; matrix products, arithmetic and copies ran while one was open for 0% of the time, Pallas kernels for 38%

profile of v15, /device:TPU:0, one launch (start us, length us, event | category | flops | bytes accessed | tf_op | source)
XLA Modules:
  0.0 23.4 jit_solution(12651407380975638317)
XLA Ops:
  0.0 2.9 %collective-permute-start = (bf16[16,4096]{1,0:T(8,128)(2,1)}, bf16[16,4096]{1,0:T(8,128)(2,1)S(1)}, u32[]{:S(2)}, u32[]{:S(2)}) collective-permute-start(bf16[16,4096]{1,0:T(8,128)(2,1)} %refs_0_.1), channel_id=1, source_target_pairs={{0,2},{2,0},{1,3},{3,1},{4,6},{6,4},{5,7},{7,5},{8,10},{10,8},{9,1... | collective-permute-start | bytes 393224 | tf_op jit(solution)/shard_map/ppermute | solution.py:437
  2.9 0.0 collective-permute-start.1
  2.9 4.0 %up.1 = (f32[32,4096]{1,0:T(8,128)S(1)}, bf16[16,4096]{1,0:T(8,128)(2,1)S(1)}, s32[6,4,8]{2,1,0:T(4,128)S(1)}, s32[2,32]{1,0:T(2,128)S(1)}, s32[8,32]{1,0:T(8,12...) custom-call(f32[32,32,64]{2,1,0:T(8,128)} %bitcast.6, ...), custom_call_target="tpu_custom_call" | custom-call | bytes 12915000 | tf_op jit(solution)/shard_map/up/pallas_call | solution.py:451
  6.9 0.0 collective-permute-done.1.refs_1_
  6.9 0.0 collective-permute-done.refs_0_.refs_3_
  6.9 0.6 %collective-permute-start.5 = (bf16[32,2,128,128]{3,2,1,0:T(8,128)(2,1)S(1)}, bf16[32,2,128,128]{3,2,1,0:T(8,128)(2,1)S(1)}, u32[]{:S(2)}, u32[]{:S(2)}) collective-permute-start(bf16[32,2,128,128]{3,2,1,0:T(8,128)(2,1)S(1)} %get-tuple-element.57.refs_7_), channel_id=1, source_target_pairs={{0,1},{1,0},{2,3},{3,2},{4,5},{5,4},{6,7},{7,6},{8,9},{9,8},{10,11... | collective-permute-start | bytes 6291464 | tf_op jit(solution)/shard_map/ppermute | solution.py:437
  7.5 0.2 select.1
  7.7 2.7 %collective-permute-start.2 = (bf16[144,128]{1,0:T(8,128)(2,1)S(1)}, bf16[144,128]{1,0:T(8,128)(2,1)S(1)}, u32[]{:S(2)}, u32[]{:S(2)}) collective-permute-start(bf16[144,128]{1,0:T(8,128)(2,1)S(1)} %get-tuple-element.54), channel_id=1, source_target_pairs={{0,16},{4,20},{8,24},{12,28},{16,0},{20,4},{24,8},{28,12},{1,17},{... | collective-permute-start | bytes 110600 | tf_op jit(solution)/shard_map/ppermute | solution.py:440
  10.3 1.6 %collective-permute-start.3 = (bf16[144,128]{1,0:T(8,128)(2,1)S(1)}, bf16[144,128]{1,0:T(8,128)(2,1)S(1)}, u32[]{:S(2)}, u32[]{:S(2)}) collective-permute-start(bf16[144,128]{1,0:T(8,128)(2,1)S(1)} %get-tuple-element.55), channel_id=1, source_target_pairs={{0,8},{4,12},{8,0},{12,4},{16,24},{20,28},{24,16},{28,20},{1,9},{5... | collective-permute-start | bytes 110600 | tf_op jit(solution)/shard_map/ppermute | solution.py:440
  11.9 1.5 %collective-permute-start.4 = (bf16[144,128]{1,0:T(8,128)(2,1)S(1)}, bf16[144,128]{1,0:T(8,128)(2,1)S(1)}, u32[]{:S(2)}, u32[]{:S(2)}) collective-permute-start(bf16[144,128]{1,0:T(8,128)(2,1)S(1)} %get-tuple-element.56), channel_id=1, source_target_pairs={{0,4},{4,0},{8,12},{12,8},{16,20},{20,16},{24,28},{28,24},{1,5},{5... | collective-permute-start | bytes 110600 | tf_op jit(solution)/shard_map/ppermute | solution.py:440
  13.4 0.8 %couple.1 = (bf16[1024,32]{1,0:T(8,128)(2,1)S(1)}, f32[16,512]{1,0:T(8,128)S(1)}) custom-call(s32[8,32]{1,0:T(8,128)S(1)} %get-tuple-element.58.table_ref, f32[32,8,32,32]{3,2,1,0:T(8,128)S(1)} %get-tuple-element.59.coupling_ref, bf16[16,4096]{1,0:T(8,128)(2,1)S(1)} %get-tuple-element.53.dens_ref.refs_2_, f32[32,4096]{1,0:T(8,128)S(1)} %get-tuple-element.60.bases_ref), custom_call_target="tpu_custom_call" | custom-call | bytes 7380000 | tf_op jit(solution)/shard_map/couple/pallas_call | solution.py:493
  14.3 0.0 collective-permute-done.2.refs_4_.refs_1_
  14.3 0.5 %collective-permute-start.6 = (bf16[64,128]{1,0:T(8,128)(2,1)S(1)}, bf16[64,128]{1,0:T(8,128)(2,1)S(1)}, u32[]{:S(2)}, u32[]{:S(2)}) collective-permute-start(bf16[64,128]{1,0:T(8,128)(2,1)S(1)} %slice.16), channel_id=1, source_target_pairs={{0,8},{4,12},{8,0},{12,4},{16,24},{20,28},{24,16},{28,20},{1,9},{5... | collective-permute-start | bytes 49160 | tf_op jit(solution)/shard_map/ppermute | solution.py:440
  14.8 0.0 collective-permute-done.3.refs_5_.refs_2_
  14.8 1.1 %collective-permute-done.4.refs_6_.refs_3_ = bf16[144,128]{1,0:T(8,128)(2,1)S(1)} collective-permute-done((bf16[144,128]{1,0:T(8,128)(2,1)S(1)}, bf16[144,128]{1,0:T(8,128)(2,1)S(1)}, u32[]{:S(2)}, u32[]{:S(2)}) %collective-permute-start.4) | collective-permute-done | bytes 36896 | tf_op jit(solution)/shard_map/ppermute | solution.py:440
  15.9 0.0 collective-permute-done.5.refs_8_
  15.9 1.5 %near.1 = (f32[16,4096]{1,0:T(8,128)S(1)}, s16[16,4352]{1,0:T(8,128)(2,1)S(1)}) custom-call(s32[2,32]{1,0:T(2,128)S(1)} %get-tuple-element.44.refs_0_, s32[2,32]{1,0:T(2,128)S(1)} %collective-permute-done.1.refs_1_, bf16[16,4096]{1,0:T(8,128)(2,1)S(1)} %get-tuple-element.53.dens_ref.refs_2_, bf16[16,4096]{1,0:T(8,128)(2,1)S(1)} %collective-permute-done.refs_0_.refs_3_, ...), custom_call_target="tpu_custom_call" | custom-call | bytes 11070000 | tf_op jit(solution)/shard_map/near/pallas_call | solution.py:523
  17.4 1.0 %collective-permute-start.8 = (s16[16,4352]{1,0:T(8,128)(2,1)S(1)}, s16[16,4352]{1,0:T(8,128)(2,1)S(1)}, u32[]{:S(2)}, u32[]{:S(2)}) collective-permute-start(s16[16,4352]{1,0:T(8,128)(2,1)S(1)} %get-tuple-element.72), channel_id=1, source_target_pairs={{0,2},{2,0},{1,3},{3,1},{4,6},{6,4},{5,7},{7,5},{8,10},{10,8},{9,1... | collective-permute-start | bytes 417800 | tf_op jit(solution)/shard_map/ppermute | solution.py:437
  18.3 0.0 collective-permute-done.6.refs_4_
  18.3 1.6 %collective-permute-start.7 = (bf16[48,128]{1,0:T(8,128)(2,1)S(1)}, bf16[48,128]{1,0:T(8,128)(2,1)S(1)}, u32[]{:S(2)}, u32[]{:S(2)}) collective-permute-start(bf16[48,128]{1,0:T(8,128)(2,1)S(1)} %pad_maximum_fusion), channel_id=1, source_target_pairs={{0,4},{4,0},{8,12},{12,8},{16,20},{20,16},{24,28},{28,24},{1,5},{5... | collective-permute-start | bytes 36872 | tf_op jit(solution)/shard_map/ppermute | solution.py:440
  19.9 0.5 %paths.1 = (bf16[32,1024]{1,0:T(8,128)(2,1)S(1)}, bf16[32,1024]{1,0:T(8,128)(2,1)S(1)}) custom-call(f32[16,32,32]{2,1,0:T(8,128)S(1)} %get-tuple-element.64.upper_ref, f32[16,3,32,32]{3,2,1,0:T(8,128)S(1)} %get-tuple-element.65.cross_ref), custom_call_target="tpu_custom_call" | custom-call | bytes 2583000 | tf_op jit(solution)/shard_map/paths/pallas_call | solution.py:540
  20.5 1.3 %project.1.term_ref = f32[16,4096]{1,0:T(8,128)S(1)} custom-call(s32[8,32]{1,0:T(8,128)S(1)} %get-tuple-element.58.table_ref, f32[32,8,32,32]{3,2,1,0:T(8,128)S(1)} %get-tuple-element.59.coupling_ref, bf16[1024,32]{1,0:T(8,128)(2,1)S(1)} %get-tuple-element.69.turned_ref, f32[16,512]{1,0:T(8,128)S(1)} %get-tuple-element.62.refs_9_.first_ref, ...), custom_call_target="tpu_custom_call" | custom-call | bytes 5535000 | tf_op jit(solution)/shard_map/project/pallas_call | solution.py:551
  21.8 0.3 %collective-permute-done.7.refs_5_ = bf16[48,128]{1,0:T(8,128)(2,1)S(1)} collective-permute-done((bf16[48,128]{1,0:T(8,128)(2,1)S(1)}, bf16[48,128]{1,0:T(8,128)(2,1)S(1)}, u32[]{:S(2)}, u32[]{:S(2)}) %collective-permute-start.7) | collective-permute-done | bytes 12320 | tf_op jit(solution)/shard_map/ppermute | solution.py:440
  22.1 0.5 %far.1.term_ref = f32[16,4096]{1,0:T(8,128)S(1)} custom-call(bf16[32,1024]{1,0:T(8,128)(2,1)S(1)} %get-tuple-element.66.path_high_ref, bf16[32,1024]{1,0:T(8,128)(2,1)S(1)} %get-tuple-element.67.path_low_ref, bf16[64,4096]{1,0:T(8,128)(2,1)S(1)} %get-tuple-element.68.halves_ref, f32[16,4096]{1,0:T(8,128)S(1)} %project.1.term_ref, ...), custom_call_target="tpu_custom_call" | custom-call | bytes 2214000 | tf_op jit(solution)/shard_map/far/pallas_call | solution.py:560
  22.6 0.0 collective-permute-done.8.refs_0_
  22.6 0.8 %add.1 = f32[16,4096]{1,0:T(8,128)} custom-call(f32[16,4096]{1,0:T(8,128)S(1)} %far.1.term_ref, s16[16,4352]{1,0:T(8,128)(2,1)S(1)} %collective-permute-done.8.refs_0_), custom_call_target="tpu_custom_call" | custom-call | bytes 1845000 | tf_op jit(solution)/shard_map/add/pallas_call | solution.py:569
  (5 shorter events, 0.0 us)
Async XLA Ops:
  0.0 6.9 %collective-permute-start = (bf16[16,4096]{1,0:T(8,128)(2,1)}, bf16[16,4096]{1,0:T(8,128)(2,1)S(1)}, u32[]{:S(2)}, u32[]{:S(2)}) collective-permute-start(bf16[16,4096]{1,0:T(8,128)(2,1)} %refs_0_.1), channel_id=1, source_target_pairs={{0,2},{2,0},{1,3},{3,1},{4,6},{6,4},{5,7},{7,5},{8,10},{10,8},{9,1... | collective-permute-start | bytes 393224 | tf_op jit(solution)/shard_map/ppermute | solution.py:437
  2.9 4.0 %collective-permute-start.1 = (s32[2,32]{1,0:T(2,128)}, s32[2,32]{1,0:T(2,128)S(1)}, u32[]{:S(2)}, u32[]{:S(2)}) collective-permute-start(s32[2,32]{1,0:T(2,128)} %bitcast.9), channel_id=1, source_target_pairs={{0,1},{1,0},{2,3},{3,2},{4,5},{5,4},{6,7},{7,6},{8,9},{9,8},{10,11... | collective-permute-start | bytes 776 | tf_op jit(solution)/shard_map/ppermute | solution.py:437
  6.9 8.9 %collective-permute-start.5 = (bf16[32,2,128,128]{3,2,1,0:T(8,128)(2,1)S(1)}, bf16[32,2,128,128]{3,2,1,0:T(8,128)(2,1)S(1)}, u32[]{:S(2)}, u32[]{:S(2)}) collective-permute-start(bf16[32,2,128,128]{3,2,1,0:T(8,128)(2,1)S(1)} %get-tuple-element.57.refs_7_), channel_id=1, source_target_pairs={{0,1},{1,0},{2,3},{3,2},{4,5},{5,4},{6,7},{7,6},{8,9},{9,8},{10,11... | collective-permute-start | bytes 6291464 | tf_op jit(solution)/shard_map/ppermute | solution.py:437
  7.7 6.6 %collective-permute-start.2 = (bf16[144,128]{1,0:T(8,128)(2,1)S(1)}, bf16[144,128]{1,0:T(8,128)(2,1)S(1)}, u32[]{:S(2)}, u32[]{:S(2)}) collective-permute-start(bf16[144,128]{1,0:T(8,128)(2,1)S(1)} %get-tuple-element.54), channel_id=1, source_target_pairs={{0,16},{4,20},{8,24},{12,28},{16,0},{20,4},{24,8},{28,12},{1,17},{... | collective-permute-start | bytes 110600 | tf_op jit(solution)/shard_map/ppermute | solution.py:440
  10.3 4.5 %collective-permute-start.3 = (bf16[144,128]{1,0:T(8,128)(2,1)S(1)}, bf16[144,128]{1,0:T(8,128)(2,1)S(1)}, u32[]{:S(2)}, u32[]{:S(2)}) collective-permute-start(bf16[144,128]{1,0:T(8,128)(2,1)S(1)} %get-tuple-element.55), channel_id=1, source_target_pairs={{0,8},{4,12},{8,0},{12,4},{16,24},{20,28},{24,16},{28,20},{1,9},{5... | collective-permute-start | bytes 110600 | tf_op jit(solution)/shard_map/ppermute | solution.py:440
  11.9 4.0 %collective-permute-start.4 = (bf16[144,128]{1,0:T(8,128)(2,1)S(1)}, bf16[144,128]{1,0:T(8,128)(2,1)S(1)}, u32[]{:S(2)}, u32[]{:S(2)}) collective-permute-start(bf16[144,128]{1,0:T(8,128)(2,1)S(1)} %get-tuple-element.56), channel_id=1, source_target_pairs={{0,4},{4,0},{8,12},{12,8},{16,20},{20,16},{24,28},{28,24},{1,5},{5... | collective-permute-start | bytes 110600 | tf_op jit(solution)/shard_map/ppermute | solution.py:440
  14.3 4.0 %collective-permute-start.6 = (bf16[64,128]{1,0:T(8,128)(2,1)S(1)}, bf16[64,128]{1,0:T(8,128)(2,1)S(1)}, u32[]{:S(2)}, u32[]{:S(2)}) collective-permute-start(bf16[64,128]{1,0:T(8,128)(2,1)S(1)} %slice.16), channel_id=1, source_target_pairs={{0,8},{4,12},{8,0},{12,4},{16,24},{20,28},{24,16},{28,20},{1,9},{5... | collective-permute-start | bytes 49160 | tf_op jit(solution)/shard_map/ppermute | solution.py:440
  17.4 5.3 %collective-permute-start.8 = (s16[16,4352]{1,0:T(8,128)(2,1)S(1)}, s16[16,4352]{1,0:T(8,128)(2,1)S(1)}, u32[]{:S(2)}, u32[]{:S(2)}) collective-permute-start(s16[16,4352]{1,0:T(8,128)(2,1)S(1)} %get-tuple-element.72), channel_id=1, source_target_pairs={{0,2},{2,0},{1,3},{3,1},{4,6},{6,4},{5,7},{7,5},{8,10},{10,8},{9,1... | collective-permute-start | bytes 417800 | tf_op jit(solution)/shard_map/ppermute | solution.py:437
  18.3 3.8 %collective-permute-start.7 = (bf16[48,128]{1,0:T(8,128)(2,1)S(1)}, bf16[48,128]{1,0:T(8,128)(2,1)S(1)}, u32[]{:S(2)}, u32[]{:S(2)}) collective-permute-start(bf16[48,128]{1,0:T(8,128)(2,1)S(1)} %pad_maximum_fusion), channel_id=1, source_target_pairs={{0,4},{4,0},{8,12},{12,8},{16,20},{20,16},{24,28},{28,24},{1,5},{5... | collective-permute-start | bytes 36872 | tf_op jit(solution)/shard_map/ppermute | solution.py:440

commit v16 on v15

--- a/solution.py
+++ b/solution.py
@@ -224,7 +224,8 @@
             for blocks_ref in (block_ref, *mate_refs)
             for block in range(near_count)
         ]
-        total = dot_nt(jnp.concatenate(panels, axis=1), jnp.concatenate(blocks, axis=1))
+        panels, blocks = jnp.concatenate(panels, axis=1), jnp.concatenate(blocks, axis=1)
+        total = dot_nt(panels, blocks) if leaf % 2 else dot_nt(blocks, panels).T
         lanes = slice(leaf * width, (leaf + 1) * width)
         own_ref[:, lanes] = total[:columns]
         for part, (sent_ref, power_ref) in enumerate(zip(sent_refs, power_refs), 1):

time: 23.5 us -> 23.5 us (level)
  no operation moved by 1% of the time
where the time goes in v16:
time: 23.5 us; the launch traced here: 23.4 us
  starting transfers between devices  12.3 us (52%)
  Pallas kernels  9.55 us (41%)
  waiting for transfers between devices  1.4 us (6%)
    ppermute x5, starting transfers between devices, crossed(): lax.ppermute(value, 'leaf', [(i, i ^ turn) for i in range(leaf_devices)])  7.84 us
    ppermute x4, starting transfers between devices, rotated(): lax.ppermute(value, axis, [(i, (i - shift) % count) for i in range(count)])  4.47 us
    pallas_call x1, Pallas kernels, local(): pl.pallas_call(up_kernel, out_shape=[jax.ShapeDtypeStruct(value.shape, va...  3.97 us
    pallas_call x1, Pallas kernels, local(): pl.pallas_call(functools.partial(near_kernel, faces, far_groups, share),...  1.47 us
    ppermute x5, waiting for transfers between devices, crossed(): lax.ppermute(value, 'leaf', [(i, i ^ turn) for i in range(leaf_devices)])  1.39 us
    pallas_call x1, Pallas kernels, local(): pl.pallas_call(project_kernel, out_shape=jax.ShapeDtypeStruct((columns, p...  1.3 us
    pallas_call x1, Pallas kernels, local(): pl.pallas_call(couple_kernel, out_shape=[jax.ShapeDtypeStruct((leaf_count...  0.85 us
    pallas_call x1, Pallas kernels, local(): pl.pallas_call(functools.partial(add_kernel, leaf_count), out_shape=jax.S...  0.75 us
  transfers between devices with their start and end apart: 9, of which 2 were waited for; matrix products, arithmetic and copies ran while one was open for 0% of the time, Pallas kernels for 38%

profile of v16, /device:TPU:0, one launch (start us, length us, event | category | flops | bytes accessed | tf_op | source)
XLA Modules:
  0.0 23.4 jit_solution(15711132756453361640)
XLA Ops:
  0.0 2.9 %collective-permute-start = (bf16[16,4096]{1,0:T(8,128)(2,1)}, bf16[16,4096]{1,0:T(8,128)(2,1)S(1)}, u32[]{:S(2)}, u32[]{:S(2)}) collective-permute-start(bf16[16,4096]{1,0:T(8,128)(2,1)} %refs_0_.1), channel_id=1, source_target_pairs={{0,2},{2,0},{1,3},{3,1},{4,6},{6,4},{5,7},{7,5},{8,10},{10,8},{9,1... | collective-permute-start | bytes 393224 | tf_op jit(solution)/shard_map/ppermute | solution.py:438
  2.9 0.0 collective-permute-start.1
  2.9 4.0 %up.1 = (f32[32,4096]{1,0:T(8,128)S(1)}, bf16[16,4096]{1,0:T(8,128)(2,1)S(1)}, s32[6,4,8]{2,1,0:T(4,128)S(1)}, s32[2,32]{1,0:T(2,128)S(1)}, s32[8,32]{1,0:T(8,12...) custom-call(f32[32,32,64]{2,1,0:T(8,128)} %bitcast.6, ...), custom_call_target="tpu_custom_call" | custom-call | bytes 12915000 | tf_op jit(solution)/shard_map/up/pallas_call | solution.py:452
  6.9 0.0 collective-permute-done.1.refs_1_
  6.9 0.0 collective-permute-done.refs_0_.refs_3_
  6.9 0.6 %collective-permute-start.5 = (bf16[32,2,128,128]{3,2,1,0:T(8,128)(2,1)S(1)}, bf16[32,2,128,128]{3,2,1,0:T(8,128)(2,1)S(1)}, u32[]{:S(2)}, u32[]{:S(2)}) collective-permute-start(bf16[32,2,128,128]{3,2,1,0:T(8,128)(2,1)S(1)} %get-tuple-element.57.refs_7_), channel_id=1, source_target_pairs={{0,1},{1,0},{2,3},{3,2},{4,5},{5,4},{6,7},{7,6},{8,9},{9,8},{10,11... | collective-permute-start | bytes 6291464 | tf_op jit(solution)/shard_map/ppermute | solution.py:438
  7.5 0.2 select.1
  7.7 2.7 %collective-permute-start.2 = (bf16[144,128]{1,0:T(8,128)(2,1)S(1)}, bf16[144,128]{1,0:T(8,128)(2,1)S(1)}, u32[]{:S(2)}, u32[]{:S(2)}) collective-permute-start(bf16[144,128]{1,0:T(8,128)(2,1)S(1)} %get-tuple-element.54), channel_id=1, source_target_pairs={{0,16},{4,20},{8,24},{12,28},{16,0},{20,4},{24,8},{28,12},{1,17},{... | collective-permute-start | bytes 110600 | tf_op jit(solution)/shard_map/ppermute | solution.py:441
  10.3 1.6 %collective-permute-start.3 = (bf16[144,128]{1,0:T(8,128)(2,1)S(1)}, bf16[144,128]{1,0:T(8,128)(2,1)S(1)}, u32[]{:S(2)}, u32[]{:S(2)}) collective-permute-start(bf16[144,128]{1,0:T(8,128)(2,1)S(1)} %get-tuple-element.55), channel_id=1, source_target_pairs={{0,8},{4,12},{8,0},{12,4},{16,24},{20,28},{24,16},{28,20},{1,9},{5... | collective-permute-start | bytes 110600 | tf_op jit(solution)/shard_map/ppermute | solution.py:441
  11.9 1.5 %collective-permute-start.4 = (bf16[144,128]{1,0:T(8,128)(2,1)S(1)}, bf16[144,128]{1,0:T(8,128)(2,1)S(1)}, u32[]{:S(2)}, u32[]{:S(2)}) collective-permute-start(bf16[144,128]{1,0:T(8,128)(2,1)S(1)} %get-tuple-element.56), channel_id=1, source_target_pairs={{0,4},{4,0},{8,12},{12,8},{16,20},{20,16},{24,28},{28,24},{1,5},{5... | collective-permute-start | bytes 110600 | tf_op jit(solution)/shard_map/ppermute | solution.py:441
  13.4 0.8 %couple.1 = (bf16[1024,32]{1,0:T(8,128)(2,1)S(1)}, f32[16,512]{1,0:T(8,128)S(1)}) custom-call(s32[8,32]{1,0:T(8,128)S(1)} %get-tuple-element.58.table_ref, f32[32,8,32,32]{3,2,1,0:T(8,128)S(1)} %get-tuple-element.59.coupling_ref, bf16[16,4096]{1,0:T(8,128)(2,1)S(1)} %get-tuple-element.53.dens_ref.refs_2_, f32[32,4096]{1,0:T(8,128)S(1)} %get-tuple-element.60.bases_ref), custom_call_target="tpu_custom_call" | custom-call | bytes 7380000 | tf_op jit(solution)/shard_map/couple/pallas_call | solution.py:494
  14.3 0.0 collective-permute-done.2.refs_4_.refs_1_
  14.3 0.5 %collective-permute-start.6 = (bf16[64,128]{1,0:T(8,128)(2,1)S(1)}, bf16[64,128]{1,0:T(8,128)(2,1)S(1)}, u32[]{:S(2)}, u32[]{:S(2)}) collective-permute-start(bf16[64,128]{1,0:T(8,128)(2,1)S(1)} %slice.16), channel_id=1, source_target_pairs={{0,8},{4,12},{8,0},{12,4},{16,24},{20,28},{24,16},{28,20},{1,9},{5... | collective-permute-start | bytes 49160 | tf_op jit(solution)/shard_map/ppermute | solution.py:441
  14.8 0.0 collective-permute-done.3.refs_5_.refs_2_
  14.8 1.1 %collective-permute-done.4.refs_6_.refs_3_ = bf16[144,128]{1,0:T(8,128)(2,1)S(1)} collective-permute-done((bf16[144,128]{1,0:T(8,128)(2,1)S(1)}, bf16[144,128]{1,0:T(8,128)(2,1)S(1)}, u32[]{:S(2)}, u32[]{:S(2)}) %collective-permute-start.4) | collective-permute-done | bytes 36896 | tf_op jit(solution)/shard_map/ppermute | solution.py:441
  15.9 0.0 collective-permute-done.5.refs_8_
  15.9 1.5 %near.1 = (f32[16,4096]{1,0:T(8,128)S(1)}, s16[16,4352]{1,0:T(8,128)(2,1)S(1)}) custom-call(s32[2,32]{1,0:T(2,128)S(1)} %get-tuple-element.44.refs_0_, s32[2,32]{1,0:T(2,128)S(1)} %collective-permute-done.1.refs_1_, bf16[16,4096]{1,0:T(8,128)(2,1)S(1)} %get-tuple-element.53.dens_ref.refs_2_, bf16[16,4096]{1,0:T(8,128)(2,1)S(1)} %collective-permute-done.refs_0_.refs_3_, ...), custom_call_target="tpu_custom_call" | custom-call | bytes 11070000 | tf_op jit(solution)/shard_map/near/pallas_call | solution.py:524
  17.3 1.0 %collective-permute-start.8 = (s16[16,4352]{1,0:T(8,128)(2,1)S(1)}, s16[16,4352]{1,0:T(8,128)(2,1)S(1)}, u32[]{:S(2)}, u32[]{:S(2)}) collective-permute-start(s16[16,4352]{1,0:T(8,128)(2,1)S(1)} %get-tuple-element.72), channel_id=1, source_target_pairs={{0,2},{2,0},{1,3},{3,1},{4,6},{6,4},{5,7},{7,5},{8,10},{10,8},{9,1... | collective-permute-start | bytes 417800 | tf_op jit(solution)/shard_map/ppermute | solution.py:438
  18.3 0.0 collective-permute-done.6.refs_4_
  18.3 1.6 %collective-permute-start.7 = (bf16[48,128]{1,0:T(8,128)(2,1)S(1)}, bf16[48,128]{1,0:T(8,128)(2,1)S(1)}, u32[]{:S(2)}, u32[]{:S(2)}) collective-permute-start(bf16[48,128]{1,0:T(8,128)(2,1)S(1)} %pad_maximum_fusion), channel_id=1, source_target_pairs={{0,4},{4,0},{8,12},{12,8},{16,20},{20,16},{24,28},{28,24},{1,5},{5... | collective-permute-start | bytes 36872 | tf_op jit(solution)/shard_map/ppermute | solution.py:441
  19.9 0.5 %paths.1 = (bf16[32,1024]{1,0:T(8,128)(2,1)S(1)}, bf16[32,1024]{1,0:T(8,128)(2,1)S(1)}) custom-call(f32[16,32,32]{2,1,0:T(8,128)S(1)} %get-tuple-element.64.upper_ref, f32[16,3,32,32]{3,2,1,0:T(8,128)S(1)} %get-tuple-element.65.cross_ref), custom_call_target="tpu_custom_call" | custom-call | bytes 2583000 | tf_op jit(solution)/shard_map/paths/pallas_call | solution.py:541
  20.5 1.3 %project.1.term_ref = f32[16,4096]{1,0:T(8,128)S(1)} custom-call(s32[8,32]{1,0:T(8,128)S(1)} %get-tuple-element.58.table_ref, f32[32,8,32,32]{3,2,1,0:T(8,128)S(1)} %get-tuple-element.59.coupling_ref, bf16[1024,32]{1,0:T(8,128)(2,1)S(1)} %get-tuple-element.69.turned_ref, f32[16,512]{1,0:T(8,128)S(1)} %get-tuple-element.62.refs_9_.first_ref, ...), custom_call_target="tpu_custom_call" | custom-call | bytes 5535000 | tf_op jit(solution)/shard_map/project/pallas_call | solution.py:552
  21.8 0.3 %collective-permute-done.7.refs_5_ = bf16[48,128]{1,0:T(8,128)(2,1)S(1)} collective-permute-done((bf16[48,128]{1,0:T(8,128)(2,1)S(1)}, bf16[48,128]{1,0:T(8,128)(2,1)S(1)}, u32[]{:S(2)}, u32[]{:S(2)}) %collective-permute-start.7) | collective-permute-done | bytes 12320 | tf_op jit(solution)/shard_map/ppermute | solution.py:441
  22.1 0.5 %far.1.term_ref = f32[16,4096]{1,0:T(8,128)S(1)} custom-call(bf16[32,1024]{1,0:T(8,128)(2,1)S(1)} %get-tuple-element.66.path_high_ref, bf16[32,1024]{1,0:T(8,128)(2,1)S(1)} %get-tuple-element.67.path_low_ref, bf16[64,4096]{1,0:T(8,128)(2,1)S(1)} %get-tuple-element.68.halves_ref, f32[16,4096]{1,0:T(8,128)S(1)} %project.1.term_ref, ...), custom_call_target="tpu_custom_call" | custom-call | bytes 2214000 | tf_op jit(solution)/shard_map/far/pallas_call | solution.py:561
  22.6 0.0 collective-permute-done.8.refs_0_
  22.6 0.8 %add.1 = f32[16,4096]{1,0:T(8,128)} custom-call(f32[16,4096]{1,0:T(8,128)S(1)} %far.1.term_ref, s16[16,4352]{1,0:T(8,128)(2,1)S(1)} %collective-permute-done.8.refs_0_), custom_call_target="tpu_custom_call" | custom-call | bytes 1845000 | tf_op jit(solution)/shard_map/add/pallas_call | solution.py:570
  (5 shorter events, 0.0 us)
Async XLA Ops:
  0.0 6.9 %collective-permute-start = (bf16[16,4096]{1,0:T(8,128)(2,1)}, bf16[16,4096]{1,0:T(8,128)(2,1)S(1)}, u32[]{:S(2)}, u32[]{:S(2)}) collective-permute-start(bf16[16,4096]{1,0:T(8,128)(2,1)} %refs_0_.1), channel_id=1, source_target_pairs={{0,2},{2,0},{1,3},{3,1},{4,6},{6,4},{5,7},{7,5},{8,10},{10,8},{9,1... | collective-permute-start | bytes 393224 | tf_op jit(solution)/shard_map/ppermute | solution.py:438
  2.9 4.0 %collective-permute-start.1 = (s32[2,32]{1,0:T(2,128)}, s32[2,32]{1,0:T(2,128)S(1)}, u32[]{:S(2)}, u32[]{:S(2)}) collective-permute-start(s32[2,32]{1,0:T(2,128)} %bitcast.9), channel_id=1, source_target_pairs={{0,1},{1,0},{2,3},{3,2},{4,5},{5,4},{6,7},{7,6},{8,9},{9,8},{10,11... | collective-permute-start | bytes 776 | tf_op jit(solution)/shard_map/ppermute | solution.py:438
  6.9 8.9 %collective-permute-start.5 = (bf16[32,2,128,128]{3,2,1,0:T(8,128)(2,1)S(1)}, bf16[32,2,128,128]{3,2,1,0:T(8,128)(2,1)S(1)}, u32[]{:S(2)}, u32[]{:S(2)}) collective-permute-start(bf16[32,2,128,128]{3,2,1,0:T(8,128)(2,1)S(1)} %get-tuple-element.57.refs_7_), channel_id=1, source_target_pairs={{0,1},{1,0},{2,3},{3,2},{4,5},{5,4},{6,7},{7,6},{8,9},{9,8},{10,11... | collective-permute-start | bytes 6291464 | tf_op jit(solution)/shard_map/ppermute | solution.py:438
  7.7 6.6 %collective-permute-start.2 = (bf16[144,128]{1,0:T(8,128)(2,1)S(1)}, bf16[144,128]{1,0:T(8,128)(2,1)S(1)}, u32[]{:S(2)}, u32[]{:S(2)}) collective-permute-start(bf16[144,128]{1,0:T(8,128)(2,1)S(1)} %get-tuple-element.54), channel_id=1, source_target_pairs={{0,16},{4,20},{8,24},{12,28},{16,0},{20,4},{24,8},{28,12},{1,17},{... | collective-permute-start | bytes 110600 | tf_op jit(solution)/shard_map/ppermute | solution.py:441
  10.3 4.5 %collective-permute-start.3 = (bf16[144,128]{1,0:T(8,128)(2,1)S(1)}, bf16[144,128]{1,0:T(8,128)(2,1)S(1)}, u32[]{:S(2)}, u32[]{:S(2)}) collective-permute-start(bf16[144,128]{1,0:T(8,128)(2,1)S(1)} %get-tuple-element.55), channel_id=1, source_target_pairs={{0,8},{4,12},{8,0},{12,4},{16,24},{20,28},{24,16},{28,20},{1,9},{5... | collective-permute-start | bytes 110600 | tf_op jit(solution)/shard_map/ppermute | solution.py:441
  11.9 4.0 %collective-permute-start.4 = (bf16[144,128]{1,0:T(8,128)(2,1)S(1)}, bf16[144,128]{1,0:T(8,128)(2,1)S(1)}, u32[]{:S(2)}, u32[]{:S(2)}) collective-permute-start(bf16[144,128]{1,0:T(8,128)(2,1)S(1)} %get-tuple-element.56), channel_id=1, source_target_pairs={{0,4},{4,0},{8,12},{12,8},{16,20},{20,16},{24,28},{28,24},{1,5},{5... | collective-permute-start | bytes 110600 | tf_op jit(solution)/shard_map/ppermute | solution.py:441
  14.3 4.0 %collective-permute-start.6 = (bf16[64,128]{1,0:T(8,128)(2,1)S(1)}, bf16[64,128]{1,0:T(8,128)(2,1)S(1)}, u32[]{:S(2)}, u32[]{:S(2)}) collective-permute-start(bf16[64,128]{1,0:T(8,128)(2,1)S(1)} %slice.16), channel_id=1, source_target_pairs={{0,8},{4,12},{8,0},{12,4},{16,24},{20,28},{24,16},{28,20},{1,9},{5... | collective-permute-start | bytes 49160 | tf_op jit(solution)/shard_map/ppermute | solution.py:441
  17.3 5.2 %collective-permute-start.8 = (s16[16,4352]{1,0:T(8,128)(2,1)S(1)}, s16[16,4352]{1,0:T(8,128)(2,1)S(1)}, u32[]{:S(2)}, u32[]{:S(2)}) collective-permute-start(s16[16,4352]{1,0:T(8,128)(2,1)S(1)} %get-tuple-element.72), channel_id=1, source_target_pairs={{0,2},{2,0},{1,3},{3,1},{4,6},{6,4},{5,7},{7,5},{8,10},{10,8},{9,1... | collective-permute-start | bytes 417800 | tf_op jit(solution)/shard_map/ppermute | solution.py:438
  18.3 3.8 %collective-permute-start.7 = (bf16[48,128]{1,0:T(8,128)(2,1)S(1)}, bf16[48,128]{1,0:T(8,128)(2,1)S(1)}, u32[]{:S(2)}, u32[]{:S(2)}) collective-permute-start(bf16[48,128]{1,0:T(8,128)(2,1)S(1)} %pad_maximum_fusion), channel_id=1, source_target_pairs={{0,4},{4,0},{8,12},{12,8},{16,20},{20,16},{24,28},{28,24},{1,5},{5... | collective-permute-start | bytes 36872 | tf_op jit(solution)/shard_map/ppermute | solution.py:441

commit v17 on v15

--- a/solution.py
+++ b/solution.py
@@ -489,7 +489,7 @@
         name="select",
     )(send, dens, root, *others)
     outgoing, dens = lax.optimization_barrier((outgoing, dens))
-    first_leaves = leaf_count // 2
+    first_leaves = 3 * leaf_count // 4
     turned, leaf_local = pl.pallas_call(
         couple_kernel,
         out_shape=[
@@ -505,12 +505,12 @@
     tail = cap * far_groups * columns
     if side == 2:
         arrived = [crossed(value, stride) for (_, stride), value in zip(faces, outgoing)]
-        far_one, near_two, _ = (value[tail : tail + columns] for value in arrived)
+        far_one, _, near_one = (value[tail : tail + columns] for value in arrived)
         later, leaf_local = lax.optimization_barrier((arrived[0][-4 * columns :], leaf_local))
-        across = crossed(later, 2)
-        held = jnp.concatenate([near_two, far_one, across[-columns:]], axis=0)
-        beside = crossed(held, 1)
-        turns = [0] + [stride for _, stride in faces] + [6, 3, 5, 7]
+        across = crossed(later, 1)
+        held = jnp.concatenate([near_one, far_one, across[-columns:]], axis=0)
+        beside = crossed(held, 2)
+        turns = [0] + [stride for _, stride in faces] + [5, 3, 6, 7]
         roots = [([0], root)] + [([tail], value) for value in arrived]
         roots += [([3 * columns], across), ([0, columns, 2 * columns], beside)]
     else:

time: 23.5 us -> 23.6 us (level)
  waiting for transfers between devices: 1.4 us -> 2.67 us
  starting transfers between devices: 12.3 us -> 11.2 us
    ppermute x5, waiting for transfers between devices: 1.39 us -> 2.66 us  [crossed(): lax.ppermute(value, 'leaf', [(i, i ^ turn) for i in range(leaf_devices)])]
    ppermute x5, starting transfers between devices: 7.84 us -> 6.76 us  [crossed(): lax.ppermute(value, 'leaf', [(i, i ^ turn) for i in range(leaf_devices)])]
    pallas_call x1, Pallas kernels: 1.3 us -> 0.82 us  [local(): pl.pallas_call(project_kernel, out_shape=jax.ShapeDtypeStruct((columns, p...]
    pallas_call x1, Pallas kernels: 0.85 us -> 1.19 us  [local(): pl.pallas_call(couple_kernel, out_shape=[jax.ShapeDtypeStruct((leaf_count...]
  transfers between devices with their start and end apart: 9 -> 9, of which waited for: 2 -> 3; matrix products, arithmetic and copies ran while one was open for 0% -> 0% of each run, Pallas kernels for 38% -> 37%
where the time goes in v17:
time: 23.6 us; the launch traced here: 23.4 us
  starting transfers between devices  11.2 us (47%)
  Pallas kernels  9.43 us (40%)
  waiting for transfers between devices  2.67 us (11%)
    ppermute x5, starting transfers between devices, crossed(): lax.ppermute(value, 'leaf', [(i, i ^ turn) for i in range(leaf_devices)])  6.76 us
    ppermute x4, starting transfers between devices, rotated(): lax.ppermute(value, axis, [(i, (i - shift) % count) for i in range(count)])  4.47 us
    pallas_call x1, Pallas kernels, local(): pl.pallas_call(up_kernel, out_shape=[jax.ShapeDtypeStruct(value.shape, va...  3.97 us
    ppermute x5, waiting for transfers between devices, crossed(): lax.ppermute(value, 'leaf', [(i, i ^ turn) for i in range(leaf_devices)])  2.66 us
    pallas_call x1, Pallas kernels, local(): pl.pallas_call(functools.partial(near_kernel, faces, far_groups, share),...  1.49 us
    pallas_call x1, Pallas kernels, local(): pl.pallas_call(couple_kernel, out_shape=[jax.ShapeDtypeStruct((leaf_count...  1.19 us
    pallas_call x1, Pallas kernels, local(): pl.pallas_call(project_kernel, out_shape=jax.ShapeDtypeStruct((columns, p...  0.82 us
    pallas_call x1, Pallas kernels, local(): pl.pallas_call(functools.partial(add_kernel, leaf_count), out_shape=jax.S...  0.75 us
  transfers between devices with their start and end apart: 9, of which 3 were waited for; matrix products, arithmetic and copies ran while one was open for 0% of the time, Pallas kernels for 37%

profile of v17, /device:TPU:0, one launch (start us, length us, event | category | flops | bytes accessed | tf_op | source)
XLA Modules:
  0.0 23.4 jit_solution(7977000497738078255)
XLA Ops:
  0.0 2.9 %collective-permute-start = (bf16[16,4096]{1,0:T(8,128)(2,1)}, bf16[16,4096]{1,0:T(8,128)(2,1)S(1)}, u32[]{:S(2)}, u32[]{:S(2)}) collective-permute-start(bf16[16,4096]{1,0:T(8,128)(2,1)} %refs_0_.1), channel_id=1, source_target_pairs={{0,2},{2,0},{1,3},{3,1},{4,6},{6,4},{5,7},{7,5},{8,10},{10,8},{9,1... | collective-permute-start | bytes 393224 | tf_op jit(solution)/shard_map/ppermute | solution.py:437
  2.9 0.0 collective-permute-start.1
  2.9 4.0 %up.1 = (f32[32,4096]{1,0:T(8,128)S(1)}, bf16[16,4096]{1,0:T(8,128)(2,1)S(1)}, s32[6,4,8]{2,1,0:T(4,128)S(1)}, s32[2,32]{1,0:T(2,128)S(1)}, s32[8,32]{1,0:T(8,12...) custom-call(f32[32,32,64]{2,1,0:T(8,128)} %bitcast.6, ...), custom_call_target="tpu_custom_call" | custom-call | bytes 12915000 | tf_op jit(solution)/shard_map/up/pallas_call | solution.py:451
  6.9 0.0 collective-permute-done.1.refs_1_
  6.9 0.0 collective-permute-done.refs_0_.refs_3_
  6.9 0.6 %collective-permute-start.5 = (bf16[32,2,128,128]{3,2,1,0:T(8,128)(2,1)S(1)}, bf16[32,2,128,128]{3,2,1,0:T(8,128)(2,1)S(1)}, u32[]{:S(2)}, u32[]{:S(2)}) collective-permute-start(bf16[32,2,128,128]{3,2,1,0:T(8,128)(2,1)S(1)} %get-tuple-element.57.refs_7_), channel_id=1, source_target_pairs={{0,1},{1,0},{2,3},{3,2},{4,5},{5,4},{6,7},{7,6},{8,9},{9,8},{10,11... | collective-permute-start | bytes 6291464 | tf_op jit(solution)/shard_map/ppermute | solution.py:437
  7.5 0.2 select.1
  7.7 2.7 %collective-permute-start.2 = (bf16[144,128]{1,0:T(8,128)(2,1)S(1)}, bf16[144,128]{1,0:T(8,128)(2,1)S(1)}, u32[]{:S(2)}, u32[]{:S(2)}) collective-permute-start(bf16[144,128]{1,0:T(8,128)(2,1)S(1)} %get-tuple-element.54), channel_id=1, source_target_pairs={{0,16},{4,20},{8,24},{12,28},{16,0},{20,4},{24,8},{28,12},{1,17},{... | collective-permute-start | bytes 110600 | tf_op jit(solution)/shard_map/ppermute | solution.py:440
  10.3 1.6 %collective-permute-start.3 = (bf16[144,128]{1,0:T(8,128)(2,1)S(1)}, bf16[144,128]{1,0:T(8,128)(2,1)S(1)}, u32[]{:S(2)}, u32[]{:S(2)}) collective-permute-start(bf16[144,128]{1,0:T(8,128)(2,1)S(1)} %get-tuple-element.55), channel_id=1, source_target_pairs={{0,8},{4,12},{8,0},{12,4},{16,24},{20,28},{24,16},{28,20},{1,9},{5... | collective-permute-start | bytes 110600 | tf_op jit(solution)/shard_map/ppermute | solution.py:440
  11.9 1.5 %collective-permute-start.4 = (bf16[144,128]{1,0:T(8,128)(2,1)S(1)}, bf16[144,128]{1,0:T(8,128)(2,1)S(1)}, u32[]{:S(2)}, u32[]{:S(2)}) collective-permute-start(bf16[144,128]{1,0:T(8,128)(2,1)S(1)} %get-tuple-element.56), channel_id=1, source_target_pairs={{0,4},{4,0},{8,12},{12,8},{16,20},{20,16},{24,28},{28,24},{1,5},{5... | collective-permute-start | bytes 110600 | tf_op jit(solution)/shard_map/ppermute | solution.py:440
  13.4 1.2 %couple.1 = (bf16[1024,32]{1,0:T(8,128)(2,1)S(1)}, f32[16,768]{1,0:T(8,128)S(1)}) custom-call(s32[8,32]{1,0:T(8,128)S(1)} %get-tuple-element.58.table_ref, f32[32,8,32,32]{3,2,1,0:T(8,128)S(1)} %get-tuple-element.59.coupling_ref, bf16[16,4096]{1,0:T(8,128)(2,1)S(1)} %get-tuple-element.53.dens_ref.refs_2_, f32[32,4096]{1,0:T(8,128)S(1)} %get-tuple-element.60.bases_ref), custom_call_target="tpu_custom_call" | custom-call | bytes 7380000 | tf_op jit(solution)/shard_map/couple/pallas_call | solution.py:493
  14.6 0.0 collective-permute-done.2.refs_4_.refs_1_
  14.6 0.6 %collective-permute-start.6 = (bf16[64,128]{1,0:T(8,128)(2,1)S(1)}, bf16[64,128]{1,0:T(8,128)(2,1)S(1)}, u32[]{:S(2)}, u32[]{:S(2)}) collective-permute-start(bf16[64,128]{1,0:T(8,128)(2,1)S(1)} %slice.16), channel_id=1, source_target_pairs={{0,4},{4,0},{8,12},{12,8},{16,20},{20,16},{24,28},{28,24},{1,5},{5... | collective-permute-start | bytes 49160 | tf_op jit(solution)/shard_map/ppermute | solution.py:440
  15.2 0.0 collective-permute-done.3.refs_5_.refs_2_
  15.2 0.7 %collective-permute-done.4.refs_6_.refs_3_ = bf16[144,128]{1,0:T(8,128)(2,1)S(1)} collective-permute-done((bf16[144,128]{1,0:T(8,128)(2,1)S(1)}, bf16[144,128]{1,0:T(8,128)(2,1)S(1)}, u32[]{:S(2)}, u32[]{:S(2)}) %collective-permute-start.4) | collective-permute-done | bytes 36896 | tf_op jit(solution)/shard_map/ppermute | solution.py:440
  15.9 0.0 collective-permute-done.5.refs_8_
  15.9 1.5 %near.1 = (f32[16,4096]{1,0:T(8,128)S(1)}, s16[16,4352]{1,0:T(8,128)(2,1)S(1)}) custom-call(s32[2,32]{1,0:T(2,128)S(1)} %get-tuple-element.44.refs_0_, s32[2,32]{1,0:T(2,128)S(1)} %collective-permute-done.1.refs_1_, bf16[16,4096]{1,0:T(8,128)(2,1)S(1)} %get-tuple-element.53.dens_ref.refs_2_, bf16[16,4096]{1,0:T(8,128)(2,1)S(1)} %collective-permute-done.refs_0_.refs_3_, ...), custom_call_target="tpu_custom_call" | custom-call | bytes 11070000 | tf_op jit(solution)/shard_map/near/pallas_call | solution.py:523
  17.4 1.0 %collective-permute-start.8 = (s16[16,4352]{1,0:T(8,128)(2,1)S(1)}, s16[16,4352]{1,0:T(8,128)(2,1)S(1)}, u32[]{:S(2)}, u32[]{:S(2)}) collective-permute-start(s16[16,4352]{1,0:T(8,128)(2,1)S(1)} %get-tuple-element.72), channel_id=1, source_target_pairs={{0,2},{2,0},{1,3},{3,1},{4,6},{6,4},{5,7},{7,5},{8,10},{10,8},{9,1... | collective-permute-start | bytes 417800 | tf_op jit(solution)/shard_map/ppermute | solution.py:437
  18.3 0.1 collective-permute-done.6.refs_4_
  18.4 0.4 %collective-permute-start.7 = (bf16[48,128]{1,0:T(8,128)(2,1)S(1)}, bf16[48,128]{1,0:T(8,128)(2,1)S(1)}, u32[]{:S(2)}, u32[]{:S(2)}) collective-permute-start(bf16[48,128]{1,0:T(8,128)(2,1)S(1)} %pad_maximum_fusion), channel_id=1, source_target_pairs={{0,8},{4,12},{8,0},{12,4},{16,24},{20,28},{24,16},{28,20},{1,9},{5... | collective-permute-start | bytes 36872 | tf_op jit(solution)/shard_map/ppermute | solution.py:440
  18.9 0.5 %paths.1 = (bf16[32,1024]{1,0:T(8,128)(2,1)S(1)}, bf16[32,1024]{1,0:T(8,128)(2,1)S(1)}) custom-call(f32[16,32,32]{2,1,0:T(8,128)S(1)} %get-tuple-element.64.upper_ref, f32[16,3,32,32]{3,2,1,0:T(8,128)S(1)} %get-tuple-element.65.cross_ref), custom_call_target="tpu_custom_call" | custom-call | bytes 2583000 | tf_op jit(solution)/shard_map/paths/pallas_call | solution.py:540
  19.4 0.8 %project.1.term_ref = f32[16,4096]{1,0:T(8,128)S(1)} custom-call(s32[8,32]{1,0:T(8,128)S(1)} %get-tuple-element.58.table_ref, f32[32,8,32,32]{3,2,1,0:T(8,128)S(1)} %get-tuple-element.59.coupling_ref, bf16[1024,32]{1,0:T(8,128)(2,1)S(1)} %get-tuple-element.69.turned_ref, f32[16,768]{1,0:T(8,128)S(1)} %get-tuple-element.62.refs_9_.first_ref, ...), custom_call_target="tpu_custom_call" | custom-call | bytes 5535000 | tf_op jit(solution)/shard_map/project/pallas_call | solution.py:551
  20.3 1.9 %collective-permute-done.7.refs_5_ = bf16[48,128]{1,0:T(8,128)(2,1)S(1)} collective-permute-done((bf16[48,128]{1,0:T(8,128)(2,1)S(1)}, bf16[48,128]{1,0:T(8,128)(2,1)S(1)}, u32[]{:S(2)}, u32[]{:S(2)}) %collective-permute-start.7) | collective-permute-done | bytes 12320 | tf_op jit(solution)/shard_map/ppermute | solution.py:440
  22.1 0.5 %far.1.term_ref = f32[16,4096]{1,0:T(8,128)S(1)} custom-call(bf16[32,1024]{1,0:T(8,128)(2,1)S(1)} %get-tuple-element.66.path_high_ref, bf16[32,1024]{1,0:T(8,128)(2,1)S(1)} %get-tuple-element.67.path_low_ref, bf16[64,4096]{1,0:T(8,128)(2,1)S(1)} %get-tuple-element.68.halves_ref, f32[16,4096]{1,0:T(8,128)S(1)} %project.1.term_ref, ...), custom_call_target="tpu_custom_call" | custom-call | bytes 2214000 | tf_op jit(solution)/shard_map/far/pallas_call | solution.py:560
  22.7 0.0 collective-permute-done.8.refs_0_
  22.7 0.8 %add.1 = f32[16,4096]{1,0:T(8,128)} custom-call(f32[16,4096]{1,0:T(8,128)S(1)} %far.1.term_ref, s16[16,4352]{1,0:T(8,128)(2,1)S(1)} %collective-permute-done.8.refs_0_), custom_call_target="tpu_custom_call" | custom-call | bytes 1845000 | tf_op jit(solution)/shard_map/add/pallas_call | solution.py:569
  (5 shorter events, 0.0 us)
Async XLA Ops:
  0.0 6.9 %collective-permute-start = (bf16[16,4096]{1,0:T(8,128)(2,1)}, bf16[16,4096]{1,0:T(8,128)(2,1)S(1)}, u32[]{:S(2)}, u32[]{:S(2)}) collective-permute-start(bf16[16,4096]{1,0:T(8,128)(2,1)} %refs_0_.1), channel_id=1, source_target_pairs={{0,2},{2,0},{1,3},{3,1},{4,6},{6,4},{5,7},{7,5},{8,10},{10,8},{9,1... | collective-permute-start | bytes 393224 | tf_op jit(solution)/shard_map/ppermute | solution.py:437
  2.9 4.0 %collective-permute-start.1 = (s32[2,32]{1,0:T(2,128)}, s32[2,32]{1,0:T(2,128)S(1)}, u32[]{:S(2)}, u32[]{:S(2)}) collective-permute-start(s32[2,32]{1,0:T(2,128)} %bitcast.9), channel_id=1, source_target_pairs={{0,1},{1,0},{2,3},{3,2},{4,5},{5,4},{6,7},{7,6},{8,9},{9,8},{10,11... | collective-permute-start | bytes 776 | tf_op jit(solution)/shard_map/ppermute | solution.py:437
  6.9 8.9 %collective-permute-start.5 = (bf16[32,2,128,128]{3,2,1,0:T(8,128)(2,1)S(1)}, bf16[32,2,128,128]{3,2,1,0:T(8,128)(2,1)S(1)}, u32[]{:S(2)}, u32[]{:S(2)}) collective-permute-start(bf16[32,2,128,128]{3,2,1,0:T(8,128)(2,1)S(1)} %get-tuple-element.57.refs_7_), channel_id=1, source_target_pairs={{0,1},{1,0},{2,3},{3,2},{4,5},{5,4},{6,7},{7,6},{8,9},{9,8},{10,11... | collective-permute-start | bytes 6291464 | tf_op jit(solution)/shard_map/ppermute | solution.py:437
  7.7 6.9 %collective-permute-start.2 = (bf16[144,128]{1,0:T(8,128)(2,1)S(1)}, bf16[144,128]{1,0:T(8,128)(2,1)S(1)}, u32[]{:S(2)}, u32[]{:S(2)}) collective-permute-start(bf16[144,128]{1,0:T(8,128)(2,1)S(1)} %get-tuple-element.54), channel_id=1, source_target_pairs={{0,16},{4,20},{8,24},{12,28},{16,0},{20,4},{24,8},{28,12},{1,17},{... | collective-permute-start | bytes 110600 | tf_op jit(solution)/shard_map/ppermute | solution.py:440
  10.3 4.9 %collective-permute-start.3 = (bf16[144,128]{1,0:T(8,128)(2,1)S(1)}, bf16[144,128]{1,0:T(8,128)(2,1)S(1)}, u32[]{:S(2)}, u32[]{:S(2)}) collective-permute-start(bf16[144,128]{1,0:T(8,128)(2,1)S(1)} %get-tuple-element.55), channel_id=1, source_target_pairs={{0,8},{4,12},{8,0},{12,4},{16,24},{20,28},{24,16},{28,20},{1,9},{5... | collective-permute-start | bytes 110600 | tf_op jit(solution)/shard_map/ppermute | solution.py:440
  11.9 4.0 %collective-permute-start.4 = (bf16[144,128]{1,0:T(8,128)(2,1)S(1)}, bf16[144,128]{1,0:T(8,128)(2,1)S(1)}, u32[]{:S(2)}, u32[]{:S(2)}) collective-permute-start(bf16[144,128]{1,0:T(8,128)(2,1)S(1)} %get-tuple-element.56), channel_id=1, source_target_pairs={{0,4},{4,0},{8,12},{12,8},{16,20},{20,16},{24,28},{28,24},{1,5},{5... | collective-permute-start | bytes 110600 | tf_op jit(solution)/shard_map/ppermute | solution.py:440
  14.6 3.8 %collective-permute-start.6 = (bf16[64,128]{1,0:T(8,128)(2,1)S(1)}, bf16[64,128]{1,0:T(8,128)(2,1)S(1)}, u32[]{:S(2)}, u32[]{:S(2)}) collective-permute-start(bf16[64,128]{1,0:T(8,128)(2,1)S(1)} %slice.16), channel_id=1, source_target_pairs={{0,4},{4,0},{8,12},{12,8},{16,20},{20,16},{24,28},{28,24},{1,5},{5... | collective-permute-start | bytes 49160 | tf_op jit(solution)/shard_map/ppermute | solution.py:440
  17.4 5.3 %collective-permute-start.8 = (s16[16,4352]{1,0:T(8,128)(2,1)S(1)}, s16[16,4352]{1,0:T(8,128)(2,1)S(1)}, u32[]{:S(2)}, u32[]{:S(2)}) collective-permute-start(s16[16,4352]{1,0:T(8,128)(2,1)S(1)} %get-tuple-element.72), channel_id=1, source_target_pairs={{0,2},{2,0},{1,3},{3,1},{4,6},{6,4},{5,7},{7,5},{8,10},{10,8},{9,1... | collective-permute-start | bytes 417800 | tf_op jit(solution)/shard_map/ppermute | solution.py:437
  18.4 3.7 %collective-permute-start.7 = (bf16[48,128]{1,0:T(8,128)(2,1)S(1)}, bf16[48,128]{1,0:T(8,128)(2,1)S(1)}, u32[]{:S(2)}, u32[]{:S(2)}) collective-permute-start(bf16[48,128]{1,0:T(8,128)(2,1)S(1)} %pad_maximum_fusion), channel_id=1, source_target_pairs={{0,8},{4,12},{8,0},{12,4},{16,24},{20,28},{24,16},{28,20},{1,9},{5... | collective-permute-start | bytes 36872 | tf_op jit(solution)/shard_map/ppermute | solution.py:440

commit v18 on v15

--- a/solution.py
+++ b/solution.py
@@ -232,13 +232,16 @@
             peak = jnp.max(jnp.abs(term), axis=0, keepdims=True)
             power = jnp.floor(jnp.log2(jnp.maximum(peak, 2.0**-100))) + 1.0
             steps = jnp.floor(term * (STEPS * jnp.exp2(-power)) + 0.5)
-            sent_ref[:, lanes] = steps.astype(jnp.int32).astype(jnp.int16)
+            steps = steps.astype(jnp.int32).astype(jnp.int16)
+            for copy in range(sent_ref.shape[0]):
+                sent_ref[copy, :, lanes] = steps
             power_ref[leaf : leaf + 1, :] = power
     for sent_ref, power_ref in zip(sent_refs, power_refs):
         power = power_ref[...].astype(jnp.int32).astype(jnp.int16)
         for first in range(0, leaf_count, columns):
             spot = points + first // columns * width
-            sent_ref[:, spot : spot + width] = power[first : first + columns]
+            for copy in range(sent_ref.shape[0]):
+                sent_ref[copy, :, spot : spot + width] = power[first : first + columns]
 
 
 def coupled(leaves, table_ref, coupling_ref, turned_ref):
@@ -369,12 +372,17 @@
 
 def add_kernel(leaf_count, term_ref, *refs):
     sent_refs, (out_hbm, sum_ref, sems) = refs[:-3], refs[-3:]
+    count = len(sent_refs) + 1
+    own = lax.axis_index("far")
+    sent_refs = [
+        sent_ref.at[lax.rem(own + count - part, count)] for part, sent_ref in enumerate(sent_refs, 1)
+    ]
     columns, points = sum_ref.shape
     width = points // leaf_count
     factors = []
     for sent_ref in sent_refs:
         powers = [
-            sent_ref[:, points + first // columns * width :][:, :width]
+            sent_ref[:, points + first // columns * width : points + first // columns * width + width]
             for first in range(0, leaf_count, columns)
         ]
         power = jnp.concatenate([p.astype(jnp.int32).astype(F32) for p in powers], axis=0)
@@ -523,7 +531,7 @@
     partials = pl.pallas_call(
         functools.partial(near_kernel, faces, far_groups, share),
         out_shape=[jax.ShapeDtypeStruct((columns, points), F32)]
-        + [jax.ShapeDtypeStruct((columns, points + tables), jnp.int16)] * (far_groups - 1),
+        + [jax.ShapeDtypeStruct((far_groups, columns, points + tables), jnp.int16)] * (far_groups - 1),
         in_specs=[VMEM] * (2 * share + far_groups + len(faces) + 1),
         out_specs=[VMEM] * far_groups,
         scratch_shapes=[pltpu.VMEM((leaf_count, width), F32)] * (far_groups - 1)
@@ -547,7 +555,9 @@
         cost_estimate=hint(0.7),
         name="paths",
     )(upper, cross)
-    received = [rotated(partials[part], "far", -part) for part in range(1, far_groups)]
+    received = [
+        lax.all_to_all(partials[part], "far", 0, 0, tiled=True) for part in range(1, far_groups)
+    ]
     partial = pl.pallas_call(
         project_kernel,
         out_shape=jax.ShapeDtypeStruct((columns, points), F32),

time: 23.5 us -> 28.8 us (1.23)
  starting transfers between devices: 12.3 us -> 14.8 us
  local copies, waits for them, and re-layouts: 0.01 us -> 2.2 us
  Pallas kernels: 9.57 us -> 10.4 us
  waiting for transfers between devices: 1.4 us -> 1.08 us
    all_to_all x0 -> x1, starting transfers between devices: none -> 3.44 us  [local(): lax.all_to_all(partials[part], 'far', 0, 0, tiled=True)]
    unnamed x0 -> x4, local copies, waits for them, and re-layouts: none -> 2.19 us
    ppermute x4 -> x3, starting transfers between devices: 4.47 us -> 3.52 us  [rotated(): lax.ppermute(value, axis, [(i, (i - shift) % count) for i in range(count)])]
    pallas_call x1, Pallas kernels: 1.49 us -> 2.25 us  [local(): pl.pallas_call(functools.partial(near_kernel, faces, far_groups, share),...]
    ppermute x5, waiting for transfers between devices: 1.39 us -> 1.06 us  [crossed(): lax.ppermute(value, 'leaf', [(i, i ^ turn) for i in range(leaf_devices)])]
  transfers between devices with their start and end apart: 9 -> 9, of which waited for: 2 -> 1; matrix products, arithmetic and copies ran while one was open for 0% -> 0% of each run, Pallas kernels for 38% -> 34%
where the time goes in v18:
time: 28.8 us; the launch traced here: 28.6 us
  starting transfers between devices  14.8 us (51%)
  Pallas kernels  10.4 us (36%)
  local copies, waits for them, and re-layouts  2.2 us (8%)
  waiting for transfers between devices  1.08 us (4%)
    ppermute x5, starting transfers between devices, crossed(): lax.ppermute(value, 'leaf', [(i, i ^ turn) for i in range(leaf_devices)])  7.84 us
    pallas_call x1, Pallas kernels, local(): pl.pallas_call(up_kernel, out_shape=[jax.ShapeDtypeStruct(value.shape, va...  3.97 us
    ppermute x3, starting transfers between devices, rotated(): lax.ppermute(value, axis, [(i, (i - shift) % count) for i in range(count)])  3.52 us
    all_to_all x1, starting transfers between devices, local(): lax.all_to_all(partials[part], 'far', 0, 0, tiled=True)  3.44 us
    pallas_call x1, Pallas kernels, local(): pl.pallas_call(functools.partial(near_kernel, faces, far_groups, share),...  2.25 us
    unnamed x4, local copies, waits for them, and re-layouts  2.19 us
    pallas_call x1, Pallas kernels, local(): pl.pallas_call(project_kernel, out_shape=jax.ShapeDtypeStruct((columns, p...  1.31 us
    ppermute x5, waiting for transfers between devices, crossed(): lax.ppermute(value, 'leaf', [(i, i ^ turn) for i in range(leaf_devices)])  1.06 us
  transfers between devices with their start and end apart: 9, of which 1 were waited for; matrix products, arithmetic and copies ran while one was open for 0% of the time, Pallas kernels for 34%

profile of v18, /device:TPU:0, one launch (start us, length us, event | category | flops | bytes accessed | tf_op | source)
XLA Modules:
  0.0 28.6 jit_solution(17408907215329869170)
XLA Ops:
  0.0 2.9 %collective-permute-start = (bf16[16,4096]{1,0:T(8,128)(2,1)}, bf16[16,4096]{1,0:T(8,128)(2,1)S(1)}, u32[]{:S(2)}, u32[]{:S(2)}) collective-permute-start(bf16[16,4096]{1,0:T(8,128)(2,1)} %refs_0_.1), channel_id=1, source_target_pairs={{0,2},{2,0},{1,3},{3,1},{4,6},{6,4},{5,7},{7,5},{8,10},{10,8},{9,1... | collective-permute-start | bytes 393224 | tf_op jit(solution)/shard_map/ppermute | solution.py:445
  2.9 0.0 collective-permute-start.1
  2.9 4.0 %up.1 = (f32[32,4096]{1,0:T(8,128)S(1)}, bf16[16,4096]{1,0:T(8,128)(2,1)S(1)}, s32[6,4,8]{2,1,0:T(4,128)S(1)}, s32[2,32]{1,0:T(2,128)S(1)}, s32[8,32]{1,0:T(8,12...) custom-call(f32[32,32,64]{2,1,0:T(8,128)} %bitcast.6, ...), custom_call_target="tpu_custom_call" | custom-call | bytes 12915000 | tf_op jit(solution)/shard_map/up/pallas_call | solution.py:459
  6.9 0.0 copy-start
  6.9 0.0 collective-permute-done.1.refs_1_
  6.9 0.0 collective-permute-done.refs_0_.refs_3_
  6.9 0.6 %collective-permute-start.5 = (bf16[32,2,128,128]{3,2,1,0:T(8,128)(2,1)S(1)}, bf16[32,2,128,128]{3,2,1,0:T(8,128)(2,1)S(1)}, u32[]{:S(2)}, u32[]{:S(2)}) collective-permute-start(bf16[32,2,128,128]{3,2,1,0:T(8,128)(2,1)S(1)} %get-tuple-element.57.refs_7_), channel_id=1, source_target_pairs={{0,1},{1,0},{2,3},{3,2},{4,5},{5,4},{6,7},{7,6},{8,9},{9,8},{10,11... | collective-permute-start | bytes 6291464 | tf_op jit(solution)/shard_map/ppermute | solution.py:445
  7.5 0.2 select.1
  7.7 2.7 %collective-permute-start.2 = (bf16[144,128]{1,0:T(8,128)(2,1)S(1)}, bf16[144,128]{1,0:T(8,128)(2,1)S(1)}, u32[]{:S(2)}, u32[]{:S(2)}) collective-permute-start(bf16[144,128]{1,0:T(8,128)(2,1)S(1)} %get-tuple-element.54), channel_id=1, source_target_pairs={{0,16},{4,20},{8,24},{12,28},{16,0},{20,4},{24,8},{28,12},{1,17},{... | collective-permute-start | bytes 110600 | tf_op jit(solution)/shard_map/ppermute | solution.py:448
  10.3 1.6 %collective-permute-start.3 = (bf16[144,128]{1,0:T(8,128)(2,1)S(1)}, bf16[144,128]{1,0:T(8,128)(2,1)S(1)}, u32[]{:S(2)}, u32[]{:S(2)}) collective-permute-start(bf16[144,128]{1,0:T(8,128)(2,1)S(1)} %get-tuple-element.55), channel_id=1, source_target_pairs={{0,8},{4,12},{8,0},{12,4},{16,24},{20,28},{24,16},{28,20},{1,9},{5... | collective-permute-start | bytes 110600 | tf_op jit(solution)/shard_map/ppermute | solution.py:448
  11.9 1.5 %collective-permute-start.4 = (bf16[144,128]{1,0:T(8,128)(2,1)S(1)}, bf16[144,128]{1,0:T(8,128)(2,1)S(1)}, u32[]{:S(2)}, u32[]{:S(2)}) collective-permute-start(bf16[144,128]{1,0:T(8,128)(2,1)S(1)} %get-tuple-element.56), channel_id=1, source_target_pairs={{0,4},{4,0},{8,12},{12,8},{16,20},{20,16},{24,28},{28,24},{1,5},{5... | collective-permute-start | bytes 110600 | tf_op jit(solution)/shard_map/ppermute | solution.py:448
  13.4 0.9 %couple.1 = (bf16[1024,32]{1,0:T(8,128)(2,1)S(1)}, f32[16,512]{1,0:T(8,128)S(1)}) custom-call(s32[8,32]{1,0:T(8,128)S(1)} %get-tuple-element.58.table_ref, f32[32,8,32,32]{3,2,1,0:T(8,128)S(1)} %get-tuple-element.59.coupling_ref, bf16[16,4096]{1,0:T(8,128)(2,1)S(1)} %get-tuple-element.53.dens_ref.refs_2_, f32[32,4096]{1,0:T(8,128)S(1)} %get-tuple-element.60.bases_ref), custom_call_target="tpu_custom_call" | custom-call | bytes 7380000 | tf_op jit(solution)/shard_map/couple/pallas_call | solution.py:501
  14.3 0.0 copy-done
  14.3 0.0 collective-permute-done.2.refs_4_.refs_1_
  14.3 0.5 %collective-permute-start.6 = (bf16[64,128]{1,0:T(8,128)(2,1)S(1)}, bf16[64,128]{1,0:T(8,128)(2,1)S(1)}, u32[]{:S(2)}, u32[]{:S(2)}) collective-permute-start(bf16[64,128]{1,0:T(8,128)(2,1)S(1)} %slice.16), channel_id=1, source_target_pairs={{0,8},{4,12},{8,0},{12,4},{16,24},{20,28},{24,16},{28,20},{1,9},{5... | collective-permute-start | bytes 49160 | tf_op jit(solution)/shard_map/ppermute | solution.py:448
  14.8 0.0 collective-permute-done.3.refs_5_.refs_2_
  14.8 1.0 %collective-permute-done.4.refs_6_.refs_3_ = bf16[144,128]{1,0:T(8,128)(2,1)S(1)} collective-permute-done((bf16[144,128]{1,0:T(8,128)(2,1)S(1)}, bf16[144,128]{1,0:T(8,128)(2,1)S(1)}, u32[]{:S(2)}, u32[]{:S(2)}) %collective-permute-start.4) | collective-permute-done | bytes 36896 | tf_op jit(solution)/shard_map/ppermute | solution.py:448
  15.9 0.0 collective-permute-done.5.refs_8_
  15.9 2.2 %near.1 = (f32[16,4096]{1,0:T(8,128)S(1)}, s16[2,16,4352]{2,1,0:T(8,128)(2,1)}) custom-call(s32[2,32]{1,0:T(2,128)S(1)} %get-tuple-element.44.refs_0_, s32[2,32]{1,0:T(2,128)S(1)} %collective-permute-done.1.refs_1_, bf16[16,4096]{1,0:T(8,128)(2,1)S(1)} %get-tuple-element.53.dens_ref.refs_2_, bf16[16,4096]{1,0:T(8,128)(2,1)S(1)} %collective-permute-done.refs_0_.refs_3_, ...), custom_call_target="tpu_custom_call" | custom-call | bytes 11070000 | tf_op jit(solution)/shard_map/near/pallas_call | solution.py:531
  18.1 3.4 %all-to-all-start = ((s16[2,16,4352]{2,1,0:T(8,128)(2,1)}), s16[2,16,4352]{2,1,0:T(8,128)(2,1)S(1)}, u32[]{:S(2)}, u32[]{:S(2)}) async-start(s16[2,16,4352]{2,1,0:T(8,128)(2,1)} %get-tuple-element.72), calls=%async_computation | async-start | bytes 557056 | tf_op jit(solution)/shard_map/all_to_all | solution.py:559
  21.6 0.0 collective-permute-done.6.refs_4_
  21.6 1.6 %collective-permute-start.7 = (bf16[48,128]{1,0:T(8,128)(2,1)S(1)}, bf16[48,128]{1,0:T(8,128)(2,1)S(1)}, u32[]{:S(2)}, u32[]{:S(2)}) collective-permute-start(bf16[48,128]{1,0:T(8,128)(2,1)S(1)} %pad_maximum_fusion), channel_id=1, source_target_pairs={{0,4},{4,0},{8,12},{12,8},{16,20},{20,16},{24,28},{28,24},{1,5},{5... | collective-permute-start | bytes 36872 | tf_op jit(solution)/shard_map/ppermute | solution.py:448
  23.2 0.5 %paths.1 = (bf16[32,1024]{1,0:T(8,128)(2,1)S(1)}, bf16[32,1024]{1,0:T(8,128)(2,1)S(1)}) custom-call(f32[16,32,32]{2,1,0:T(8,128)S(1)} %get-tuple-element.64.upper_ref, f32[16,3,32,32]{3,2,1,0:T(8,128)S(1)} %get-tuple-element.65.cross_ref), custom_call_target="tpu_custom_call" | custom-call | bytes 2583000 | tf_op jit(solution)/shard_map/paths/pallas_call | solution.py:548
  23.8 0.0 copy-start.1
  23.8 2.2 %copy-done.1 = f32[32,8,32,32]{3,2,1,0:T(8,128)S(1)} copy-done((f32[32,8,32,32]{3,2,1,0:T(8,128)S(1)}, f32[32,8,32,32]{3,2,1,0:T(8,128)}, u32[]{:S(2)}) %copy-start.1) | copy-done | bytes 1048600
  26.0 1.3 %project.1.term_ref = f32[16,4096]{1,0:T(8,128)S(1)} custom-call(s32[8,32]{1,0:T(8,128)S(1)} %get-tuple-element.58.table_ref, f32[32,8,32,32]{3,2,1,0:T(8,128)S(1)} %copy-done.1, bf16[1024,32]{1,0:T(8,128)(2,1)S(1)} %get-tuple-element.69.turned_ref, f32[16,512]{1,0:T(8,128)S(1)} %get-tuple-element.62.refs_9_.first_ref, ...), custom_call_target="tpu_custom_call" | custom-call | bytes 5535000 | tf_op jit(solution)/shard_map/project/pallas_call | solution.py:561
  27.3 0.0 collective-permute-done.7.refs_5_
  27.3 0.5 %far.1.term_ref = f32[16,4096]{1,0:T(8,128)S(1)} custom-call(bf16[32,1024]{1,0:T(8,128)(2,1)S(1)} %get-tuple-element.66.path_high_ref, bf16[32,1024]{1,0:T(8,128)(2,1)S(1)} %get-tuple-element.67.path_low_ref, bf16[64,4096]{1,0:T(8,128)(2,1)S(1)} %get-tuple-element.68.halves_ref, f32[16,4096]{1,0:T(8,128)S(1)} %project.1.term_ref, ...), custom_call_target="tpu_custom_call" | custom-call | bytes 2214000 | tf_op jit(solution)/shard_map/far/pallas_call | solution.py:570
  27.8 0.0 all-to-all-done.refs_0_
  27.8 0.8 %add.1 = f32[16,4096]{1,0:T(8,128)} custom-call(f32[16,4096]{1,0:T(8,128)S(1)} %far.1.term_ref, s16[2,16,4352]{2,1,0:T(8,128)(2,1)S(1)} %all-to-all-done.refs_0_), custom_call_target="tpu_custom_call" | custom-call | bytes 1845000 | tf_op jit(solution)/shard_map/add/pallas_call | solution.py:579
  (5 shorter events, 0.0 us)
Async XLA Ops:
  0.0 6.9 %collective-permute-start = (bf16[16,4096]{1,0:T(8,128)(2,1)}, bf16[16,4096]{1,0:T(8,128)(2,1)S(1)}, u32[]{:S(2)}, u32[]{:S(2)}) collective-permute-start(bf16[16,4096]{1,0:T(8,128)(2,1)} %refs_0_.1), channel_id=1, source_target_pairs={{0,2},{2,0},{1,3},{3,1},{4,6},{6,4},{5,7},{7,5},{8,10},{10,8},{9,1... | collective-permute-start | bytes 393224 | tf_op jit(solution)/shard_map/ppermute | solution.py:445
  2.9 4.0 %collective-permute-start.1 = (s32[2,32]{1,0:T(2,128)}, s32[2,32]{1,0:T(2,128)S(1)}, u32[]{:S(2)}, u32[]{:S(2)}) collective-permute-start(s32[2,32]{1,0:T(2,128)} %bitcast.9), channel_id=1, source_target_pairs={{0,1},{1,0},{2,3},{3,2},{4,5},{5,4},{6,7},{7,6},{8,9},{9,8},{10,11... | collective-permute-start | bytes 776 | tf_op jit(solution)/shard_map/ppermute | solution.py:445
  6.9 7.4 %copy-start = (f32[32,8,32,32]{3,2,1,0:T(8,128)}, f32[32,8,32,32]{3,2,1,0:T(8,128)S(1)}, u32[]{:S(2)}) copy-start(f32[32,8,32,32]{3,2,1,0:T(8,128)S(1)} %get-tuple-element.59.coupling_ref) | copy-start | bytes 3145732
  6.9 8.9 %collective-permute-start.5 = (bf16[32,2,128,128]{3,2,1,0:T(8,128)(2,1)S(1)}, bf16[32,2,128,128]{3,2,1,0:T(8,128)(2,1)S(1)}, u32[]{:S(2)}, u32[]{:S(2)}) collective-permute-start(bf16[32,2,128,128]{3,2,1,0:T(8,128)(2,1)S(1)} %get-tuple-element.57.refs_7_), channel_id=1, source_target_pairs={{0,1},{1,0},{2,3},{3,2},{4,5},{5,4},{6,7},{7,6},{8,9},{9,8},{10,11... | collective-permute-start | bytes 6291464 | tf_op jit(solution)/shard_map/ppermute | solution.py:445
  7.7 6.6 %collective-permute-start.2 = (bf16[144,128]{1,0:T(8,128)(2,1)S(1)}, bf16[144,128]{1,0:T(8,128)(2,1)S(1)}, u32[]{:S(2)}, u32[]{:S(2)}) collective-permute-start(bf16[144,128]{1,0:T(8,128)(2,1)S(1)} %get-tuple-element.54), channel_id=1, source_target_pairs={{0,16},{4,20},{8,24},{12,28},{16,0},{20,4},{24,8},{28,12},{1,17},{... | collective-permute-start | bytes 110600 | tf_op jit(solution)/shard_map/ppermute | solution.py:448
  10.3 4.5 %collective-permute-start.3 = (bf16[144,128]{1,0:T(8,128)(2,1)S(1)}, bf16[144,128]{1,0:T(8,128)(2,1)S(1)}, u32[]{:S(2)}, u32[]{:S(2)}) collective-permute-start(bf16[144,128]{1,0:T(8,128)(2,1)S(1)} %get-tuple-element.55), channel_id=1, source_target_pairs={{0,8},{4,12},{8,0},{12,4},{16,24},{20,28},{24,16},{28,20},{1,9},{5... | collective-permute-start | bytes 110600 | tf_op jit(solution)/shard_map/ppermute | solution.py:448
  11.9 4.0 %collective-permute-start.4 = (bf16[144,128]{1,0:T(8,128)(2,1)S(1)}, bf16[144,128]{1,0:T(8,128)(2,1)S(1)}, u32[]{:S(2)}, u32[]{:S(2)}) collective-permute-start(bf16[144,128]{1,0:T(8,128)(2,1)S(1)} %get-tuple-element.56), channel_id=1, source_target_pairs={{0,4},{4,0},{8,12},{12,8},{16,20},{20,16},{24,28},{28,24},{1,5},{5... | collective-permute-start | bytes 110600 | tf_op jit(solution)/shard_map/ppermute | solution.py:448
  14.3 7.3 %collective-permute-start.6 = (bf16[64,128]{1,0:T(8,128)(2,1)S(1)}, bf16[64,128]{1,0:T(8,128)(2,1)S(1)}, u32[]{:S(2)}, u32[]{:S(2)}) collective-permute-start(bf16[64,128]{1,0:T(8,128)(2,1)S(1)} %slice.16), channel_id=1, source_target_pairs={{0,8},{4,12},{8,0},{12,4},{16,24},{20,28},{24,16},{28,20},{1,9},{5... | collective-permute-start | bytes 49160 | tf_op jit(solution)/shard_map/ppermute | solution.py:448
  18.1 9.7 %all-to-all-start = ((s16[2,16,4352]{2,1,0:T(8,128)(2,1)}), s16[2,16,4352]{2,1,0:T(8,128)(2,1)S(1)}, u32[]{:S(2)}, u32[]{:S(2)}) async-start(s16[2,16,4352]{2,1,0:T(8,128)(2,1)} %get-tuple-element.72), calls=%async_computation | async-start | bytes 557056 | tf_op jit(solution)/shard_map/all_to_all | solution.py:559
  21.6 5.6 %collective-permute-start.7 = (bf16[48,128]{1,0:T(8,128)(2,1)S(1)}, bf16[48,128]{1,0:T(8,128)(2,1)S(1)}, u32[]{:S(2)}, u32[]{:S(2)}) collective-permute-start(bf16[48,128]{1,0:T(8,128)(2,1)S(1)} %pad_maximum_fusion), channel_id=1, source_target_pairs={{0,4},{4,0},{8,12},{12,8},{16,20},{20,16},{24,28},{28,24},{1,5},{5... | collective-permute-start | bytes 36872 | tf_op jit(solution)/shard_map/ppermute | solution.py:448
  23.8 2.2 %copy-start.1 = (f32[32,8,32,32]{3,2,1,0:T(8,128)S(1)}, f32[32,8,32,32]{3,2,1,0:T(8,128)}, u32[]{:S(2)}) copy-start(f32[32,8,32,32]{3,2,1,0:T(8,128)} %copy-done) | copy-start | bytes 3145732

commit v19 on v15

--- a/solution.py
+++ b/solution.py
@@ -95,7 +95,9 @@
     count = (len(refs) - 7) // 2
     hbm_refs, bases_ref, vmem_refs = refs[:count], refs[count], refs[count + 1 : 2 * count + 1]
     halves_ref, root_ref, maps_ref, spread_ref, chain_ref, sems = refs[2 * count + 1 :]
-    dens_ref = vmem_refs[0]
+    dens_ref, source_ref, shared_ref = vmem_refs[0], vmem_refs[2], vmem_refs[-1]
+    block_rows = hbm_refs[-1].shape[0]
+    vmem_refs = (*vmem_refs[:-1], shared_ref.at[pl.ds(0, block_rows)])
     copies = fetch(
         [(maps_hbm, maps_ref), (bases_hbm, bases_ref), *zip(hbm_refs, vmem_refs)], sems
     )
@@ -163,6 +165,13 @@
     root_ref[...] = packed.astype(BF16)
     for copy in copies[3:]:
         copy.wait()
+    near_count, leaf_count = source_ref.shape
+    tile_rows = shared_ref.shape[0] - block_rows
+    sources = jnp.concatenate(
+        [source_ref[...].astype(F32), jnp.zeros((near_count, LANES - leaf_count), F32)], axis=1
+    )
+    sources = jnp.concatenate([sources, jnp.zeros((tile_rows - near_count, LANES), F32)], axis=0)
+    shared_ref[block_rows:, :] = sources.astype(BF16)
 
 
 def select_kernel(
@@ -191,7 +200,6 @@
 def near_kernel(
     faces, far_groups, share, *refs,
 ):
-    source_refs, refs = refs[:share], refs[share:]
     dens_ref, refs = refs[0], refs[1:]
     other_refs, refs = refs[: far_groups - 1], refs[far_groups - 1 :]
     got_refs, refs = refs[: len(faces)], refs[len(faces) :]
@@ -202,7 +210,10 @@
     power_refs, refs = refs[: far_groups - 1], refs[far_groups - 1 :]
     (buffer_ref,) = refs
     columns, points = dens_ref.shape
-    leaf_count, near_count, width, _ = block_ref.shape
+    width = block_ref.shape[1]
+    leaf_count = points // width
+    block_rows = block_ref.shape[0] // width * width
+    near_count = block_rows // width // leaf_count
     cap = (buffer_ref.shape[0] - leaf_count) // len(FACE_SIGNS)
     for (directions, _), got_ref in zip(faces, got_refs):
         for direction in directions:
@@ -215,12 +226,14 @@
         rows = slice(part * columns, (part + 1) * columns)
         for leaf in range(leaf_count):
             buffer_ref[leaf, rows, :] = panel_ref[:, leaf * width : (leaf + 1) * width]
-    words = packed_words(jnp.concatenate([source_ref[...] for source_ref in source_refs], axis=0))
+    tables = [ref[block_rows:, :].astype(F32) for ref in (block_ref, *mate_refs)]
+    tables = jnp.concatenate([table[:near_count] for table in tables], axis=0)
+    words = packed_words(tables.astype(jnp.int32))
     own_ref, sent_refs = out_refs[0], out_refs[1:]
     for leaf in range(leaf_count):
         panels = [buffer_ref[slot] for slot in unpacked(words, near_count * share, leaf)]
         blocks = [
-            blocks_ref[leaf, block]
+            blocks_ref[(leaf * near_count + block) * width : (leaf * near_count + block + 1) * width, :]
             for blocks_ref in (block_ref, *mate_refs)
             for block in range(near_count)
         ]
@@ -441,16 +454,17 @@
 
     sources = near_src.T
     others = [rotated(densities, "far", part) for part in range(1, far_groups)]
-    all_sources = [sources] + [rotated(sources, "mate", part) for part in range(1, share)]
     send = send_leaf.transpose(1, 2, 0)
     moved = [
-        densities, send, sources, far_src.T, upper_transfer, up_coupling, leaf_coupling, near_blocks,
+        densities, send, sources, far_src.T, upper_transfer, up_coupling, leaf_coupling,
+        near_blocks.reshape(-1, width),
     ]
     (
         basis, dens, send, sources, far_table, upper, cross, coupling, blocks, subtree, root,
     ) = pl.pallas_call(
         up_kernel,
-        out_shape=[jax.ShapeDtypeStruct(value.shape, value.dtype) for value in (bases, *moved)]
+        out_shape=[jax.ShapeDtypeStruct(value.shape, value.dtype) for value in (bases, *moved[:-1])]
+        + [jax.ShapeDtypeStruct((moved[-1].shape[0] + 16, width), BF16)]
         + [
             jax.ShapeDtypeStruct((2 * rank, points), BF16),
             jax.ShapeDtypeStruct((columns, LANES), BF16),
@@ -467,11 +481,8 @@
         cost_estimate=hint(3.5),
         name="up",
     )(hbm(local_transfer[0].transpose(1, 2, 0)), hbm(bases), *map(hbm, moved))
-    all_sources[0] = sources
-
-    later_blocks, others, all_sources, root = lax.optimization_barrier(
-        (blocks, others, all_sources, root)
-    )
+
+    later_blocks, others, root = lax.optimization_barrier((blocks, others, root))
     mate_blocks = [rotated(later_blocks, "mate", part) for part in range(1, share)]
 
     if side == 2:
@@ -524,7 +535,7 @@
         functools.partial(near_kernel, faces, far_groups, share),
         out_shape=[jax.ShapeDtypeStruct((columns, points), F32)]
         + [jax.ShapeDtypeStruct((columns, points + tables), jnp.int16)] * (far_groups - 1),
-        in_specs=[VMEM] * (2 * share + far_groups + len(faces) + 1),
+        in_specs=[VMEM] * (share + far_groups + len(faces) + 1),
         out_specs=[VMEM] * far_groups,
         scratch_shapes=[pltpu.VMEM((leaf_count, width), F32)] * (far_groups - 1)
         + [
@@ -534,7 +545,7 @@
         cost_estimate=hint(3),
         name="near",
     )(
-        *all_sources, dens, *others, *arrived, blocks, *mate_blocks, leaf_local,
+        dens, *others, *arrived, blocks, *mate_blocks, leaf_local,
     )
     upper, cross, near_own = lax.optimization_barrier((upper, cross, partials[0]))
     paths = pl.pallas_call(

time: 23.5 us -> 23.5 us (level)
  Pallas kernels: 9.57 us -> 10.2 us
  starting transfers between devices: 12.3 us -> 11.7 us
    ppermute x4 -> x3, starting transfers between devices: 4.47 us -> 3.89 us  [rotated(): lax.ppermute(value, axis, [(i, (i - shift) % count) for i in range(count)])]
    pallas_call x1, Pallas kernels: 3.97 us -> 4.53 us  [local(): pl.pallas_call(up_kernel, out_shape=[jax.ShapeDtypeStruct(value.shape, va...]
  transfers between devices with their start and end apart: 9 -> 8, of which waited for: 2 -> 2; matrix products, arithmetic and copies ran while one was open for 0% -> 0% of each run, Pallas kernels for 38% -> 40%
where the time goes in v19:
time: 23.5 us; the launch traced here: 23.4 us
  starting transfers between devices  11.7 us (50%)
  Pallas kernels  10.2 us (43%)
  waiting for transfers between devices  1.38 us (6%)
    ppermute x5, starting transfers between devices, crossed(): lax.ppermute(value, 'leaf', [(i, i ^ turn) for i in range(leaf_devices)])  7.84 us
    pallas_call x1, Pallas kernels, local(): pl.pallas_call(up_kernel, out_shape=[jax.ShapeDtypeStruct(value.shape, va...  4.53 us
    ppermute x3, starting transfers between devices, rotated(): lax.ppermute(value, axis, [(i, (i - shift) % count) for i in range(count)])  3.89 us
    pallas_call x1, Pallas kernels, local(): pl.pallas_call(functools.partial(near_kernel, faces, far_groups, share),...  1.52 us
    ppermute x5, waiting for transfers between devices, crossed(): lax.ppermute(value, 'leaf', [(i, i ^ turn) for i in range(leaf_devices)])  1.37 us
    pallas_call x1, Pallas kernels, local(): pl.pallas_call(project_kernel, out_shape=jax.ShapeDtypeStruct((columns, p...  1.31 us
    pallas_call x1, Pallas kernels, local(): pl.pallas_call(couple_kernel, out_shape=[jax.ShapeDtypeStruct((leaf_count...  0.86 us
    pallas_call x1, Pallas kernels, local(): pl.pallas_call(functools.partial(add_kernel, leaf_count), out_shape=jax.S...  0.75 us
  transfers between devices with their start and end apart: 8, of which 2 were waited for; matrix products, arithmetic and copies ran while one was open for 0% of the time, Pallas kernels for 40%

profile of v19, /device:TPU:0, one launch (start us, length us, event | category | flops | bytes accessed | tf_op | source)
XLA Modules:
  0.0 23.4 jit_solution(7662970669090451341)
XLA Ops:
  0.0 2.9 %collective-permute-start = (bf16[16,4096]{1,0:T(8,128)(2,1)}, bf16[16,4096]{1,0:T(8,128)(2,1)S(1)}, u32[]{:S(2)}, u32[]{:S(2)}) collective-permute-start(bf16[16,4096]{1,0:T(8,128)(2,1)} %refs_0_.1), channel_id=1, source_target_pairs={{0,2},{2,0},{1,3},{3,1},{4,6},{6,4},{5,7},{7,5},{8,10},{10,8},{9,1... | collective-permute-start | bytes 393224 | tf_op jit(solution)/shard_map/ppermute | solution.py:450
  2.9 4.5 %up.1 = (f32[32,4096]{1,0:T(8,128)S(1)}, bf16[16,4096]{1,0:T(8,128)(2,1)S(1)}, s32[6,4,8]{2,1,0:T(4,128)S(1)}, s32[2,32]{1,0:T(2,128)}, s32[8,32]{1,0:T(8,128)S(...) custom-call(f32[32,32,64]{2,1,0:T(8,128)} %bitcast.8, ...), custom_call_target="tpu_custom_call" | custom-call | bytes 12915000 | tf_op jit(solution)/shard_map/up/pallas_call | solution.py:464
  7.5 0.0 collective-permute-done.refs_0_.refs_1_
  7.5 0.1 collective-permute-start.4
  7.6 0.2 select.1
  7.7 2.7 %collective-permute-start.1 = (bf16[144,128]{1,0:T(8,128)(2,1)S(1)}, bf16[144,128]{1,0:T(8,128)(2,1)S(1)}, u32[]{:S(2)}, u32[]{:S(2)}) collective-permute-start(bf16[144,128]{1,0:T(8,128)(2,1)S(1)} %get-tuple-element.48), channel_id=1, source_target_pairs={{0,16},{4,20},{8,24},{12,28},{16,0},{20,4},{24,8},{28,12},{1,17},{... | collective-permute-start | bytes 110600 | tf_op jit(solution)/shard_map/ppermute | solution.py:453
  10.4 1.6 %collective-permute-start.2 = (bf16[144,128]{1,0:T(8,128)(2,1)S(1)}, bf16[144,128]{1,0:T(8,128)(2,1)S(1)}, u32[]{:S(2)}, u32[]{:S(2)}) collective-permute-start(bf16[144,128]{1,0:T(8,128)(2,1)S(1)} %get-tuple-element.49), channel_id=1, source_target_pairs={{0,8},{4,12},{8,0},{12,4},{16,24},{20,28},{24,16},{28,20},{1,9},{5... | collective-permute-start | bytes 110600 | tf_op jit(solution)/shard_map/ppermute | solution.py:453
  12.0 1.5 %collective-permute-start.3 = (bf16[144,128]{1,0:T(8,128)(2,1)S(1)}, bf16[144,128]{1,0:T(8,128)(2,1)S(1)}, u32[]{:S(2)}, u32[]{:S(2)}) collective-permute-start(bf16[144,128]{1,0:T(8,128)(2,1)S(1)} %get-tuple-element.50), channel_id=1, source_target_pairs={{0,4},{4,0},{8,12},{12,8},{16,20},{20,16},{24,28},{28,24},{1,5},{5... | collective-permute-start | bytes 110600 | tf_op jit(solution)/shard_map/ppermute | solution.py:453
  13.5 0.9 %couple.1 = (bf16[1024,32]{1,0:T(8,128)(2,1)S(1)}, f32[16,512]{1,0:T(8,128)S(1)}) custom-call(s32[8,32]{1,0:T(8,128)S(1)} %get-tuple-element.52.table_ref, f32[32,8,32,32]{3,2,1,0:T(8,128)S(1)} %get-tuple-element.53.coupling_ref, bf16[16,4096]{1,0:T(8,128)(2,1)S(1)} %get-tuple-element.47.dens_ref.refs_0_, f32[32,4096]{1,0:T(8,128)S(1)} %get-tuple-element.54.bases_ref), custom_call_target="tpu_custom_call" | custom-call | bytes 7380000 | tf_op jit(solution)/shard_map/couple/pallas_call | solution.py:504
  14.3 0.0 collective-permute-done.1.refs_2_.refs_1_
  14.4 0.5 %collective-permute-start.5 = (bf16[64,128]{1,0:T(8,128)(2,1)S(1)}, bf16[64,128]{1,0:T(8,128)(2,1)S(1)}, u32[]{:S(2)}, u32[]{:S(2)}) collective-permute-start(bf16[64,128]{1,0:T(8,128)(2,1)S(1)} %slice.16), channel_id=1, source_target_pairs={{0,8},{4,12},{8,0},{12,4},{16,24},{20,28},{24,16},{28,20},{1,9},{5... | collective-permute-start | bytes 49160 | tf_op jit(solution)/shard_map/ppermute | solution.py:453
  14.9 0.0 collective-permute-done.2.refs_3_.refs_2_
  14.9 1.0 %collective-permute-done.3.refs_4_.refs_3_ = bf16[144,128]{1,0:T(8,128)(2,1)S(1)} collective-permute-done((bf16[144,128]{1,0:T(8,128)(2,1)S(1)}, bf16[144,128]{1,0:T(8,128)(2,1)S(1)}, u32[]{:S(2)}, u32[]{:S(2)}) %collective-permute-start.3) | collective-permute-done | bytes 36896 | tf_op jit(solution)/shard_map/ppermute | solution.py:453
  15.9 0.0 collective-permute-done.4.refs_6_
  15.9 1.5 %near.1 = (f32[16,4096]{1,0:T(8,128)S(1)}, s16[16,4352]{1,0:T(8,128)(2,1)S(1)}) custom-call(bf16[16,4096]{1,0:T(8,128)(2,1)S(1)} %get-tuple-element.47.dens_ref.refs_0_, bf16[16,4096]{1,0:T(8,128)(2,1)S(1)} %collective-permute-done.refs_0_.refs_1_, bf16[144,128]{1,0:T(8,128)(2,1)S(1)} %collective-permute-done.1.refs_2_.refs_1_, ...), custom_call_target="tpu_custom_call" | custom-call | bytes 11070000 | tf_op jit(solution)/shard_map/near/pallas_call | solution.py:534
  17.5 0.9 %collective-permute-start.7 = (s16[16,4352]{1,0:T(8,128)(2,1)S(1)}, s16[16,4352]{1,0:T(8,128)(2,1)S(1)}, u32[]{:S(2)}, u32[]{:S(2)}) collective-permute-start(s16[16,4352]{1,0:T(8,128)(2,1)S(1)} %get-tuple-element.66), channel_id=1, source_target_pairs={{0,2},{2,0},{1,3},{3,1},{4,6},{6,4},{5,7},{7,5},{8,10},{10,8},{9,1... | collective-permute-start | bytes 417800 | tf_op jit(solution)/shard_map/ppermute | solution.py:450
  18.3 0.0 collective-permute-done.5.refs_4_
  18.4 1.6 %collective-permute-start.6 = (bf16[48,128]{1,0:T(8,128)(2,1)S(1)}, bf16[48,128]{1,0:T(8,128)(2,1)S(1)}, u32[]{:S(2)}, u32[]{:S(2)}) collective-permute-start(bf16[48,128]{1,0:T(8,128)(2,1)S(1)} %pad_maximum_fusion), channel_id=1, source_target_pairs={{0,4},{4,0},{8,12},{12,8},{16,20},{20,16},{24,28},{28,24},{1,5},{5... | collective-permute-start | bytes 36872 | tf_op jit(solution)/shard_map/ppermute | solution.py:453
  20.0 0.5 %paths.1 = (bf16[32,1024]{1,0:T(8,128)(2,1)S(1)}, bf16[32,1024]{1,0:T(8,128)(2,1)S(1)}) custom-call(f32[16,32,32]{2,1,0:T(8,128)S(1)} %get-tuple-element.58.upper_ref, f32[16,3,32,32]{3,2,1,0:T(8,128)S(1)} %get-tuple-element.59.cross_ref), custom_call_target="tpu_custom_call" | custom-call | bytes 2583000 | tf_op jit(solution)/shard_map/paths/pallas_call | solution.py:551
  20.5 1.3 %project.1.term_ref = f32[16,4096]{1,0:T(8,128)S(1)} custom-call(s32[8,32]{1,0:T(8,128)S(1)} %get-tuple-element.52.table_ref, f32[32,8,32,32]{3,2,1,0:T(8,128)S(1)} %get-tuple-element.53.coupling_ref, bf16[1024,32]{1,0:T(8,128)(2,1)S(1)} %get-tuple-element.63.turned_ref, f32[16,512]{1,0:T(8,128)S(1)} %get-tuple-element.56.refs_7_.first_ref, ...), custom_call_target="tpu_custom_call" | custom-call | bytes 5535000 | tf_op jit(solution)/shard_map/project/pallas_call | solution.py:562
  21.8 0.3 %collective-permute-done.6.refs_5_ = bf16[48,128]{1,0:T(8,128)(2,1)S(1)} collective-permute-done((bf16[48,128]{1,0:T(8,128)(2,1)S(1)}, bf16[48,128]{1,0:T(8,128)(2,1)S(1)}, u32[]{:S(2)}, u32[]{:S(2)}) %collective-permute-start.6) | collective-permute-done | bytes 12320 | tf_op jit(solution)/shard_map/ppermute | solution.py:453
  22.1 0.5 %far.1.term_ref = f32[16,4096]{1,0:T(8,128)S(1)} custom-call(bf16[32,1024]{1,0:T(8,128)(2,1)S(1)} %get-tuple-element.60.path_high_ref, bf16[32,1024]{1,0:T(8,128)(2,1)S(1)} %get-tuple-element.61.path_low_ref, bf16[64,4096]{1,0:T(8,128)(2,1)S(1)} %get-tuple-element.62.halves_ref, f32[16,4096]{1,0:T(8,128)S(1)} %project.1.term_ref, ...), custom_call_target="tpu_custom_call" | custom-call | bytes 2214000 | tf_op jit(solution)/shard_map/far/pallas_call | solution.py:571
  22.6 0.0 collective-permute-done.7.refs_0_
  22.7 0.8 %add.1 = f32[16,4096]{1,0:T(8,128)} custom-call(f32[16,4096]{1,0:T(8,128)S(1)} %far.1.term_ref, s16[16,4352]{1,0:T(8,128)(2,1)S(1)} %collective-permute-done.7.refs_0_), custom_call_target="tpu_custom_call" | custom-call | bytes 1845000 | tf_op jit(solution)/shard_map/add/pallas_call | solution.py:580
  (5 shorter events, 0.0 us)
Async XLA Ops:
  0.0 7.5 %collective-permute-start = (bf16[16,4096]{1,0:T(8,128)(2,1)}, bf16[16,4096]{1,0:T(8,128)(2,1)S(1)}, u32[]{:S(2)}, u32[]{:S(2)}) collective-permute-start(bf16[16,4096]{1,0:T(8,128)(2,1)} %refs_0_.1), channel_id=1, source_target_pairs={{0,2},{2,0},{1,3},{3,1},{4,6},{6,4},{5,7},{7,5},{8,10},{10,8},{9,1... | collective-permute-start | bytes 393224 | tf_op jit(solution)/shard_map/ppermute | solution.py:450
  7.5 8.5 %collective-permute-start.4 = (bf16[8208,128]{1,0:T(8,128)(2,1)S(1)}, bf16[8208,128]{1,0:T(8,128)(2,1)S(1)}, u32[]{:S(2)}, u32[]{:S(2)}) collective-permute-start(bf16[8208,128]{1,0:T(8,128)(2,1)S(1)} %get-tuple-element.51.refs_5_), channel_id=1, source_target_pairs={{0,1},{1,0},{2,3},{3,2},{4,5},{5,4},{6,7},{7,6},{8,9},{9,8},{10,11... | collective-permute-start | bytes 6303752 | tf_op jit(solution)/shard_map/ppermute | solution.py:450
  7.7 6.6 %collective-permute-start.1 = (bf16[144,128]{1,0:T(8,128)(2,1)S(1)}, bf16[144,128]{1,0:T(8,128)(2,1)S(1)}, u32[]{:S(2)}, u32[]{:S(2)}) collective-permute-start(bf16[144,128]{1,0:T(8,128)(2,1)S(1)} %get-tuple-element.48), channel_id=1, source_target_pairs={{0,16},{4,20},{8,24},{12,28},{16,0},{20,4},{24,8},{28,12},{1,17},{... | collective-permute-start | bytes 110600 | tf_op jit(solution)/shard_map/ppermute | solution.py:453
  10.4 4.5 %collective-permute-start.2 = (bf16[144,128]{1,0:T(8,128)(2,1)S(1)}, bf16[144,128]{1,0:T(8,128)(2,1)S(1)}, u32[]{:S(2)}, u32[]{:S(2)}) collective-permute-start(bf16[144,128]{1,0:T(8,128)(2,1)S(1)} %get-tuple-element.49), channel_id=1, source_target_pairs={{0,8},{4,12},{8,0},{12,4},{16,24},{20,28},{24,16},{28,20},{1,9},{5... | collective-permute-start | bytes 110600 | tf_op jit(solution)/shard_map/ppermute | solution.py:453
  12.0 4.0 %collective-permute-start.3 = (bf16[144,128]{1,0:T(8,128)(2,1)S(1)}, bf16[144,128]{1,0:T(8,128)(2,1)S(1)}, u32[]{:S(2)}, u32[]{:S(2)}) collective-permute-start(bf16[144,128]{1,0:T(8,128)(2,1)S(1)} %get-tuple-element.50), channel_id=1, source_target_pairs={{0,4},{4,0},{8,12},{12,8},{16,20},{20,16},{24,28},{28,24},{1,5},{5... | collective-permute-start | bytes 110600 | tf_op jit(solution)/shard_map/ppermute | solution.py:453
  14.4 4.0 %collective-permute-start.5 = (bf16[64,128]{1,0:T(8,128)(2,1)S(1)}, bf16[64,128]{1,0:T(8,128)(2,1)S(1)}, u32[]{:S(2)}, u32[]{:S(2)}) collective-permute-start(bf16[64,128]{1,0:T(8,128)(2,1)S(1)} %slice.16), channel_id=1, source_target_pairs={{0,8},{4,12},{8,0},{12,4},{16,24},{20,28},{24,16},{28,20},{1,9},{5... | collective-permute-start | bytes 49160 | tf_op jit(solution)/shard_map/ppermute | solution.py:453
  17.5 5.2 %collective-permute-start.7 = (s16[16,4352]{1,0:T(8,128)(2,1)S(1)}, s16[16,4352]{1,0:T(8,128)(2,1)S(1)}, u32[]{:S(2)}, u32[]{:S(2)}) collective-permute-start(s16[16,4352]{1,0:T(8,128)(2,1)S(1)} %get-tuple-element.66), channel_id=1, source_target_pairs={{0,2},{2,0},{1,3},{3,1},{4,6},{6,4},{5,7},{7,5},{8,10},{10,8},{9,1... | collective-permute-start | bytes 417800 | tf_op jit(solution)/shard_map/ppermute | solution.py:450
  18.4 3.8 %collective-permute-start.6 = (bf16[48,128]{1,0:T(8,128)(2,1)S(1)}, bf16[48,128]{1,0:T(8,128)(2,1)S(1)}, u32[]{:S(2)}, u32[]{:S(2)}) collective-permute-start(bf16[48,128]{1,0:T(8,128)(2,1)S(1)} %pad_maximum_fusion), channel_id=1, source_target_pairs={{0,4},{4,0},{8,12},{12,8},{16,20},{20,16},{24,28},{28,24},{1,5},{5... | collective-permute-start | bytes 36872 | tf_op jit(solution)/shard_map/ppermute | solution.py:453

commit v20 on v19

--- a/solution.py
+++ b/solution.py
@@ -141,6 +141,14 @@
         level *= 2
     copies[1].wait()
     copies[2].wait()
+    copies[4].wait()
+    near_count = source_ref.shape[0]
+    tile_rows = shared_ref.shape[0] - block_rows
+    sources = jnp.concatenate(
+        [source_ref[...].astype(F32), jnp.zeros((near_count, LANES - leaf_count), F32)], axis=1
+    )
+    sources = jnp.concatenate([sources, jnp.zeros((tile_rows - near_count, LANES), F32)], axis=0)
+    shared_ref[block_rows:, :] = sources.astype(BF16)
     step = group * width
     root = jnp.zeros((columns, rank), F32)
     for index in range(leaf_count // group):
@@ -163,15 +171,9 @@
     last = (rest - middle).astype(BF16).astype(F32)
     packed = high + pltpu.roll(middle, rank, 1) + pltpu.roll(last, 2 * rank, 1)
     root_ref[...] = packed.astype(BF16)
-    for copy in copies[3:]:
+    copies[3].wait()
+    for copy in copies[5:]:
         copy.wait()
-    near_count, leaf_count = source_ref.shape
-    tile_rows = shared_ref.shape[0] - block_rows
-    sources = jnp.concatenate(
-        [source_ref[...].astype(F32), jnp.zeros((near_count, LANES - leaf_count), F32)], axis=1
-    )
-    sources = jnp.concatenate([sources, jnp.zeros((tile_rows - near_count, LANES), F32)], axis=0)
-    shared_ref[block_rows:, :] = sources.astype(BF16)
 
 
 def select_kernel(

time: 23.5 us -> 23.6 us (level)
  no operation moved by 1% of the time
where the time goes in v20:
time: 23.6 us; the launch traced here: 23.4 us
  starting transfers between devices  11.7 us (50%)
  Pallas kernels  10.2 us (43%)
  waiting for transfers between devices  1.37 us (6%)
    ppermute x5, starting transfers between devices, crossed(): lax.ppermute(value, 'leaf', [(i, i ^ turn) for i in range(leaf_devices)])  7.85 us
    pallas_call x1, Pallas kernels, local(): pl.pallas_call(up_kernel, out_shape=[jax.ShapeDtypeStruct(value.shape, va...  4.52 us
    ppermute x3, starting transfers between devices, rotated(): lax.ppermute(value, axis, [(i, (i - shift) % count) for i in range(count)])  3.9 us
    pallas_call x1, Pallas kernels, local(): pl.pallas_call(functools.partial(near_kernel, faces, far_groups, share),...  1.52 us
    ppermute x5, waiting for transfers between devices, crossed(): lax.ppermute(value, 'leaf', [(i, i ^ turn) for i in range(leaf_devices)])  1.36 us
    pallas_call x1, Pallas kernels, local(): pl.pallas_call(project_kernel, out_shape=jax.ShapeDtypeStruct((columns, p...  1.31 us
    pallas_call x1, Pallas kernels, local(): pl.pallas_call(couple_kernel, out_shape=[jax.ShapeDtypeStruct((leaf_count...  0.85 us
    pallas_call x1, Pallas kernels, local(): pl.pallas_call(functools.partial(add_kernel, leaf_count), out_shape=jax.S...  0.75 us
  transfers between devices with their start and end apart: 8, of which 2 were waited for; matrix products, arithmetic and copies ran while one was open for 0% of the time, Pallas kernels for 40%

profile of v20, /device:TPU:0, one launch (start us, length us, event | category | flops | bytes accessed | tf_op | source)
XLA Modules:
  0.0 23.4 jit_solution(146918936980300710)
XLA Ops:
  0.0 2.9 %collective-permute-start = (bf16[16,4096]{1,0:T(8,128)(2,1)}, bf16[16,4096]{1,0:T(8,128)(2,1)S(1)}, u32[]{:S(2)}, u32[]{:S(2)}) collective-permute-start(bf16[16,4096]{1,0:T(8,128)(2,1)} %refs_0_.1), channel_id=1, source_target_pairs={{0,2},{2,0},{1,3},{3,1},{4,6},{6,4},{5,7},{7,5},{8,10},{10,8},{9,1... | collective-permute-start | bytes 393224 | tf_op jit(solution)/shard_map/ppermute | solution.py:452
  2.9 4.5 %up.1 = (f32[32,4096]{1,0:T(8,128)S(1)}, bf16[16,4096]{1,0:T(8,128)(2,1)S(1)}, s32[6,4,8]{2,1,0:T(4,128)S(1)}, s32[2,32]{1,0:T(2,128)}, s32[8,32]{1,0:T(8,128)S(...) custom-call(f32[32,32,64]{2,1,0:T(8,128)} %bitcast.8, ...), custom_call_target="tpu_custom_call" | custom-call | bytes 12915000 | tf_op jit(solution)/shard_map/up/pallas_call | solution.py:466
  7.5 0.0 collective-permute-done.refs_0_.refs_1_
  7.5 0.1 collective-permute-start.4
  7.6 0.2 select.1
  7.7 2.7 %collective-permute-start.1 = (bf16[144,128]{1,0:T(8,128)(2,1)S(1)}, bf16[144,128]{1,0:T(8,128)(2,1)S(1)}, u32[]{:S(2)}, u32[]{:S(2)}) collective-permute-start(bf16[144,128]{1,0:T(8,128)(2,1)S(1)} %get-tuple-element.48), channel_id=1, source_target_pairs={{0,16},{4,20},{8,24},{12,28},{16,0},{20,4},{24,8},{28,12},{1,17},{... | collective-permute-start | bytes 110600 | tf_op jit(solution)/shard_map/ppermute | solution.py:455
  10.4 1.6 %collective-permute-start.2 = (bf16[144,128]{1,0:T(8,128)(2,1)S(1)}, bf16[144,128]{1,0:T(8,128)(2,1)S(1)}, u32[]{:S(2)}, u32[]{:S(2)}) collective-permute-start(bf16[144,128]{1,0:T(8,128)(2,1)S(1)} %get-tuple-element.49), channel_id=1, source_target_pairs={{0,8},{4,12},{8,0},{12,4},{16,24},{20,28},{24,16},{28,20},{1,9},{5... | collective-permute-start | bytes 110600 | tf_op jit(solution)/shard_map/ppermute | solution.py:455
  12.0 1.5 %collective-permute-start.3 = (bf16[144,128]{1,0:T(8,128)(2,1)S(1)}, bf16[144,128]{1,0:T(8,128)(2,1)S(1)}, u32[]{:S(2)}, u32[]{:S(2)}) collective-permute-start(bf16[144,128]{1,0:T(8,128)(2,1)S(1)} %get-tuple-element.50), channel_id=1, source_target_pairs={{0,4},{4,0},{8,12},{12,8},{16,20},{20,16},{24,28},{28,24},{1,5},{5... | collective-permute-start | bytes 110600 | tf_op jit(solution)/shard_map/ppermute | solution.py:455
  13.5 0.9 %couple.1 = (bf16[1024,32]{1,0:T(8,128)(2,1)S(1)}, f32[16,512]{1,0:T(8,128)S(1)}) custom-call(s32[8,32]{1,0:T(8,128)S(1)} %get-tuple-element.52.table_ref, f32[32,8,32,32]{3,2,1,0:T(8,128)S(1)} %get-tuple-element.53.coupling_ref, bf16[16,4096]{1,0:T(8,128)(2,1)S(1)} %get-tuple-element.47.dens_ref.refs_0_, f32[32,4096]{1,0:T(8,128)S(1)} %get-tuple-element.54.bases_ref), custom_call_target="tpu_custom_call" | custom-call | bytes 7380000 | tf_op jit(solution)/shard_map/couple/pallas_call | solution.py:506
  14.3 0.0 collective-permute-done.1.refs_2_.refs_1_
  14.4 0.5 %collective-permute-start.5 = (bf16[64,128]{1,0:T(8,128)(2,1)S(1)}, bf16[64,128]{1,0:T(8,128)(2,1)S(1)}, u32[]{:S(2)}, u32[]{:S(2)}) collective-permute-start(bf16[64,128]{1,0:T(8,128)(2,1)S(1)} %slice.16), channel_id=1, source_target_pairs={{0,8},{4,12},{8,0},{12,4},{16,24},{20,28},{24,16},{28,20},{1,9},{5... | collective-permute-start | bytes 49160 | tf_op jit(solution)/shard_map/ppermute | solution.py:455
  14.9 0.0 collective-permute-done.2.refs_3_.refs_2_
  14.9 1.0 %collective-permute-done.3.refs_4_.refs_3_ = bf16[144,128]{1,0:T(8,128)(2,1)S(1)} collective-permute-done((bf16[144,128]{1,0:T(8,128)(2,1)S(1)}, bf16[144,128]{1,0:T(8,128)(2,1)S(1)}, u32[]{:S(2)}, u32[]{:S(2)}) %collective-permute-start.3) | collective-permute-done | bytes 36896 | tf_op jit(solution)/shard_map/ppermute | solution.py:455
  15.9 0.0 collective-permute-done.4.refs_6_
  15.9 1.5 %near.1 = (f32[16,4096]{1,0:T(8,128)S(1)}, s16[16,4352]{1,0:T(8,128)(2,1)S(1)}) custom-call(bf16[16,4096]{1,0:T(8,128)(2,1)S(1)} %get-tuple-element.47.dens_ref.refs_0_, bf16[16,4096]{1,0:T(8,128)(2,1)S(1)} %collective-permute-done.refs_0_.refs_1_, bf16[144,128]{1,0:T(8,128)(2,1)S(1)} %collective-permute-done.1.refs_2_.refs_1_, ...), custom_call_target="tpu_custom_call" | custom-call | bytes 11070000 | tf_op jit(solution)/shard_map/near/pallas_call | solution.py:536
  17.5 0.9 %collective-permute-start.7 = (s16[16,4352]{1,0:T(8,128)(2,1)S(1)}, s16[16,4352]{1,0:T(8,128)(2,1)S(1)}, u32[]{:S(2)}, u32[]{:S(2)}) collective-permute-start(s16[16,4352]{1,0:T(8,128)(2,1)S(1)} %get-tuple-element.66), channel_id=1, source_target_pairs={{0,2},{2,0},{1,3},{3,1},{4,6},{6,4},{5,7},{7,5},{8,10},{10,8},{9,1... | collective-permute-start | bytes 417800 | tf_op jit(solution)/shard_map/ppermute | solution.py:452
  18.4 0.0 collective-permute-done.5.refs_4_
  18.4 1.6 %collective-permute-start.6 = (bf16[48,128]{1,0:T(8,128)(2,1)S(1)}, bf16[48,128]{1,0:T(8,128)(2,1)S(1)}, u32[]{:S(2)}, u32[]{:S(2)}) collective-permute-start(bf16[48,128]{1,0:T(8,128)(2,1)S(1)} %pad_maximum_fusion), channel_id=1, source_target_pairs={{0,4},{4,0},{8,12},{12,8},{16,20},{20,16},{24,28},{28,24},{1,5},{5... | collective-permute-start | bytes 36872 | tf_op jit(solution)/shard_map/ppermute | solution.py:455
  20.0 0.5 %paths.1 = (bf16[32,1024]{1,0:T(8,128)(2,1)S(1)}, bf16[32,1024]{1,0:T(8,128)(2,1)S(1)}) custom-call(f32[16,32,32]{2,1,0:T(8,128)S(1)} %get-tuple-element.58.upper_ref, f32[16,3,32,32]{3,2,1,0:T(8,128)S(1)} %get-tuple-element.59.cross_ref), custom_call_target="tpu_custom_call" | custom-call | bytes 2583000 | tf_op jit(solution)/shard_map/paths/pallas_call | solution.py:553
  20.5 1.3 %project.1.term_ref = f32[16,4096]{1,0:T(8,128)S(1)} custom-call(s32[8,32]{1,0:T(8,128)S(1)} %get-tuple-element.52.table_ref, f32[32,8,32,32]{3,2,1,0:T(8,128)S(1)} %get-tuple-element.53.coupling_ref, bf16[1024,32]{1,0:T(8,128)(2,1)S(1)} %get-tuple-element.63.turned_ref, f32[16,512]{1,0:T(8,128)S(1)} %get-tuple-element.56.refs_7_.first_ref, ...), custom_call_target="tpu_custom_call" | custom-call | bytes 5535000 | tf_op jit(solution)/shard_map/project/pallas_call | solution.py:564
  21.8 0.3 %collective-permute-done.6.refs_5_ = bf16[48,128]{1,0:T(8,128)(2,1)S(1)} collective-permute-done((bf16[48,128]{1,0:T(8,128)(2,1)S(1)}, bf16[48,128]{1,0:T(8,128)(2,1)S(1)}, u32[]{:S(2)}, u32[]{:S(2)}) %collective-permute-start.6) | collective-permute-done | bytes 12320 | tf_op jit(solution)/shard_map/ppermute | solution.py:455
  22.1 0.5 %far.1.term_ref = f32[16,4096]{1,0:T(8,128)S(1)} custom-call(bf16[32,1024]{1,0:T(8,128)(2,1)S(1)} %get-tuple-element.60.path_high_ref, bf16[32,1024]{1,0:T(8,128)(2,1)S(1)} %get-tuple-element.61.path_low_ref, bf16[64,4096]{1,0:T(8,128)(2,1)S(1)} %get-tuple-element.62.halves_ref, f32[16,4096]{1,0:T(8,128)S(1)} %project.1.term_ref, ...), custom_call_target="tpu_custom_call" | custom-call | bytes 2214000 | tf_op jit(solution)/shard_map/far/pallas_call | solution.py:573
  22.7 0.0 collective-permute-done.7.refs_0_
  22.7 0.8 %add.1 = f32[16,4096]{1,0:T(8,128)} custom-call(f32[16,4096]{1,0:T(8,128)S(1)} %far.1.term_ref, s16[16,4352]{1,0:T(8,128)(2,1)S(1)} %collective-permute-done.7.refs_0_), custom_call_target="tpu_custom_call" | custom-call | bytes 1845000 | tf_op jit(solution)/shard_map/add/pallas_call | solution.py:582
  (5 shorter events, 0.0 us)
Async XLA Ops:
  0.0 7.5 %collective-permute-start = (bf16[16,4096]{1,0:T(8,128)(2,1)}, bf16[16,4096]{1,0:T(8,128)(2,1)S(1)}, u32[]{:S(2)}, u32[]{:S(2)}) collective-permute-start(bf16[16,4096]{1,0:T(8,128)(2,1)} %refs_0_.1), channel_id=1, source_target_pairs={{0,2},{2,0},{1,3},{3,1},{4,6},{6,4},{5,7},{7,5},{8,10},{10,8},{9,1... | collective-permute-start | bytes 393224 | tf_op jit(solution)/shard_map/ppermute | solution.py:452
  7.5 8.5 %collective-permute-start.4 = (bf16[8208,128]{1,0:T(8,128)(2,1)S(1)}, bf16[8208,128]{1,0:T(8,128)(2,1)S(1)}, u32[]{:S(2)}, u32[]{:S(2)}) collective-permute-start(bf16[8208,128]{1,0:T(8,128)(2,1)S(1)} %get-tuple-element.51.refs_5_), channel_id=1, source_target_pairs={{0,1},{1,0},{2,3},{3,2},{4,5},{5,4},{6,7},{7,6},{8,9},{9,8},{10,11... | collective-permute-start | bytes 6303752 | tf_op jit(solution)/shard_map/ppermute | solution.py:452
  7.7 6.6 %collective-permute-start.1 = (bf16[144,128]{1,0:T(8,128)(2,1)S(1)}, bf16[144,128]{1,0:T(8,128)(2,1)S(1)}, u32[]{:S(2)}, u32[]{:S(2)}) collective-permute-start(bf16[144,128]{1,0:T(8,128)(2,1)S(1)} %get-tuple-element.48), channel_id=1, source_target_pairs={{0,16},{4,20},{8,24},{12,28},{16,0},{20,4},{24,8},{28,12},{1,17},{... | collective-permute-start | bytes 110600 | tf_op jit(solution)/shard_map/ppermute | solution.py:455
  10.4 4.5 %collective-permute-start.2 = (bf16[144,128]{1,0:T(8,128)(2,1)S(1)}, bf16[144,128]{1,0:T(8,128)(2,1)S(1)}, u32[]{:S(2)}, u32[]{:S(2)}) collective-permute-start(bf16[144,128]{1,0:T(8,128)(2,1)S(1)} %get-tuple-element.49), channel_id=1, source_target_pairs={{0,8},{4,12},{8,0},{12,4},{16,24},{20,28},{24,16},{28,20},{1,9},{5... | collective-permute-start | bytes 110600 | tf_op jit(solution)/shard_map/ppermute | solution.py:455
  12.0 4.0 %collective-permute-start.3 = (bf16[144,128]{1,0:T(8,128)(2,1)S(1)}, bf16[144,128]{1,0:T(8,128)(2,1)S(1)}, u32[]{:S(2)}, u32[]{:S(2)}) collective-permute-start(bf16[144,128]{1,0:T(8,128)(2,1)S(1)} %get-tuple-element.50), channel_id=1, source_target_pairs={{0,4},{4,0},{8,12},{12,8},{16,20},{20,16},{24,28},{28,24},{1,5},{5... | collective-permute-start | bytes 110600 | tf_op jit(solution)/shard_map/ppermute | solution.py:455
  14.4 4.0 %collective-permute-start.5 = (bf16[64,128]{1,0:T(8,128)(2,1)S(1)}, bf16[64,128]{1,0:T(8,128)(2,1)S(1)}, u32[]{:S(2)}, u32[]{:S(2)}) collective-permute-start(bf16[64,128]{1,0:T(8,128)(2,1)S(1)} %slice.16), channel_id=1, source_target_pairs={{0,8},{4,12},{8,0},{12,4},{16,24},{20,28},{24,16},{28,20},{1,9},{5... | collective-permute-start | bytes 49160 | tf_op jit(solution)/shard_map/ppermute | solution.py:455
  17.5 5.2 %collective-permute-start.7 = (s16[16,4352]{1,0:T(8,128)(2,1)S(1)}, s16[16,4352]{1,0:T(8,128)(2,1)S(1)}, u32[]{:S(2)}, u32[]{:S(2)}) collective-permute-start(s16[16,4352]{1,0:T(8,128)(2,1)S(1)} %get-tuple-element.66), channel_id=1, source_target_pairs={{0,2},{2,0},{1,3},{3,1},{4,6},{6,4},{5,7},{7,5},{8,10},{10,8},{9,1... | collective-permute-start | bytes 417800 | tf_op jit(solution)/shard_map/ppermute | solution.py:452
  18.4 3.8 %collective-permute-start.6 = (bf16[48,128]{1,0:T(8,128)(2,1)S(1)}, bf16[48,128]{1,0:T(8,128)(2,1)S(1)}, u32[]{:S(2)}, u32[]{:S(2)}) collective-permute-start(bf16[48,128]{1,0:T(8,128)(2,1)S(1)} %pad_maximum_fusion), channel_id=1, source_target_pairs={{0,4},{4,0},{8,12},{12,8},{16,20},{20,16},{24,28},{28,24},{1,5},{5... | collective-permute-start | bytes 36872 | tf_op jit(solution)/shard_map/ppermute | solution.py:455

commit v21 on v20

--- a/solution.py
+++ b/solution.py
@@ -92,15 +92,17 @@
 def up_kernel(
     maps_hbm, bases_hbm, *refs,
 ):
-    count = (len(refs) - 7) // 2
+    count = (len(refs) - 8) // 2
     hbm_refs, bases_ref, vmem_refs = refs[:count], refs[count], refs[count + 1 : 2 * count + 1]
-    halves_ref, root_ref, maps_ref, spread_ref, chain_ref, sems = refs[2 * count + 1 :]
+    halves_ref, root_ref, maps_ref, spread_ref, chain_ref, sems, chunk_sems = refs[2 * count + 1 :]
     dens_ref, source_ref, shared_ref = vmem_refs[0], vmem_refs[2], vmem_refs[-1]
     block_rows = hbm_refs[-1].shape[0]
-    vmem_refs = (*vmem_refs[:-1], shared_ref.at[pl.ds(0, block_rows)])
+    pieces = chunk_sems.shape[0]
+    pieces = [pl.ds(index * (block_rows // pieces), block_rows // pieces) for index in range(pieces)]
     copies = fetch(
-        [(maps_hbm, maps_ref), (bases_hbm, bases_ref), *zip(hbm_refs, vmem_refs)], sems
+        [(maps_hbm, maps_ref), (bases_hbm, bases_ref), *zip(hbm_refs[:-1], vmem_refs[:-1])], sems
     )
+    copies += fetch([(hbm_refs[-1].at[piece], shared_ref.at[piece]) for piece in pieces], chunk_sems)
     columns, points = dens_ref.shape
     rank, _, node_count = maps_ref.shape
     group = LANES // rank
@@ -477,7 +479,8 @@
             pltpu.VMEM((rank, rank, node_count), F32),
             pltpu.VMEM((node_count * rank, LANES), F32),
             pltpu.VMEM((rank, node_count * rank), F32),
-            dma((2 + len(moved),)),
+            dma((1 + len(moved),)),
+            dma((8,)),
         ],
         compiler_params=params,
         cost_estimate=hint(3.5),

time: 23.6 us -> 23.7 us (level)
  transfers between devices with their start and end apart: 8 -> 8, of which waited for: 2 -> 4; matrix products, arithmetic and copies ran while one was open for 0% -> 0% of each run, Pallas kernels for 40% -> 41%
where the time goes in v21:
time: 23.7 us; the launch traced here: 23.6 us
  starting transfers between devices  11.5 us (49%)
  Pallas kernels  10.4 us (44%)
  waiting for transfers between devices  1.59 us (7%)
    ppermute x5, starting transfers between devices, crossed(): lax.ppermute(value, 'leaf', [(i, i ^ turn) for i in range(leaf_devices)])  7.8 us
    pallas_call x1, Pallas kernels, local(): pl.pallas_call(up_kernel, out_shape=[jax.ShapeDtypeStruct(value.shape, va...  4.76 us
    ppermute x3, starting transfers between devices, rotated(): lax.ppermute(value, axis, [(i, (i - shift) % count) for i in range(count)])  3.66 us
    pallas_call x1, Pallas kernels, local(): pl.pallas_call(functools.partial(near_kernel, faces, far_groups, share),...  1.52 us
    ppermute x5, waiting for transfers between devices, crossed(): lax.ppermute(value, 'leaf', [(i, i ^ turn) for i in range(leaf_devices)])  1.42 us
    pallas_call x1, Pallas kernels, local(): pl.pallas_call(project_kernel, out_shape=jax.ShapeDtypeStruct((columns, p...  1.31 us
    pallas_call x1, Pallas kernels, local(): pl.pallas_call(couple_kernel, out_shape=[jax.ShapeDtypeStruct((leaf_count...  0.86 us
    pallas_call x1, Pallas kernels, local(): pl.pallas_call(functools.partial(add_kernel, leaf_count), out_shape=jax.S...  0.74 us
  transfers between devices with their start and end apart: 8, of which 4 were waited for; matrix products, arithmetic and copies ran while one was open for 0% of the time, Pallas kernels for 41%

profile of v21, /device:TPU:0, one launch (start us, length us, event | category | flops | bytes accessed | tf_op | source)
XLA Modules:
  0.0 23.6 jit_solution(1699827642459321985)
XLA Ops:
  0.0 2.9 %collective-permute-start = (bf16[16,4096]{1,0:T(8,128)(2,1)}, bf16[16,4096]{1,0:T(8,128)(2,1)S(1)}, u32[]{:S(2)}, u32[]{:S(2)}) collective-permute-start(bf16[16,4096]{1,0:T(8,128)(2,1)} %refs_0_.1), channel_id=1, source_target_pairs={{0,2},{2,0},{1,3},{3,1},{4,6},{6,4},{5,7},{7,5},{8,10},{10,8},{9,1... | collective-permute-start | bytes 393224 | tf_op jit(solution)/shard_map/ppermute | solution.py:454
  2.9 4.8 %up.1 = (f32[32,4096]{1,0:T(8,128)S(1)}, bf16[16,4096]{1,0:T(8,128)(2,1)S(1)}, s32[6,4,8]{2,1,0:T(4,128)S(1)}, s32[2,32]{1,0:T(2,128)}, s32[8,32]{1,0:T(8,128)S(...) custom-call(f32[32,32,64]{2,1,0:T(8,128)} %bitcast.8, ...), custom_call_target="tpu_custom_call" | custom-call | bytes 12915000 | tf_op jit(solution)/shard_map/up/pallas_call | solution.py:468
  7.7 0.0 collective-permute-done.refs_0_.refs_1_
  7.7 0.1 collective-permute-start.4
  7.8 0.2 select.1
  8.0 2.7 %collective-permute-start.1 = (bf16[144,128]{1,0:T(8,128)(2,1)S(1)}, bf16[144,128]{1,0:T(8,128)(2,1)S(1)}, u32[]{:S(2)}, u32[]{:S(2)}) collective-permute-start(bf16[144,128]{1,0:T(8,128)(2,1)S(1)} %get-tuple-element.48), channel_id=1, source_target_pairs={{0,16},{4,20},{8,24},{12,28},{16,0},{20,4},{24,8},{28,12},{1,17},{... | collective-permute-start | bytes 110600 | tf_op jit(solution)/shard_map/ppermute | solution.py:457
  10.6 1.6 %collective-permute-start.2 = (bf16[144,128]{1,0:T(8,128)(2,1)S(1)}, bf16[144,128]{1,0:T(8,128)(2,1)S(1)}, u32[]{:S(2)}, u32[]{:S(2)}) collective-permute-start(bf16[144,128]{1,0:T(8,128)(2,1)S(1)} %get-tuple-element.49), channel_id=1, source_target_pairs={{0,8},{4,12},{8,0},{12,4},{16,24},{20,28},{24,16},{28,20},{1,9},{5... | collective-permute-start | bytes 110600 | tf_op jit(solution)/shard_map/ppermute | solution.py:457
  12.2 1.5 %collective-permute-start.3 = (bf16[144,128]{1,0:T(8,128)(2,1)S(1)}, bf16[144,128]{1,0:T(8,128)(2,1)S(1)}, u32[]{:S(2)}, u32[]{:S(2)}) collective-permute-start(bf16[144,128]{1,0:T(8,128)(2,1)S(1)} %get-tuple-element.50), channel_id=1, source_target_pairs={{0,4},{4,0},{8,12},{12,8},{16,20},{20,16},{24,28},{28,24},{1,5},{5... | collective-permute-start | bytes 110600 | tf_op jit(solution)/shard_map/ppermute | solution.py:457
  13.7 0.9 %couple.1 = (bf16[1024,32]{1,0:T(8,128)(2,1)S(1)}, f32[16,512]{1,0:T(8,128)S(1)}) custom-call(s32[8,32]{1,0:T(8,128)S(1)} %get-tuple-element.52.table_ref, f32[32,8,32,32]{3,2,1,0:T(8,128)S(1)} %get-tuple-element.53.coupling_ref, bf16[16,4096]{1,0:T(8,128)(2,1)S(1)} %get-tuple-element.47.dens_ref.refs_0_, f32[32,4096]{1,0:T(8,128)S(1)} %get-tuple-element.54.bases_ref), custom_call_target="tpu_custom_call" | custom-call | bytes 7380000 | tf_op jit(solution)/shard_map/couple/pallas_call | solution.py:509
  14.6 0.0 collective-permute-done.1.refs_2_.refs_1_
  14.6 0.5 %collective-permute-start.5 = (bf16[64,128]{1,0:T(8,128)(2,1)S(1)}, bf16[64,128]{1,0:T(8,128)(2,1)S(1)}, u32[]{:S(2)}, u32[]{:S(2)}) collective-permute-start(bf16[64,128]{1,0:T(8,128)(2,1)S(1)} %slice.16), channel_id=1, source_target_pairs={{0,8},{4,12},{8,0},{12,4},{16,24},{20,28},{24,16},{28,20},{1,9},{5... | collective-permute-start | bytes 49160 | tf_op jit(solution)/shard_map/ppermute | solution.py:457
  15.1 0.0 collective-permute-done.2.refs_3_.refs_2_
  15.1 1.0 %collective-permute-done.3.refs_4_.refs_3_ = bf16[144,128]{1,0:T(8,128)(2,1)S(1)} collective-permute-done((bf16[144,128]{1,0:T(8,128)(2,1)S(1)}, bf16[144,128]{1,0:T(8,128)(2,1)S(1)}, u32[]{:S(2)}, u32[]{:S(2)}) %collective-permute-start.3) | collective-permute-done | bytes 36896 | tf_op jit(solution)/shard_map/ppermute | solution.py:457
  16.2 0.0 collective-permute-done.4.refs_6_
  16.2 1.5 %near.1 = (f32[16,4096]{1,0:T(8,128)S(1)}, s16[16,4352]{1,0:T(8,128)(2,1)S(1)}) custom-call(bf16[16,4096]{1,0:T(8,128)(2,1)S(1)} %get-tuple-element.47.dens_ref.refs_0_, bf16[16,4096]{1,0:T(8,128)(2,1)S(1)} %collective-permute-done.refs_0_.refs_1_, bf16[144,128]{1,0:T(8,128)(2,1)S(1)} %collective-permute-done.1.refs_2_.refs_1_, ...), custom_call_target="tpu_custom_call" | custom-call | bytes 11070000 | tf_op jit(solution)/shard_map/near/pallas_call | solution.py:539
  17.7 0.7 %collective-permute-start.7 = (s16[16,4352]{1,0:T(8,128)(2,1)S(1)}, s16[16,4352]{1,0:T(8,128)(2,1)S(1)}, u32[]{:S(2)}, u32[]{:S(2)}) collective-permute-start(s16[16,4352]{1,0:T(8,128)(2,1)S(1)} %get-tuple-element.66), channel_id=1, source_target_pairs={{0,2},{2,0},{1,3},{3,1},{4,6},{6,4},{5,7},{7,5},{8,10},{10,8},{9,1... | collective-permute-start | bytes 417800 | tf_op jit(solution)/shard_map/ppermute | solution.py:454
  18.4 0.1 collective-permute-done.5.refs_4_
  18.4 1.5 %collective-permute-start.6 = (bf16[48,128]{1,0:T(8,128)(2,1)S(1)}, bf16[48,128]{1,0:T(8,128)(2,1)S(1)}, u32[]{:S(2)}, u32[]{:S(2)}) collective-permute-start(bf16[48,128]{1,0:T(8,128)(2,1)S(1)} %pad_maximum_fusion), channel_id=1, source_target_pairs={{0,4},{4,0},{8,12},{12,8},{16,20},{20,16},{24,28},{28,24},{1,5},{5... | collective-permute-start | bytes 36872 | tf_op jit(solution)/shard_map/ppermute | solution.py:457
  20.0 0.5 %paths.1 = (bf16[32,1024]{1,0:T(8,128)(2,1)S(1)}, bf16[32,1024]{1,0:T(8,128)(2,1)S(1)}) custom-call(f32[16,32,32]{2,1,0:T(8,128)S(1)} %get-tuple-element.58.upper_ref, f32[16,3,32,32]{3,2,1,0:T(8,128)S(1)} %get-tuple-element.59.cross_ref), custom_call_target="tpu_custom_call" | custom-call | bytes 2583000 | tf_op jit(solution)/shard_map/paths/pallas_call | solution.py:556
  20.5 1.3 %project.1.term_ref = f32[16,4096]{1,0:T(8,128)S(1)} custom-call(s32[8,32]{1,0:T(8,128)S(1)} %get-tuple-element.52.table_ref, f32[32,8,32,32]{3,2,1,0:T(8,128)S(1)} %get-tuple-element.53.coupling_ref, bf16[1024,32]{1,0:T(8,128)(2,1)S(1)} %get-tuple-element.63.turned_ref, f32[16,512]{1,0:T(8,128)S(1)} %get-tuple-element.56.refs_7_.first_ref, ...), custom_call_target="tpu_custom_call" | custom-call | bytes 5535000 | tf_op jit(solution)/shard_map/project/pallas_call | solution.py:567
  21.8 0.3 %collective-permute-done.6.refs_5_ = bf16[48,128]{1,0:T(8,128)(2,1)S(1)} collective-permute-done((bf16[48,128]{1,0:T(8,128)(2,1)S(1)}, bf16[48,128]{1,0:T(8,128)(2,1)S(1)}, u32[]{:S(2)}, u32[]{:S(2)}) %collective-permute-start.6) | collective-permute-done | bytes 12320 | tf_op jit(solution)/shard_map/ppermute | solution.py:457
  22.1 0.5 %far.1.term_ref = f32[16,4096]{1,0:T(8,128)S(1)} custom-call(bf16[32,1024]{1,0:T(8,128)(2,1)S(1)} %get-tuple-element.60.path_high_ref, bf16[32,1024]{1,0:T(8,128)(2,1)S(1)} %get-tuple-element.61.path_low_ref, bf16[64,4096]{1,0:T(8,128)(2,1)S(1)} %get-tuple-element.62.halves_ref, f32[16,4096]{1,0:T(8,128)S(1)} %project.1.term_ref, ...), custom_call_target="tpu_custom_call" | custom-call | bytes 2214000 | tf_op jit(solution)/shard_map/far/pallas_call | solution.py:576
  22.6 0.2 collective-permute-done.7.refs_0_
  22.8 0.7 %add.1 = f32[16,4096]{1,0:T(8,128)} custom-call(f32[16,4096]{1,0:T(8,128)S(1)} %far.1.term_ref, s16[16,4352]{1,0:T(8,128)(2,1)S(1)} %collective-permute-done.7.refs_0_), custom_call_target="tpu_custom_call" | custom-call | bytes 1845000 | tf_op jit(solution)/shard_map/add/pallas_call | solution.py:585
  (5 shorter events, 0.0 us)
Async XLA Ops:
  0.0 7.7 %collective-permute-start = (bf16[16,4096]{1,0:T(8,128)(2,1)}, bf16[16,4096]{1,0:T(8,128)(2,1)S(1)}, u32[]{:S(2)}, u32[]{:S(2)}) collective-permute-start(bf16[16,4096]{1,0:T(8,128)(2,1)} %refs_0_.1), channel_id=1, source_target_pairs={{0,2},{2,0},{1,3},{3,1},{4,6},{6,4},{5,7},{7,5},{8,10},{10,8},{9,1... | collective-permute-start | bytes 393224 | tf_op jit(solution)/shard_map/ppermute | solution.py:454
  7.7 8.5 %collective-permute-start.4 = (bf16[8208,128]{1,0:T(8,128)(2,1)S(1)}, bf16[8208,128]{1,0:T(8,128)(2,1)S(1)}, u32[]{:S(2)}, u32[]{:S(2)}) collective-permute-start(bf16[8208,128]{1,0:T(8,128)(2,1)S(1)} %get-tuple-element.51.refs_5_), channel_id=1, source_target_pairs={{0,1},{1,0},{2,3},{3,2},{4,5},{5,4},{6,7},{7,6},{8,9},{9,8},{10,11... | collective-permute-start | bytes 6303752 | tf_op jit(solution)/shard_map/ppermute | solution.py:454
  8.0 6.6 %collective-permute-start.1 = (bf16[144,128]{1,0:T(8,128)(2,1)S(1)}, bf16[144,128]{1,0:T(8,128)(2,1)S(1)}, u32[]{:S(2)}, u32[]{:S(2)}) collective-permute-start(bf16[144,128]{1,0:T(8,128)(2,1)S(1)} %get-tuple-element.48), channel_id=1, source_target_pairs={{0,16},{4,20},{8,24},{12,28},{16,0},{20,4},{24,8},{28,12},{1,17},{... | collective-permute-start | bytes 110600 | tf_op jit(solution)/shard_map/ppermute | solution.py:457
  10.6 4.5 %collective-permute-start.2 = (bf16[144,128]{1,0:T(8,128)(2,1)S(1)}, bf16[144,128]{1,0:T(8,128)(2,1)S(1)}, u32[]{:S(2)}, u32[]{:S(2)}) collective-permute-start(bf16[144,128]{1,0:T(8,128)(2,1)S(1)} %get-tuple-element.49), channel_id=1, source_target_pairs={{0,8},{4,12},{8,0},{12,4},{16,24},{20,28},{24,16},{28,20},{1,9},{5... | collective-permute-start | bytes 110600 | tf_op jit(solution)/shard_map/ppermute | solution.py:457
  12.2 4.0 %collective-permute-start.3 = (bf16[144,128]{1,0:T(8,128)(2,1)S(1)}, bf16[144,128]{1,0:T(8,128)(2,1)S(1)}, u32[]{:S(2)}, u32[]{:S(2)}) collective-permute-start(bf16[144,128]{1,0:T(8,128)(2,1)S(1)} %get-tuple-element.50), channel_id=1, source_target_pairs={{0,4},{4,0},{8,12},{12,8},{16,20},{20,16},{24,28},{28,24},{1,5},{5... | collective-permute-start | bytes 110600 | tf_op jit(solution)/shard_map/ppermute | solution.py:457
  14.6 3.8 %collective-permute-start.5 = (bf16[64,128]{1,0:T(8,128)(2,1)S(1)}, bf16[64,128]{1,0:T(8,128)(2,1)S(1)}, u32[]{:S(2)}, u32[]{:S(2)}) collective-permute-start(bf16[64,128]{1,0:T(8,128)(2,1)S(1)} %slice.16), channel_id=1, source_target_pairs={{0,8},{4,12},{8,0},{12,4},{16,24},{20,28},{24,16},{28,20},{1,9},{5... | collective-permute-start | bytes 49160 | tf_op jit(solution)/shard_map/ppermute | solution.py:457
  17.7 5.1 %collective-permute-start.7 = (s16[16,4352]{1,0:T(8,128)(2,1)S(1)}, s16[16,4352]{1,0:T(8,128)(2,1)S(1)}, u32[]{:S(2)}, u32[]{:S(2)}) collective-permute-start(s16[16,4352]{1,0:T(8,128)(2,1)S(1)} %get-tuple-element.66), channel_id=1, source_target_pairs={{0,2},{2,0},{1,3},{3,1},{4,6},{6,4},{5,7},{7,5},{8,10},{10,8},{9,1... | collective-permute-start | bytes 417800 | tf_op jit(solution)/shard_map/ppermute | solution.py:454
  18.4 3.7 %collective-permute-start.6 = (bf16[48,128]{1,0:T(8,128)(2,1)S(1)}, bf16[48,128]{1,0:T(8,128)(2,1)S(1)}, u32[]{:S(2)}, u32[]{:S(2)}) collective-permute-start(bf16[48,128]{1,0:T(8,128)(2,1)S(1)} %pad_maximum_fusion), channel_id=1, source_target_pairs={{0,4},{4,0},{8,12},{12,8},{16,20},{20,16},{24,28},{28,24},{1,5},{5... | collective-permute-start | bytes 36872 | tf_op jit(solution)/shard_map/ppermute | solution.py:457

commit v22 on v20

--- a/solution.py
+++ b/solution.py
@@ -99,7 +99,7 @@
     block_rows = hbm_refs[-1].shape[0]
     vmem_refs = (*vmem_refs[:-1], shared_ref.at[pl.ds(0, block_rows)])
     copies = fetch(
-        [(maps_hbm, maps_ref), (bases_hbm, bases_ref), *zip(hbm_refs, vmem_refs)], sems
+        [(maps_hbm, maps_ref), (bases_hbm, bases_ref), *zip(hbm_refs[:-2], vmem_refs[:-2])], sems
     )
     columns, points = dens_ref.shape
     rank, _, node_count = maps_ref.shape
@@ -107,6 +107,7 @@
     leaf_count = node_count // 2
     width = points // leaf_count
     copies[0].wait()
+    copies += fetch(zip(hbm_refs[-2:], vmem_refs[-2:]), sems.at[pl.ds(count, 2)])
     node = lax.broadcasted_iota(jnp.int32, (node_count, LANES), 0)
     block = lax.broadcasted_iota(jnp.int32, (node_count, LANES), 1) // rank
     parent = node // 2 % group

time: 23.6 us -> 23.6 us (level)
  transfers between devices with their start and end apart: 8 -> 8, of which waited for: 2 -> 3; matrix products, arithmetic and copies ran while one was open for 0% -> 0% of each run, Pallas kernels for 40% -> 41%
where the time goes in v22:
time: 23.6 us; the launch traced here: 23.4 us
  starting transfers between devices  11.6 us (49%)
  Pallas kernels  10.3 us (44%)
  waiting for transfers between devices  1.42 us (6%)
    ppermute x5, starting transfers between devices, crossed(): lax.ppermute(value, 'leaf', [(i, i ^ turn) for i in range(leaf_devices)])  7.85 us
    pallas_call x1, Pallas kernels, local(): pl.pallas_call(up_kernel, out_shape=[jax.ShapeDtypeStruct(value.shape, va...  4.63 us
    ppermute x3, starting transfers between devices, rotated(): lax.ppermute(value, axis, [(i, (i - shift) % count) for i in range(count)])  3.78 us
    pallas_call x1, Pallas kernels, local(): pl.pallas_call(functools.partial(near_kernel, faces, far_groups, share),...  1.52 us
    ppermute x5, waiting for transfers between devices, crossed(): lax.ppermute(value, 'leaf', [(i, i ^ turn) for i in range(leaf_devices)])  1.37 us
    pallas_call x1, Pallas kernels, local(): pl.pallas_call(project_kernel, out_shape=jax.ShapeDtypeStruct((columns, p...  1.31 us
    pallas_call x1, Pallas kernels, local(): pl.pallas_call(couple_kernel, out_shape=[jax.ShapeDtypeStruct((leaf_count...  0.85 us
    pallas_call x1, Pallas kernels, local(): pl.pallas_call(functools.partial(add_kernel, leaf_count), out_shape=jax.S...  0.74 us
  transfers between devices with their start and end apart: 8, of which 3 were waited for; matrix products, arithmetic and copies ran while one was open for 0% of the time, Pallas kernels for 41%

profile of v22, /device:TPU:0, one launch (start us, length us, event | category | flops | bytes accessed | tf_op | source)
XLA Modules:
  0.0 23.4 jit_solution(16240391760683781875)
XLA Ops:
  0.0 2.9 %collective-permute-start = (bf16[16,4096]{1,0:T(8,128)(2,1)}, bf16[16,4096]{1,0:T(8,128)(2,1)S(1)}, u32[]{:S(2)}, u32[]{:S(2)}) collective-permute-start(bf16[16,4096]{1,0:T(8,128)(2,1)} %refs_0_.1), channel_id=1, source_target_pairs={{0,2},{2,0},{1,3},{3,1},{4,6},{6,4},{5,7},{7,5},{8,10},{10,8},{9,1... | collective-permute-start | bytes 393224 | tf_op jit(solution)/shard_map/ppermute | solution.py:453
  2.9 4.6 %up.1 = (f32[32,4096]{1,0:T(8,128)S(1)}, bf16[16,4096]{1,0:T(8,128)(2,1)S(1)}, s32[6,4,8]{2,1,0:T(4,128)S(1)}, s32[2,32]{1,0:T(2,128)}, s32[8,32]{1,0:T(8,128)S(...) custom-call(f32[32,32,64]{2,1,0:T(8,128)} %bitcast.8, ...), custom_call_target="tpu_custom_call" | custom-call | bytes 12915000 | tf_op jit(solution)/shard_map/up/pallas_call | solution.py:467
  7.6 0.0 collective-permute-done.refs_0_.refs_1_
  7.6 0.1 collective-permute-start.4
  7.7 0.2 select.1
  7.9 2.7 %collective-permute-start.1 = (bf16[144,128]{1,0:T(8,128)(2,1)S(1)}, bf16[144,128]{1,0:T(8,128)(2,1)S(1)}, u32[]{:S(2)}, u32[]{:S(2)}) collective-permute-start(bf16[144,128]{1,0:T(8,128)(2,1)S(1)} %get-tuple-element.48), channel_id=1, source_target_pairs={{0,16},{4,20},{8,24},{12,28},{16,0},{20,4},{24,8},{28,12},{1,17},{... | collective-permute-start | bytes 110600 | tf_op jit(solution)/shard_map/ppermute | solution.py:456
  10.5 1.6 %collective-permute-start.2 = (bf16[144,128]{1,0:T(8,128)(2,1)S(1)}, bf16[144,128]{1,0:T(8,128)(2,1)S(1)}, u32[]{:S(2)}, u32[]{:S(2)}) collective-permute-start(bf16[144,128]{1,0:T(8,128)(2,1)S(1)} %get-tuple-element.49), channel_id=1, source_target_pairs={{0,8},{4,12},{8,0},{12,4},{16,24},{20,28},{24,16},{28,20},{1,9},{5... | collective-permute-start | bytes 110600 | tf_op jit(solution)/shard_map/ppermute | solution.py:456
  12.1 1.5 %collective-permute-start.3 = (bf16[144,128]{1,0:T(8,128)(2,1)S(1)}, bf16[144,128]{1,0:T(8,128)(2,1)S(1)}, u32[]{:S(2)}, u32[]{:S(2)}) collective-permute-start(bf16[144,128]{1,0:T(8,128)(2,1)S(1)} %get-tuple-element.50), channel_id=1, source_target_pairs={{0,4},{4,0},{8,12},{12,8},{16,20},{20,16},{24,28},{28,24},{1,5},{5... | collective-permute-start | bytes 110600 | tf_op jit(solution)/shard_map/ppermute | solution.py:456
  13.6 0.9 %couple.1 = (bf16[1024,32]{1,0:T(8,128)(2,1)S(1)}, f32[16,512]{1,0:T(8,128)S(1)}) custom-call(s32[8,32]{1,0:T(8,128)S(1)} %get-tuple-element.52.table_ref, f32[32,8,32,32]{3,2,1,0:T(8,128)S(1)} %get-tuple-element.53.coupling_ref, bf16[16,4096]{1,0:T(8,128)(2,1)S(1)} %get-tuple-element.47.dens_ref.refs_0_, f32[32,4096]{1,0:T(8,128)S(1)} %get-tuple-element.54.bases_ref), custom_call_target="tpu_custom_call" | custom-call | bytes 7380000 | tf_op jit(solution)/shard_map/couple/pallas_call | solution.py:507
  14.5 0.0 collective-permute-done.1.refs_2_.refs_1_
  14.5 0.5 %collective-permute-start.5 = (bf16[64,128]{1,0:T(8,128)(2,1)S(1)}, bf16[64,128]{1,0:T(8,128)(2,1)S(1)}, u32[]{:S(2)}, u32[]{:S(2)}) collective-permute-start(bf16[64,128]{1,0:T(8,128)(2,1)S(1)} %slice.16), channel_id=1, source_target_pairs={{0,8},{4,12},{8,0},{12,4},{16,24},{20,28},{24,16},{28,20},{1,9},{5... | collective-permute-start | bytes 49160 | tf_op jit(solution)/shard_map/ppermute | solution.py:456
  15.0 0.0 collective-permute-done.2.refs_3_.refs_2_
  15.0 1.0 %collective-permute-done.3.refs_4_.refs_3_ = bf16[144,128]{1,0:T(8,128)(2,1)S(1)} collective-permute-done((bf16[144,128]{1,0:T(8,128)(2,1)S(1)}, bf16[144,128]{1,0:T(8,128)(2,1)S(1)}, u32[]{:S(2)}, u32[]{:S(2)}) %collective-permute-start.3) | collective-permute-done | bytes 36896 | tf_op jit(solution)/shard_map/ppermute | solution.py:456
  16.0 0.0 collective-permute-done.4.refs_6_
  16.0 1.5 %near.1 = (f32[16,4096]{1,0:T(8,128)S(1)}, s16[16,4352]{1,0:T(8,128)(2,1)S(1)}) custom-call(bf16[16,4096]{1,0:T(8,128)(2,1)S(1)} %get-tuple-element.47.dens_ref.refs_0_, bf16[16,4096]{1,0:T(8,128)(2,1)S(1)} %collective-permute-done.refs_0_.refs_1_, bf16[144,128]{1,0:T(8,128)(2,1)S(1)} %collective-permute-done.1.refs_2_.refs_1_, ...), custom_call_target="tpu_custom_call" | custom-call | bytes 11070000 | tf_op jit(solution)/shard_map/near/pallas_call | solution.py:537
  17.6 0.8 %collective-permute-start.7 = (s16[16,4352]{1,0:T(8,128)(2,1)S(1)}, s16[16,4352]{1,0:T(8,128)(2,1)S(1)}, u32[]{:S(2)}, u32[]{:S(2)}) collective-permute-start(s16[16,4352]{1,0:T(8,128)(2,1)S(1)} %get-tuple-element.66), channel_id=1, source_target_pairs={{0,2},{2,0},{1,3},{3,1},{4,6},{6,4},{5,7},{7,5},{8,10},{10,8},{9,1... | collective-permute-start | bytes 417800 | tf_op jit(solution)/shard_map/ppermute | solution.py:453
  18.4 0.0 collective-permute-done.5.refs_4_
  18.4 1.6 %collective-permute-start.6 = (bf16[48,128]{1,0:T(8,128)(2,1)S(1)}, bf16[48,128]{1,0:T(8,128)(2,1)S(1)}, u32[]{:S(2)}, u32[]{:S(2)}) collective-permute-start(bf16[48,128]{1,0:T(8,128)(2,1)S(1)} %pad_maximum_fusion), channel_id=1, source_target_pairs={{0,4},{4,0},{8,12},{12,8},{16,20},{20,16},{24,28},{28,24},{1,5},{5... | collective-permute-start | bytes 36872 | tf_op jit(solution)/shard_map/ppermute | solution.py:456
  20.0 0.5 %paths.1 = (bf16[32,1024]{1,0:T(8,128)(2,1)S(1)}, bf16[32,1024]{1,0:T(8,128)(2,1)S(1)}) custom-call(f32[16,32,32]{2,1,0:T(8,128)S(1)} %get-tuple-element.58.upper_ref, f32[16,3,32,32]{3,2,1,0:T(8,128)S(1)} %get-tuple-element.59.cross_ref), custom_call_target="tpu_custom_call" | custom-call | bytes 2583000 | tf_op jit(solution)/shard_map/paths/pallas_call | solution.py:554
  20.5 1.3 %project.1.term_ref = f32[16,4096]{1,0:T(8,128)S(1)} custom-call(s32[8,32]{1,0:T(8,128)S(1)} %get-tuple-element.52.table_ref, f32[32,8,32,32]{3,2,1,0:T(8,128)S(1)} %get-tuple-element.53.coupling_ref, bf16[1024,32]{1,0:T(8,128)(2,1)S(1)} %get-tuple-element.63.turned_ref, f32[16,512]{1,0:T(8,128)S(1)} %get-tuple-element.56.refs_7_.first_ref, ...), custom_call_target="tpu_custom_call" | custom-call | bytes 5535000 | tf_op jit(solution)/shard_map/project/pallas_call | solution.py:565
  21.8 0.3 %collective-permute-done.6.refs_5_ = bf16[48,128]{1,0:T(8,128)(2,1)S(1)} collective-permute-done((bf16[48,128]{1,0:T(8,128)(2,1)S(1)}, bf16[48,128]{1,0:T(8,128)(2,1)S(1)}, u32[]{:S(2)}, u32[]{:S(2)}) %collective-permute-start.6) | collective-permute-done | bytes 12320 | tf_op jit(solution)/shard_map/ppermute | solution.py:456
  22.1 0.5 %far.1.term_ref = f32[16,4096]{1,0:T(8,128)S(1)} custom-call(bf16[32,1024]{1,0:T(8,128)(2,1)S(1)} %get-tuple-element.60.path_high_ref, bf16[32,1024]{1,0:T(8,128)(2,1)S(1)} %get-tuple-element.61.path_low_ref, bf16[64,4096]{1,0:T(8,128)(2,1)S(1)} %get-tuple-element.62.halves_ref, f32[16,4096]{1,0:T(8,128)S(1)} %project.1.term_ref, ...), custom_call_target="tpu_custom_call" | custom-call | bytes 2214000 | tf_op jit(solution)/shard_map/far/pallas_call | solution.py:574
  22.6 0.1 collective-permute-done.7.refs_0_
  22.7 0.7 %add.1 = f32[16,4096]{1,0:T(8,128)} custom-call(f32[16,4096]{1,0:T(8,128)S(1)} %far.1.term_ref, s16[16,4352]{1,0:T(8,128)(2,1)S(1)} %collective-permute-done.7.refs_0_), custom_call_target="tpu_custom_call" | custom-call | bytes 1845000 | tf_op jit(solution)/shard_map/add/pallas_call | solution.py:583
  (5 shorter events, 0.0 us)
Async XLA Ops:
  0.0 7.6 %collective-permute-start = (bf16[16,4096]{1,0:T(8,128)(2,1)}, bf16[16,4096]{1,0:T(8,128)(2,1)S(1)}, u32[]{:S(2)}, u32[]{:S(2)}) collective-permute-start(bf16[16,4096]{1,0:T(8,128)(2,1)} %refs_0_.1), channel_id=1, source_target_pairs={{0,2},{2,0},{1,3},{3,1},{4,6},{6,4},{5,7},{7,5},{8,10},{10,8},{9,1... | collective-permute-start | bytes 393224 | tf_op jit(solution)/shard_map/ppermute | solution.py:453
  7.6 8.5 %collective-permute-start.4 = (bf16[8208,128]{1,0:T(8,128)(2,1)S(1)}, bf16[8208,128]{1,0:T(8,128)(2,1)S(1)}, u32[]{:S(2)}, u32[]{:S(2)}) collective-permute-start(bf16[8208,128]{1,0:T(8,128)(2,1)S(1)} %get-tuple-element.51.refs_5_), channel_id=1, source_target_pairs={{0,1},{1,0},{2,3},{3,2},{4,5},{5,4},{6,7},{7,6},{8,9},{9,8},{10,11... | collective-permute-start | bytes 6303752 | tf_op jit(solution)/shard_map/ppermute | solution.py:453
  7.9 6.6 %collective-permute-start.1 = (bf16[144,128]{1,0:T(8,128)(2,1)S(1)}, bf16[144,128]{1,0:T(8,128)(2,1)S(1)}, u32[]{:S(2)}, u32[]{:S(2)}) collective-permute-start(bf16[144,128]{1,0:T(8,128)(2,1)S(1)} %get-tuple-element.48), channel_id=1, source_target_pairs={{0,16},{4,20},{8,24},{12,28},{16,0},{20,4},{24,8},{28,12},{1,17},{... | collective-permute-start | bytes 110600 | tf_op jit(solution)/shard_map/ppermute | solution.py:456
  10.5 4.5 %collective-permute-start.2 = (bf16[144,128]{1,0:T(8,128)(2,1)S(1)}, bf16[144,128]{1,0:T(8,128)(2,1)S(1)}, u32[]{:S(2)}, u32[]{:S(2)}) collective-permute-start(bf16[144,128]{1,0:T(8,128)(2,1)S(1)} %get-tuple-element.49), channel_id=1, source_target_pairs={{0,8},{4,12},{8,0},{12,4},{16,24},{20,28},{24,16},{28,20},{1,9},{5... | collective-permute-start | bytes 110600 | tf_op jit(solution)/shard_map/ppermute | solution.py:456
  12.1 4.0 %collective-permute-start.3 = (bf16[144,128]{1,0:T(8,128)(2,1)S(1)}, bf16[144,128]{1,0:T(8,128)(2,1)S(1)}, u32[]{:S(2)}, u32[]{:S(2)}) collective-permute-start(bf16[144,128]{1,0:T(8,128)(2,1)S(1)} %get-tuple-element.50), channel_id=1, source_target_pairs={{0,4},{4,0},{8,12},{12,8},{16,20},{20,16},{24,28},{28,24},{1,5},{5... | collective-permute-start | bytes 110600 | tf_op jit(solution)/shard_map/ppermute | solution.py:456
  14.5 3.9 %collective-permute-start.5 = (bf16[64,128]{1,0:T(8,128)(2,1)S(1)}, bf16[64,128]{1,0:T(8,128)(2,1)S(1)}, u32[]{:S(2)}, u32[]{:S(2)}) collective-permute-start(bf16[64,128]{1,0:T(8,128)(2,1)S(1)} %slice.16), channel_id=1, source_target_pairs={{0,8},{4,12},{8,0},{12,4},{16,24},{20,28},{24,16},{28,20},{1,9},{5... | collective-permute-start | bytes 49160 | tf_op jit(solution)/shard_map/ppermute | solution.py:456
  17.6 5.1 %collective-permute-start.7 = (s16[16,4352]{1,0:T(8,128)(2,1)S(1)}, s16[16,4352]{1,0:T(8,128)(2,1)S(1)}, u32[]{:S(2)}, u32[]{:S(2)}) collective-permute-start(s16[16,4352]{1,0:T(8,128)(2,1)S(1)} %get-tuple-element.66), channel_id=1, source_target_pairs={{0,2},{2,0},{1,3},{3,1},{4,6},{6,4},{5,7},{7,5},{8,10},{10,8},{9,1... | collective-permute-start | bytes 417800 | tf_op jit(solution)/shard_map/ppermute | solution.py:453
  18.4 3.8 %collective-permute-start.6 = (bf16[48,128]{1,0:T(8,128)(2,1)S(1)}, bf16[48,128]{1,0:T(8,128)(2,1)S(1)}, u32[]{:S(2)}, u32[]{:S(2)}) collective-permute-start(bf16[48,128]{1,0:T(8,128)(2,1)S(1)} %pad_maximum_fusion), channel_id=1, source_target_pairs={{0,4},{4,0},{8,12},{12,8},{16,20},{20,16},{24,28},{28,24},{1,5},{5... | collective-permute-start | bytes 36872 | tf_op jit(solution)/shard_map/ppermute | solution.py:456

commit v23 on v15

--- a/solution.py
+++ b/solution.py
@@ -571,7 +571,7 @@
         out_shape=jax.ShapeDtypeStruct((columns, points), F32),
         in_specs=[VMEM] * (1 + len(received)),
         out_specs=HBM,
-        scratch_shapes=[pltpu.VMEM((columns, points), F32), dma((4,))],
+        scratch_shapes=[pltpu.VMEM((columns, points), F32), dma((2,))],
         compiler_params=params,
         cost_estimate=hint(0.5),
         name="add",

time: 23.5 us -> 23.5 us (level)
  no operation moved by 1% of the time
where the time goes in v23:
time: 23.5 us; the launch traced here: 23.4 us
  starting transfers between devices  12.3 us (52%)
  Pallas kernels  9.57 us (41%)
  waiting for transfers between devices  1.4 us (6%)
    ppermute x5, starting transfers between devices, crossed(): lax.ppermute(value, 'leaf', [(i, i ^ turn) for i in range(leaf_devices)])  7.84 us
    ppermute x4, starting transfers between devices, rotated(): lax.ppermute(value, axis, [(i, (i - shift) % count) for i in range(count)])  4.47 us
    pallas_call x1, Pallas kernels, local(): pl.pallas_call(up_kernel, out_shape=[jax.ShapeDtypeStruct(value.shape, va...  3.97 us
    pallas_call x1, Pallas kernels, local(): pl.pallas_call(functools.partial(near_kernel, faces, far_groups, share),...  1.49 us
    ppermute x5, waiting for transfers between devices, crossed(): lax.ppermute(value, 'leaf', [(i, i ^ turn) for i in range(leaf_devices)])  1.39 us
    pallas_call x1, Pallas kernels, local(): pl.pallas_call(project_kernel, out_shape=jax.ShapeDtypeStruct((columns, p...  1.3 us
    pallas_call x1, Pallas kernels, local(): pl.pallas_call(couple_kernel, out_shape=[jax.ShapeDtypeStruct((leaf_count...  0.85 us
    pallas_call x1, Pallas kernels, local(): pl.pallas_call(functools.partial(add_kernel, leaf_count), out_shape=jax.S...  0.75 us
  transfers between devices with their start and end apart: 9, of which 2 were waited for; matrix products, arithmetic and copies ran while one was open for 0% of the time, Pallas kernels for 38%

profile of v23, /device:TPU:0, one launch (start us, length us, event | category | flops | bytes accessed | tf_op | source)
XLA Modules:
  0.0 23.4 jit_solution(14455688076214272756)
XLA Ops:
  0.0 2.9 %collective-permute-start = (bf16[16,4096]{1,0:T(8,128)(2,1)}, bf16[16,4096]{1,0:T(8,128)(2,1)S(1)}, u32[]{:S(2)}, u32[]{:S(2)}) collective-permute-start(bf16[16,4096]{1,0:T(8,128)(2,1)} %refs_0_.1), channel_id=1, source_target_pairs={{0,2},{2,0},{1,3},{3,1},{4,6},{6,4},{5,7},{7,5},{8,10},{10,8},{9,1... | collective-permute-start | bytes 393224 | tf_op jit(solution)/shard_map/ppermute | solution.py:437
  2.9 0.0 collective-permute-start.1
  2.9 4.0 %up.1 = (f32[32,4096]{1,0:T(8,128)S(1)}, bf16[16,4096]{1,0:T(8,128)(2,1)S(1)}, s32[6,4,8]{2,1,0:T(4,128)S(1)}, s32[2,32]{1,0:T(2,128)S(1)}, s32[8,32]{1,0:T(8,12...) custom-call(f32[32,32,64]{2,1,0:T(8,128)} %bitcast.6, ...), custom_call_target="tpu_custom_call" | custom-call | bytes 12915000 | tf_op jit(solution)/shard_map/up/pallas_call | solution.py:451
  6.9 0.0 collective-permute-done.1.refs_1_
  6.9 0.0 collective-permute-done.refs_0_.refs_3_
  6.9 0.6 %collective-permute-start.5 = (bf16[32,2,128,128]{3,2,1,0:T(8,128)(2,1)S(1)}, bf16[32,2,128,128]{3,2,1,0:T(8,128)(2,1)S(1)}, u32[]{:S(2)}, u32[]{:S(2)}) collective-permute-start(bf16[32,2,128,128]{3,2,1,0:T(8,128)(2,1)S(1)} %get-tuple-element.57.refs_7_), channel_id=1, source_target_pairs={{0,1},{1,0},{2,3},{3,2},{4,5},{5,4},{6,7},{7,6},{8,9},{9,8},{10,11... | collective-permute-start | bytes 6291464 | tf_op jit(solution)/shard_map/ppermute | solution.py:437
  7.5 0.2 select.1
  7.7 2.7 %collective-permute-start.2 = (bf16[144,128]{1,0:T(8,128)(2,1)S(1)}, bf16[144,128]{1,0:T(8,128)(2,1)S(1)}, u32[]{:S(2)}, u32[]{:S(2)}) collective-permute-start(bf16[144,128]{1,0:T(8,128)(2,1)S(1)} %get-tuple-element.54), channel_id=1, source_target_pairs={{0,16},{4,20},{8,24},{12,28},{16,0},{20,4},{24,8},{28,12},{1,17},{... | collective-permute-start | bytes 110600 | tf_op jit(solution)/shard_map/ppermute | solution.py:440
  10.3 1.6 %collective-permute-start.3 = (bf16[144,128]{1,0:T(8,128)(2,1)S(1)}, bf16[144,128]{1,0:T(8,128)(2,1)S(1)}, u32[]{:S(2)}, u32[]{:S(2)}) collective-permute-start(bf16[144,128]{1,0:T(8,128)(2,1)S(1)} %get-tuple-element.55), channel_id=1, source_target_pairs={{0,8},{4,12},{8,0},{12,4},{16,24},{20,28},{24,16},{28,20},{1,9},{5... | collective-permute-start | bytes 110600 | tf_op jit(solution)/shard_map/ppermute | solution.py:440
  11.9 1.5 %collective-permute-start.4 = (bf16[144,128]{1,0:T(8,128)(2,1)S(1)}, bf16[144,128]{1,0:T(8,128)(2,1)S(1)}, u32[]{:S(2)}, u32[]{:S(2)}) collective-permute-start(bf16[144,128]{1,0:T(8,128)(2,1)S(1)} %get-tuple-element.56), channel_id=1, source_target_pairs={{0,4},{4,0},{8,12},{12,8},{16,20},{20,16},{24,28},{28,24},{1,5},{5... | collective-permute-start | bytes 110600 | tf_op jit(solution)/shard_map/ppermute | solution.py:440
  13.4 0.8 %couple.1 = (bf16[1024,32]{1,0:T(8,128)(2,1)S(1)}, f32[16,512]{1,0:T(8,128)S(1)}) custom-call(s32[8,32]{1,0:T(8,128)S(1)} %get-tuple-element.58.table_ref, f32[32,8,32,32]{3,2,1,0:T(8,128)S(1)} %get-tuple-element.59.coupling_ref, bf16[16,4096]{1,0:T(8,128)(2,1)S(1)} %get-tuple-element.53.dens_ref.refs_2_, f32[32,4096]{1,0:T(8,128)S(1)} %get-tuple-element.60.bases_ref), custom_call_target="tpu_custom_call" | custom-call | bytes 7380000 | tf_op jit(solution)/shard_map/couple/pallas_call | solution.py:493
  14.3 0.0 collective-permute-done.2.refs_4_.refs_1_
  14.3 0.5 %collective-permute-start.6 = (bf16[64,128]{1,0:T(8,128)(2,1)S(1)}, bf16[64,128]{1,0:T(8,128)(2,1)S(1)}, u32[]{:S(2)}, u32[]{:S(2)}) collective-permute-start(bf16[64,128]{1,0:T(8,128)(2,1)S(1)} %slice.16), channel_id=1, source_target_pairs={{0,8},{4,12},{8,0},{12,4},{16,24},{20,28},{24,16},{28,20},{1,9},{5... | collective-permute-start | bytes 49160 | tf_op jit(solution)/shard_map/ppermute | solution.py:440
  14.8 0.0 collective-permute-done.3.refs_5_.refs_2_
  14.8 1.1 %collective-permute-done.4.refs_6_.refs_3_ = bf16[144,128]{1,0:T(8,128)(2,1)S(1)} collective-permute-done((bf16[144,128]{1,0:T(8,128)(2,1)S(1)}, bf16[144,128]{1,0:T(8,128)(2,1)S(1)}, u32[]{:S(2)}, u32[]{:S(2)}) %collective-permute-start.4) | collective-permute-done | bytes 36896 | tf_op jit(solution)/shard_map/ppermute | solution.py:440
  15.9 0.0 collective-permute-done.5.refs_8_
  15.9 1.5 %near.1 = (f32[16,4096]{1,0:T(8,128)S(1)}, s16[16,4352]{1,0:T(8,128)(2,1)S(1)}) custom-call(s32[2,32]{1,0:T(2,128)S(1)} %get-tuple-element.44.refs_0_, s32[2,32]{1,0:T(2,128)S(1)} %collective-permute-done.1.refs_1_, bf16[16,4096]{1,0:T(8,128)(2,1)S(1)} %get-tuple-element.53.dens_ref.refs_2_, bf16[16,4096]{1,0:T(8,128)(2,1)S(1)} %collective-permute-done.refs_0_.refs_3_, ...), custom_call_target="tpu_custom_call" | custom-call | bytes 11070000 | tf_op jit(solution)/shard_map/near/pallas_call | solution.py:523
  17.4 1.0 %collective-permute-start.8 = (s16[16,4352]{1,0:T(8,128)(2,1)S(1)}, s16[16,4352]{1,0:T(8,128)(2,1)S(1)}, u32[]{:S(2)}, u32[]{:S(2)}) collective-permute-start(s16[16,4352]{1,0:T(8,128)(2,1)S(1)} %get-tuple-element.72), channel_id=1, source_target_pairs={{0,2},{2,0},{1,3},{3,1},{4,6},{6,4},{5,7},{7,5},{8,10},{10,8},{9,1... | collective-permute-start | bytes 417800 | tf_op jit(solution)/shard_map/ppermute | solution.py:437
  18.3 0.0 collective-permute-done.6.refs_4_
  18.3 1.6 %collective-permute-start.7 = (bf16[48,128]{1,0:T(8,128)(2,1)S(1)}, bf16[48,128]{1,0:T(8,128)(2,1)S(1)}, u32[]{:S(2)}, u32[]{:S(2)}) collective-permute-start(bf16[48,128]{1,0:T(8,128)(2,1)S(1)} %pad_maximum_fusion), channel_id=1, source_target_pairs={{0,4},{4,0},{8,12},{12,8},{16,20},{20,16},{24,28},{28,24},{1,5},{5... | collective-permute-start | bytes 36872 | tf_op jit(solution)/shard_map/ppermute | solution.py:440
  19.9 0.5 %paths.1 = (bf16[32,1024]{1,0:T(8,128)(2,1)S(1)}, bf16[32,1024]{1,0:T(8,128)(2,1)S(1)}) custom-call(f32[16,32,32]{2,1,0:T(8,128)S(1)} %get-tuple-element.64.upper_ref, f32[16,3,32,32]{3,2,1,0:T(8,128)S(1)} %get-tuple-element.65.cross_ref), custom_call_target="tpu_custom_call" | custom-call | bytes 2583000 | tf_op jit(solution)/shard_map/paths/pallas_call | solution.py:540
  20.5 1.3 %project.1.term_ref = f32[16,4096]{1,0:T(8,128)S(1)} custom-call(s32[8,32]{1,0:T(8,128)S(1)} %get-tuple-element.58.table_ref, f32[32,8,32,32]{3,2,1,0:T(8,128)S(1)} %get-tuple-element.59.coupling_ref, bf16[1024,32]{1,0:T(8,128)(2,1)S(1)} %get-tuple-element.69.turned_ref, f32[16,512]{1,0:T(8,128)S(1)} %get-tuple-element.62.refs_9_.first_ref, ...), custom_call_target="tpu_custom_call" | custom-call | bytes 5535000 | tf_op jit(solution)/shard_map/project/pallas_call | solution.py:551
  21.8 0.3 %collective-permute-done.7.refs_5_ = bf16[48,128]{1,0:T(8,128)(2,1)S(1)} collective-permute-done((bf16[48,128]{1,0:T(8,128)(2,1)S(1)}, bf16[48,128]{1,0:T(8,128)(2,1)S(1)}, u32[]{:S(2)}, u32[]{:S(2)}) %collective-permute-start.7) | collective-permute-done | bytes 12320 | tf_op jit(solution)/shard_map/ppermute | solution.py:440
  22.1 0.5 %far.1.term_ref = f32[16,4096]{1,0:T(8,128)S(1)} custom-call(bf16[32,1024]{1,0:T(8,128)(2,1)S(1)} %get-tuple-element.66.path_high_ref, bf16[32,1024]{1,0:T(8,128)(2,1)S(1)} %get-tuple-element.67.path_low_ref, bf16[64,4096]{1,0:T(8,128)(2,1)S(1)} %get-tuple-element.68.halves_ref, f32[16,4096]{1,0:T(8,128)S(1)} %project.1.term_ref, ...), custom_call_target="tpu_custom_call" | custom-call | bytes 2214000 | tf_op jit(solution)/shard_map/far/pallas_call | solution.py:560
  22.6 0.0 collective-permute-done.8.refs_0_
  22.6 0.7 %add.1 = f32[16,4096]{1,0:T(8,128)} custom-call(f32[16,4096]{1,0:T(8,128)S(1)} %far.1.term_ref, s16[16,4352]{1,0:T(8,128)(2,1)S(1)} %collective-permute-done.8.refs_0_), custom_call_target="tpu_custom_call" | custom-call | bytes 1845000 | tf_op jit(solution)/shard_map/add/pallas_call | solution.py:569
  (5 shorter events, 0.0 us)
Async XLA Ops:
  0.0 6.9 %collective-permute-start = (bf16[16,4096]{1,0:T(8,128)(2,1)}, bf16[16,4096]{1,0:T(8,128)(2,1)S(1)}, u32[]{:S(2)}, u32[]{:S(2)}) collective-permute-start(bf16[16,4096]{1,0:T(8,128)(2,1)} %refs_0_.1), channel_id=1, source_target_pairs={{0,2},{2,0},{1,3},{3,1},{4,6},{6,4},{5,7},{7,5},{8,10},{10,8},{9,1... | collective-permute-start | bytes 393224 | tf_op jit(solution)/shard_map/ppermute | solution.py:437
  2.9 4.0 %collective-permute-start.1 = (s32[2,32]{1,0:T(2,128)}, s32[2,32]{1,0:T(2,128)S(1)}, u32[]{:S(2)}, u32[]{:S(2)}) collective-permute-start(s32[2,32]{1,0:T(2,128)} %bitcast.9), channel_id=1, source_target_pairs={{0,1},{1,0},{2,3},{3,2},{4,5},{5,4},{6,7},{7,6},{8,9},{9,8},{10,11... | collective-permute-start | bytes 776 | tf_op jit(solution)/shard_map/ppermute | solution.py:437
  6.9 8.9 %collective-permute-start.5 = (bf16[32,2,128,128]{3,2,1,0:T(8,128)(2,1)S(1)}, bf16[32,2,128,128]{3,2,1,0:T(8,128)(2,1)S(1)}, u32[]{:S(2)}, u32[]{:S(2)}) collective-permute-start(bf16[32,2,128,128]{3,2,1,0:T(8,128)(2,1)S(1)} %get-tuple-element.57.refs_7_), channel_id=1, source_target_pairs={{0,1},{1,0},{2,3},{3,2},{4,5},{5,4},{6,7},{7,6},{8,9},{9,8},{10,11... | collective-permute-start | bytes 6291464 | tf_op jit(solution)/shard_map/ppermute | solution.py:437
  7.7 6.6 %collective-permute-start.2 = (bf16[144,128]{1,0:T(8,128)(2,1)S(1)}, bf16[144,128]{1,0:T(8,128)(2,1)S(1)}, u32[]{:S(2)}, u32[]{:S(2)}) collective-permute-start(bf16[144,128]{1,0:T(8,128)(2,1)S(1)} %get-tuple-element.54), channel_id=1, source_target_pairs={{0,16},{4,20},{8,24},{12,28},{16,0},{20,4},{24,8},{28,12},{1,17},{... | collective-permute-start | bytes 110600 | tf_op jit(solution)/shard_map/ppermute | solution.py:440
  10.3 4.5 %collective-permute-start.3 = (bf16[144,128]{1,0:T(8,128)(2,1)S(1)}, bf16[144,128]{1,0:T(8,128)(2,1)S(1)}, u32[]{:S(2)}, u32[]{:S(2)}) collective-permute-start(bf16[144,128]{1,0:T(8,128)(2,1)S(1)} %get-tuple-element.55), channel_id=1, source_target_pairs={{0,8},{4,12},{8,0},{12,4},{16,24},{20,28},{24,16},{28,20},{1,9},{5... | collective-permute-start | bytes 110600 | tf_op jit(solution)/shard_map/ppermute | solution.py:440
  11.9 4.0 %collective-permute-start.4 = (bf16[144,128]{1,0:T(8,128)(2,1)S(1)}, bf16[144,128]{1,0:T(8,128)(2,1)S(1)}, u32[]{:S(2)}, u32[]{:S(2)}) collective-permute-start(bf16[144,128]{1,0:T(8,128)(2,1)S(1)} %get-tuple-element.56), channel_id=1, source_target_pairs={{0,4},{4,0},{8,12},{12,8},{16,20},{20,16},{24,28},{28,24},{1,5},{5... | collective-permute-start | bytes 110600 | tf_op jit(solution)/shard_map/ppermute | solution.py:440
  14.3 4.0 %collective-permute-start.6 = (bf16[64,128]{1,0:T(8,128)(2,1)S(1)}, bf16[64,128]{1,0:T(8,128)(2,1)S(1)}, u32[]{:S(2)}, u32[]{:S(2)}) collective-permute-start(bf16[64,128]{1,0:T(8,128)(2,1)S(1)} %slice.16), channel_id=1, source_target_pairs={{0,8},{4,12},{8,0},{12,4},{16,24},{20,28},{24,16},{28,20},{1,9},{5... | collective-permute-start | bytes 49160 | tf_op jit(solution)/shard_map/ppermute | solution.py:440
  17.4 5.3 %collective-permute-start.8 = (s16[16,4352]{1,0:T(8,128)(2,1)S(1)}, s16[16,4352]{1,0:T(8,128)(2,1)S(1)}, u32[]{:S(2)}, u32[]{:S(2)}) collective-permute-start(s16[16,4352]{1,0:T(8,128)(2,1)S(1)} %get-tuple-element.72), channel_id=1, source_target_pairs={{0,2},{2,0},{1,3},{3,1},{4,6},{6,4},{5,7},{7,5},{8,10},{10,8},{9,1... | collective-permute-start | bytes 417800 | tf_op jit(solution)/shard_map/ppermute | solution.py:437
  18.3 3.8 %collective-permute-start.7 = (bf16[48,128]{1,0:T(8,128)(2,1)S(1)}, bf16[48,128]{1,0:T(8,128)(2,1)S(1)}, u32[]{:S(2)}, u32[]{:S(2)}) collective-permute-start(bf16[48,128]{1,0:T(8,128)(2,1)S(1)} %pad_maximum_fusion), channel_id=1, source_target_pairs={{0,4},{4,0},{8,12},{12,8},{16,20},{20,16},{24,28},{28,24},{1,5},{5... | collective-permute-start | bytes 36872 | tf_op jit(solution)/shard_map/ppermute | solution.py:440
